TPU v7x, 32 devices: a whole 2x2x4 slice. The times are simulated.
32 devices in a mesh: clu: 16 (over z, y, x), grp: 2 (over core).
Axes of the slice: x: 2, y: 2, z: 4, core: 2. Of those that a mesh axis runs over, the one named last changes fastest.
Arguments:
- embeddings: bfloat16 [4096, 512], P(('clu', 'grp')), may hold values from -60 to 60
- cluster_id: int32 [4096], P(('clu', 'grp')), may hold values from 0 to 63, as said below
- cluster_group: int32 [64], replicated, may hold values from 0 to 15, as said below
Outputs:
- best_similarity: float32 [4096], P(('clu', 'grp'))
Inputs may be any that keep to these rules, and one draw needn't show every extreme that they name: `cluster_id`: on every device's rows, at most 32 rows belong to clusters of one group, and exactly 32 for some group. `cluster_group`: every group is named by exactly 4 clusters.
All inputs are finite; a program needn't handle non-finite values.
Results may differ from a plain program's by a relative error of at most 0.0015.
Values may be sent and summed in bfloat16 or wider, within the bound.
No kernel may reach another device: no remote copies, remote signals or barrier semaphores. Data moves between devices by JAX's collectives and lax.ppermute only.
A program may use at most 64 MiB of HBM per device.

v0:
```python
import jax
import jax.numpy as jnp
from jax import lax
from jax.sharding import PartitionSpec as P


def normalize(embeddings):
    values = embeddings.astype(jnp.float32)
    scale = lax.rsqrt(jnp.sum(values * values, axis=-1, keepdims=True) + 1e-06)
    return (values * scale).astype(jnp.bfloat16)


def tile_max(best, queries, query_cl, query_pos, keys, key_cl, key_pos):
    sims = lax.dot_general(
        queries, keys, (((1,), (1,)), ((), ())), preferred_element_type=jnp.float32
    )
    score = jnp.where(query_cl[:, None] == key_cl[None, :], sims, 0.5 * sims)
    mask = (key_cl[None, :] >= 0) & (key_pos[None, :] < query_pos[:, None])
    return jnp.maximum(best, jnp.max(jnp.where(mask, score, -1.0), axis=1))


def shards(embeddings, cluster_id, cluster_group):
    rows, width = embeddings.shape
    n_clu = lax.axis_size("clu")
    slots = 4 * rows // n_clu
    block = slots * n_clu
    clusters = cluster_group.shape[0]
    unit = normalize(embeddings)
    table = cluster_id[:, None] == jnp.arange(clusters, dtype=jnp.int32)[None, :]
    dest = jnp.sum(jnp.where(table, cluster_group[None, :], 0), axis=1)
    dest_hot = (dest[:, None] == jnp.arange(n_clu, dtype=jnp.int32)[None, :]).astype(jnp.int32)
    position = jnp.sum(jnp.cumsum(dest_hot, axis=0) * dest_hot, axis=1) - 1
    send_units = jnp.zeros((n_clu, slots, width), jnp.bfloat16).at[dest, position].set(unit)
    send_clusters = jnp.full((n_clu, slots), -1, jnp.int32).at[dest, position].set(cluster_id)
    recv_units, recv_clusters = (
        lax.all_to_all(send_units, "clu", split_axis=0, concat_axis=0, tiled=True),
        lax.all_to_all(send_clusters, "clu", split_axis=0, concat_axis=0, tiled=True),
    )
    queries = recv_units.reshape(block, width)
    query_cl = recv_clusters.reshape(block)
    mine = lax.axis_index("grp")
    query_pos = mine * block + jnp.arange(block, dtype=jnp.int32)
    initial = jnp.full((block,), -1.0, jnp.float32)
    keys = lax.all_gather(queries, "grp", axis=0, tiled=True)
    key_cl = lax.all_gather(query_cl, "grp", axis=0, tiled=True)
    count = keys.shape[0]
    key_pos = jnp.arange(count, dtype=jnp.int32)

    def work(carry):
        return tile_max(carry, queries, query_cl, query_pos, keys, key_cl, key_pos)

    best = lax.cond(jnp.int32(0) < mine * block + block, work, lambda carry: carry, initial)
    returned = lax.all_to_all(
        best.reshape(n_clu, slots), "clu", split_axis=0, concat_axis=0, tiled=True
    )
    return returned[dest, position]


def solution(mesh):
    placed = (P(("clu", "grp"), None), P(("clu", "grp")), P())
    return jax.shard_map(
        shards, mesh=mesh, in_specs=placed, out_specs=P(("clu", "grp")), check_vma=False
    )
```

profile of v0, /device:TPU:0, one launch (start us, length us, event | category | flops | bytes accessed | tf_op | source)
XLA Modules:
  0.0 97.4 jit_solution(15044143123242450918)
XLA Ops:
  6.5 0.0 all-gather.3.cloned.1.call-start
  6.5 0.8 select_reduce_fusion.1
  7.3 0.1 fusion.4
  7.4 0.2 reduce_window_sum.11
  7.6 0.2 select_reduce_fusion
  7.8 1.0 %fusion.2 = f32[128]{0:T(128)S(1)} fusion(bf16[128,512]{1,0:T(8,128)(2,1)} %param.5), kind=kLoop, calls=%fused_computation.11 | loop fusion | flops 196480 | bytes 131584 | tf_op jit(solution)/shard_map/reduce_sum | solution.py:9
  8.8 1.0 %fusion.3 = bf16[128,512]{1,0:T(8,128)(2,1)S(1)} fusion(bf16[128,512]{1,0:T(8,128)(2,1)} %param.5, f32[128]{0:T(128)S(1)} %add_rsqrt_fusion), kind=kLoop, calls=%fused_computation.12 | loop fusion | flops 196608 | bytes 262656 | tf_op jit(solution)/shard_map/convert_element_type | solution.py:10
  9.8 7.6 %scatter_fusion.1 = bf16[16,32,512]{2,1,0:T(8,128)(2,1)S(1)} fusion(bf16[16,32,512]{2,1,0:T(8,128)(2,1)S(1)} %broadcast_in_dim.27, s32[128]{0:T(128)S(1)} %get-tuple-element.47, bf16[128,512]{1,0:T(8,128)(2,1)S(1)} %fusion.3), kind=kCustom, calls=%fused_computation.2 | custom fusion | bytes 394240 | tf_op jit(solution)/shard_map/scatter | solution.py:33
  17.4 0.0 copy-start.1
  17.4 23.4 %all_to_all.26 = bf16[16,32,512]{2,1,0:T(8,128)(2,1)} all-to-all(bf16[16,32,512]{2,1,0:T(8,128)(2,1)S(1)} %scatter_fusion.1), channel_id=1, replica_groups=mesh['clu'=16,'grp'=2] {'clu'}, dimensions={0} | all-to-all | bytes 1048576 | tf_op jit(solution)/shard_map/all_to_all | solution.py:36
  40.8 0.0 copy-start
  40.8 0.0 all-gather.3.cloned.1.call-update
  40.8 0.6 broadcast_in_dim.24
  41.4 0.0 copy-done.1
  41.4 19.4 %scatter_fusion = s32[16,32]{1,0:T(8,128)} fusion(s32[16,32]{1,0:T(8,128)} %broadcast_in_dim.24, s32[128]{0:T(128)S(1)} %get-tuple-element.47, s32[128]{0:T(128)S(1)} %copy-done.1), kind=kCustom, calls=%fused_computation.1 | custom fusion | bytes 2560 | tf_op jit(solution)/shard_map/scatter | solution.py:34
  60.8 3.9 %all-to-all-start = ((s32[16,1,32]{2,1,0:T(1,128)}), s32[16,1,32]{2,1,0:T(1,128)S(1)}, u32[]{:S(2)}, u32[]{:S(2)}) async-start(s32[16,1,32]{2,1,0:T(1,128)} %bitcast.5), calls=%async_computation | async-start | bytes 16384 | tf_op jit(solution)/shard_map/all_to_all | solution.py:37
  64.7 7.3 %all-to-all-done = s32[16,1,32]{2,1,0:T(1,128)S(1)} async-done(((s32[16,1,32]{2,1,0:T(1,128)}), s32[16,1,32]{2,1,0:T(1,128)S(1)}, u32[]{:S(2)}, u32[]{:S(2)}) %all-to-all-start) | async-done | bytes 2080 | tf_op jit(solution)/shard_map/all_to_all | solution.py:37
  72.0 0.5 broadcast.183
  72.6 0.6 reduce.7
  73.2 0.1 reshape.83
  73.3 1.8 %all-gather = s32[2,1,512]{2,1,0:T(1,128)S(1)} all-gather(s32[1,1,512]{2,1,0:T(1,128)S(1)} %reshape.83), channel_id=1, replica_groups=mesh['clu'=16,'grp'=2] {'grp'}, dimensions={0}, use_global_device_ids=true | all-gather | bytes 6144 | tf_op jit(solution)/shard_map/all_gather | solution.py:45
  75.0 0.0 all-gather.3.cloned.1.call-done
  75.1 0.0 copy-done
  75.1 3.7 %conditional.1 = (f32[512]{0:T(512)S(1)}) conditional(s32[]{:T(128)} %convert_element_type.12, () %tuple.11, (s32[1024]{0:T(1024)S(1)}, s32[1024]{0:T(1024)S(1)}, s32[]{:T(128)}, s32[512]{0:T(512)S(1)}, s32[16,1,32]{2,1,0:T(1,128)S(1)}, /*index=5*/bf16[512,512]{1,0:T(8,128)(2,1)S(1)}, bf16[1024,512]{1,0:T(8,128)(2,1)}) %tuple.21), branch_computations={%region_6.7_spmd, %region_7.9_spmd} | conditional | flops 540542464 | bytes 1609752 | solution.py:52
  75.1 0.6 broadcast.182
  75.7 0.7 reduce.6
  76.4 0.1 eq.0
  76.5 2.3 %fusion.1 = f32[512]{0:T(512)S(1)} fusion(s32[1024]{0:T(1024)S(1)} %get-tuple-element.25, s32[1024]{0:T(1024)S(1)} %get-tuple-element.26, s32[512]{0:T(512)S(1)} %eq.0, s32[512]{0:T(512)S(1)} %broadcast_add_fusion, pred[1024]{0:T(1024)(128)(4,1)S(1)} %broadcast_compare_fusion, bf16[512,512]{1,0:T(8,128)(2,1)S(1)} %get-tuple-element.30, ...), kind=kOutput, calls=%fused_computation.5 | convolution fusion | flops 540540416 | bytes 1588224 | tf_op jit(solution)/shard_map/cond/branch_1_fun/dot_general | solution.py:14
  78.8 0.1 all_to_all.20
  78.9 9.9 %all_to_all.27 = f32[16,1,32]{2,1,0:T(1,128)S(1)} all-to-all(f32[16,1,32]{2,1,0:T(1,128)S(1)} %all_to_all.20), channel_id=1, replica_groups=mesh['clu'=16,'grp'=2] {'clu'}, dimensions={0} | all-to-all | bytes 4096 | tf_op jit(solution)/shard_map/all_to_all | solution.py:53
  88.7 1.8 %gather_fusion = f32[128]{0:T(128)} fusion(f32[16,32]{1,0:T(8,128)S(1)} %bitcast.42, s32[128]{0:T(128)S(1)} %get-tuple-element.46), kind=kCustom, calls=%fused_computation | custom fusion | bytes 2048 | tf_op jit(solution)/shard_map/gather | solution.py:56
  (8 shorter events, 0.1 us)
Async XLA Ops:
  6.5 68.5 %all-gather.3.cloned.1.call-start = ((), (), s32[]{:S(2)}) async-start(), calls=%async_computation.3 | async-start | bytes 1572864 | tf_op jit(solution)/shard_map/all_gather | solution.py:44
  17.4 24.0 %copy-start.1 = (s32[128]{0:T(128)S(1)}, s32[128]{0:T(128)}, u32[]{:S(2)}) copy-start(s32[128]{0:T(128)} %param.6) | copy-start | bytes 1540
  40.8 34.3 %copy-start = (bf16[16,32,512]{2,1,0:T(8,128)(2,1)S(1)}, bf16[16,32,512]{2,1,0:T(8,128)(2,1)}, u32[]{:S(2)}) copy-start(bf16[16,32,512]{2,1,0:T(8,128)(2,1)} %all_to_all.26) | copy-start | bytes 1572868
  60.8 11.2 %all-to-all-start = ((s32[16,1,32]{2,1,0:T(1,128)}), s32[16,1,32]{2,1,0:T(1,128)S(1)}, u32[]{:S(2)}, u32[]{:S(2)}) async-start(s32[16,1,32]{2,1,0:T(1,128)} %bitcast.5), calls=%async_computation | async-start | bytes 16384 | tf_op jit(solution)/shard_map/all_to_all | solution.py:37
Sparse Core Ops, SparseCore 0:
  40.9 7.3 all-gather.2
where the time goes:
time: 98.1 us; the launch traced here: 97.4 us
  blocking collectives  35 us (36%)
  local copies, waits for them, and re-layouts  30.8 us (31%)
  between operations  13.5 us (14%)
  waiting for transfers between devices  7.3 us (7%)
  other arithmetic  4.58 us (5%)
  starting transfers between devices  3.9 us (4%)
  matrix products  2.28 us (2%)
    all_to_all x1, blocking collectives, shards(): lax.all_to_all(send_units, 'clu', split_axis=0, concat_axis=0, tiled=True)  23.4 us
    scatter x1, local copies, waits for them, and re-layouts, shards(): jnp.full((n_clu, slots), -1, jnp.int32).at[dest, position].set(cluster_id)  19.4 us
    all_to_all x1, blocking collectives, shards(): lax.all_to_all(best.reshape(n_clu, slots), 'clu', split_axis=0, concat_ax...  9.85 us
    scatter x1, local copies, waits for them, and re-layouts, shards(): jnp.zeros((n_clu, slots, width), jnp.bfloat16).at[dest, position].set(unit)  7.57 us
    all_to_all x1, waiting for transfers between devices, shards(): lax.all_to_all(send_clusters, 'clu', split_axis=0, concat_axis=0, tiled=T...  7.27 us
    all_to_all x1, starting transfers between devices, shards(): lax.all_to_all(send_clusters, 'clu', split_axis=0, concat_axis=0, tiled=T...  3.89 us
    dot_general x1, matrix products, tile_max(): lax.dot_general(queries, keys, (((1,), (1,)), ((), ())), preferred_elemen...  2.28 us
  transfers between devices with their start and end apart: 2, of which 1 were waited for; matrix products, arithmetic and copies ran while one was open for 22% of the time, Pallas kernels for 0%

commit v1 on v0

--- a/solution.py
+++ b/solution.py
@@ -1,7 +1,98 @@
+import functools
+
 import jax
 import jax.numpy as jnp
 from jax import lax
+from jax.experimental import pallas as pl
+from jax.experimental.pallas import tpu as pltpu
 from jax.sharding import PartitionSpec as P
+
+AUX = 16
+CHUNK = 4
+DIGIT = 256
+
+
+def pack_kernel(emb_ref, id_ref, out_ref):
+    rows, width = emb_ref.shape
+    values = emb_ref[...].astype(jnp.float32)
+    scale = lax.rsqrt(jnp.sum(values * values, axis=-1, keepdims=True) + 1e-06)
+    out_ref[:rows, :] = (values * scale).astype(jnp.bfloat16)
+    ids = jnp.broadcast_to(id_ref[...], (AUX, rows))
+    row = lax.broadcasted_iota(jnp.int32, (AUX, rows), 0)
+    digits = jnp.where(row == 0, ids % DIGIT, ids // DIGIT)
+    if width > rows:
+        digits = jnp.concatenate([digits, jnp.zeros((AUX, width - rows), jnp.int32)], axis=1)
+    out_ref[rows:, :] = digits.astype(jnp.float32).astype(jnp.bfloat16)
+
+
+def pack(embeddings, cluster_id):
+    rows, width = embeddings.shape
+    return pl.pallas_call(
+        pack_kernel,
+        out_shape=jax.ShapeDtypeStruct((rows + AUX, width), jnp.bfloat16),
+    )(embeddings, cluster_id.reshape(1, rows))
+
+
+def one_hot(digits, clusters):
+    number = digits[0:1].astype(jnp.int32) + DIGIT * digits[1:2].astype(jnp.int32)
+    index = lax.broadcasted_iota(jnp.int32, (clusters, digits.shape[1]), 0)
+    return jnp.where(index == number, 1.0, 0.0).astype(jnp.bfloat16)
+
+
+def weights_table(group_ref, groups):
+    clusters = group_ref.shape[1]
+    index = lax.broadcasted_iota(jnp.int32, (groups, clusters), 0)
+    member = jnp.where(index == group_ref[...], 1.0, 0.0).astype(jnp.bfloat16)
+    same = lax.dot_general(member, member, (((0,), (0,)), ((), ())), preferred_element_type=jnp.float32)
+    a = lax.broadcasted_iota(jnp.int32, (clusters, clusters), 0)
+    b = lax.broadcasted_iota(jnp.int32, (clusters, clusters), 1)
+    return jnp.where(a == b, 1.0, 0.5 * same).astype(jnp.bfloat16)
+
+
+def best_kernel(n_grp, rows, groups, place_ref, all_ref, own_ref, group_ref, out_ref):
+    blocks = all_ref.shape[0]
+    clusters = group_ref.shape[1]
+    n_clu = blocks // n_grp
+    base = place_ref[0]
+    table = weights_table(group_ref, groups)
+    queries = own_ref[:rows, :]
+    own_hot = one_hot(own_ref[rows:, :rows].astype(jnp.float32), clusters)
+    mixed = jnp.dot(table, own_hot, preferred_element_type=jnp.float32).astype(jnp.bfloat16)
+    chunk = min(CHUNK, blocks)
+    best = jnp.full((1, rows), -1.0, jnp.float32)
+    for first in range(0, blocks, chunk):
+        keys = all_ref[first : first + chunk, :rows, :].reshape(chunk * rows, -1)
+        hot = jnp.concatenate(
+            [one_hot(all_ref[d, rows:, :rows].astype(jnp.float32), clusters) for d in range(first, first + chunk)],
+            axis=1,
+        )
+        weight = lax.dot_general(hot, mixed, (((0,), (0,)), ((), ())), preferred_element_type=jnp.float32)
+        sims = lax.dot_general(keys, queries, (((1,), (1,)), ((), ())), preferred_element_type=jnp.float32)
+        local = lax.broadcasted_iota(jnp.int32, (rows, rows), 0)
+        mine = lax.broadcasted_iota(jnp.int32, (rows, rows), 1) + base
+        order = jnp.concatenate(
+            [local + ((d % n_grp) * n_clu + d // n_grp) * rows - mine for d in range(first, first + chunk)], axis=0
+        )
+        score = jnp.where((weight > 0) & (order < 0), weight * sims, -1.0)
+        best = jnp.maximum(best, jnp.max(score, axis=0, keepdims=True))
+    out_ref[...] = best
+
+
+def gathered(n_grp, embeddings, cluster_id, cluster_group):
+    rows, width = embeddings.shape
+    n_clu = lax.axis_size("clu")
+    own = pack(embeddings, cluster_id)
+    every = lax.all_gather(own, ("clu", "grp"), axis=0)
+    base = (lax.axis_index("grp") * n_clu + lax.axis_index("clu")) * rows
+    vmem = pl.BlockSpec(memory_space=pltpu.VMEM)
+    best = pl.pallas_call(
+        functools.partial(best_kernel, n_grp, rows, n_clu),
+        out_shape=jax.ShapeDtypeStruct((1, rows), jnp.float32),
+        in_specs=[pl.BlockSpec(memory_space=pltpu.SMEM), vmem, vmem, vmem],
+        out_specs=vmem,
+        compiler_params=pltpu.CompilerParams(vmem_limit_bytes=40 * 2**20),
+    )(base.reshape(1).astype(jnp.int32), every, own, cluster_group.reshape(1, -1))
+    return best.reshape(rows)
 
 
 def normalize(embeddings):
@@ -19,7 +110,7 @@
     return jnp.maximum(best, jnp.max(jnp.where(mask, score, -1.0), axis=1))
 
 
-def shards(embeddings, cluster_id, cluster_group):
+def routed(embeddings, cluster_id, cluster_group):
     rows, width = embeddings.shape
     n_clu = lax.axis_size("clu")
     slots = 4 * rows // n_clu
@@ -43,13 +134,8 @@
     initial = jnp.full((block,), -1.0, jnp.float32)
     keys = lax.all_gather(queries, "grp", axis=0, tiled=True)
     key_cl = lax.all_gather(query_cl, "grp", axis=0, tiled=True)
-    count = keys.shape[0]
-    key_pos = jnp.arange(count, dtype=jnp.int32)
-
-    def work(carry):
-        return tile_max(carry, queries, query_cl, query_pos, keys, key_cl, key_pos)
-
-    best = lax.cond(jnp.int32(0) < mine * block + block, work, lambda carry: carry, initial)
+    key_pos = jnp.arange(keys.shape[0], dtype=jnp.int32)
+    best = tile_max(initial, queries, query_cl, query_pos, keys, key_cl, key_pos)
     returned = lax.all_to_all(
         best.reshape(n_clu, slots), "clu", split_axis=0, concat_axis=0, tiled=True
     )
@@ -57,6 +143,15 @@
 
 
 def solution(mesh):
+    n_grp = mesh.shape["grp"]
+    devices = n_grp * mesh.shape["clu"]
+
+    def shards(embeddings, cluster_id, cluster_group):
+        rows, width = embeddings.shape
+        if devices * (rows + AUX) * width * 2 > 16 * 2**20:
+            return routed(embeddings, cluster_id, cluster_group)
+        return gathered(n_grp, embeddings, cluster_id, cluster_group)
+
     placed = (P(("clu", "grp"), None), P(("clu", "grp")), P())
     return jax.shard_map(
         shards, mesh=mesh, in_specs=placed, out_specs=P(("clu", "grp")), check_vma=False

time: 98.1 us -> 89.9 us (0.916)
  waiting for transfers between devices: 7.3 us -> 68.4 us
  blocking collectives: 35 us -> 0 us
  local copies, waits for them, and re-layouts: 30.8 us -> 3.9 us
  other arithmetic: 4.58 us -> 0 us
  Pallas kernels: 0 us -> 4.03 us
  starting transfers between devices: 3.9 us -> 0.01 us
  matrix products: 2.28 us -> 0 us
    all_gather x1, waiting for transfers between devices: 0.01 us -> 68.4 us  [gathered(): every = lax.all_gather(own, ('clu', 'grp'), axis=0)]
    all_to_all x2 -> x0, blocking collectives: 33.2 us -> none  [the longest x1 23.4 us: shards(): lax.all_to_all(send_units, 'clu', split_axis=0, concat_axis=0, tiled=True)]
    scatter x2 -> x0, local copies, waits for them, and re-layouts: 27 us -> none  [the longest x1 19.4 us: shards(): jnp.full((n_clu, slots), -1, jnp.int32).at[dest, position].set(cluster_id)]
    all_to_all x1 -> x0, waiting for transfers between devices: 7.27 us -> none  [shards(): lax.all_to_all(send_clusters, 'clu', split_axis=0, concat_axis=0, tiled=T...]
    pallas_call x0 -> x2, Pallas kernels: none -> 4.03 us  [the longest x1 2.36 us: gathered(): pl.pallas_call(functools.partial(best_kernel, n_grp, rows, n_clu), out_sh...]
    all_to_all x1 -> x0, starting transfers between devices: 3.89 us -> none  [shards(): lax.all_to_all(send_clusters, 'clu', split_axis=0, concat_axis=0, tiled=T...]
    unnamed x5 -> x6, local copies, waits for them, and re-layouts: 0.09 us -> 3.9 us
    dot_general x1 -> x0, matrix products: 2.28 us -> none  [tile_max(): lax.dot_general(queries, keys, (((1,), (1,)), ((), ())), preferred_elemen...]
  transfers between devices with their start and end apart: 2 -> 1, of which waited for: 1 -> 1; matrix products, arithmetic and copies ran while one was open for 22% -> 0% of each run, Pallas kernels for 0% -> 0%
where the time goes in v1:
time: 89.9 us; the launch traced here: 89.7 us
  waiting for transfers between devices  68.4 us (76%)
  between operations  13.4 us (15%)
  Pallas kernels  4.03 us (4%)
  local copies, waits for them, and re-layouts  3.9 us (4%)
    all_gather x1, waiting for transfers between devices, gathered(): every = lax.all_gather(own, ('clu', 'grp'), axis=0)  68.4 us
    unnamed x6, local copies, waits for them, and re-layouts  3.9 us
    pallas_call x1, Pallas kernels, gathered(): pl.pallas_call(functools.partial(best_kernel, n_grp, rows, n_clu), out_sh...  2.36 us
  transfers between devices with their start and end apart: 1, of which 1 were waited for; matrix products, arithmetic and copies ran while one was open for 0% of the time, Pallas kernels for 0%

profile of v1, /device:TPU:0, one launch (start us, length us, event | category | flops | bytes accessed | tf_op | source)
XLA Modules:
  0.0 89.7 jit_solution(2062737086886752378)
XLA Ops:
  6.5 0.0 all-gather.3.cloned.1.call-start
  6.5 1.7 %shard_map.37.own_ref = bf16[144,512]{1,0:T(8,128)(2,1)} custom-call(bf16[128,512]{1,0:T(8,128)(2,1)} %emb_ref.1, s32[1,128]{1,0:T(1,128)} %bitcast.7), custom_call_target="tpu_custom_call" | custom-call | tf_op jit(solution)/shard_map/pallas_call | solution.py:30
  8.2 0.0 all-gather.3.cloned.1.call-update
  8.2 68.4 %all-gather.3.cloned.1.call-done = bf16[4608,512]{1,0:T(8,128)(2,1)} async-done(((bf16[144,512]{1,0:T(8,128)(2,1)}), bf16[4608,512]{1,0:T(8,128)(2,1)}) %all-gather.3.cloned.1.call-update) | async-done | bytes 4718608 | tf_op jit(solution)/shard_map/all_gather | solution.py:85
  76.6 0.0 copy-start
  76.6 2.3 %copy-done = bf16[4608,512]{1,0:T(8,128)(2,1)S(1)} copy-done((bf16[4608,512]{1,0:T(8,128)(2,1)S(1)}, bf16[4608,512]{1,0:T(8,128)(2,1)}, u32[]{:S(2)}) %copy-start) | copy-done | bytes 4718616
  79.0 0.0 copy-start.1
  79.0 0.9 %copy-done.1 = bf16[144,512]{1,0:T(8,128)(2,1)S(1)} copy-done((bf16[144,512]{1,0:T(8,128)(2,1)S(1)}, bf16[144,512]{1,0:T(8,128)(2,1)}, u32[]{:S(2)}) %copy-start.1) | copy-done | bytes 147480
  79.9 0.0 copy-start.2
  79.9 0.7 copy-done.2
  80.5 2.4 %shard_map.38 = f32[1,128]{1,0:T(1,128)} custom-call(s32[1]{0:T(128)} %bitcast.place_ref, bf16[32,144,512]{2,1,0:T(8,128)(2,1)S(1)} %bitcast.5, bf16[144,512]{1,0:T(8,128)(2,1)S(1)} %copy-done.1, s32[1,64]{1,0:T(1,128)S(1)} %bitcast.6), custom_call_target="tpu_custom_call" | custom-call | tf_op jit(solution)/shard_map/pallas_call | solution.py:88
Async XLA Ops:
  6.5 70.1 %all-gather.3.cloned.1.call-start = ((), (), s32[]{:S(2)}) async-start(), calls=%async_computation | async-start | bytes 4866048 | tf_op jit(solution)/shard_map/all_gather | solution.py:85
  76.6 2.3 %copy-start = (bf16[4608,512]{1,0:T(8,128)(2,1)S(1)}, bf16[4608,512]{1,0:T(8,128)(2,1)}, u32[]{:S(2)}) copy-start(bf16[4608,512]{1,0:T(8,128)(2,1)} %all-gather.3.cloned.1.call-done) | copy-start | bytes 14155780
  79.0 0.9 %copy-start.1 = (bf16[144,512]{1,0:T(8,128)(2,1)S(1)}, bf16[144,512]{1,0:T(8,128)(2,1)}, u32[]{:S(2)}) copy-start(bf16[144,512]{1,0:T(8,128)(2,1)} %shard_map.37.own_ref) | copy-start | bytes 442372
  79.9 0.7 copy-start.2
Sparse Core Ops, SparseCore 0:
  10.3 66.3 all-gather.2

commit v2 on v0

v2 whole, which is shorter than its diff:
```python
import functools
import math

import jax
import jax.numpy as jnp
from jax import lax
from jax.experimental import pallas as pl
from jax.experimental.pallas import tpu as pltpu
from jax.sharding import PartitionSpec as P

AUX = 16
DIGIT = 256


def pack_kernel(emb_ref, id_ref, out_ref):
    rows, width = emb_ref.shape
    values = emb_ref[...].astype(jnp.float32)
    scale = lax.rsqrt(jnp.sum(values * values, axis=-1, keepdims=True) + 1e-06)
    out_ref[:rows, :] = (values * scale).astype(jnp.bfloat16)
    ids = jnp.broadcast_to(id_ref[...], (AUX, rows))
    row = lax.broadcasted_iota(jnp.int32, (AUX, rows), 0)
    digits = jnp.where(row == 0, ids % DIGIT, jnp.where(row == 1, ids // DIGIT, 1))
    if width > rows:
        digits = jnp.concatenate([digits, jnp.zeros((AUX, width - rows), jnp.int32)], axis=1)
    out_ref[rows:, :] = digits.astype(jnp.float32).astype(jnp.bfloat16)


def pack(embeddings, cluster_id):
    rows, width = embeddings.shape
    return pl.pallas_call(
        pack_kernel,
        out_shape=jax.ShapeDtypeStruct((rows + AUX, width), jnp.bfloat16),
    )(embeddings, cluster_id.reshape(1, rows))


def one_hot(digits, clusters):
    number = digits[0:1].astype(jnp.int32) + DIGIT * digits[1:2].astype(jnp.int32)
    index = lax.broadcasted_iota(jnp.int32, (clusters, digits.shape[1]), 0)
    return jnp.where((index == number) & (digits[2:3] > 0), 1.0, 0.0).astype(jnp.bfloat16)


def weights_table(group_ref, groups):
    clusters = group_ref.shape[1]
    index = lax.broadcasted_iota(jnp.int32, (groups, clusters), 0)
    member = jnp.where(index == group_ref[...], 1.0, 0.0).astype(jnp.bfloat16)
    same = lax.dot_general(member, member, (((0,), (0,)), ((), ())), preferred_element_type=jnp.float32)
    a = lax.broadcasted_iota(jnp.int32, (clusters, clusters), 0)
    b = lax.broadcasted_iota(jnp.int32, (clusters, clusters), 1)
    return jnp.where(a == b, 1.0, 0.5 * same).astype(jnp.bfloat16)


def dot_t(a, b):
    return lax.dot_general(a, b, (((1,), (1,)), ((), ())), preferred_element_type=jnp.float32)


def dot_0(a, b):
    return lax.dot_general(a, b, (((0,), (0,)), ((), ())), preferred_element_type=jnp.float32)


def best_kernel(n_plane, n_line, groups, order_ref, group_ref, *refs):
    blocks = refs[: n_plane + n_line]
    outs = refs[n_plane + n_line :]
    rows = blocks[0].shape[0] - AUX
    clusters = group_ref.shape[1]
    table = weights_table(group_ref, groups)
    hots = [one_hot(b[rows:, :rows].astype(jnp.float32), clusters) for b in blocks]
    plane_hot = jnp.concatenate(hots[:n_plane], axis=1)
    plane = jnp.concatenate([b[:rows, :] for b in blocks[:n_plane]], axis=0)
    plane_mix = jnp.dot(table, plane_hot, preferred_element_type=jnp.float32).astype(jnp.bfloat16)

    def scored(weight, sims):
        return jnp.where(weight > 0, weight * sims, -1.0)

    def column_max(score):
        return jnp.max(score, axis=0, keepdims=True)

    def part(score, i):
        return score[i * rows : (i + 1) * rows, :]

    own = blocks[0][:rows, :]
    score = scored(dot_0(plane_hot, plane_mix[:, :rows]), dot_t(plane, own))
    k = lax.broadcasted_iota(jnp.int32, (rows, rows), 0)
    q = lax.broadcasted_iota(jnp.int32, (rows, rows), 1)
    best = column_max(jnp.where(k < q, part(score, 0), -1.0))
    for i in range(1, n_plane):
        best = jnp.maximum(best, jnp.where(order_ref[i] < order_ref[0], column_max(part(score, i)), -1.0))
    outs[0][...] = best
    back = [jnp.full((1, rows), -1.0, jnp.float32) for _ in range(n_plane)]
    for j in range(n_line):
        line = blocks[n_plane + j][:rows, :]
        line_hot = hots[n_plane + j]
        line_order = order_ref[n_plane + j]
        score = scored(dot_0(plane_hot, jnp.dot(table, line_hot, preferred_element_type=jnp.float32).astype(jnp.bfloat16)), dot_t(plane, line))
        best = jnp.full((1, rows), -1.0, jnp.float32)
        for i in range(n_plane):
            best = jnp.maximum(best, jnp.where(order_ref[i] < line_order, column_max(part(score, i)), -1.0))
        outs[n_plane + j][...] = best
        score = column_max(scored(dot_0(line_hot, plane_mix), dot_t(line, plane)))
        for i in range(n_plane):
            mine = score[:, i * rows : (i + 1) * rows]
            back[i] = jnp.maximum(back[i], jnp.where(line_order < order_ref[i], mine, -1.0))
    outs[0][...] = jnp.maximum(outs[0][...], back[0])
    for i in range(1, n_plane):
        outs[i][...] = back[i]


def shifted(i, s, n):
    return i ^ s if n & (n - 1) == 0 else (i + s) % n


class Plan:
    def __init__(self, n_clu, n_grp):
        self.n_clu, self.n_grp = n_clu, n_grp
        target = math.sqrt(n_clu * n_grp)
        wide = min(a for a in range(1, n_clu + 1) if n_clu % a == 0 and (a * n_grp >= target or a == n_clu))
        length = n_clu // wide
        self.plane, self.line = [], []
        for s in range(wide):
            for t in range(n_grp):
                if s or t:
                    self.plane.append({
                        (z * wide + a) * n_grp + g: (z * wide + shifted(a, s, wide)) * n_grp + shifted(g, t, n_grp)
                        for z in range(length) for a in range(wide) for g in range(n_grp)
                    })
        for s in range(1, length // 2 + 1):
            pairs = [((z + s) % length, z) for z in range(length)]
            if 2 * s == length:
                pairs = [(z + s, z) if z % 2 == 0 else (z, z + s) for z in range(s)]
            self.line.append({
                (to * wide + a) * n_grp + g: (at * wide + a) * n_grp + g
                for to, at in pairs for a in range(wide) for g in range(n_grp)
            })

    def table(self):
        n = self.n_clu * self.n_grp
        rank = [(d % self.n_grp) * self.n_clu + d // self.n_grp for d in range(n)]
        rows = [[rank[d]] + [rank[m[d]] if d in m else -1 for m in self.plane + self.line] for d in range(n)]
        return jnp.array(rows, jnp.int32)


def send(x, mapping):
    return lax.ppermute(x, ("clu", "grp"), [(at, to) for to, at in mapping.items()])


def send_back(x, mapping):
    return lax.ppermute(x, ("clu", "grp"), list(mapping.items()))


def solution(mesh):
    n_clu, n_grp = mesh.shape["clu"], mesh.shape["grp"]
    plan = Plan(n_clu, n_grp)
    n_plane, n_line = 1 + len(plan.plane), len(plan.line)

    def shards(embeddings, cluster_id, cluster_group):
        rows = embeddings.shape[0]
        own = pack(embeddings, cluster_id)
        line = [send(own, m) for m in plan.line]
        plane = [own] + [send(own, m) for m in plan.plane]
        device = lax.axis_index("clu") * n_grp + lax.axis_index("grp")
        order = lax.dynamic_index_in_dim(plan.table(), device, 0, keepdims=False)
        vmem = pl.BlockSpec(memory_space=pltpu.VMEM)
        count = n_plane + n_line
        best = pl.pallas_call(
            functools.partial(best_kernel, n_plane, n_line, n_clu),
            out_shape=[jax.ShapeDtypeStruct((1, rows), jnp.float32)] * count,
            in_specs=[pl.BlockSpec(memory_space=pltpu.SMEM)] + [vmem] * (1 + count),
            out_specs=[vmem] * count,
            compiler_params=pltpu.CompilerParams(vmem_limit_bytes=48 * 2**20),
        )(order, cluster_group.reshape(1, -1), *plane, *line)
        found = [best[0]]
        for x, m in zip(best[1:], plan.plane + plan.line):
            back = send_back(x, m)
            if len(m) < n_clu * n_grp:
                got = jnp.isin(device, jnp.array(sorted(m.values()), jnp.int32))
                back = jnp.where(got, back, -1.0)
            found.append(back)
        return functools.reduce(jnp.maximum, found).reshape(rows)

    placed = (P(("clu", "grp"), None), P(("clu", "grp")), P())
    return jax.shard_map(
        shards, mesh=mesh, in_specs=placed, out_specs=P(("clu", "grp")), check_vma=False
    )
```

time: 98.1 us -> 46.1 us (0.47)
  blocking collectives: 35 us -> 0 us
  local copies, waits for them, and re-layouts: 30.8 us -> 1.61 us
  starting transfers between devices: 3.9 us -> 23.5 us
  between operations: 13.5 us -> 0.07 us
  waiting for transfers between devices: 7.3 us -> 14.3 us
  Pallas kernels: 0 us -> 4.51 us
  other arithmetic: 4.58 us -> 1.92 us
  matrix products: 2.28 us -> 0 us
    all_to_all x2 -> x0, blocking collectives: 33.2 us -> none  [the longest x1 23.4 us: shards(): lax.all_to_all(send_units, 'clu', split_axis=0, concat_axis=0, tiled=True)]
    scatter x2 -> x0, local copies, waits for them, and re-layouts: 27 us -> none  [the longest x1 19.4 us: shards(): jnp.full((n_clu, slots), -1, jnp.int32).at[dest, position].set(cluster_id)]
    ppermute x0 -> x18, starting transfers between devices: none -> 23.5 us  [the longest x9 13 us: send(): lax.ppermute(x, ('clu', 'grp'), [(at, to) for to, at in mapping.items()])]
    ppermute x0 -> x18, waiting for transfers between devices: none -> 14.3 us  [the longest x9 10 us: send(): lax.ppermute(x, ('clu', 'grp'), [(at, to) for to, at in mapping.items()])]
    all_to_all x1 -> x0, waiting for transfers between devices: 7.27 us -> none  [shards(): lax.all_to_all(send_clusters, 'clu', split_axis=0, concat_axis=0, tiled=T...]
    pallas_call x0 -> x2, Pallas kernels: none -> 4.51 us  [the longest x1 2.84 us: shards(): pl.pallas_call(functools.partial(best_kernel, n_plane, n_line, n_clu), ou...]
    all_to_all x1 -> x0, starting transfers between devices: 3.89 us -> none  [shards(): lax.all_to_all(send_clusters, 'clu', split_axis=0, concat_axis=0, tiled=T...]
    dot_general x1 -> x0, matrix products: 2.28 us -> none  [tile_max(): lax.dot_general(queries, keys, (((1,), (1,)), ((), ())), preferred_elemen...]
  transfers between devices with their start and end apart: 2 -> 18, of which waited for: 1 -> 7; matrix products, arithmetic and copies ran while one was open for 22% -> 3% of each run, Pallas kernels for 0% -> 0%
where the time goes in v2:
time: 46.1 us; the launch traced here: 45.9 us
  starting transfers between devices  23.5 us (51%)
  waiting for transfers between devices  14.3 us (31%)
  Pallas kernels  4.51 us (10%)
  other arithmetic  1.92 us (4%)
  local copies, waits for them, and re-layouts  1.61 us (3%)
    ppermute x9, starting transfers between devices, send(): lax.ppermute(x, ('clu', 'grp'), [(at, to) for to, at in mapping.items()])  13 us
    ppermute x9, starting transfers between devices, send_back(): return lax.ppermute(x, ('clu', 'grp'), list(mapping.items()))  10.5 us
    ppermute x9, waiting for transfers between devices, send(): lax.ppermute(x, ('clu', 'grp'), [(at, to) for to, at in mapping.items()])  10 us
    ppermute x9, waiting for transfers between devices, send_back(): return lax.ppermute(x, ('clu', 'grp'), list(mapping.items()))  4.31 us
    pallas_call x1, Pallas kernels, shards(): pl.pallas_call(functools.partial(best_kernel, n_plane, n_line, n_clu), ou...  2.84 us
    pallas_call x1, Pallas kernels, pack(): pl.pallas_call(pack_kernel, out_shape=jax.ShapeDtypeStruct((rows + AUX, w...  1.67 us
    reshape x1, other arithmetic, shards(): return functools.reduce(jnp.maximum, found).reshape(rows)  1.21 us
  transfers between devices with their start and end apart: 18, of which 7 were waited for; matrix products, arithmetic and copies ran while one was open for 3% of the time, Pallas kernels for 0%

profile of v2, /device:TPU:0, one launch (start us, length us, event | category | flops | bytes accessed | tf_op | source)
XLA Modules:
  0.0 45.9 jit_solution(13558403070691558333)
XLA Ops:
  0.0 1.7 %shard_map.55.refs_0_ = bf16[144,512]{1,0:T(8,128)(2,1)} custom-call(bf16[128,512]{1,0:T(8,128)(2,1)} %emb_ref.1, s32[1,128]{1,0:T(1,128)} %bitcast.7), custom_call_target="tpu_custom_call" | custom-call | tf_op jit(solution)/shard_map/pallas_call | solution.py:30
  1.7 5.9 %collective-permute-start.8 = (bf16[144,512]{1,0:T(8,128)(2,1)}, bf16[144,512]{1,0:T(8,128)(2,1)S(1)}, u32[]{:S(2)}, u32[]{:S(2)}) collective-permute-start(bf16[144,512]{1,0:T(8,128)(2,1)} %shard_map.55.refs_0_), channel_id=1, source_target_pairs={{0,16},{1,17},{2,18},{3,19},{4,20},{5,21},{6,22},{7,23},{24,8},{25... | collective-permute-start | bytes 442376 | tf_op jit(solution)/shard_map/ppermute | solution.py:142
  7.6 0.1 collective-permute-start.7
  7.7 1.7 %collective-permute-start.6 = (bf16[144,512]{1,0:T(8,128)(2,1)}, bf16[144,512]{1,0:T(8,128)(2,1)S(1)}, u32[]{:S(2)}, u32[]{:S(2)}) collective-permute-start(bf16[144,512]{1,0:T(8,128)(2,1)} %shard_map.55.refs_0_), channel_id=1, source_target_pairs={{7,0},{6,1},{5,2},{4,3},{3,4},{2,5},{1,6},{0,7},{15,8},{14,9},{13,... | collective-permute-start | bytes 442376 | tf_op jit(solution)/shard_map/ppermute | solution.py:142
  9.4 0.9 %collective-permute-start.5 = (bf16[144,512]{1,0:T(8,128)(2,1)}, bf16[144,512]{1,0:T(8,128)(2,1)S(1)}, u32[]{:S(2)}, u32[]{:S(2)}) collective-permute-start(bf16[144,512]{1,0:T(8,128)(2,1)} %shard_map.55.refs_0_), channel_id=1, source_target_pairs={{6,0},{7,1},{4,2},{5,3},{2,4},{3,5},{0,6},{1,7},{14,8},{15,9},{12,... | collective-permute-start | bytes 442376 | tf_op jit(solution)/shard_map/ppermute | solution.py:142
  10.3 1.4 %collective-permute-start.4 = (bf16[144,512]{1,0:T(8,128)(2,1)}, bf16[144,512]{1,0:T(8,128)(2,1)S(1)}, u32[]{:S(2)}, u32[]{:S(2)}) collective-permute-start(bf16[144,512]{1,0:T(8,128)(2,1)} %shard_map.55.refs_0_), channel_id=1, source_target_pairs={{5,0},{4,1},{7,2},{6,3},{1,4},{0,5},{3,6},{2,7},{13,8},{12,9},{15,... | collective-permute-start | bytes 442376 | tf_op jit(solution)/shard_map/ppermute | solution.py:142
  11.6 0.5 %collective-permute-done.8.refs_9_ = bf16[144,512]{1,0:T(8,128)(2,1)S(1)} collective-permute-done((bf16[144,512]{1,0:T(8,128)(2,1)}, bf16[144,512]{1,0:T(8,128)(2,1)S(1)}, u32[]{:S(2)}, u32[]{:S(2)}) %collective-permute-start.8) | collective-permute-done | bytes 147488 | tf_op jit(solution)/shard_map/ppermute | solution.py:142
  12.2 1.5 %collective-permute-start.3 = (bf16[144,512]{1,0:T(8,128)(2,1)}, bf16[144,512]{1,0:T(8,128)(2,1)S(1)}, u32[]{:S(2)}, u32[]{:S(2)}) collective-permute-start(bf16[144,512]{1,0:T(8,128)(2,1)} %shard_map.55.refs_0_), channel_id=1, source_target_pairs={{4,0},{5,1},{6,2},{7,3},{0,4},{1,5},{2,6},{3,7},{12,8},{13,9},{14,... | collective-permute-start | bytes 442376 | tf_op jit(solution)/shard_map/ppermute | solution.py:142
  13.7 2.2 %collective-permute-done.7.refs_8_ = bf16[144,512]{1,0:T(8,128)(2,1)S(1)} collective-permute-done((bf16[144,512]{1,0:T(8,128)(2,1)}, bf16[144,512]{1,0:T(8,128)(2,1)S(1)}, u32[]{:S(2)}, u32[]{:S(2)}) %collective-permute-start.7) | collective-permute-done | bytes 147488 | tf_op jit(solution)/shard_map/ppermute | solution.py:142
  15.9 0.3 collective-permute-start.2
  16.2 0.0 collective-permute-done.6.refs_7_
  16.2 1.2 %collective-permute-start.1 = (bf16[144,512]{1,0:T(8,128)(2,1)}, bf16[144,512]{1,0:T(8,128)(2,1)S(1)}, u32[]{:S(2)}, u32[]{:S(2)}) collective-permute-start(bf16[144,512]{1,0:T(8,128)(2,1)} %shard_map.55.refs_0_), channel_id=1, source_target_pairs={{2,0},{3,1},{0,2},{1,3},{6,4},{7,5},{4,6},{5,7},{10,8},{11,9},{8,1... | collective-permute-start | bytes 442376 | tf_op jit(solution)/shard_map/ppermute | solution.py:142
  17.4 0.9 %collective-permute-done.5.refs_6_ = bf16[144,512]{1,0:T(8,128)(2,1)S(1)} collective-permute-done((bf16[144,512]{1,0:T(8,128)(2,1)}, bf16[144,512]{1,0:T(8,128)(2,1)S(1)}, u32[]{:S(2)}, u32[]{:S(2)}) %collective-permute-start.5) | collective-permute-done | bytes 147488 | tf_op jit(solution)/shard_map/ppermute | solution.py:142
  18.3 0.0 collective-permute-start
  18.3 0.7 %dynamic-slice_bitcast_fusion.order_ref = s32[10]{0:T(128)S(1)} fusion(s32[32,10]{1,0:T(8,128)} %constant.25.clone, s32[]{:T(128)S(6)} %select_n.12), kind=kLoop, calls=%fused_computation.4 | loop fusion | bytes 84 | tf_op jit(solution)/shard_map/jit(dynamic_index_in_dim)/squeeze | solution.py:160
  19.0 0.0 copy-start.1
  19.0 2.3 %collective-permute-done.4.refs_5_ = bf16[144,512]{1,0:T(8,128)(2,1)S(1)} collective-permute-done((bf16[144,512]{1,0:T(8,128)(2,1)}, bf16[144,512]{1,0:T(8,128)(2,1)S(1)}, u32[]{:S(2)}, u32[]{:S(2)}) %collective-permute-start.4) | collective-permute-done | bytes 147488 | tf_op jit(solution)/shard_map/ppermute | solution.py:142
  21.3 3.2 %collective-permute-done.3.refs_4_ = bf16[144,512]{1,0:T(8,128)(2,1)S(1)} collective-permute-done((bf16[144,512]{1,0:T(8,128)(2,1)}, bf16[144,512]{1,0:T(8,128)(2,1)S(1)}, u32[]{:S(2)}, u32[]{:S(2)}) %collective-permute-start.3) | collective-permute-done | bytes 147488 | tf_op jit(solution)/shard_map/ppermute | solution.py:142
  24.5 0.0 collective-permute-done.2.refs_3_
  24.5 0.9 %collective-permute-done.1.refs_2_ = bf16[144,512]{1,0:T(8,128)(2,1)S(1)} collective-permute-done((bf16[144,512]{1,0:T(8,128)(2,1)}, bf16[144,512]{1,0:T(8,128)(2,1)S(1)}, u32[]{:S(2)}, u32[]{:S(2)}) %collective-permute-start.1) | collective-permute-done | bytes 147488 | tf_op jit(solution)/shard_map/ppermute | solution.py:142
  25.4 0.0 collective-permute-done.refs_1_
  25.4 0.0 copy-done.1
  25.4 0.0 copy-start
  25.4 0.9 %copy-done = bf16[144,512]{1,0:T(8,128)(2,1)S(1)} copy-done((bf16[144,512]{1,0:T(8,128)(2,1)S(1)}, bf16[144,512]{1,0:T(8,128)(2,1)}, u32[]{:S(2)}) %copy-start) | copy-done | bytes 147480
  26.3 2.8 %shard_map.56 = (f32[1,128]{1,0:T(1,128)S(1)}, f32[1,128]{1,0:T(1,128)S(1)}, f32[1,128]{1,0:T(1,128)S(1)}, f32[1,128]{1,0:T(1,128)S(1)}, f32[1,128]{1,0:T(1,128)...) custom-call(s32[10]{0:T(128)S(1)} %dynamic-slice_bitcast_fusion.orde, ...), custom_call_target="tpu_custom_call" | custom-call | tf_op jit(solution)/shard_map/pallas_call | solution.py:163
  29.2 0.1 collective-permute-start.9
  29.3 0.7 %collective-permute-start.10 = (f32[1,128]{1,0:T(1,128)S(1)}, f32[1,128]{1,0:T(1,128)S(1)}, u32[]{:S(2)}, u32[]{:S(2)}) collective-permute-start(f32[1,128]{1,0:T(1,128)S(1)} %get-tuple-element.17), channel_id=1, source_target_pairs={{0,2},{1,3},{2,0},{3,1},{4,6},{5,7},{6,4},{7,5},{8,10},{9,11},{10,... | collective-permute-start | bytes 1544 | tf_op jit(solution)/shard_map/ppermute | solution.py:146
  30.0 1.1 %collective-permute-start.11 = (f32[1,128]{1,0:T(1,128)S(1)}, f32[1,128]{1,0:T(1,128)S(1)}, u32[]{:S(2)}, u32[]{:S(2)}) collective-permute-start(f32[1,128]{1,0:T(1,128)S(1)} %get-tuple-element.18), channel_id=1, source_target_pairs={{0,3},{1,2},{2,1},{3,0},{4,7},{5,6},{6,5},{7,4},{8,11},{9,10},{10,... | collective-permute-start | bytes 1544 | tf_op jit(solution)/shard_map/ppermute | solution.py:146
  31.1 1.5 %collective-permute-start.12 = (f32[1,128]{1,0:T(1,128)S(1)}, f32[1,128]{1,0:T(1,128)S(1)}, u32[]{:S(2)}, u32[]{:S(2)}) collective-permute-start(f32[1,128]{1,0:T(1,128)S(1)} %get-tuple-element.19), channel_id=1, source_target_pairs={{0,4},{1,5},{2,6},{3,7},{4,0},{5,1},{6,2},{7,3},{8,12},{9,13},{10,... | collective-permute-start | bytes 1544 | tf_op jit(solution)/shard_map/ppermute | solution.py:146
  32.6 0.2 collective-permute-start.13
  32.8 0.0 collective-permute-done.9
  32.8 1.6 %collective-permute-start.14 = (f32[1,128]{1,0:T(1,128)S(1)}, f32[1,128]{1,0:T(1,128)S(1)}, u32[]{:S(2)}, u32[]{:S(2)}) collective-permute-start(f32[1,128]{1,0:T(1,128)S(1)} %get-tuple-element.21), channel_id=1, source_target_pairs={{0,6},{1,7},{2,4},{3,5},{4,2},{5,3},{6,0},{7,1},{8,14},{9,15},{10,... | collective-permute-start | bytes 1544 | tf_op jit(solution)/shard_map/ppermute | solution.py:146
  34.4 0.0 collective-permute-done.10
  34.4 1.1 %collective-permute-start.15 = (f32[1,128]{1,0:T(1,128)S(1)}, f32[1,128]{1,0:T(1,128)S(1)}, u32[]{:S(2)}, u32[]{:S(2)}) collective-permute-start(f32[1,128]{1,0:T(1,128)S(1)} %get-tuple-element.22), channel_id=1, source_target_pairs={{0,7},{1,6},{2,5},{3,4},{4,3},{5,2},{6,1},{7,0},{8,15},{9,14},{10,... | collective-permute-start | bytes 1544 | tf_op jit(solution)/shard_map/ppermute | solution.py:146
  35.5 0.0 collective-permute-done.11
  35.5 0.0 copy-start.2
  35.5 2.9 %collective-permute-start.16 = (f32[1,128]{1,0:T(1,128)S(1)}, f32[1,128]{1,0:T(1,128)S(1)}, u32[]{:S(2)}, u32[]{:S(2)}) collective-permute-start(f32[1,128]{1,0:T(1,128)S(1)} %get-tuple-element.23), channel_id=1, source_target_pairs={{8,0},{9,1},{10,2},{11,3},{12,4},{13,5},{14,6},{15,7},{16,8},{17,9... | collective-permute-start | bytes 1544 | tf_op jit(solution)/shard_map/ppermute | solution.py:146
  38.4 0.0 collective-permute-done.12
  38.4 1.3 %collective-permute-start.17 = (f32[1,128]{1,0:T(1,128)S(1)}, f32[1,128]{1,0:T(1,128)S(1)}, u32[]{:S(2)}, u32[]{:S(2)}) collective-permute-start(f32[1,128]{1,0:T(1,128)S(1)} %get-tuple-element.24), channel_id=1, source_target_pairs={{16,0},{17,1},{18,2},{19,3},{20,4},{21,5},{22,6},{23,7},{8,24},{9,... | collective-permute-start | bytes 1544 | tf_op jit(solution)/shard_map/ppermute | solution.py:146
  39.7 0.0 copy-done.2
  39.7 0.7 %compare_reduce_fusion = pred[]{:T(512)} fusion(s32[16]{0:T(128)S(1)} %copy-done.2, s32[]{:T(128)S(6)} %add.7), kind=kLoop, calls=%fused_computation | loop fusion | flops 31 | bytes 69 | tf_op jit(solution)/shard_map/jit(_in1d)/reduce_or | solution.py:174
  40.4 0.0 collective-permute-done.13
  40.4 0.0 collective-permute-done.14
  40.4 0.0 collective-permute-done.15
  40.4 0.0 collective-permute-done.16
  40.4 4.3 %collective-permute-done.17 = f32[1,128]{1,0:T(1,128)S(1)} collective-permute-done((f32[1,128]{1,0:T(1,128)S(1)}, f32[1,128]{1,0:T(1,128)S(1)}, u32[]{:S(2)}, u32[]{:S(2)}) %collective-permute-start.17) | collective-permute-done | bytes 544 | tf_op jit(solution)/shard_map/ppermute | solution.py:146
  44.7 1.2 %fusion.1 = f32[128]{0:T(128)} fusion(f32[1,128]{1,0:T(1,128)S(1)} %collective-permute-done.17, pred[]{:T(512)} %compare_reduce_fusion, f32[1,128]{1,0:T(1,128)S(1)} %collective-permute-done.16, f32[1,128]{1,0:T(1,128)S(1)} %collective-permute-done.15, f32[1,128]{1,0:T(1,128)S(1)} %collective-permute-done.14, f32[1,128]{1,0:T(1,128)S(1)} %collective-permute-done.13, ...), kind=kLoop, calls=%fused_computation.3 | loop fusion | flops 1280 | bytes 5633 | tf_op jit(solution)/shard_map/reshape | solution.py:177
Async XLA Ops:
  1.7 10.5 %collective-permute-start.8 = (bf16[144,512]{1,0:T(8,128)(2,1)}, bf16[144,512]{1,0:T(8,128)(2,1)S(1)}, u32[]{:S(2)}, u32[]{:S(2)}) collective-permute-start(bf16[144,512]{1,0:T(8,128)(2,1)} %shard_map.55.refs_0_), channel_id=1, source_target_pairs={{0,16},{1,17},{2,18},{3,19},{4,20},{5,21},{6,22},{7,23},{24,8},{25... | collective-permute-start | bytes 442376 | tf_op jit(solution)/shard_map/ppermute | solution.py:142
  7.6 8.3 %collective-permute-start.7 = (bf16[144,512]{1,0:T(8,128)(2,1)}, bf16[144,512]{1,0:T(8,128)(2,1)S(1)}, u32[]{:S(2)}, u32[]{:S(2)}) collective-permute-start(bf16[144,512]{1,0:T(8,128)(2,1)} %shard_map.55.refs_0_), channel_id=1, source_target_pairs={{0,8},{1,9},{2,10},{3,11},{4,12},{5,13},{6,14},{7,15},{8,16},{9,17... | collective-permute-start | bytes 442376 | tf_op jit(solution)/shard_map/ppermute | solution.py:142
  7.7 8.5 %collective-permute-start.6 = (bf16[144,512]{1,0:T(8,128)(2,1)}, bf16[144,512]{1,0:T(8,128)(2,1)S(1)}, u32[]{:S(2)}, u32[]{:S(2)}) collective-permute-start(bf16[144,512]{1,0:T(8,128)(2,1)} %shard_map.55.refs_0_), channel_id=1, source_target_pairs={{7,0},{6,1},{5,2},{4,3},{3,4},{2,5},{1,6},{0,7},{15,8},{14,9},{13,... | collective-permute-start | bytes 442376 | tf_op jit(solution)/shard_map/ppermute | solution.py:142
  9.4 8.9 %collective-permute-start.5 = (bf16[144,512]{1,0:T(8,128)(2,1)}, bf16[144,512]{1,0:T(8,128)(2,1)S(1)}, u32[]{:S(2)}, u32[]{:S(2)}) collective-permute-start(bf16[144,512]{1,0:T(8,128)(2,1)} %shard_map.55.refs_0_), channel_id=1, source_target_pairs={{6,0},{7,1},{4,2},{5,3},{2,4},{3,5},{0,6},{1,7},{14,8},{15,9},{12,... | collective-permute-start | bytes 442376 | tf_op jit(solution)/shard_map/ppermute | solution.py:142
  10.3 11.0 %collective-permute-start.4 = (bf16[144,512]{1,0:T(8,128)(2,1)}, bf16[144,512]{1,0:T(8,128)(2,1)S(1)}, u32[]{:S(2)}, u32[]{:S(2)}) collective-permute-start(bf16[144,512]{1,0:T(8,128)(2,1)} %shard_map.55.refs_0_), channel_id=1, source_target_pairs={{5,0},{4,1},{7,2},{6,3},{1,4},{0,5},{3,6},{2,7},{13,8},{12,9},{15,... | collective-permute-start | bytes 442376 | tf_op jit(solution)/shard_map/ppermute | solution.py:142
  12.2 12.3 %collective-permute-start.3 = (bf16[144,512]{1,0:T(8,128)(2,1)}, bf16[144,512]{1,0:T(8,128)(2,1)S(1)}, u32[]{:S(2)}, u32[]{:S(2)}) collective-permute-start(bf16[144,512]{1,0:T(8,128)(2,1)} %shard_map.55.refs_0_), channel_id=1, source_target_pairs={{4,0},{5,1},{6,2},{7,3},{0,4},{1,5},{2,6},{3,7},{12,8},{13,9},{14,... | collective-permute-start | bytes 442376 | tf_op jit(solution)/shard_map/ppermute | solution.py:142
  15.9 8.6 %collective-permute-start.2 = (bf16[144,512]{1,0:T(8,128)(2,1)}, bf16[144,512]{1,0:T(8,128)(2,1)S(1)}, u32[]{:S(2)}, u32[]{:S(2)}) collective-permute-start(bf16[144,512]{1,0:T(8,128)(2,1)} %shard_map.55.refs_0_), channel_id=1, source_target_pairs={{3,0},{2,1},{1,2},{0,3},{7,4},{6,5},{5,6},{4,7},{11,8},{10,9},{9,1... | collective-permute-start | bytes 442376 | tf_op jit(solution)/shard_map/ppermute | solution.py:142
  16.2 9.2 %collective-permute-start.1 = (bf16[144,512]{1,0:T(8,128)(2,1)}, bf16[144,512]{1,0:T(8,128)(2,1)S(1)}, u32[]{:S(2)}, u32[]{:S(2)}) collective-permute-start(bf16[144,512]{1,0:T(8,128)(2,1)} %shard_map.55.refs_0_), channel_id=1, source_target_pairs={{2,0},{3,1},{0,2},{1,3},{6,4},{7,5},{4,6},{5,7},{10,8},{11,9},{8,1... | collective-permute-start | bytes 442376 | tf_op jit(solution)/shard_map/ppermute | solution.py:142
  18.3 7.1 %collective-permute-start = (bf16[144,512]{1,0:T(8,128)(2,1)}, bf16[144,512]{1,0:T(8,128)(2,1)S(1)}, u32[]{:S(2)}, u32[]{:S(2)}) collective-permute-start(bf16[144,512]{1,0:T(8,128)(2,1)} %shard_map.55.refs_0_), channel_id=1, source_target_pairs={{1,0},{0,1},{3,2},{2,3},{5,4},{4,5},{7,6},{6,7},{9,8},{8,9},{11,10... | collective-permute-start | bytes 442376 | tf_op jit(solution)/shard_map/ppermute | solution.py:142
  19.0 6.4 %copy-start.1 = (s32[64]{0:T(128)S(1)}, s32[64]{0:T(128)}, u32[]{:S(2)}) copy-start(s32[64]{0:T(128)} %param.7) | copy-start | bytes 772
  25.4 0.9 %copy-start = (bf16[144,512]{1,0:T(8,128)(2,1)S(1)}, bf16[144,512]{1,0:T(8,128)(2,1)}, u32[]{:S(2)}) copy-start(bf16[144,512]{1,0:T(8,128)(2,1)} %shard_map.55.refs_0_) | copy-start | bytes 442372
  29.2 3.6 %collective-permute-start.9 = (f32[1,128]{1,0:T(1,128)S(1)}, f32[1,128]{1,0:T(1,128)S(1)}, u32[]{:S(2)}, u32[]{:S(2)}) collective-permute-start(f32[1,128]{1,0:T(1,128)S(1)} %get-tuple-element.16), channel_id=1, source_target_pairs={{0,1},{1,0},{2,3},{3,2},{4,5},{5,4},{6,7},{7,6},{8,9},{9,8},{10,11... | collective-permute-start | bytes 1544 | tf_op jit(solution)/shard_map/ppermute | solution.py:146
  29.3 5.1 %collective-permute-start.10 = (f32[1,128]{1,0:T(1,128)S(1)}, f32[1,128]{1,0:T(1,128)S(1)}, u32[]{:S(2)}, u32[]{:S(2)}) collective-permute-start(f32[1,128]{1,0:T(1,128)S(1)} %get-tuple-element.17), channel_id=1, source_target_pairs={{0,2},{1,3},{2,0},{3,1},{4,6},{5,7},{6,4},{7,5},{8,10},{9,11},{10,... | collective-permute-start | bytes 1544 | tf_op jit(solution)/shard_map/ppermute | solution.py:146
  30.0 5.5 %collective-permute-start.11 = (f32[1,128]{1,0:T(1,128)S(1)}, f32[1,128]{1,0:T(1,128)S(1)}, u32[]{:S(2)}, u32[]{:S(2)}) collective-permute-start(f32[1,128]{1,0:T(1,128)S(1)} %get-tuple-element.18), channel_id=1, source_target_pairs={{0,3},{1,2},{2,1},{3,0},{4,7},{5,6},{6,5},{7,4},{8,11},{9,10},{10,... | collective-permute-start | bytes 1544 | tf_op jit(solution)/shard_map/ppermute | solution.py:146
  31.1 7.3 %collective-permute-start.12 = (f32[1,128]{1,0:T(1,128)S(1)}, f32[1,128]{1,0:T(1,128)S(1)}, u32[]{:S(2)}, u32[]{:S(2)}) collective-permute-start(f32[1,128]{1,0:T(1,128)S(1)} %get-tuple-element.19), channel_id=1, source_target_pairs={{0,4},{1,5},{2,6},{3,7},{4,0},{5,1},{6,2},{7,3},{8,12},{9,13},{10,... | collective-permute-start | bytes 1544 | tf_op jit(solution)/shard_map/ppermute | solution.py:146
  32.6 7.8 %collective-permute-start.13 = (f32[1,128]{1,0:T(1,128)S(1)}, f32[1,128]{1,0:T(1,128)S(1)}, u32[]{:S(2)}, u32[]{:S(2)}) collective-permute-start(f32[1,128]{1,0:T(1,128)S(1)} %get-tuple-element.20), channel_id=1, source_target_pairs={{0,5},{1,4},{2,7},{3,6},{4,1},{5,0},{6,3},{7,2},{8,13},{9,12},{10,... | collective-permute-start | bytes 1544 | tf_op jit(solution)/shard_map/ppermute | solution.py:146
  32.8 7.6 %collective-permute-start.14 = (f32[1,128]{1,0:T(1,128)S(1)}, f32[1,128]{1,0:T(1,128)S(1)}, u32[]{:S(2)}, u32[]{:S(2)}) collective-permute-start(f32[1,128]{1,0:T(1,128)S(1)} %get-tuple-element.21), channel_id=1, source_target_pairs={{0,6},{1,7},{2,4},{3,5},{4,2},{5,3},{6,0},{7,1},{8,14},{9,15},{10,... | collective-permute-start | bytes 1544 | tf_op jit(solution)/shard_map/ppermute | solution.py:146
  34.4 6.0 %collective-permute-start.15 = (f32[1,128]{1,0:T(1,128)S(1)}, f32[1,128]{1,0:T(1,128)S(1)}, u32[]{:S(2)}, u32[]{:S(2)}) collective-permute-start(f32[1,128]{1,0:T(1,128)S(1)} %get-tuple-element.22), channel_id=1, source_target_pairs={{0,7},{1,6},{2,5},{3,4},{4,3},{5,2},{6,1},{7,0},{8,15},{9,14},{10,... | collective-permute-start | bytes 1544 | tf_op jit(solution)/shard_map/ppermute | solution.py:146
  35.5 4.2 %copy-start.2 = (s32[16]{0:T(128)S(1)}, s32[16]{0:T(128)}, u32[]{:S(2)}) copy-start(s32[16]{0:T(128)} %constant.26.clone) | copy-start | bytes 196
  35.5 4.9 %collective-permute-start.16 = (f32[1,128]{1,0:T(1,128)S(1)}, f32[1,128]{1,0:T(1,128)S(1)}, u32[]{:S(2)}, u32[]{:S(2)}) collective-permute-start(f32[1,128]{1,0:T(1,128)S(1)} %get-tuple-element.23), channel_id=1, source_target_pairs={{8,0},{9,1},{10,2},{11,3},{12,4},{13,5},{14,6},{15,7},{16,8},{17,9... | collective-permute-start | bytes 1544 | tf_op jit(solution)/shard_map/ppermute | solution.py:146
  38.4 6.3 %collective-permute-start.17 = (f32[1,128]{1,0:T(1,128)S(1)}, f32[1,128]{1,0:T(1,128)S(1)}, u32[]{:S(2)}, u32[]{:S(2)}) collective-permute-start(f32[1,128]{1,0:T(1,128)S(1)} %get-tuple-element.24), channel_id=1, source_target_pairs={{16,0},{17,1},{18,2},{19,3},{20,4},{21,5},{22,6},{23,7},{8,24},{9,... | collective-permute-start | bytes 1544 | tf_op jit(solution)/shard_map/ppermute | solution.py:146

commit v3 on v2

v3 whole, which is shorter than its diff:
```python
import functools
import math

import jax
import jax.numpy as jnp
from jax import lax
from jax.experimental import pallas as pl
from jax.experimental.pallas import tpu as pltpu
from jax.sharding import PartitionSpec as P

AUX = 16
DIGIT = 256


def pack_kernel(emb_ref, id_ref, out_ref):
    rows, width = emb_ref.shape
    values = emb_ref[...].astype(jnp.float32)
    scale = lax.rsqrt(jnp.sum(values * values, axis=-1, keepdims=True) + 1e-06)
    out_ref[:rows, :] = (values * scale).astype(jnp.bfloat16)
    ids = jnp.broadcast_to(id_ref[...], (AUX, rows))
    row = lax.broadcasted_iota(jnp.int32, (AUX, rows), 0)
    digits = jnp.where(row == 0, ids % DIGIT, jnp.where(row == 1, ids // DIGIT, 1))
    if width > rows:
        digits = jnp.concatenate([digits, jnp.zeros((AUX, width - rows), jnp.int32)], axis=1)
    out_ref[rows:, :] = digits.astype(jnp.float32).astype(jnp.bfloat16)


def pack(embeddings, cluster_id):
    rows, width = embeddings.shape
    return pl.pallas_call(
        pack_kernel,
        out_shape=jax.ShapeDtypeStruct((rows + AUX, width), jnp.bfloat16),
    )(embeddings, cluster_id.reshape(1, rows))


def one_hot(digits, clusters):
    number = digits[0:1].astype(jnp.int32) + DIGIT * digits[1:2].astype(jnp.int32)
    index = lax.broadcasted_iota(jnp.int32, (clusters, digits.shape[1]), 0)
    return jnp.where((index == number) & (digits[2:3] > 0), 1.0, 0.0).astype(jnp.bfloat16)


def weights_table(group_ref, groups):
    clusters = group_ref.shape[1]
    index = lax.broadcasted_iota(jnp.int32, (groups, clusters), 0)
    member = jnp.where(index == group_ref[...], 1.0, 0.0).astype(jnp.bfloat16)
    same = lax.dot_general(member, member, (((0,), (0,)), ((), ())), preferred_element_type=jnp.float32)
    a = lax.broadcasted_iota(jnp.int32, (clusters, clusters), 0)
    b = lax.broadcasted_iota(jnp.int32, (clusters, clusters), 1)
    return jnp.where(a == b, 1.0, 0.5 * same).astype(jnp.bfloat16)


def best_kernel(n_keys, groups, order_ref, group_ref, *refs):
    n_in = (len(refs) + n_keys - 1) // 2
    blocks, outs = refs[:n_in], refs[n_in:]
    rows = blocks[0].shape[0] - AUX
    clusters = group_ref.shape[1]
    table = weights_table(group_ref, groups)
    hots = [one_hot(b[rows:, :rows].astype(jnp.float32), clusters) for b in blocks]
    key_hot = jnp.concatenate(hots[:n_keys], axis=1)
    keys = jnp.concatenate([b[:rows, :] for b in blocks[:n_keys]], axis=0)
    for out, j in zip(outs, [0, *range(n_keys, n_in)]):
        mixed = jnp.dot(table, hots[j], preferred_element_type=jnp.float32).astype(jnp.bfloat16)
        weight = lax.dot_general(key_hot, mixed, (((0,), (0,)), ((), ())), preferred_element_type=jnp.float32)
        sims = lax.dot_general(
            keys, blocks[j][:rows, :], (((1,), (1,)), ((), ())), preferred_element_type=jnp.float32
        )
        score = jnp.where(weight > 0, weight * sims, -1.0)
        best = jnp.full((1, rows), -1.0, jnp.float32)
        for i in range(n_keys):
            part = score[i * rows : (i + 1) * rows, :]
            if i == j:
                k = lax.broadcasted_iota(jnp.int32, (rows, rows), 0)
                q = lax.broadcasted_iota(jnp.int32, (rows, rows), 1)
                part = jnp.where(k < q, part, -1.0)
            found = jnp.max(part, axis=0, keepdims=True)
            if i != j:
                found = jnp.where(order_ref[i] < order_ref[j], found, -1.0)
            best = jnp.maximum(best, found)
        out[...] = best


def solution(mesh):
    n_clu, n_grp = mesh.shape["clu"], mesh.shape["grp"]
    target = math.sqrt(n_clu * n_grp)
    wide = min(a for a in range(1, n_clu + 1) if n_clu % a == 0 and (a * n_grp >= target or a == n_clu))
    length = n_clu // wide

    def permute(x, move):
        pairs = []
        for z in range(length):
            for a in range(wide):
                for g in range(n_grp):
                    at = move(z, a, g)
                    if at is not None:
                        pairs.append((((at[0] * wide) + at[1]) * n_grp + at[2], (z * wide + a) * n_grp + g))
        return pairs, lax.ppermute(x, ("clu", "grp"), pairs)

    def turned(a, s):
        return a ^ s if wide & (wide - 1) == 0 else (a + s) % wide

    def shards(embeddings, cluster_id, cluster_group):
        rows = embeddings.shape[0]
        own = pack(embeddings, cluster_id)
        clu, grp = lax.axis_index("clu"), lax.axis_index("grp")
        line, place = clu // wide, clu % wide

        def rank(z, a, g):
            return jnp.where(g < 0, n_clu * n_grp, g * n_clu + z * wide + a)

        visitors, ways, visitor_rank = [], [], []
        for s in range(1, length):
            def visit(z, a, g, s=s):
                at = (z + s) % length
                return (at, a, g) if g > 0 or at > z else None

            pairs, block = permute(own, visit)
            visitors.append(block)
            ways.append(pairs)
            visitor_rank.append(rank((line + s) % length, place, grp))
        keys, key_rank = [own], [rank(line, place, grp)]
        for s in range(1, wide):
            keys.append(permute(own, lambda z, a, g: (z, turned(a, s), g))[1])
            key_rank.append(rank(line, turned(place, s), grp))
        for i in range(wide):
            for t in range(1, n_grp):
                keys.append(permute(keys[i], lambda z, a, g: (z, a, g - t) if g >= t else None)[1])
                key_rank.append(rank(line, turned(place, i), grp - t))
        vmem = pl.BlockSpec(memory_space=pltpu.VMEM)
        best = pl.pallas_call(
            functools.partial(best_kernel, len(keys), n_clu),
            out_shape=[jax.ShapeDtypeStruct((1, rows), jnp.float32)] * length,
            in_specs=[pl.BlockSpec(memory_space=pltpu.SMEM)] + [vmem] * (1 + len(keys) + len(visitors)),
            out_specs=[vmem] * length,
            compiler_params=pltpu.CompilerParams(vmem_limit_bytes=48 * 2**20),
        )(jnp.stack(key_rank + visitor_rank).astype(jnp.int32), cluster_group.reshape(1, -1), *keys, *visitors)
        found = [best[0]]
        for s, pairs in zip(range(1, length), ways):
            back = lax.ppermute(best[s], ("clu", "grp"), [(to, at) for at, to in pairs])
            found.append(jnp.where((grp > 0) | (line >= s), back, -1.0))
        return functools.reduce(jnp.maximum, found).reshape(rows)

    placed = (P(("clu", "grp"), None), P(("clu", "grp")), P())
    return jax.shard_map(
        shards, mesh=mesh, in_specs=placed, out_specs=P(("clu", "grp")), check_vma=False
    )
```

time: 46.1 us -> 38.6 us (0.84)
  the two profiles are of different devices: /device:TPU:0 before, /device:TPU:1 now
where the time goes in v3:
time: 38.6 us; the launch traced here: 38.3 us
  starting transfers between devices  27.1 us (70%)
  waiting for transfers between devices  6.08 us (16%)
  Pallas kernels  4.17 us (11%)
  other arithmetic  0.52 us (1%)
    ppermute x10, starting transfers between devices, permute(): return (pairs, lax.ppermute(x, ('clu', 'grp'), pairs))  18.1 us
    ppermute x3, starting transfers between devices, shards(): back = lax.ppermute(best[s], ('clu', 'grp'), [(to, at) for at, to in pairs])  9 us
    ppermute x10, waiting for transfers between devices, permute(): return (pairs, lax.ppermute(x, ('clu', 'grp'), pairs))  4.93 us
    pallas_call x1, Pallas kernels, shards(): pl.pallas_call(functools.partial(best_kernel, len(keys), n_clu), out_shap...  2.49 us
    pallas_call x1, Pallas kernels, pack(): pl.pallas_call(pack_kernel, out_shape=jax.ShapeDtypeStruct((rows + AUX, w...  1.68 us
    ppermute x3, waiting for transfers between devices, shards(): back = lax.ppermute(best[s], ('clu', 'grp'), [(to, at) for at, to in pairs])  1.15 us
  transfers between devices with their start and end apart: 13, of which 2 were waited for; matrix products, arithmetic and copies ran while one was open for 0% of the time, Pallas kernels for 0%

profile of v3, /device:TPU:1, one launch (start us, length us, event | category | flops | bytes accessed | tf_op | source)
XLA Modules:
  0.0 38.3 jit_solution(8087306988437382308)
XLA Ops:
  0.0 1.7 %shard_map.37.refs_0_ = bf16[144,512]{1,0:T(8,128)(2,1)} custom-call(bf16[128,512]{1,0:T(8,128)(2,1)} %emb_ref.1, s32[1,128]{1,0:T(1,128)} %bitcast.16), custom_call_target="tpu_custom_call" | custom-call | tf_op jit(solution)/shard_map/pallas_call | solution.py:30
  1.7 0.0 copy-start
  1.7 2.0 %collective-permute-start = (bf16[144,512]{1,0:T(8,128)(2,1)}, bf16[144,512]{1,0:T(8,128)(2,1)S(1)}, u32[]{:S(2)}, u32[]{:S(2)}) collective-permute-start(bf16[144,512]{1,0:T(8,128)(2,1)} %shard_map.37.refs_0_), channel_id=1, source_target_pairs={{2,0},{3,1},{0,2},{1,3},{6,4},{7,5},{4,6},{5,7},{10,8},{11,9},{8,1... | collective-permute-start | bytes 442376 | tf_op jit(solution)/shard_map/ppermute | solution.py:96
  3.7 1.2 %collective-permute-start.1 = (bf16[144,512]{1,0:T(8,128)(2,1)}, bf16[144,512]{1,0:T(8,128)(2,1)S(1)}, u32[]{:S(2)}, u32[]{:S(2)}) collective-permute-start(bf16[144,512]{1,0:T(8,128)(2,1)} %shard_map.37.refs_0_), channel_id=1, source_target_pairs={{4,0},{5,1},{6,2},{7,3},{0,4},{1,5},{2,6},{3,7},{12,8},{13,9},{14,... | collective-permute-start | bytes 442376 | tf_op jit(solution)/shard_map/ppermute | solution.py:96
  5.0 0.0 collective-permute-start.2
  5.0 1.3 %collective-permute-start.3 = (bf16[144,512]{1,0:T(8,128)(2,1)}, bf16[144,512]{1,0:T(8,128)(2,1)S(1)}, u32[]{:S(2)}, u32[]{:S(2)}) collective-permute-start(bf16[144,512]{1,0:T(8,128)(2,1)} %shard_map.37.refs_0_), channel_id=1, source_target_pairs={{0,1},{2,3},{4,5},{6,7},{8,9},{10,11},{12,13},{14,15},{16,17},{18,... | collective-permute-start | bytes 442376 | tf_op jit(solution)/shard_map/ppermute | solution.py:96
  6.3 5.4 %collective-permute-start.7 = (bf16[144,512]{1,0:T(8,128)(2,1)}, bf16[144,512]{1,0:T(8,128)(2,1)S(1)}, u32[]{:S(2)}, u32[]{:S(2)}) collective-permute-start(bf16[144,512]{1,0:T(8,128)(2,1)} %shard_map.37.refs_0_), channel_id=1, source_target_pairs={{8,0},{9,1},{10,2},{11,3},{12,4},{13,5},{14,6},{15,7},{16,8},{17,9... | collective-permute-start | bytes 442376 | tf_op jit(solution)/shard_map/ppermute | solution.py:96
  11.7 0.0 collective-permute-done.refs_1_
  11.7 1.9 %collective-permute-start.8 = (bf16[144,512]{1,0:T(8,128)(2,1)}, bf16[144,512]{1,0:T(8,128)(2,1)S(1)}, u32[]{:S(2)}, u32[]{:S(2)}) collective-permute-start(bf16[144,512]{1,0:T(8,128)(2,1)} %shard_map.37.refs_0_), channel_id=1, source_target_pairs={{16,0},{17,1},{18,2},{19,3},{20,4},{21,5},{22,6},{23,7},{24,8},{25... | collective-permute-start | bytes 442376 | tf_op jit(solution)/shard_map/ppermute | solution.py:96
  13.6 0.0 collective-permute-done.1.refs_2_
  13.6 2.3 %collective-permute-start.9 = (bf16[144,512]{1,0:T(8,128)(2,1)}, bf16[144,512]{1,0:T(8,128)(2,1)S(1)}, u32[]{:S(2)}, u32[]{:S(2)}) collective-permute-start(bf16[144,512]{1,0:T(8,128)(2,1)} %shard_map.37.refs_0_), channel_id=1, source_target_pairs={{24,0},{25,1},{26,2},{27,3},{28,4},{29,5},{30,6},{31,7},{1,9},{3,1... | collective-permute-start | bytes 442376 | tf_op jit(solution)/shard_map/ppermute | solution.py:96
  16.0 0.0 collective-permute-done.2.refs_3_
  16.0 1.3 %collective-permute-start.4 = (bf16[144,512]{1,0:T(8,128)(2,1)S(1)}, bf16[144,512]{1,0:T(8,128)(2,1)S(1)}, u32[]{:S(2)}, u32[]{:S(2)}) collective-permute-start(bf16[144,512]{1,0:T(8,128)(2,1)S(1)} %collective-permute-done.refs_1_), channel_id=1, source_target_pairs={{0,1},{2,3},{4,5},{6,7},{8,9},{10,11},{12,13},{14,15},{16,17},{18,... | collective-permute-start | bytes 442376 | tf_op jit(solution)/shard_map/ppermute | solution.py:96
  17.3 0.0 collective-permute-done.3.refs_4_
  17.3 1.3 %collective-permute-start.5 = (bf16[144,512]{1,0:T(8,128)(2,1)S(1)}, bf16[144,512]{1,0:T(8,128)(2,1)S(1)}, u32[]{:S(2)}, u32[]{:S(2)}) collective-permute-start(bf16[144,512]{1,0:T(8,128)(2,1)S(1)} %collective-permute-done.1.refs_2_), channel_id=1, source_target_pairs={{0,1},{2,3},{4,5},{6,7},{8,9},{10,11},{12,13},{14,15},{16,17},{18,... | collective-permute-start | bytes 442376 | tf_op jit(solution)/shard_map/ppermute | solution.py:96
  18.6 0.0 collective-permute-done.7.refs_8_
  18.6 1.3 %collective-permute-start.6 = (bf16[144,512]{1,0:T(8,128)(2,1)S(1)}, bf16[144,512]{1,0:T(8,128)(2,1)S(1)}, u32[]{:S(2)}, u32[]{:S(2)}) collective-permute-start(bf16[144,512]{1,0:T(8,128)(2,1)S(1)} %collective-permute-done.2.refs_3_), channel_id=1, source_target_pairs={{0,1},{2,3},{4,5},{6,7},{8,9},{10,11},{12,13},{14,15},{16,17},{18,... | collective-permute-start | bytes 442376 | tf_op jit(solution)/shard_map/ppermute | solution.py:96
  20.0 0.1 stack.47.order_ref
  20.1 0.0 copy-start.1
  20.1 4.9 %collective-permute-done.8.refs_9_ = bf16[144,512]{1,0:T(8,128)(2,1)S(1)} collective-permute-done((bf16[144,512]{1,0:T(8,128)(2,1)}, bf16[144,512]{1,0:T(8,128)(2,1)S(1)}, u32[]{:S(2)}, u32[]{:S(2)}) %collective-permute-start.8) | collective-permute-done | bytes 147488 | tf_op jit(solution)/shard_map/ppermute | solution.py:96
  25.0 0.0 collective-permute-done.9.refs_10_
  25.0 0.0 collective-permute-done.4.refs_5_
  25.0 0.0 collective-permute-done.5.refs_6_
  25.0 0.0 collective-permute-done.6.refs_7_
  25.0 0.0 copy-done
  25.1 0.0 copy-done.1
  25.1 2.5 %shard_map.38 = (f32[1,128]{1,0:T(1,128)S(1)}, f32[1,128]{1,0:T(1,128)S(1)}, f32[1,128]{1,0:T(1,128)S(1)}, f32[1,128]{1,0:T(1,128)S(1)}) custom-call(s32[11]{0:T(128)S(1)} %stack.47.order_ref, s32[1,64]{1,0:T(1,128)S(1)} %bitcast.15, bf16[144,512]{1,0:T(8,128)(2,1)S(1)} %copy-done, bf16[144,512]{1,0:T(8,128)(2,1)S(1)} %collective-permute-done.refs_1_, ...), custom_call_target="tpu_custom_call" | custom-call | tf_op jit(solution)/shard_map/pallas_call | solution.py:129
  27.6 1.9 %collective-permute-start.10 = (f32[1,128]{1,0:T(1,128)S(1)}, f32[1,128]{1,0:T(1,128)S(1)}, u32[]{:S(2)}, u32[]{:S(2)}) collective-permute-start(f32[1,128]{1,0:T(1,128)S(1)} %get-tuple-element.10), channel_id=1, source_target_pairs={{0,8},{1,9},{2,10},{3,11},{4,12},{5,13},{6,14},{7,15},{8,16},{9,17... | collective-permute-start | bytes 1544 | tf_op jit(solution)/shard_map/ppermute | solution.py:138
  29.5 1.9 %collective-permute-start.11 = (f32[1,128]{1,0:T(1,128)S(1)}, f32[1,128]{1,0:T(1,128)S(1)}, u32[]{:S(2)}, u32[]{:S(2)}) collective-permute-start(f32[1,128]{1,0:T(1,128)S(1)} %get-tuple-element.11), channel_id=1, source_target_pairs={{0,16},{1,17},{2,18},{3,19},{4,20},{5,21},{6,22},{7,23},{8,24},{9,... | collective-permute-start | bytes 1544 | tf_op jit(solution)/shard_map/ppermute | solution.py:138
  31.4 5.2 %collective-permute-start.12 = (f32[1,128]{1,0:T(1,128)S(1)}, f32[1,128]{1,0:T(1,128)S(1)}, u32[]{:S(2)}, u32[]{:S(2)}) collective-permute-start(f32[1,128]{1,0:T(1,128)S(1)} %get-tuple-element.12), channel_id=1, source_target_pairs={{0,24},{1,25},{2,26},{3,27},{4,28},{5,29},{6,30},{7,31},{9,1},{11,... | collective-permute-start | bytes 1544 | tf_op jit(solution)/shard_map/ppermute | solution.py:138
  36.6 0.0 collective-permute-done.10
  36.6 0.0 collective-permute-done.11
  36.6 1.1 %collective-permute-done.12 = f32[1,128]{1,0:T(1,128)S(1)} collective-permute-done((f32[1,128]{1,0:T(1,128)S(1)}, f32[1,128]{1,0:T(1,128)S(1)}, u32[]{:S(2)}, u32[]{:S(2)}) %collective-permute-start.12) | collective-permute-done | bytes 544 | tf_op jit(solution)/shard_map/ppermute | solution.py:138
  37.8 0.5 %fusion.3 = f32[128]{0:T(128)} fusion(f32[1,128]{1,0:T(1,128)S(1)} %collective-permute-done.12, pred[]{:T(512)S(6)} %or.11, f32[1,128]{1,0:T(1,128)S(1)} %collective-permute-done.11, pred[]{:T(512)S(6)} %or.10, f32[1,128]{1,0:T(1,128)S(1)} %get-tuple-element.9, f32[1,128]{1,0:T(1,128)S(1)} %collective-permute-done.10, pred[]{:T(512)S(6)} %or.9), kind=kLoop, calls=%fused_computation.6 | loop fusion | flops 768 | bytes 2563 | tf_op jit(solution)/shard_map/reshape | solution.py:140
Async XLA Ops:
  1.7 23.4 %copy-start = (bf16[144,512]{1,0:T(8,128)(2,1)S(1)}, bf16[144,512]{1,0:T(8,128)(2,1)}, u32[]{:S(2)}) copy-start(bf16[144,512]{1,0:T(8,128)(2,1)} %shard_map.37.refs_0_) | copy-start | bytes 442372
  1.7 10.0 %collective-permute-start = (bf16[144,512]{1,0:T(8,128)(2,1)}, bf16[144,512]{1,0:T(8,128)(2,1)S(1)}, u32[]{:S(2)}, u32[]{:S(2)}) collective-permute-start(bf16[144,512]{1,0:T(8,128)(2,1)} %shard_map.37.refs_0_), channel_id=1, source_target_pairs={{2,0},{3,1},{0,2},{1,3},{6,4},{7,5},{4,6},{5,7},{10,8},{11,9},{8,1... | collective-permute-start | bytes 442376 | tf_op jit(solution)/shard_map/ppermute | solution.py:96
  3.7 9.9 %collective-permute-start.1 = (bf16[144,512]{1,0:T(8,128)(2,1)}, bf16[144,512]{1,0:T(8,128)(2,1)S(1)}, u32[]{:S(2)}, u32[]{:S(2)}) collective-permute-start(bf16[144,512]{1,0:T(8,128)(2,1)} %shard_map.37.refs_0_), channel_id=1, source_target_pairs={{4,0},{5,1},{6,2},{7,3},{0,4},{1,5},{2,6},{3,7},{12,8},{13,9},{14,... | collective-permute-start | bytes 442376 | tf_op jit(solution)/shard_map/ppermute | solution.py:96
  5.0 11.0 %collective-permute-start.2 = (bf16[144,512]{1,0:T(8,128)(2,1)}, bf16[144,512]{1,0:T(8,128)(2,1)S(1)}, u32[]{:S(2)}, u32[]{:S(2)}) collective-permute-start(bf16[144,512]{1,0:T(8,128)(2,1)} %shard_map.37.refs_0_), channel_id=1, source_target_pairs={{6,0},{7,1},{4,2},{5,3},{2,4},{3,5},{0,6},{1,7},{14,8},{15,9},{12,... | collective-permute-start | bytes 442376 | tf_op jit(solution)/shard_map/ppermute | solution.py:96
  5.0 12.3 %collective-permute-start.3 = (bf16[144,512]{1,0:T(8,128)(2,1)}, bf16[144,512]{1,0:T(8,128)(2,1)S(1)}, u32[]{:S(2)}, u32[]{:S(2)}) collective-permute-start(bf16[144,512]{1,0:T(8,128)(2,1)} %shard_map.37.refs_0_), channel_id=1, source_target_pairs={{0,1},{2,3},{4,5},{6,7},{8,9},{10,11},{12,13},{14,15},{16,17},{18,... | collective-permute-start | bytes 442376 | tf_op jit(solution)/shard_map/ppermute | solution.py:96
  6.3 12.4 %collective-permute-start.7 = (bf16[144,512]{1,0:T(8,128)(2,1)}, bf16[144,512]{1,0:T(8,128)(2,1)S(1)}, u32[]{:S(2)}, u32[]{:S(2)}) collective-permute-start(bf16[144,512]{1,0:T(8,128)(2,1)} %shard_map.37.refs_0_), channel_id=1, source_target_pairs={{8,0},{9,1},{10,2},{11,3},{12,4},{13,5},{14,6},{15,7},{16,8},{17,9... | collective-permute-start | bytes 442376 | tf_op jit(solution)/shard_map/ppermute | solution.py:96
  11.7 13.3 %collective-permute-start.8 = (bf16[144,512]{1,0:T(8,128)(2,1)}, bf16[144,512]{1,0:T(8,128)(2,1)S(1)}, u32[]{:S(2)}, u32[]{:S(2)}) collective-permute-start(bf16[144,512]{1,0:T(8,128)(2,1)} %shard_map.37.refs_0_), channel_id=1, source_target_pairs={{16,0},{17,1},{18,2},{19,3},{20,4},{21,5},{22,6},{23,7},{24,8},{25... | collective-permute-start | bytes 442376 | tf_op jit(solution)/shard_map/ppermute | solution.py:96
  13.6 11.4 %collective-permute-start.9 = (bf16[144,512]{1,0:T(8,128)(2,1)}, bf16[144,512]{1,0:T(8,128)(2,1)S(1)}, u32[]{:S(2)}, u32[]{:S(2)}) collective-permute-start(bf16[144,512]{1,0:T(8,128)(2,1)} %shard_map.37.refs_0_), channel_id=1, source_target_pairs={{24,0},{25,1},{26,2},{27,3},{28,4},{29,5},{30,6},{31,7},{1,9},{3,1... | collective-permute-start | bytes 442376 | tf_op jit(solution)/shard_map/ppermute | solution.py:96
  16.0 9.0 %collective-permute-start.4 = (bf16[144,512]{1,0:T(8,128)(2,1)S(1)}, bf16[144,512]{1,0:T(8,128)(2,1)S(1)}, u32[]{:S(2)}, u32[]{:S(2)}) collective-permute-start(bf16[144,512]{1,0:T(8,128)(2,1)S(1)} %collective-permute-done.refs_1_), channel_id=1, source_target_pairs={{0,1},{2,3},{4,5},{6,7},{8,9},{10,11},{12,13},{14,15},{16,17},{18,... | collective-permute-start | bytes 442376 | tf_op jit(solution)/shard_map/ppermute | solution.py:96
  17.3 7.7 %collective-permute-start.5 = (bf16[144,512]{1,0:T(8,128)(2,1)S(1)}, bf16[144,512]{1,0:T(8,128)(2,1)S(1)}, u32[]{:S(2)}, u32[]{:S(2)}) collective-permute-start(bf16[144,512]{1,0:T(8,128)(2,1)S(1)} %collective-permute-done.1.refs_2_), channel_id=1, source_target_pairs={{0,1},{2,3},{4,5},{6,7},{8,9},{10,11},{12,13},{14,15},{16,17},{18,... | collective-permute-start | bytes 442376 | tf_op jit(solution)/shard_map/ppermute | solution.py:96
  18.6 6.4 %collective-permute-start.6 = (bf16[144,512]{1,0:T(8,128)(2,1)S(1)}, bf16[144,512]{1,0:T(8,128)(2,1)S(1)}, u32[]{:S(2)}, u32[]{:S(2)}) collective-permute-start(bf16[144,512]{1,0:T(8,128)(2,1)S(1)} %collective-permute-done.2.refs_3_), channel_id=1, source_target_pairs={{0,1},{2,3},{4,5},{6,7},{8,9},{10,11},{12,13},{14,15},{16,17},{18,... | collective-permute-start | bytes 442376 | tf_op jit(solution)/shard_map/ppermute | solution.py:96
  20.1 4.9 %copy-start.1 = (s32[64]{0:T(128)S(1)}, s32[64]{0:T(128)}, u32[]{:S(2)}) copy-start(s32[64]{0:T(128)} %param.5) | copy-start | bytes 772
  27.6 9.0 %collective-permute-start.10 = (f32[1,128]{1,0:T(1,128)S(1)}, f32[1,128]{1,0:T(1,128)S(1)}, u32[]{:S(2)}, u32[]{:S(2)}) collective-permute-start(f32[1,128]{1,0:T(1,128)S(1)} %get-tuple-element.10), channel_id=1, source_target_pairs={{0,8},{1,9},{2,10},{3,11},{4,12},{5,13},{6,14},{7,15},{8,16},{9,17... | collective-permute-start | bytes 1544 | tf_op jit(solution)/shard_map/ppermute | solution.py:138
  29.5 7.1 %collective-permute-start.11 = (f32[1,128]{1,0:T(1,128)S(1)}, f32[1,128]{1,0:T(1,128)S(1)}, u32[]{:S(2)}, u32[]{:S(2)}) collective-permute-start(f32[1,128]{1,0:T(1,128)S(1)} %get-tuple-element.11), channel_id=1, source_target_pairs={{0,16},{1,17},{2,18},{3,19},{4,20},{5,21},{6,22},{7,23},{8,24},{9,... | collective-permute-start | bytes 1544 | tf_op jit(solution)/shard_map/ppermute | solution.py:138
  31.4 6.4 %collective-permute-start.12 = (f32[1,128]{1,0:T(1,128)S(1)}, f32[1,128]{1,0:T(1,128)S(1)}, u32[]{:S(2)}, u32[]{:S(2)}) collective-permute-start(f32[1,128]{1,0:T(1,128)S(1)} %get-tuple-element.12), channel_id=1, source_target_pairs={{0,24},{1,25},{2,26},{3,27},{4,28},{5,29},{6,30},{7,31},{9,1},{11,... | collective-permute-start | bytes 1544 | tf_op jit(solution)/shard_map/ppermute | solution.py:138

commit v4 on v3

v4 whole, which is shorter than its diff:
```python
import functools
import math

import jax
import jax.numpy as jnp
from jax import lax
from jax.experimental import pallas as pl
from jax.experimental.pallas import tpu as pltpu
from jax.sharding import PartitionSpec as P

AUX = 16
DIGIT = 256


def pack_kernel(emb_ref, id_ref, out_ref):
    rows, width = emb_ref.shape
    values = emb_ref[...].astype(jnp.float32)
    scale = lax.rsqrt(jnp.sum(values * values, axis=-1, keepdims=True) + 1e-06)
    unit = (values * scale).astype(jnp.bfloat16)
    ids = jnp.broadcast_to(id_ref[...], (AUX, rows))
    row = lax.broadcasted_iota(jnp.int32, (AUX, rows), 0)
    digits = jnp.where(row == 0, ids % DIGIT, ids // DIGIT)
    if width > rows:
        digits = jnp.concatenate([digits, jnp.zeros((AUX, width - rows), jnp.int32)], axis=1)
    digits = digits.astype(jnp.float32).astype(jnp.bfloat16)
    for i in range(out_ref.shape[0]):
        out_ref[i, :rows, :] = unit
        out_ref[i, rows:, :] = digits


def pack(embeddings, cluster_id, copies):
    rows, width = embeddings.shape
    return pl.pallas_call(
        pack_kernel,
        out_shape=jax.ShapeDtypeStruct((copies, rows + AUX, width), jnp.bfloat16),
    )(embeddings, cluster_id.reshape(1, rows))


def one_hot(digits, clusters):
    number = digits[0:1].astype(jnp.int32) + DIGIT * digits[1:2].astype(jnp.int32)
    index = lax.broadcasted_iota(jnp.int32, (clusters, digits.shape[1]), 0)
    return jnp.where(index == number, 1.0, 0.0).astype(jnp.bfloat16)


def weights_table(group_ref, groups):
    clusters = group_ref.shape[1]
    index = lax.broadcasted_iota(jnp.int32, (groups, clusters), 0)
    member = jnp.where(index == group_ref[...], 1.0, 0.0).astype(jnp.bfloat16)
    same = lax.dot_general(member, member, (((0,), (0,)), ((), ())), preferred_element_type=jnp.float32)
    a = lax.broadcasted_iota(jnp.int32, (clusters, clusters), 0)
    b = lax.broadcasted_iota(jnp.int32, (clusters, clusters), 1)
    return jnp.where(a == b, 1.0, 0.5 * same).astype(jnp.bfloat16)


def best_kernel(groups, rank_ref, group_ref, visit_ref, *refs):
    key_refs, out_ref = refs[:-1], refs[-1]
    count, rows = visit_ref.shape[0], visit_ref.shape[1] - AUX
    clusters = group_ref.shape[1]
    table = weights_table(group_ref, groups)

    def hot(ref, i):
        return one_hot(ref[i, rows:, :rows].astype(jnp.float32), clusters)

    slots = [(ref, i) for ref in key_refs for i in range(ref.shape[0])]
    key_hot = jnp.concatenate([hot(ref, i) for ref, i in slots], axis=1)
    keys = jnp.concatenate([ref[i, :rows, :] for ref, i in slots], axis=0)
    k = lax.broadcasted_iota(jnp.int32, (rows, rows), 0)
    q = lax.broadcasted_iota(jnp.int32, (rows, rows), 1)
    for j in range(count):
        mixed = jnp.dot(table, hot(visit_ref, j), preferred_element_type=jnp.float32).astype(jnp.bfloat16)
        weight = lax.dot_general(key_hot, mixed, (((0,), (0,)), ((), ())), preferred_element_type=jnp.float32)
        sims = lax.dot_general(
            keys, visit_ref[j, :rows, :], (((1,), (1,)), ((), ())), preferred_element_type=jnp.float32
        )
        best = jnp.full((rows, rows), -1.0, jnp.float32)
        for i in range(len(slots)):
            at = slice(i * rows, (i + 1) * rows)
            earlier = k - q < (rank_ref[j] - rank_ref[count + i]) * rows
            best = jnp.maximum(best, jnp.where((weight[at] > 0) & earlier, weight[at] * sims[at], -1.0))
        out_ref[j : j + 1, :] = jnp.max(best, axis=0, keepdims=True)


def solution(mesh):
    n_clu, n_grp = mesh.shape["clu"], mesh.shape["grp"]
    target = math.sqrt(n_clu * n_grp)
    wide = min(a for a in range(1, n_clu + 1) if n_clu % a == 0 and (a * n_grp >= target or a == n_clu))
    length = n_clu // wide
    planes = [[z * wide + a for a in range(wide)] for z in range(length)]
    lines = [[z * wide + a for z in range(length)] for a in range(wide)]

    def exchange(x, groups):
        return lax.all_to_all(x, "clu", 0, 0, axis_index_groups=groups, tiled=True)

    def shards(embeddings, cluster_id, cluster_group):
        rows = embeddings.shape[0]
        own = pack(embeddings, cluster_id, max(wide, length))
        clu, grp = lax.axis_index("clu"), lax.axis_index("grp")
        line, place = clu // wide, clu % wide
        visitors = exchange(own[:length], lines)
        keys = [exchange(own[:wide], planes)]
        visit_rank = grp * n_clu + jnp.arange(length) * wide + place
        key_rank = [grp * n_clu + line * wide + jnp.arange(wide)]
        for t in range(1, n_grp):
            keys.append(lax.ppermute(keys[0], "grp", [(g, (g + t) % n_grp) for g in range(n_grp)]))
            key_rank.append((grp - t) % n_grp * n_clu + line * wide + jnp.arange(wide))
        vmem = pl.BlockSpec(memory_space=pltpu.VMEM)
        best = pl.pallas_call(
            functools.partial(best_kernel, n_clu),
            out_shape=jax.ShapeDtypeStruct((length, rows), jnp.float32),
            in_specs=[pl.BlockSpec(memory_space=pltpu.SMEM)] + [vmem] * (2 + len(keys)),
            out_specs=vmem,
            compiler_params=pltpu.CompilerParams(vmem_limit_bytes=48 * 2**20),
        )(jnp.concatenate([visit_rank] + key_rank).astype(jnp.int32), cluster_group.reshape(1, -1), visitors, *keys)
        return jnp.max(exchange(best, lines), axis=0)

    placed = (P(("clu", "grp"), None), P(("clu", "grp")), P())
    return jax.shard_map(
        shards, mesh=mesh, in_specs=placed, out_specs=P(("clu", "grp")), check_vma=False
    )
```

time: 38.6 us -> 47.2 us (1.22)
  the two profiles are of different devices: /device:TPU:1 before, /device:TPU:0 now
where the time goes in v4:
time: 47.2 us; the launch traced here: 46.9 us
  blocking collectives  22.6 us (48%)
  waiting for transfers between devices  14.4 us (31%)
  starting transfers between devices  4.88 us (10%)
  Pallas kernels  4.32 us (9%)
  other arithmetic  0.62 us (1%)
    all_to_all x2, blocking collectives, exchange(): return lax.all_to_all(x, 'clu', 0, 0, axis_index_groups=groups, tiled=True)  22.6 us
    all_to_all x1, waiting for transfers between devices, exchange(): return lax.all_to_all(x, 'clu', 0, 0, axis_index_groups=groups, tiled=True)  14.4 us
    all_to_all x1, starting transfers between devices, exchange(): return lax.all_to_all(x, 'clu', 0, 0, axis_index_groups=groups, tiled=True)  4.88 us
    pallas_call x1, Pallas kernels, shards(): pl.pallas_call(functools.partial(best_kernel, n_clu), out_shape=jax.Shape...  2.48 us
    pallas_call x1, Pallas kernels, pack(): pl.pallas_call(pack_kernel, out_shape=jax.ShapeDtypeStruct((copies, rows...  1.84 us
  transfers between devices with their start and end apart: 2, of which 1 were waited for; matrix products, arithmetic and copies ran while one was open for 0% of the time, Pallas kernels for 0%

profile of v4, /device:TPU:0, one launch (start us, length us, event | category | flops | bytes accessed | tf_op | source)
XLA Modules:
  0.0 46.9 jit_solution(6971635565335645494)
XLA Ops:
  0.0 1.8 %shard_map.37 = bf16[4,144,512]{2,1,0:T(8,128)(2,1)} custom-call(bf16[128,512]{1,0:T(8,128)(2,1)} %emb_ref.1, s32[1,128]{1,0:T(1,128)} %bitcast.7), custom_call_target="tpu_custom_call" | custom-call | tf_op jit(solution)/shard_map/pallas_call | solution.py:33
  1.8 14.6 %all_to_all.19.refs_0_ = bf16[4,144,512]{2,1,0:T(8,128)(2,1)S(1)} all-to-all(bf16[4,144,512]{2,1,0:T(8,128)(2,1)} %shard_map.37), channel_id=1, replica_groups={{0,2,4,6},{8,10,12,14},{16,18,20,22},{24,26,28,30},{1,3,5,7},{9,11,13,1..., dimensions={0} | all-to-all | bytes 1179648 | tf_op jit(solution)/shard_map/all_to_all | solution.py:92
  16.4 4.9 %all-to-all-start = ((bf16[4,144,512]{2,1,0:T(8,128)(2,1)}), bf16[4,144,512]{2,1,0:T(8,128)(2,1)S(1)}, u32[]{:S(2)}, u32[]{:S(2)}) async-start(bf16[4,144,512]{2,1,0:T(8,128)(2,1)} %shard_map.37), calls=%async_computation | async-start | bytes 1179648 | tf_op jit(solution)/shard_map/all_to_all | solution.py:92
  21.3 0.0 collective-permute-start
  21.3 0.1 pad_add_fusion.rank_ref
  21.4 0.0 copy-start
  21.4 14.4 %all-to-all-done.visit_ref = bf16[4,144,512]{2,1,0:T(8,128)(2,1)S(1)} async-done(((bf16[4,144,512]{2,1,0:T(8,128)(2,1)}), bf16[4,144,512]{2,1,0:T(8,128)(2,1)S(1)}, u32[]{:S(2)}, u32[]{:S(2)}) %all-to-all-start) | async-done | bytes 589856 | tf_op jit(solution)/shard_map/all_to_all | solution.py:92
  35.8 0.0 collective-permute-done.refs_1_
  35.8 0.0 copy-done
  35.8 2.5 %shard_map.38 = f32[4,128]{1,0:T(4,128)S(1)} custom-call(s32[12]{0:T(128)S(1)} %pad_add_fusion.rank_ref, s32[1,64]{1,0:T(1,128)S(1)} %bitcast.6, bf16[4,144,512]{2,1,0:T(8,128)(2,1)S(1)} %all-to-all-done.visit_ref, bf16[4,144,512]{2,1,0:T(8,128)(2,1)S(1)} %all_to_all.19.refs_0_, bf16[4,144,512]{2,1,0:T(8,128)(2,1)S(1)} %collective-permute-done.refs_1_), custom_call_target="tpu_custom_call" | custom-call | tf_op jit(solution)/shard_map/pallas_call | solution.py:107
  38.3 8.1 %all_to_all.20 = f32[4,1,128]{2,1,0:T(1,128)S(1)} all-to-all(f32[4,1,128]{2,1,0:T(1,128)S(1)} %bitcast.5), channel_id=1, replica_groups={{0,8,16,24},{2,10,18,26},{4,12,20,28},{6,14,22,30},{1,9,17,25},{3,11,19..., dimensions={0} | all-to-all | bytes 4096 | tf_op jit(solution)/shard_map/all_to_all | solution.py:92
  46.4 0.5 %reduce_max.9 = f32[128]{0:T(128)} reduce(f32[4,1,128]{2,1,0:T(1,128)S(1)} %all_to_all.20, f32[]{:T(128)} %constant.48.clone.1), dimensions={0,1}, to_apply=%region_0.1 | reduce | flops 384 | bytes 2564 | tf_op jit(solution)/shard_map/reduce_max | solution.py:114
  (2 shorter events, 0.0 us)
Async XLA Ops:
  16.4 19.4 %all-to-all-start = ((bf16[4,144,512]{2,1,0:T(8,128)(2,1)}), bf16[4,144,512]{2,1,0:T(8,128)(2,1)S(1)}, u32[]{:S(2)}, u32[]{:S(2)}) async-start(bf16[4,144,512]{2,1,0:T(8,128)(2,1)} %shard_map.37), calls=%async_computation | async-start | bytes 1179648 | tf_op jit(solution)/shard_map/all_to_all | solution.py:92
  21.3 14.5 %collective-permute-start = (bf16[4,144,512]{2,1,0:T(8,128)(2,1)S(1)}, bf16[4,144,512]{2,1,0:T(8,128)(2,1)S(1)}, u32[]{:S(2)}, u32[]{:S(2)}) collective-permute-start(bf16[4,144,512]{2,1,0:T(8,128)(2,1)S(1)} %all_to_all.19.refs_0_), channel_id=1, source_target_pairs={{0,1},{1,0},{2,3},{3,2},{4,5},{5,4},{6,7},{7,6},{8,9},{9,8},{10,11... | collective-permute-start | bytes 1769480 | tf_op jit(solution)/shard_map/ppermute | solution.py:104
  21.4 14.4 %copy-start = (s32[64]{0:T(128)S(1)}, s32[64]{0:T(128)}, u32[]{:S(2)}) copy-start(s32[64]{0:T(128)} %param.5) | copy-start | bytes 772

commit v5 on v3

--- a/solution.py
+++ b/solution.py
@@ -95,8 +95,8 @@
                         pairs.append((((at[0] * wide) + at[1]) * n_grp + at[2], (z * wide + a) * n_grp + g))
         return pairs, lax.ppermute(x, ("clu", "grp"), pairs)
 
-    def turned(a, s):
-        return a ^ s if wide & (wide - 1) == 0 else (a + s) % wide
+    def turned(a, s, n):
+        return a ^ s if n & (n - 1) == 0 else (a + s) % n
 
     def shards(embeddings, cluster_id, cluster_group):
         rows = embeddings.shape[0]
@@ -110,21 +110,19 @@
         visitors, ways, visitor_rank = [], [], []
         for s in range(1, length):
             def visit(z, a, g, s=s):
-                at = (z + s) % length
+                at = turned(z, s, length)
                 return (at, a, g) if g > 0 or at > z else None
 
             pairs, block = permute(own, visit)
             visitors.append(block)
             ways.append(pairs)
-            visitor_rank.append(rank((line + s) % length, place, grp))
+            visitor_rank.append(rank(turned(line, s, length), place, grp))
         keys, key_rank = [own], [rank(line, place, grp)]
-        for s in range(1, wide):
-            keys.append(permute(own, lambda z, a, g: (z, turned(a, s), g))[1])
-            key_rank.append(rank(line, turned(place, s), grp))
-        for i in range(wide):
-            for t in range(1, n_grp):
-                keys.append(permute(keys[i], lambda z, a, g: (z, a, g - t) if g >= t else None)[1])
-                key_rank.append(rank(line, turned(place, i), grp - t))
+        for t in reversed(range(n_grp)):
+            for s in range(wide):
+                if s or t:
+                    keys.append(permute(own, lambda z, a, g: (z, turned(a, s, wide), g - t) if g >= t else None)[1])
+                    key_rank.append(rank(line, turned(place, s, wide), grp - t))
         vmem = pl.BlockSpec(memory_space=pltpu.VMEM)
         best = pl.pallas_call(
             functools.partial(best_kernel, len(keys), n_clu),
@@ -136,7 +134,8 @@
         found = [best[0]]
         for s, pairs in zip(range(1, length), ways):
             back = lax.ppermute(best[s], ("clu", "grp"), [(to, at) for at, to in pairs])
-            found.append(jnp.where((grp > 0) | (line >= s), back, -1.0))
+            at = line ^ s if length & (length - 1) == 0 else (line - s) % length
+            found.append(jnp.where((grp > 0) | (at < line), back, -1.0))
         return functools.reduce(jnp.maximum, found).reshape(rows)
 
     placed = (P(("clu", "grp"), None), P(("clu", "grp")), P())

time: 38.6 us -> 43.9 us (1.14)
  waiting for transfers between devices: 6.08 us -> 11.2 us
    ppermute x10, waiting for transfers between devices: 4.93 us -> 10.3 us  [permute(): return (pairs, lax.ppermute(x, ('clu', 'grp'), pairs))]
  transfers between devices with their start and end apart: 13 -> 13, of which waited for: 2 -> 5; matrix products, arithmetic and copies ran while one was open for 0% -> 0% of each run, Pallas kernels for 0% -> 0%
where the time goes in v5:
time: 43.9 us; the launch traced here: 43.6 us
  starting transfers between devices  27.4 us (62%)
  waiting for transfers between devices  11.2 us (26%)
  Pallas kernels  4.17 us (9%)
  other arithmetic  0.52 us (1%)
    ppermute x10, starting transfers between devices, permute(): return (pairs, lax.ppermute(x, ('clu', 'grp'), pairs))  18.2 us
    ppermute x10, waiting for transfers between devices, permute(): return (pairs, lax.ppermute(x, ('clu', 'grp'), pairs))  10.3 us
    ppermute x3, starting transfers between devices, shards(): back = lax.ppermute(best[s], ('clu', 'grp'), [(to, at) for at, to in pairs])  9.27 us
    pallas_call x1, Pallas kernels, shards(): pl.pallas_call(functools.partial(best_kernel, len(keys), n_clu), out_shap...  2.49 us
    pallas_call x1, Pallas kernels, pack(): pl.pallas_call(pack_kernel, out_shape=jax.ShapeDtypeStruct((rows + AUX, w...  1.68 us
    ppermute x3, waiting for transfers between devices, shards(): back = lax.ppermute(best[s], ('clu', 'grp'), [(to, at) for at, to in pairs])  0.88 us
  transfers between devices with their start and end apart: 13, of which 5 were waited for; matrix products, arithmetic and copies ran while one was open for 0% of the time, Pallas kernels for 0%

profile of v5, /device:TPU:1, one launch (start us, length us, event | category | flops | bytes accessed | tf_op | source)
XLA Modules:
  0.0 43.6 jit_solution(8355813859365787191)
XLA Ops:
  0.0 1.7 %shard_map.37.refs_0_ = bf16[144,512]{1,0:T(8,128)(2,1)} custom-call(bf16[128,512]{1,0:T(8,128)(2,1)} %emb_ref.1, s32[1,128]{1,0:T(1,128)} %bitcast.16), custom_call_target="tpu_custom_call" | custom-call | tf_op jit(solution)/shard_map/pallas_call | solution.py:30
  1.7 0.0 copy-start
  1.7 6.2 %collective-permute-start.9 = (bf16[144,512]{1,0:T(8,128)(2,1)}, bf16[144,512]{1,0:T(8,128)(2,1)S(1)}, u32[]{:S(2)}, u32[]{:S(2)}) collective-permute-start(bf16[144,512]{1,0:T(8,128)(2,1)} %shard_map.37.refs_0_), channel_id=1, source_target_pairs={{24,0},{25,1},{26,2},{27,3},{28,4},{29,5},{30,6},{31,7},{16,8},{17... | collective-permute-start | bytes 442376 | tf_op jit(solution)/shard_map/ppermute | solution.py:96
  7.9 1.9 %collective-permute-start.8 = (bf16[144,512]{1,0:T(8,128)(2,1)}, bf16[144,512]{1,0:T(8,128)(2,1)S(1)}, u32[]{:S(2)}, u32[]{:S(2)}) collective-permute-start(bf16[144,512]{1,0:T(8,128)(2,1)} %shard_map.37.refs_0_), channel_id=1, source_target_pairs={{16,0},{17,1},{18,2},{19,3},{20,4},{21,5},{22,6},{23,7},{24,8},{25... | collective-permute-start | bytes 442376 | tf_op jit(solution)/shard_map/ppermute | solution.py:96
  9.8 2.2 %collective-permute-start.7 = (bf16[144,512]{1,0:T(8,128)(2,1)}, bf16[144,512]{1,0:T(8,128)(2,1)S(1)}, u32[]{:S(2)}, u32[]{:S(2)}) collective-permute-start(bf16[144,512]{1,0:T(8,128)(2,1)} %shard_map.37.refs_0_), channel_id=1, source_target_pairs={{8,0},{9,1},{10,2},{11,3},{12,4},{13,5},{14,6},{15,7},{1,9},{3,11}... | collective-permute-start | bytes 442376 | tf_op jit(solution)/shard_map/ppermute | solution.py:96
  12.0 2.2 %collective-permute-start.6 = (bf16[144,512]{1,0:T(8,128)(2,1)}, bf16[144,512]{1,0:T(8,128)(2,1)S(1)}, u32[]{:S(2)}, u32[]{:S(2)}) collective-permute-start(bf16[144,512]{1,0:T(8,128)(2,1)} %shard_map.37.refs_0_), channel_id=1, source_target_pairs={{6,0},{7,1},{4,2},{5,3},{2,4},{3,5},{0,6},{1,7},{14,8},{15,9},{12,... | collective-permute-start | bytes 442376 | tf_op jit(solution)/shard_map/ppermute | solution.py:96
  14.2 0.2 collective-permute-start.5
  14.5 0.0 collective-permute-done.9.refs_10_
  14.5 0.3 collective-permute-start.4
  14.7 5.4 %collective-permute-done.8.refs_9_ = bf16[144,512]{1,0:T(8,128)(2,1)S(1)} collective-permute-done((bf16[144,512]{1,0:T(8,128)(2,1)}, bf16[144,512]{1,0:T(8,128)(2,1)S(1)}, u32[]{:S(2)}, u32[]{:S(2)}) %collective-permute-start.8) | collective-permute-done | bytes 147488 | tf_op jit(solution)/shard_map/ppermute | solution.py:96
  20.1 1.3 %collective-permute-start.3 = (bf16[144,512]{1,0:T(8,128)(2,1)}, bf16[144,512]{1,0:T(8,128)(2,1)S(1)}, u32[]{:S(2)}, u32[]{:S(2)}) collective-permute-start(bf16[144,512]{1,0:T(8,128)(2,1)} %shard_map.37.refs_0_), channel_id=1, source_target_pairs={{6,1},{4,3},{2,5},{0,7},{14,9},{12,11},{10,13},{8,15},{22,17},{20,... | collective-permute-start | bytes 442376 | tf_op jit(solution)/shard_map/ppermute | solution.py:96
  21.4 0.0 collective-permute-done.7.refs_8_
  21.4 1.3 %collective-permute-start.2 = (bf16[144,512]{1,0:T(8,128)(2,1)}, bf16[144,512]{1,0:T(8,128)(2,1)S(1)}, u32[]{:S(2)}, u32[]{:S(2)}) collective-permute-start(bf16[144,512]{1,0:T(8,128)(2,1)} %shard_map.37.refs_0_), channel_id=1, source_target_pairs={{4,1},{6,3},{0,5},{2,7},{12,9},{14,11},{8,13},{10,15},{20,17},{22,... | collective-permute-start | bytes 442376 | tf_op jit(solution)/shard_map/ppermute | solution.py:96
  22.7 0.0 collective-permute-done.6.refs_7_
  22.7 1.3 %collective-permute-start.1 = (bf16[144,512]{1,0:T(8,128)(2,1)}, bf16[144,512]{1,0:T(8,128)(2,1)S(1)}, u32[]{:S(2)}, u32[]{:S(2)}) collective-permute-start(bf16[144,512]{1,0:T(8,128)(2,1)} %shard_map.37.refs_0_), channel_id=1, source_target_pairs={{2,1},{0,3},{6,5},{4,7},{10,9},{8,11},{14,13},{12,15},{18,17},{16,... | collective-permute-start | bytes 442376 | tf_op jit(solution)/shard_map/ppermute | solution.py:96
  24.0 0.0 collective-permute-done.5.refs_6_
  24.0 1.3 %collective-permute-start = (bf16[144,512]{1,0:T(8,128)(2,1)}, bf16[144,512]{1,0:T(8,128)(2,1)S(1)}, u32[]{:S(2)}, u32[]{:S(2)}) collective-permute-start(bf16[144,512]{1,0:T(8,128)(2,1)} %shard_map.37.refs_0_), channel_id=1, source_target_pairs={{0,1},{2,3},{4,5},{6,7},{8,9},{10,11},{12,13},{14,15},{16,17},{18,... | collective-permute-start | bytes 442376 | tf_op jit(solution)/shard_map/ppermute | solution.py:96
  25.4 0.1 stack.47.order_ref
  25.5 0.0 copy-start.1
  25.5 0.0 collective-permute-done.4.refs_5_
  25.5 2.4 %collective-permute-done.3.refs_4_ = bf16[144,512]{1,0:T(8,128)(2,1)S(1)} collective-permute-done((bf16[144,512]{1,0:T(8,128)(2,1)}, bf16[144,512]{1,0:T(8,128)(2,1)S(1)}, u32[]{:S(2)}, u32[]{:S(2)}) %collective-permute-start.3) | collective-permute-done | bytes 147488 | tf_op jit(solution)/shard_map/ppermute | solution.py:96
  27.9 1.5 %collective-permute-done.2.refs_3_ = bf16[144,512]{1,0:T(8,128)(2,1)S(1)} collective-permute-done((bf16[144,512]{1,0:T(8,128)(2,1)}, bf16[144,512]{1,0:T(8,128)(2,1)S(1)}, u32[]{:S(2)}, u32[]{:S(2)}) %collective-permute-start.2) | collective-permute-done | bytes 147488 | tf_op jit(solution)/shard_map/ppermute | solution.py:96
  29.4 1.0 %collective-permute-done.1.refs_2_ = bf16[144,512]{1,0:T(8,128)(2,1)S(1)} collective-permute-done((bf16[144,512]{1,0:T(8,128)(2,1)}, bf16[144,512]{1,0:T(8,128)(2,1)S(1)}, u32[]{:S(2)}, u32[]{:S(2)}) %collective-permute-start.1) | collective-permute-done | bytes 147488 | tf_op jit(solution)/shard_map/ppermute | solution.py:96
  30.4 0.0 collective-permute-done.refs_1_
  30.4 0.0 copy-done
  30.4 0.0 copy-done.1
  30.4 2.5 %shard_map.38 = (f32[1,128]{1,0:T(1,128)S(1)}, f32[1,128]{1,0:T(1,128)S(1)}, f32[1,128]{1,0:T(1,128)S(1)}, f32[1,128]{1,0:T(1,128)S(1)}) custom-call(s32[11]{0:T(128)S(1)} %stack.47.order_ref, s32[1,64]{1,0:T(1,128)S(1)} %bitcast.15, bf16[144,512]{1,0:T(8,128)(2,1)S(1)} %copy-done, bf16[144,512]{1,0:T(8,128)(2,1)S(1)} %collective-permute-done.refs_1_, ...), custom_call_target="tpu_custom_call" | custom-call | tf_op jit(solution)/shard_map/pallas_call | solution.py:127
  32.9 1.9 %collective-permute-start.10 = (f32[1,128]{1,0:T(1,128)S(1)}, f32[1,128]{1,0:T(1,128)S(1)}, u32[]{:S(2)}, u32[]{:S(2)}) collective-permute-start(f32[1,128]{1,0:T(1,128)S(1)} %get-tuple-element.10), channel_id=1, source_target_pairs={{0,8},{1,9},{2,10},{3,11},{4,12},{5,13},{6,14},{7,15},{9,1},{11,3}... | collective-permute-start | bytes 1544 | tf_op jit(solution)/shard_map/ppermute | solution.py:136
  34.8 1.9 %collective-permute-start.11 = (f32[1,128]{1,0:T(1,128)S(1)}, f32[1,128]{1,0:T(1,128)S(1)}, u32[]{:S(2)}, u32[]{:S(2)}) collective-permute-start(f32[1,128]{1,0:T(1,128)S(1)} %get-tuple-element.11), channel_id=1, source_target_pairs={{0,16},{1,17},{2,18},{3,19},{4,20},{5,21},{6,22},{7,23},{8,24},{9,... | collective-permute-start | bytes 1544 | tf_op jit(solution)/shard_map/ppermute | solution.py:136
  36.8 5.4 %collective-permute-start.12 = (f32[1,128]{1,0:T(1,128)S(1)}, f32[1,128]{1,0:T(1,128)S(1)}, u32[]{:S(2)}, u32[]{:S(2)}) collective-permute-start(f32[1,128]{1,0:T(1,128)S(1)} %get-tuple-element.12), channel_id=1, source_target_pairs={{0,24},{1,25},{2,26},{3,27},{4,28},{5,29},{6,30},{7,31},{8,16},{9,... | collective-permute-start | bytes 1544 | tf_op jit(solution)/shard_map/ppermute | solution.py:136
  42.2 0.0 collective-permute-done.10
  42.2 0.0 collective-permute-done.11
  42.2 0.9 %collective-permute-done.12 = f32[1,128]{1,0:T(1,128)S(1)} collective-permute-done((f32[1,128]{1,0:T(1,128)S(1)}, f32[1,128]{1,0:T(1,128)S(1)}, u32[]{:S(2)}, u32[]{:S(2)}) %collective-permute-start.12) | collective-permute-done | bytes 544 | tf_op jit(solution)/shard_map/ppermute | solution.py:136
  43.1 0.5 %fusion.3 = f32[128]{0:T(128)} fusion(f32[1,128]{1,0:T(1,128)S(1)} %collective-permute-done.12, pred[]{:T(512)S(6)} %or.11, f32[1,128]{1,0:T(1,128)S(1)} %collective-permute-done.11, pred[]{:T(512)S(6)} %or.10, f32[1,128]{1,0:T(1,128)S(1)} %get-tuple-element.9, f32[1,128]{1,0:T(1,128)S(1)} %collective-permute-done.10, pred[]{:T(512)S(6)} %or.9), kind=kLoop, calls=%fused_computation.6 | loop fusion | flops 768 | bytes 2563 | tf_op jit(solution)/shard_map/reshape | solution.py:139
Async XLA Ops:
  1.7 28.7 %copy-start = (bf16[144,512]{1,0:T(8,128)(2,1)S(1)}, bf16[144,512]{1,0:T(8,128)(2,1)}, u32[]{:S(2)}) copy-start(bf16[144,512]{1,0:T(8,128)(2,1)} %shard_map.37.refs_0_) | copy-start | bytes 442372
  1.7 12.8 %collective-permute-start.9 = (bf16[144,512]{1,0:T(8,128)(2,1)}, bf16[144,512]{1,0:T(8,128)(2,1)S(1)}, u32[]{:S(2)}, u32[]{:S(2)}) collective-permute-start(bf16[144,512]{1,0:T(8,128)(2,1)} %shard_map.37.refs_0_), channel_id=1, source_target_pairs={{24,0},{25,1},{26,2},{27,3},{28,4},{29,5},{30,6},{31,7},{16,8},{17... | collective-permute-start | bytes 442376 | tf_op jit(solution)/shard_map/ppermute | solution.py:96
  7.9 12.3 %collective-permute-start.8 = (bf16[144,512]{1,0:T(8,128)(2,1)}, bf16[144,512]{1,0:T(8,128)(2,1)S(1)}, u32[]{:S(2)}, u32[]{:S(2)}) collective-permute-start(bf16[144,512]{1,0:T(8,128)(2,1)} %shard_map.37.refs_0_), channel_id=1, source_target_pairs={{16,0},{17,1},{18,2},{19,3},{20,4},{21,5},{22,6},{23,7},{24,8},{25... | collective-permute-start | bytes 442376 | tf_op jit(solution)/shard_map/ppermute | solution.py:96
  9.8 11.6 %collective-permute-start.7 = (bf16[144,512]{1,0:T(8,128)(2,1)}, bf16[144,512]{1,0:T(8,128)(2,1)S(1)}, u32[]{:S(2)}, u32[]{:S(2)}) collective-permute-start(bf16[144,512]{1,0:T(8,128)(2,1)} %shard_map.37.refs_0_), channel_id=1, source_target_pairs={{8,0},{9,1},{10,2},{11,3},{12,4},{13,5},{14,6},{15,7},{1,9},{3,11}... | collective-permute-start | bytes 442376 | tf_op jit(solution)/shard_map/ppermute | solution.py:96
  12.0 10.7 %collective-permute-start.6 = (bf16[144,512]{1,0:T(8,128)(2,1)}, bf16[144,512]{1,0:T(8,128)(2,1)S(1)}, u32[]{:S(2)}, u32[]{:S(2)}) collective-permute-start(bf16[144,512]{1,0:T(8,128)(2,1)} %shard_map.37.refs_0_), channel_id=1, source_target_pairs={{6,0},{7,1},{4,2},{5,3},{2,4},{3,5},{0,6},{1,7},{14,8},{15,9},{12,... | collective-permute-start | bytes 442376 | tf_op jit(solution)/shard_map/ppermute | solution.py:96
  14.2 9.8 %collective-permute-start.5 = (bf16[144,512]{1,0:T(8,128)(2,1)}, bf16[144,512]{1,0:T(8,128)(2,1)S(1)}, u32[]{:S(2)}, u32[]{:S(2)}) collective-permute-start(bf16[144,512]{1,0:T(8,128)(2,1)} %shard_map.37.refs_0_), channel_id=1, source_target_pairs={{4,0},{5,1},{6,2},{7,3},{0,4},{1,5},{2,6},{3,7},{12,8},{13,9},{14,... | collective-permute-start | bytes 442376 | tf_op jit(solution)/shard_map/ppermute | solution.py:96
  14.5 11.0 %collective-permute-start.4 = (bf16[144,512]{1,0:T(8,128)(2,1)}, bf16[144,512]{1,0:T(8,128)(2,1)S(1)}, u32[]{:S(2)}, u32[]{:S(2)}) collective-permute-start(bf16[144,512]{1,0:T(8,128)(2,1)} %shard_map.37.refs_0_), channel_id=1, source_target_pairs={{2,0},{3,1},{0,2},{1,3},{6,4},{7,5},{4,6},{5,7},{10,8},{11,9},{8,1... | collective-permute-start | bytes 442376 | tf_op jit(solution)/shard_map/ppermute | solution.py:96
  20.1 7.8 %collective-permute-start.3 = (bf16[144,512]{1,0:T(8,128)(2,1)}, bf16[144,512]{1,0:T(8,128)(2,1)S(1)}, u32[]{:S(2)}, u32[]{:S(2)}) collective-permute-start(bf16[144,512]{1,0:T(8,128)(2,1)} %shard_map.37.refs_0_), channel_id=1, source_target_pairs={{6,1},{4,3},{2,5},{0,7},{14,9},{12,11},{10,13},{8,15},{22,17},{20,... | collective-permute-start | bytes 442376 | tf_op jit(solution)/shard_map/ppermute | solution.py:96
  21.4 8.0 %collective-permute-start.2 = (bf16[144,512]{1,0:T(8,128)(2,1)}, bf16[144,512]{1,0:T(8,128)(2,1)S(1)}, u32[]{:S(2)}, u32[]{:S(2)}) collective-permute-start(bf16[144,512]{1,0:T(8,128)(2,1)} %shard_map.37.refs_0_), channel_id=1, source_target_pairs={{4,1},{6,3},{0,5},{2,7},{12,9},{14,11},{8,13},{10,15},{20,17},{22,... | collective-permute-start | bytes 442376 | tf_op jit(solution)/shard_map/ppermute | solution.py:96
  22.7 7.7 %collective-permute-start.1 = (bf16[144,512]{1,0:T(8,128)(2,1)}, bf16[144,512]{1,0:T(8,128)(2,1)S(1)}, u32[]{:S(2)}, u32[]{:S(2)}) collective-permute-start(bf16[144,512]{1,0:T(8,128)(2,1)} %shard_map.37.refs_0_), channel_id=1, source_target_pairs={{2,1},{0,3},{6,5},{4,7},{10,9},{8,11},{14,13},{12,15},{18,17},{16,... | collective-permute-start | bytes 442376 | tf_op jit(solution)/shard_map/ppermute | solution.py:96
  24.0 6.4 %collective-permute-start = (bf16[144,512]{1,0:T(8,128)(2,1)}, bf16[144,512]{1,0:T(8,128)(2,1)S(1)}, u32[]{:S(2)}, u32[]{:S(2)}) collective-permute-start(bf16[144,512]{1,0:T(8,128)(2,1)} %shard_map.37.refs_0_), channel_id=1, source_target_pairs={{0,1},{2,3},{4,5},{6,7},{8,9},{10,11},{12,13},{14,15},{16,17},{18,... | collective-permute-start | bytes 442376 | tf_op jit(solution)/shard_map/ppermute | solution.py:96
  25.5 4.9 %copy-start.1 = (s32[64]{0:T(128)S(1)}, s32[64]{0:T(128)}, u32[]{:S(2)}) copy-start(s32[64]{0:T(128)} %param.5) | copy-start | bytes 772
  32.9 9.3 %collective-permute-start.10 = (f32[1,128]{1,0:T(1,128)S(1)}, f32[1,128]{1,0:T(1,128)S(1)}, u32[]{:S(2)}, u32[]{:S(2)}) collective-permute-start(f32[1,128]{1,0:T(1,128)S(1)} %get-tuple-element.10), channel_id=1, source_target_pairs={{0,8},{1,9},{2,10},{3,11},{4,12},{5,13},{6,14},{7,15},{9,1},{11,3}... | collective-permute-start | bytes 1544 | tf_op jit(solution)/shard_map/ppermute | solution.py:136
  34.8 7.4 %collective-permute-start.11 = (f32[1,128]{1,0:T(1,128)S(1)}, f32[1,128]{1,0:T(1,128)S(1)}, u32[]{:S(2)}, u32[]{:S(2)}) collective-permute-start(f32[1,128]{1,0:T(1,128)S(1)} %get-tuple-element.11), channel_id=1, source_target_pairs={{0,16},{1,17},{2,18},{3,19},{4,20},{5,21},{6,22},{7,23},{8,24},{9,... | collective-permute-start | bytes 1544 | tf_op jit(solution)/shard_map/ppermute | solution.py:136
  36.8 6.4 %collective-permute-start.12 = (f32[1,128]{1,0:T(1,128)S(1)}, f32[1,128]{1,0:T(1,128)S(1)}, u32[]{:S(2)}, u32[]{:S(2)}) collective-permute-start(f32[1,128]{1,0:T(1,128)S(1)} %get-tuple-element.12), channel_id=1, source_target_pairs={{0,24},{1,25},{2,26},{3,27},{4,28},{5,29},{6,30},{7,31},{8,16},{9,... | collective-permute-start | bytes 1544 | tf_op jit(solution)/shard_map/ppermute | solution.py:136

commit v6 on v5

--- a/solution.py
+++ b/solution.py
@@ -49,32 +49,39 @@
     return jnp.where(a == b, 1.0, 0.5 * same).astype(jnp.bfloat16)
 
 
-def best_kernel(n_keys, groups, order_ref, group_ref, *refs):
-    n_in = (len(refs) + n_keys - 1) // 2
-    blocks, outs = refs[:n_in], refs[n_in:]
+def best_kernel(n_keys, groups, rank_ref, group_ref, *refs):
+    key_refs = refs[:n_keys]
+    count = (len(refs) - n_keys - 1) // 2
+    visitors, outs = refs[n_keys : n_keys + count], refs[n_keys + count :]
+    blocks = [ref.at[i] for ref in key_refs for i in range(ref.shape[0])]
+    n_blocks = len(blocks)
     rows = blocks[0].shape[0] - AUX
     clusters = group_ref.shape[1]
     table = weights_table(group_ref, groups)
-    hots = [one_hot(b[rows:, :rows].astype(jnp.float32), clusters) for b in blocks]
-    key_hot = jnp.concatenate(hots[:n_keys], axis=1)
-    keys = jnp.concatenate([b[:rows, :] for b in blocks[:n_keys]], axis=0)
-    for out, j in zip(outs, [0, *range(n_keys, n_in)]):
-        mixed = jnp.dot(table, hots[j], preferred_element_type=jnp.float32).astype(jnp.bfloat16)
+
+    def hot(block):
+        return one_hot(block[rows:, :rows].astype(jnp.float32), clusters)
+
+    key_hot = jnp.concatenate([hot(b) for b in blocks], axis=1)
+    keys = jnp.concatenate([b[:rows, :] for b in blocks], axis=0)
+    for j, (out, query) in enumerate(zip(outs, [blocks[0], *visitors])):
+        mixed = jnp.dot(table, hot(query), preferred_element_type=jnp.float32).astype(jnp.bfloat16)
         weight = lax.dot_general(key_hot, mixed, (((0,), (0,)), ((), ())), preferred_element_type=jnp.float32)
         sims = lax.dot_general(
-            keys, blocks[j][:rows, :], (((1,), (1,)), ((), ())), preferred_element_type=jnp.float32
+            keys, query[:rows, :], (((1,), (1,)), ((), ())), preferred_element_type=jnp.float32
         )
         score = jnp.where(weight > 0, weight * sims, -1.0)
         best = jnp.full((1, rows), -1.0, jnp.float32)
-        for i in range(n_keys):
+        rank = rank_ref[n_blocks + j - 1] if j else rank_ref[0]
+        for i in range(n_blocks):
             part = score[i * rows : (i + 1) * rows, :]
-            if i == j:
+            if i + j == 0:
                 k = lax.broadcasted_iota(jnp.int32, (rows, rows), 0)
                 q = lax.broadcasted_iota(jnp.int32, (rows, rows), 1)
                 part = jnp.where(k < q, part, -1.0)
             found = jnp.max(part, axis=0, keepdims=True)
-            if i != j:
-                found = jnp.where(order_ref[i] < order_ref[j], found, -1.0)
+            if i + j:
+                found = jnp.where(rank_ref[i] < rank, found, -1.0)
             best = jnp.maximum(best, found)
         out[...] = best
 
@@ -85,7 +92,7 @@
     wide = min(a for a in range(1, n_clu + 1) if n_clu % a == 0 and (a * n_grp >= target or a == n_clu))
     length = n_clu // wide
 
-    def permute(x, move):
+    def pairs_of(move):
         pairs = []
         for z in range(length):
             for a in range(wide):
@@ -93,6 +100,10 @@
                     at = move(z, a, g)
                     if at is not None:
                         pairs.append((((at[0] * wide) + at[1]) * n_grp + at[2], (z * wide + a) * n_grp + g))
+        return pairs
+
+    def permute(x, move):
+        pairs = pairs_of(move)
         return pairs, lax.ppermute(x, ("clu", "grp"), pairs)
 
     def turned(a, s, n):
@@ -107,22 +118,26 @@
         def rank(z, a, g):
             return jnp.where(g < 0, n_clu * n_grp, g * n_clu + z * wide + a)
 
+        half = length // 2 if length & (length - 1) == 0 else length
         visitors, ways, visitor_rank = [], [], []
         for s in range(1, length):
-            def visit(z, a, g, s=s):
-                at = turned(z, s, length)
-                return (at, a, g) if g > 0 or at > z else None
+            hop = s % half if s > half else s
 
-            pairs, block = permute(own, visit)
-            visitors.append(block)
-            ways.append(pairs)
+            def visit(z, a, g, by):
+                home = turned(z, s, length)
+                return (turned(z, by, length), a, g) if g > 0 or home > z else None
+
+            block = visitors[half - 1] if s > half else own
+            visitors.append(permute(block, lambda z, a, g: visit(z, a, g, hop))[1])
+            ways.append(pairs_of(lambda z, a, g: visit(z, a, g, s)))
             visitor_rank.append(rank(turned(line, s, length), place, grp))
-        keys, key_rank = [own], [rank(line, place, grp)]
-        for t in reversed(range(n_grp)):
-            for s in range(wide):
-                if s or t:
-                    keys.append(permute(own, lambda z, a, g: (z, turned(a, s, wide), g - t) if g >= t else None)[1])
-                    key_rank.append(rank(line, turned(place, s, wide), grp - t))
+        near = [permute(own, lambda z, a, g: (z, turned(a, s, wide), g))[1] for s in range(1, wide)]
+        near = jnp.stack([own] + near)
+        near_rank = [rank(line, turned(place, s, wide), grp) for s in range(wide)]
+        keys, key_rank = [near], near_rank
+        for t in range(1, n_grp):
+            keys.append(permute(near, lambda z, a, g: (z, a, g - t) if g >= t else None)[1])
+            key_rank = key_rank + [rank(line, turned(place, s, wide), grp - t) for s in range(wide)]
         vmem = pl.BlockSpec(memory_space=pltpu.VMEM)
         best = pl.pallas_call(
             functools.partial(best_kernel, len(keys), n_clu),

time: 43.9 us -> 46 us (1.048)
  waiting for transfers between devices: 11.2 us -> 16.3 us
  starting transfers between devices: 27.4 us -> 23.4 us
  other arithmetic: 0.52 us -> 1.57 us
    ppermute x10 -> x7, starting transfers between devices: 18.2 us -> 14.1 us  [permute(): return (pairs, lax.ppermute(x, ('clu', 'grp'), pairs))]
    ppermute x10 -> x7, waiting for transfers between devices: 10.3 us -> 13.9 us  [permute(): return (pairs, lax.ppermute(x, ('clu', 'grp'), pairs))]
    ppermute x3, waiting for transfers between devices: 0.88 us -> 2.41 us  [shards(): back = lax.ppermute(best[s], ('clu', 'grp'), [(to, at) for at, to in pairs])]
    another operation x0 -> x1, other arithmetic: none -> 1.06 us  [shards(): near = jnp.stack([own] + near)]
  transfers between devices with their start and end apart: 13 -> 10, of which waited for: 5 -> 5; matrix products, arithmetic and copies ran while one was open for 0% -> 0% of each run, Pallas kernels for 0% -> 0%
where the time goes in v6:
time: 46 us; the launch traced here: 45.7 us
  starting transfers between devices  23.4 us (51%)
  waiting for transfers between devices  16.3 us (35%)
  Pallas kernels  4.16 us (9%)
  other arithmetic  1.57 us (3%)
    ppermute x7, starting transfers between devices, permute(): return (pairs, lax.ppermute(x, ('clu', 'grp'), pairs))  14.1 us
    ppermute x7, waiting for transfers between devices, permute(): return (pairs, lax.ppermute(x, ('clu', 'grp'), pairs))  13.9 us
    ppermute x3, starting transfers between devices, shards(): back = lax.ppermute(best[s], ('clu', 'grp'), [(to, at) for at, to in pairs])  9.27 us
    pallas_call x1, Pallas kernels, shards(): pl.pallas_call(functools.partial(best_kernel, len(keys), n_clu), out_shap...  2.48 us
    ppermute x3, waiting for transfers between devices, shards(): back = lax.ppermute(best[s], ('clu', 'grp'), [(to, at) for at, to in pairs])  2.41 us
    pallas_call x1, Pallas kernels, pack(): pl.pallas_call(pack_kernel, out_shape=jax.ShapeDtypeStruct((rows + AUX, w...  1.68 us
    another operation x1, other arithmetic, shards(): near = jnp.stack([own] + near)  1.06 us
  transfers between devices with their start and end apart: 10, of which 5 were waited for; matrix products, arithmetic and copies ran while one was open for 0% of the time, Pallas kernels for 0%

profile of v6, /device:TPU:1, one launch (start us, length us, event | category | flops | bytes accessed | tf_op | source)
XLA Modules:
  0.0 45.7 jit_solution(4656198493740493459)
XLA Ops:
  0.0 1.7 %shard_map.37 = bf16[144,512]{1,0:T(8,128)(2,1)} custom-call(bf16[128,512]{1,0:T(8,128)(2,1)} %emb_ref.1, s32[1,128]{1,0:T(1,128)} %bitcast.24), custom_call_target="tpu_custom_call" | custom-call | tf_op jit(solution)/shard_map/pallas_call | solution.py:30
  1.7 3.0 %collective-permute-start.2 = (bf16[144,512]{1,0:T(8,128)(2,1)}, bf16[144,512]{1,0:T(8,128)(2,1)S(1)}, u32[]{:S(2)}, u32[]{:S(2)}) collective-permute-start(bf16[144,512]{1,0:T(8,128)(2,1)} %shard_map.37), channel_id=1, source_target_pairs={{6,0},{7,1},{4,2},{5,3},{2,4},{3,5},{0,6},{1,7},{14,8},{15,9},{12,... | collective-permute-start | bytes 442376 | tf_op jit(solution)/shard_map/ppermute | solution.py:107
  4.7 0.2 collective-permute-start.1
  4.9 0.1 collective-permute-start
  5.0 3.5 %collective-permute-done.2 = bf16[144,512]{1,0:T(8,128)(2,1)S(1)} collective-permute-done((bf16[144,512]{1,0:T(8,128)(2,1)}, bf16[144,512]{1,0:T(8,128)(2,1)S(1)}, u32[]{:S(2)}, u32[]{:S(2)}) %collective-permute-start.2) | collective-permute-done | bytes 147488 | tf_op jit(solution)/shard_map/ppermute | solution.py:107
  8.5 3.9 %collective-permute-done.1 = bf16[144,512]{1,0:T(8,128)(2,1)S(1)} collective-permute-done((bf16[144,512]{1,0:T(8,128)(2,1)}, bf16[144,512]{1,0:T(8,128)(2,1)S(1)}, u32[]{:S(2)}, u32[]{:S(2)}) %collective-permute-start.1) | collective-permute-done | bytes 147488 | tf_op jit(solution)/shard_map/ppermute | solution.py:107
  12.3 0.0 collective-permute-done
  12.3 0.0 copy-start.1
  12.4 1.1 %pad_maximum_fusion.refs_0_ = bf16[4,144,512]{2,1,0:T(8,128)(2,1)S(1)} fusion(bf16[1,144,512]{2,1,0:T(8,128)(2,1)S(1)} %bitcast.21, bf16[1,144,512]{2,1,0:T(8,128)(2,1)S(1)} %bitcast.22, bf16[1,144,512]{2,1,0:T(8,128)(2,1)S(1)} %bitcast.23, bf16[1,144,512]{2,1,0:T(8,128)(2,1)} %bitcast.20), kind=kLoop, calls=%fused_computation | loop fusion | flops 884736 | bytes 1179648 | tf_op jit(solution)/shard_map/stack | solution.py:135
  13.4 1.3 %collective-permute-start.3 = (bf16[4,144,512]{2,1,0:T(8,128)(2,1)S(1)}, bf16[4,144,512]{2,1,0:T(8,128)(2,1)S(1)}, u32[]{:S(2)}, u32[]{:S(2)}) collective-permute-start(bf16[4,144,512]{2,1,0:T(8,128)(2,1)S(1)} %pad_maximum_fusion.refs_0_), channel_id=1, source_target_pairs={{0,1},{2,3},{4,5},{6,7},{8,9},{10,11},{12,13},{14,15},{16,17},{18,... | collective-permute-start | bytes 1769480 | tf_op jit(solution)/shard_map/ppermute | solution.py:107
  14.7 0.0 copy-done.1
  14.7 4.4 %collective-permute-start.5 = (bf16[144,512]{1,0:T(8,128)(2,1)S(1)}, bf16[144,512]{1,0:T(8,128)(2,1)S(1)}, u32[]{:S(2)}, u32[]{:S(2)}) collective-permute-start(bf16[144,512]{1,0:T(8,128)(2,1)S(1)} %copy-done.1), channel_id=1, source_target_pairs={{16,0},{17,1},{18,2},{19,3},{20,4},{21,5},{22,6},{23,7},{24,8},{25... | collective-permute-start | bytes 442376 | tf_op jit(solution)/shard_map/ppermute | solution.py:107
  19.1 3.2 %collective-permute-start.4 = (bf16[144,512]{1,0:T(8,128)(2,1)S(1)}, bf16[144,512]{1,0:T(8,128)(2,1)S(1)}, u32[]{:S(2)}, u32[]{:S(2)}) collective-permute-start(bf16[144,512]{1,0:T(8,128)(2,1)S(1)} %copy-done.1), channel_id=1, source_target_pairs={{8,0},{9,1},{10,2},{11,3},{12,4},{13,5},{14,6},{15,7},{1,9},{3,11}... | collective-permute-start | bytes 442376 | tf_op jit(solution)/shard_map/ppermute | solution.py:107
  22.4 2.7 %collective-permute-done.5.refs_3_ = bf16[144,512]{1,0:T(8,128)(2,1)S(1)} collective-permute-done((bf16[144,512]{1,0:T(8,128)(2,1)S(1)}, bf16[144,512]{1,0:T(8,128)(2,1)S(1)}, u32[]{:S(2)}, u32[]{:S(2)}) %collective-permute-start.5) | collective-permute-done | bytes 147488 | tf_op jit(solution)/shard_map/ppermute | solution.py:107
  25.1 1.9 %collective-permute-start.6 = (bf16[144,512]{1,0:T(8,128)(2,1)S(1)}, bf16[144,512]{1,0:T(8,128)(2,1)S(1)}, u32[]{:S(2)}, u32[]{:S(2)}) collective-permute-start(bf16[144,512]{1,0:T(8,128)(2,1)S(1)} %collective-permute-done.5.refs_3_), channel_id=1, source_target_pairs={{8,0},{9,1},{10,2},{11,3},{12,4},{13,5},{14,6},{15,7},{0,8},{1,9},... | collective-permute-start | bytes 442376 | tf_op jit(solution)/shard_map/ppermute | solution.py:107
  27.0 0.1 stack.62.rank_ref
  27.1 0.0 copy-start
  27.1 0.0 collective-permute-done.4.refs_2_
  27.1 3.8 %collective-permute-done.6.refs_4_ = bf16[144,512]{1,0:T(8,128)(2,1)S(1)} collective-permute-done((bf16[144,512]{1,0:T(8,128)(2,1)S(1)}, bf16[144,512]{1,0:T(8,128)(2,1)S(1)}, u32[]{:S(2)}, u32[]{:S(2)}) %collective-permute-start.6) | collective-permute-done | bytes 147488 | tf_op jit(solution)/shard_map/ppermute | solution.py:107
  30.9 0.0 collective-permute-done.3.refs_1_
  30.9 0.0 copy-done
  30.9 2.5 %shard_map.38 = (f32[1,128]{1,0:T(1,128)S(1)}, f32[1,128]{1,0:T(1,128)S(1)}, f32[1,128]{1,0:T(1,128)S(1)}, f32[1,128]{1,0:T(1,128)S(1)}) custom-call(s32[11]{0:T(128)S(1)} %stack.62.rank_ref, s32[1,64]{1,0:T(1,128)S(1)} %bitcast.19, bf16[4,144,512]{2,1,0:T(8,128)(2,1)S(1)} %pad_maximum_fusion.refs_0_, ...), custom_call_target="tpu_custom_call" | custom-call | tf_op jit(solution)/shard_map/pallas_call | solution.py:142
  33.4 1.9 %collective-permute-start.7 = (f32[1,128]{1,0:T(1,128)S(1)}, f32[1,128]{1,0:T(1,128)S(1)}, u32[]{:S(2)}, u32[]{:S(2)}) collective-permute-start(f32[1,128]{1,0:T(1,128)S(1)} %get-tuple-element.10), channel_id=1, source_target_pairs={{0,8},{1,9},{2,10},{3,11},{4,12},{5,13},{6,14},{7,15},{9,1},{11,3}... | collective-permute-start | bytes 1544 | tf_op jit(solution)/shard_map/ppermute | solution.py:151
  35.4 3.7 %collective-permute-start.8 = (f32[1,128]{1,0:T(1,128)S(1)}, f32[1,128]{1,0:T(1,128)S(1)}, u32[]{:S(2)}, u32[]{:S(2)}) collective-permute-start(f32[1,128]{1,0:T(1,128)S(1)} %get-tuple-element.11), channel_id=1, source_target_pairs={{0,16},{1,17},{2,18},{3,19},{4,20},{5,21},{6,22},{7,23},{8,24},{9,... | collective-permute-start | bytes 1544 | tf_op jit(solution)/shard_map/ppermute | solution.py:151
  39.1 3.6 %collective-permute-start.9 = (f32[1,128]{1,0:T(1,128)S(1)}, f32[1,128]{1,0:T(1,128)S(1)}, u32[]{:S(2)}, u32[]{:S(2)}) collective-permute-start(f32[1,128]{1,0:T(1,128)S(1)} %get-tuple-element.12), channel_id=1, source_target_pairs={{0,24},{1,25},{2,26},{3,27},{4,28},{5,29},{6,30},{7,31},{8,16},{9,... | collective-permute-start | bytes 1544 | tf_op jit(solution)/shard_map/ppermute | solution.py:151
  42.7 0.0 collective-permute-done.7
  42.8 0.0 collective-permute-done.8
  42.8 2.4 %collective-permute-done.9 = f32[1,128]{1,0:T(1,128)S(1)} collective-permute-done((f32[1,128]{1,0:T(1,128)S(1)}, f32[1,128]{1,0:T(1,128)S(1)}, u32[]{:S(2)}, u32[]{:S(2)}) %collective-permute-start.9) | collective-permute-done | bytes 544 | tf_op jit(solution)/shard_map/ppermute | solution.py:151
  45.2 0.5 %fusion.3 = f32[128]{0:T(128)} fusion(f32[1,128]{1,0:T(1,128)S(1)} %collective-permute-done.9, pred[]{:T(512)S(6)} %or.11, f32[1,128]{1,0:T(1,128)S(1)} %collective-permute-done.8, pred[]{:T(512)S(6)} %or.10, f32[1,128]{1,0:T(1,128)S(1)} %get-tuple-element.9, f32[1,128]{1,0:T(1,128)S(1)} %collective-permute-done.7, pred[]{:T(512)S(6)} %or.9), kind=kLoop, calls=%fused_computation.7 | loop fusion | flops 768 | bytes 2563 | tf_op jit(solution)/shard_map/reshape | solution.py:154
Async XLA Ops:
  1.7 6.8 %collective-permute-start.2 = (bf16[144,512]{1,0:T(8,128)(2,1)}, bf16[144,512]{1,0:T(8,128)(2,1)S(1)}, u32[]{:S(2)}, u32[]{:S(2)}) collective-permute-start(bf16[144,512]{1,0:T(8,128)(2,1)} %shard_map.37), channel_id=1, source_target_pairs={{6,0},{7,1},{4,2},{5,3},{2,4},{3,5},{0,6},{1,7},{14,8},{15,9},{12,... | collective-permute-start | bytes 442376 | tf_op jit(solution)/shard_map/ppermute | solution.py:107
  4.7 7.7 %collective-permute-start.1 = (bf16[144,512]{1,0:T(8,128)(2,1)}, bf16[144,512]{1,0:T(8,128)(2,1)S(1)}, u32[]{:S(2)}, u32[]{:S(2)}) collective-permute-start(bf16[144,512]{1,0:T(8,128)(2,1)} %shard_map.37), channel_id=1, source_target_pairs={{4,0},{5,1},{6,2},{7,3},{0,4},{1,5},{2,6},{3,7},{12,8},{13,9},{14,... | collective-permute-start | bytes 442376 | tf_op jit(solution)/shard_map/ppermute | solution.py:107
  4.9 7.4 %collective-permute-start = (bf16[144,512]{1,0:T(8,128)(2,1)}, bf16[144,512]{1,0:T(8,128)(2,1)S(1)}, u32[]{:S(2)}, u32[]{:S(2)}) collective-permute-start(bf16[144,512]{1,0:T(8,128)(2,1)} %shard_map.37), channel_id=1, source_target_pairs={{2,0},{3,1},{0,2},{1,3},{6,4},{7,5},{4,6},{5,7},{10,8},{11,9},{8,1... | collective-permute-start | bytes 442376 | tf_op jit(solution)/shard_map/ppermute | solution.py:107
  12.3 2.4 %copy-start.1 = (bf16[144,512]{1,0:T(8,128)(2,1)S(1)}, bf16[144,512]{1,0:T(8,128)(2,1)}, u32[]{:S(2)}) copy-start(bf16[144,512]{1,0:T(8,128)(2,1)} %shard_map.37) | copy-start | bytes 442372
  13.4 17.5 %collective-permute-start.3 = (bf16[4,144,512]{2,1,0:T(8,128)(2,1)S(1)}, bf16[4,144,512]{2,1,0:T(8,128)(2,1)S(1)}, u32[]{:S(2)}, u32[]{:S(2)}) collective-permute-start(bf16[4,144,512]{2,1,0:T(8,128)(2,1)S(1)} %pad_maximum_fusion.refs_0_), channel_id=1, source_target_pairs={{0,1},{2,3},{4,5},{6,7},{8,9},{10,11},{12,13},{14,15},{16,17},{18,... | collective-permute-start | bytes 1769480 | tf_op jit(solution)/shard_map/ppermute | solution.py:107
  14.7 10.3 %collective-permute-start.5 = (bf16[144,512]{1,0:T(8,128)(2,1)S(1)}, bf16[144,512]{1,0:T(8,128)(2,1)S(1)}, u32[]{:S(2)}, u32[]{:S(2)}) collective-permute-start(bf16[144,512]{1,0:T(8,128)(2,1)S(1)} %copy-done.1), channel_id=1, source_target_pairs={{16,0},{17,1},{18,2},{19,3},{20,4},{21,5},{22,6},{23,7},{24,8},{25... | collective-permute-start | bytes 442376 | tf_op jit(solution)/shard_map/ppermute | solution.py:107
  19.1 8.0 %collective-permute-start.4 = (bf16[144,512]{1,0:T(8,128)(2,1)S(1)}, bf16[144,512]{1,0:T(8,128)(2,1)S(1)}, u32[]{:S(2)}, u32[]{:S(2)}) collective-permute-start(bf16[144,512]{1,0:T(8,128)(2,1)S(1)} %copy-done.1), channel_id=1, source_target_pairs={{8,0},{9,1},{10,2},{11,3},{12,4},{13,5},{14,6},{15,7},{1,9},{3,11}... | collective-permute-start | bytes 442376 | tf_op jit(solution)/shard_map/ppermute | solution.py:107
  25.1 5.9 %collective-permute-start.6 = (bf16[144,512]{1,0:T(8,128)(2,1)S(1)}, bf16[144,512]{1,0:T(8,128)(2,1)S(1)}, u32[]{:S(2)}, u32[]{:S(2)}) collective-permute-start(bf16[144,512]{1,0:T(8,128)(2,1)S(1)} %collective-permute-done.5.refs_3_), channel_id=1, source_target_pairs={{8,0},{9,1},{10,2},{11,3},{12,4},{13,5},{14,6},{15,7},{0,8},{1,9},... | collective-permute-start | bytes 442376 | tf_op jit(solution)/shard_map/ppermute | solution.py:107
  27.1 3.8 %copy-start = (s32[64]{0:T(128)S(1)}, s32[64]{0:T(128)}, u32[]{:S(2)}) copy-start(s32[64]{0:T(128)} %param.5) | copy-start | bytes 772
  33.4 9.3 %collective-permute-start.7 = (f32[1,128]{1,0:T(1,128)S(1)}, f32[1,128]{1,0:T(1,128)S(1)}, u32[]{:S(2)}, u32[]{:S(2)}) collective-permute-start(f32[1,128]{1,0:T(1,128)S(1)} %get-tuple-element.10), channel_id=1, source_target_pairs={{0,8},{1,9},{2,10},{3,11},{4,12},{5,13},{6,14},{7,15},{9,1},{11,3}... | collective-permute-start | bytes 1544 | tf_op jit(solution)/shard_map/ppermute | solution.py:151
  35.4 7.4 %collective-permute-start.8 = (f32[1,128]{1,0:T(1,128)S(1)}, f32[1,128]{1,0:T(1,128)S(1)}, u32[]{:S(2)}, u32[]{:S(2)}) collective-permute-start(f32[1,128]{1,0:T(1,128)S(1)} %get-tuple-element.11), channel_id=1, source_target_pairs={{0,16},{1,17},{2,18},{3,19},{4,20},{5,21},{6,22},{7,23},{8,24},{9,... | collective-permute-start | bytes 1544 | tf_op jit(solution)/shard_map/ppermute | solution.py:151
  39.1 6.1 %collective-permute-start.9 = (f32[1,128]{1,0:T(1,128)S(1)}, f32[1,128]{1,0:T(1,128)S(1)}, u32[]{:S(2)}, u32[]{:S(2)}) collective-permute-start(f32[1,128]{1,0:T(1,128)S(1)} %get-tuple-element.12), channel_id=1, source_target_pairs={{0,24},{1,25},{2,26},{3,27},{4,28},{5,29},{6,30},{7,31},{8,16},{9,... | collective-permute-start | bytes 1544 | tf_op jit(solution)/shard_map/ppermute | solution.py:151

commit v7 on v6

--- a/solution.py
+++ b/solution.py
@@ -19,7 +19,7 @@
     out_ref[:rows, :] = (values * scale).astype(jnp.bfloat16)
     ids = jnp.broadcast_to(id_ref[...], (AUX, rows))
     row = lax.broadcasted_iota(jnp.int32, (AUX, rows), 0)
-    digits = jnp.where(row == 0, ids % DIGIT, jnp.where(row == 1, ids // DIGIT, 1))
+    digits = jnp.where(row == 0, ids % DIGIT, ids // DIGIT)
     if width > rows:
         digits = jnp.concatenate([digits, jnp.zeros((AUX, width - rows), jnp.int32)], axis=1)
     out_ref[rows:, :] = digits.astype(jnp.float32).astype(jnp.bfloat16)
@@ -36,7 +36,7 @@
 def one_hot(digits, clusters):
     number = digits[0:1].astype(jnp.int32) + DIGIT * digits[1:2].astype(jnp.int32)
     index = lax.broadcasted_iota(jnp.int32, (clusters, digits.shape[1]), 0)
-    return jnp.where((index == number) & (digits[2:3] > 0), 1.0, 0.0).astype(jnp.bfloat16)
+    return jnp.where(index == number, 1.0, 0.0).astype(jnp.bfloat16)
 
 
 def weights_table(group_ref, groups):
@@ -92,22 +92,17 @@
     wide = min(a for a in range(1, n_clu + 1) if n_clu % a == 0 and (a * n_grp >= target or a == n_clu))
     length = n_clu // wide
 
-    def pairs_of(move):
+    def permute(x, move):
         pairs = []
         for z in range(length):
             for a in range(wide):
                 for g in range(n_grp):
                     at = move(z, a, g)
-                    if at is not None:
-                        pairs.append((((at[0] * wide) + at[1]) * n_grp + at[2], (z * wide + a) * n_grp + g))
-        return pairs
-
-    def permute(x, move):
-        pairs = pairs_of(move)
-        return pairs, lax.ppermute(x, ("clu", "grp"), pairs)
+                    pairs.append(((at[0] * wide + at[1]) * n_grp + at[2], (z * wide + a) * n_grp + g))
+        return lax.ppermute(x, ("clu", "grp"), pairs)
 
     def turned(a, s, n):
-        return a ^ s if n & (n - 1) == 0 else (a + s) % n
+        return a ^ abs(s) if n & (n - 1) == 0 else (a + s) % n
 
     def shards(embeddings, cluster_id, cluster_group):
         rows = embeddings.shape[0]
@@ -116,28 +111,22 @@
         line, place = clu // wide, clu % wide
 
         def rank(z, a, g):
-            return jnp.where(g < 0, n_clu * n_grp, g * n_clu + z * wide + a)
+            return g * n_clu + z * wide + a
 
         half = length // 2 if length & (length - 1) == 0 else length
-        visitors, ways, visitor_rank = [], [], []
-        for s in range(1, length):
-            hop = s % half if s > half else s
-
-            def visit(z, a, g, by):
-                home = turned(z, s, length)
-                return (turned(z, by, length), a, g) if g > 0 or home > z else None
-
-            block = visitors[half - 1] if s > half else own
-            visitors.append(permute(block, lambda z, a, g: visit(z, a, g, hop))[1])
-            ways.append(pairs_of(lambda z, a, g: visit(z, a, g, s)))
-            visitor_rank.append(rank(turned(line, s, length), place, grp))
-        near = [permute(own, lambda z, a, g: (z, turned(a, s, wide), g))[1] for s in range(1, wide)]
+        first = [permute(own, lambda z, a, g: (turned(z, s, length), a, g)) for s in range(1, min(half + 1, length))]
+        near = [permute(own, lambda z, a, g: (z, turned(a, s, wide), g)) for s in range(1, wide)]
+        first, near = lax.optimization_barrier((first, near))
+        visitors = first + [
+            permute(first[half - 1], lambda z, a, g: (turned(z, s, length), a, g)) for s in range(1, length - half)
+        ]
+        visitor_rank = [rank(turned(line, s, length), place, grp) for s in range(1, length)]
         near = jnp.stack([own] + near)
-        near_rank = [rank(line, turned(place, s, wide), grp) for s in range(wide)]
-        keys, key_rank = [near], near_rank
+        keys = [near]
+        key_rank = [rank(line, turned(place, s, wide), grp) for s in range(wide)]
         for t in range(1, n_grp):
-            keys.append(permute(near, lambda z, a, g: (z, a, g - t) if g >= t else None)[1])
-            key_rank = key_rank + [rank(line, turned(place, s, wide), grp - t) for s in range(wide)]
+            keys.append(permute(near, lambda z, a, g: (z, a, turned(g, t, n_grp))))
+            key_rank += [rank(line, turned(place, s, wide), turned(grp, t, n_grp)) for s in range(wide)]
         vmem = pl.BlockSpec(memory_space=pltpu.VMEM)
         best = pl.pallas_call(
             functools.partial(best_kernel, len(keys), n_clu),
@@ -147,10 +136,8 @@
             compiler_params=pltpu.CompilerParams(vmem_limit_bytes=48 * 2**20),
         )(jnp.stack(key_rank + visitor_rank).astype(jnp.int32), cluster_group.reshape(1, -1), *keys, *visitors)
         found = [best[0]]
-        for s, pairs in zip(range(1, length), ways):
-            back = lax.ppermute(best[s], ("clu", "grp"), [(to, at) for at, to in pairs])
-            at = line ^ s if length & (length - 1) == 0 else (line - s) % length
-            found.append(jnp.where((grp > 0) | (at < line), back, -1.0))
+        for s in range(1, length):
+            found.append(permute(best[s], lambda z, a, g: (turned(z, -s, length), a, g)))
         return functools.reduce(jnp.maximum, found).reshape(rows)
 
     placed = (P(("clu", "grp"), None), P(("clu", "grp")), P())

time: 46 us -> 35.6 us (0.77)
  the two profiles are of different devices: /device:TPU:1 before, /device:TPU:0 now
where the time goes in v7:
time: 35.6 us; the launch traced here: 35.4 us
  starting transfers between devices  15.1 us (42%)
  waiting for transfers between devices  14.6 us (41%)
  Pallas kernels  4.16 us (12%)
  other arithmetic  1.5 us (4%)
    ppermute x10, starting transfers between devices, permute(): return lax.ppermute(x, ('clu', 'grp'), pairs)  15.1 us
    ppermute x10, waiting for transfers between devices, permute(): return lax.ppermute(x, ('clu', 'grp'), pairs)  14.6 us
    pallas_call x1, Pallas kernels, shards(): pl.pallas_call(functools.partial(best_kernel, len(keys), n_clu), out_shap...  2.49 us
    pallas_call x1, Pallas kernels, pack(): pl.pallas_call(pack_kernel, out_shape=jax.ShapeDtypeStruct((rows + AUX, w...  1.67 us
    another operation x1, other arithmetic, shards(): near = jnp.stack([own] + near)  0.98 us
  transfers between devices with their start and end apart: 10, of which 7 were waited for; matrix products, arithmetic and copies ran while one was open for 0% of the time, Pallas kernels for 0%

profile of v7, /device:TPU:0, one launch (start us, length us, event | category | flops | bytes accessed | tf_op | source)
XLA Modules:
  0.0 35.4 jit_solution(6815694488050557361)
XLA Ops:
  0.0 1.7 %shard_map.37 = bf16[144,512]{1,0:T(8,128)(2,1)} custom-call(bf16[128,512]{1,0:T(8,128)(2,1)} %emb_ref.1, s32[1,128]{1,0:T(1,128)} %bitcast.24), custom_call_target="tpu_custom_call" | custom-call | tf_op jit(solution)/shard_map/pallas_call | solution.py:30
  1.7 3.9 %collective-permute-start.4 = (bf16[144,512]{1,0:T(8,128)(2,1)}, bf16[144,512]{1,0:T(8,128)(2,1)S(1)}, u32[]{:S(2)}, u32[]{:S(2)}) collective-permute-start(bf16[144,512]{1,0:T(8,128)(2,1)} %shard_map.37), channel_id=1, source_target_pairs={{6,0},{7,1},{4,2},{5,3},{2,4},{3,5},{0,6},{1,7},{14,8},{15,9},{12,... | collective-permute-start | bytes 442376 | tf_op jit(solution)/shard_map/ppermute | solution.py:102
  5.6 0.5 %collective-permute-start.3 = (bf16[144,512]{1,0:T(8,128)(2,1)}, bf16[144,512]{1,0:T(8,128)(2,1)S(1)}, u32[]{:S(2)}, u32[]{:S(2)}) collective-permute-start(bf16[144,512]{1,0:T(8,128)(2,1)} %shard_map.37), channel_id=1, source_target_pairs={{4,0},{5,1},{6,2},{7,3},{0,4},{1,5},{2,6},{3,7},{12,8},{13,9},{14,... | collective-permute-start | bytes 442376 | tf_op jit(solution)/shard_map/ppermute | solution.py:102
  6.1 0.1 collective-permute-start.2
  6.1 3.1 %collective-permute-start.1 = (bf16[144,512]{1,0:T(8,128)(2,1)}, bf16[144,512]{1,0:T(8,128)(2,1)S(1)}, u32[]{:S(2)}, u32[]{:S(2)}) collective-permute-start(bf16[144,512]{1,0:T(8,128)(2,1)} %shard_map.37), channel_id=1, source_target_pairs={{16,0},{17,1},{18,2},{19,3},{20,4},{21,5},{22,6},{23,7},{24,8},{25... | collective-permute-start | bytes 442376 | tf_op jit(solution)/shard_map/ppermute | solution.py:102
  9.2 1.6 %collective-permute-start = (bf16[144,512]{1,0:T(8,128)(2,1)}, bf16[144,512]{1,0:T(8,128)(2,1)S(1)}, u32[]{:S(2)}, u32[]{:S(2)}) collective-permute-start(bf16[144,512]{1,0:T(8,128)(2,1)} %shard_map.37), channel_id=1, source_target_pairs={{8,0},{9,1},{10,2},{11,3},{12,4},{13,5},{14,6},{15,7},{0,8},{1,9},... | collective-permute-start | bytes 442376 | tf_op jit(solution)/shard_map/ppermute | solution.py:102
  10.8 0.0 collective-permute-done.4
  10.8 2.0 %collective-permute-done.3 = bf16[144,512]{1,0:T(8,128)(2,1)S(1)} collective-permute-done((bf16[144,512]{1,0:T(8,128)(2,1)}, bf16[144,512]{1,0:T(8,128)(2,1)S(1)}, u32[]{:S(2)}, u32[]{:S(2)}) %collective-permute-start.3) | collective-permute-done | bytes 147488 | tf_op jit(solution)/shard_map/ppermute | solution.py:102
  12.8 0.3 collective-permute-done.2
  13.1 2.6 %collective-permute-done.1.refs_3_ = bf16[144,512]{1,0:T(8,128)(2,1)S(1)} collective-permute-done((bf16[144,512]{1,0:T(8,128)(2,1)}, bf16[144,512]{1,0:T(8,128)(2,1)S(1)}, u32[]{:S(2)}, u32[]{:S(2)}) %collective-permute-start.1) | collective-permute-done | bytes 147488 | tf_op jit(solution)/shard_map/ppermute | solution.py:102
  15.7 0.3 collective-permute-done.refs_2_
  15.9 1.0 %pad_maximum_fusion.refs_0_ = bf16[4,144,512]{2,1,0:T(8,128)(2,1)S(1)} fusion(bf16[1,144,512]{2,1,0:T(8,128)(2,1)S(1)} %bitcast.21, bf16[1,144,512]{2,1,0:T(8,128)(2,1)S(1)} %bitcast.22, bf16[1,144,512]{2,1,0:T(8,128)(2,1)S(1)} %bitcast.23, bf16[1,144,512]{2,1,0:T(8,128)(2,1)} %bitcast.20), kind=kLoop, calls=%fused_computation | loop fusion | flops 884736 | bytes 1179648 | tf_op jit(solution)/shard_map/stack | solution.py:124
  16.9 0.1 collective-permute-start.5
  17.0 1.5 %collective-permute-start.6 = (bf16[144,512]{1,0:T(8,128)(2,1)S(1)}, bf16[144,512]{1,0:T(8,128)(2,1)S(1)}, u32[]{:S(2)}, u32[]{:S(2)}) collective-permute-start(bf16[144,512]{1,0:T(8,128)(2,1)S(1)} %collective-permute-done.1.refs_3_), channel_id=1, source_target_pairs={{8,0},{9,1},{10,2},{11,3},{12,4},{13,5},{14,6},{15,7},{0,8},{1,9},... | collective-permute-start | bytes 442376 | tf_op jit(solution)/shard_map/ppermute | solution.py:102
  18.4 0.1 stack.62.rank_ref
  18.5 0.0 copy-start
  18.5 4.7 %collective-permute-done.6.refs_4_ = bf16[144,512]{1,0:T(8,128)(2,1)S(1)} collective-permute-done((bf16[144,512]{1,0:T(8,128)(2,1)S(1)}, bf16[144,512]{1,0:T(8,128)(2,1)S(1)}, u32[]{:S(2)}, u32[]{:S(2)}) %collective-permute-start.6) | collective-permute-done | bytes 147488 | tf_op jit(solution)/shard_map/ppermute | solution.py:102
  23.2 0.0 collective-permute-done.5.refs_1_
  23.2 0.0 copy-done
  23.2 2.5 %shard_map.38 = (f32[1,128]{1,0:T(1,128)S(1)}, f32[1,128]{1,0:T(1,128)S(1)}, f32[1,128]{1,0:T(1,128)S(1)}, f32[1,128]{1,0:T(1,128)S(1)}) custom-call(s32[11]{0:T(128)S(1)} %stack.62.rank_ref, s32[1,64]{1,0:T(1,128)S(1)} %bitcast.19, bf16[4,144,512]{2,1,0:T(8,128)(2,1)S(1)} %pad_maximum_fusion.refs_0_, ...), custom_call_target="tpu_custom_call" | custom-call | tf_op jit(solution)/shard_map/pallas_call | solution.py:131
  25.7 1.5 %collective-permute-start.7 = (f32[1,128]{1,0:T(1,128)S(1)}, f32[1,128]{1,0:T(1,128)S(1)}, u32[]{:S(2)}, u32[]{:S(2)}) collective-permute-start(f32[1,128]{1,0:T(1,128)S(1)} %get-tuple-element.20), channel_id=1, source_target_pairs={{8,0},{9,1},{10,2},{11,3},{12,4},{13,5},{14,6},{15,7},{0,8},{1,9},... | collective-permute-start | bytes 1544 | tf_op jit(solution)/shard_map/ppermute | solution.py:102
  27.2 2.4 %collective-permute-start.8 = (f32[1,128]{1,0:T(1,128)S(1)}, f32[1,128]{1,0:T(1,128)S(1)}, u32[]{:S(2)}, u32[]{:S(2)}) collective-permute-start(f32[1,128]{1,0:T(1,128)S(1)} %get-tuple-element.21), channel_id=1, source_target_pairs={{16,0},{17,1},{18,2},{19,3},{20,4},{21,5},{22,6},{23,7},{24,8},{25... | collective-permute-start | bytes 1544 | tf_op jit(solution)/shard_map/ppermute | solution.py:102
  29.6 0.6 %collective-permute-start.9 = (f32[1,128]{1,0:T(1,128)S(1)}, f32[1,128]{1,0:T(1,128)S(1)}, u32[]{:S(2)}, u32[]{:S(2)}) collective-permute-start(f32[1,128]{1,0:T(1,128)S(1)} %get-tuple-element.22), channel_id=1, source_target_pairs={{24,0},{25,1},{26,2},{27,3},{28,4},{29,5},{30,6},{31,7},{16,8},{17... | collective-permute-start | bytes 1544 | tf_op jit(solution)/shard_map/ppermute | solution.py:102
  30.2 0.0 collective-permute-done.7
  30.2 1.4 %collective-permute-done.8 = f32[1,128]{1,0:T(1,128)S(1)} collective-permute-done((f32[1,128]{1,0:T(1,128)S(1)}, f32[1,128]{1,0:T(1,128)S(1)}, u32[]{:S(2)}, u32[]{:S(2)}) %collective-permute-start.8) | collective-permute-done | bytes 544 | tf_op jit(solution)/shard_map/ppermute | solution.py:102
  31.6 3.3 %collective-permute-done.9 = f32[1,128]{1,0:T(1,128)S(1)} collective-permute-done((f32[1,128]{1,0:T(1,128)S(1)}, f32[1,128]{1,0:T(1,128)S(1)}, u32[]{:S(2)}, u32[]{:S(2)}) %collective-permute-start.9) | collective-permute-done | bytes 544 | tf_op jit(solution)/shard_map/ppermute | solution.py:102
  34.9 0.5 %maximum_bitcast_fusion = f32[128]{0:T(128)} fusion(f32[1,128]{1,0:T(1,128)S(1)} %collective-permute-done.9, f32[1,128]{1,0:T(1,128)S(1)} %collective-permute-done.8, f32[1,128]{1,0:T(1,128)S(1)} %get-tuple-element.19, f32[1,128]{1,0:T(1,128)S(1)} %collective-permute-done.7), kind=kLoop, calls=%fused_computation.1 | loop fusion | flops 384 | bytes 2560 | tf_op jit(solution)/shard_map/reshape | solution.py:141
Async XLA Ops:
  1.7 9.1 %collective-permute-start.4 = (bf16[144,512]{1,0:T(8,128)(2,1)}, bf16[144,512]{1,0:T(8,128)(2,1)S(1)}, u32[]{:S(2)}, u32[]{:S(2)}) collective-permute-start(bf16[144,512]{1,0:T(8,128)(2,1)} %shard_map.37), channel_id=1, source_target_pairs={{6,0},{7,1},{4,2},{5,3},{2,4},{3,5},{0,6},{1,7},{14,8},{15,9},{12,... | collective-permute-start | bytes 442376 | tf_op jit(solution)/shard_map/ppermute | solution.py:102
  5.6 7.2 %collective-permute-start.3 = (bf16[144,512]{1,0:T(8,128)(2,1)}, bf16[144,512]{1,0:T(8,128)(2,1)S(1)}, u32[]{:S(2)}, u32[]{:S(2)}) collective-permute-start(bf16[144,512]{1,0:T(8,128)(2,1)} %shard_map.37), channel_id=1, source_target_pairs={{4,0},{5,1},{6,2},{7,3},{0,4},{1,5},{2,6},{3,7},{12,8},{13,9},{14,... | collective-permute-start | bytes 442376 | tf_op jit(solution)/shard_map/ppermute | solution.py:102
  6.1 7.0 %collective-permute-start.2 = (bf16[144,512]{1,0:T(8,128)(2,1)}, bf16[144,512]{1,0:T(8,128)(2,1)S(1)}, u32[]{:S(2)}, u32[]{:S(2)}) collective-permute-start(bf16[144,512]{1,0:T(8,128)(2,1)} %shard_map.37), channel_id=1, source_target_pairs={{2,0},{3,1},{0,2},{1,3},{6,4},{7,5},{4,6},{5,7},{10,8},{11,9},{8,1... | collective-permute-start | bytes 442376 | tf_op jit(solution)/shard_map/ppermute | solution.py:102
  6.1 9.5 %collective-permute-start.1 = (bf16[144,512]{1,0:T(8,128)(2,1)}, bf16[144,512]{1,0:T(8,128)(2,1)S(1)}, u32[]{:S(2)}, u32[]{:S(2)}) collective-permute-start(bf16[144,512]{1,0:T(8,128)(2,1)} %shard_map.37), channel_id=1, source_target_pairs={{16,0},{17,1},{18,2},{19,3},{20,4},{21,5},{22,6},{23,7},{24,8},{25... | collective-permute-start | bytes 442376 | tf_op jit(solution)/shard_map/ppermute | solution.py:102
  9.2 6.7 %collective-permute-start = (bf16[144,512]{1,0:T(8,128)(2,1)}, bf16[144,512]{1,0:T(8,128)(2,1)S(1)}, u32[]{:S(2)}, u32[]{:S(2)}) collective-permute-start(bf16[144,512]{1,0:T(8,128)(2,1)} %shard_map.37), channel_id=1, source_target_pairs={{8,0},{9,1},{10,2},{11,3},{12,4},{13,5},{14,6},{15,7},{0,8},{1,9},... | collective-permute-start | bytes 442376 | tf_op jit(solution)/shard_map/ppermute | solution.py:102
  16.9 6.3 %collective-permute-start.5 = (bf16[4,144,512]{2,1,0:T(8,128)(2,1)S(1)}, bf16[4,144,512]{2,1,0:T(8,128)(2,1)S(1)}, u32[]{:S(2)}, u32[]{:S(2)}) collective-permute-start(bf16[4,144,512]{2,1,0:T(8,128)(2,1)S(1)} %pad_maximum_fusion.refs_0_), channel_id=1, source_target_pairs={{1,0},{0,1},{3,2},{2,3},{5,4},{4,5},{7,6},{6,7},{9,8},{8,9},{11,10... | collective-permute-start | bytes 1769480 | tf_op jit(solution)/shard_map/ppermute | solution.py:102
  17.0 6.3 %collective-permute-start.6 = (bf16[144,512]{1,0:T(8,128)(2,1)S(1)}, bf16[144,512]{1,0:T(8,128)(2,1)S(1)}, u32[]{:S(2)}, u32[]{:S(2)}) collective-permute-start(bf16[144,512]{1,0:T(8,128)(2,1)S(1)} %collective-permute-done.1.refs_3_), channel_id=1, source_target_pairs={{8,0},{9,1},{10,2},{11,3},{12,4},{13,5},{14,6},{15,7},{0,8},{1,9},... | collective-permute-start | bytes 442376 | tf_op jit(solution)/shard_map/ppermute | solution.py:102
  18.5 4.7 %copy-start = (s32[64]{0:T(128)S(1)}, s32[64]{0:T(128)}, u32[]{:S(2)}) copy-start(s32[64]{0:T(128)} %param.5) | copy-start | bytes 772
  25.7 4.5 %collective-permute-start.7 = (f32[1,128]{1,0:T(1,128)S(1)}, f32[1,128]{1,0:T(1,128)S(1)}, u32[]{:S(2)}, u32[]{:S(2)}) collective-permute-start(f32[1,128]{1,0:T(1,128)S(1)} %get-tuple-element.20), channel_id=1, source_target_pairs={{8,0},{9,1},{10,2},{11,3},{12,4},{13,5},{14,6},{15,7},{0,8},{1,9},... | collective-permute-start | bytes 1544 | tf_op jit(solution)/shard_map/ppermute | solution.py:102
  27.2 4.4 %collective-permute-start.8 = (f32[1,128]{1,0:T(1,128)S(1)}, f32[1,128]{1,0:T(1,128)S(1)}, u32[]{:S(2)}, u32[]{:S(2)}) collective-permute-start(f32[1,128]{1,0:T(1,128)S(1)} %get-tuple-element.21), channel_id=1, source_target_pairs={{16,0},{17,1},{18,2},{19,3},{20,4},{21,5},{22,6},{23,7},{24,8},{25... | collective-permute-start | bytes 1544 | tf_op jit(solution)/shard_map/ppermute | solution.py:102
  29.6 5.3 %collective-permute-start.9 = (f32[1,128]{1,0:T(1,128)S(1)}, f32[1,128]{1,0:T(1,128)S(1)}, u32[]{:S(2)}, u32[]{:S(2)}) collective-permute-start(f32[1,128]{1,0:T(1,128)S(1)} %get-tuple-element.22), channel_id=1, source_target_pairs={{24,0},{25,1},{26,2},{27,3},{28,4},{29,5},{30,6},{31,7},{16,8},{17... | collective-permute-start | bytes 1544 | tf_op jit(solution)/shard_map/ppermute | solution.py:102

commit v8 on v7

--- a/solution.py
+++ b/solution.py
@@ -50,11 +50,9 @@
 
 
 def best_kernel(n_keys, groups, rank_ref, group_ref, *refs):
-    key_refs = refs[:n_keys]
+    blocks = refs[:n_keys]
     count = (len(refs) - n_keys - 1) // 2
     visitors, outs = refs[n_keys : n_keys + count], refs[n_keys + count :]
-    blocks = [ref.at[i] for ref in key_refs for i in range(ref.shape[0])]
-    n_blocks = len(blocks)
     rows = blocks[0].shape[0] - AUX
     clusters = group_ref.shape[1]
     table = weights_table(group_ref, groups)
@@ -72,8 +70,8 @@
         )
         score = jnp.where(weight > 0, weight * sims, -1.0)
         best = jnp.full((1, rows), -1.0, jnp.float32)
-        rank = rank_ref[n_blocks + j - 1] if j else rank_ref[0]
-        for i in range(n_blocks):
+        rank = rank_ref[n_keys + j - 1] if j else rank_ref[0]
+        for i in range(n_keys):
             part = score[i * rows : (i + 1) * rows, :]
             if i + j == 0:
                 k = lax.broadcasted_iota(jnp.int32, (rows, rows), 0)
@@ -114,19 +112,19 @@
             return g * n_clu + z * wide + a
 
         half = length // 2 if length & (length - 1) == 0 else length
+        near = [permute(own, lambda z, a, g: (z, turned(a, s, wide), g)) for s in range(1, wide)]
         first = [permute(own, lambda z, a, g: (turned(z, s, length), a, g)) for s in range(1, min(half + 1, length))]
-        near = [permute(own, lambda z, a, g: (z, turned(a, s, wide), g)) for s in range(1, wide)]
-        first, near = lax.optimization_barrier((first, near))
+        near, first = lax.optimization_barrier((near, first))
         visitors = first + [
             permute(first[half - 1], lambda z, a, g: (turned(z, s, length), a, g)) for s in range(1, length - half)
         ]
         visitor_rank = [rank(turned(line, s, length), place, grp) for s in range(1, length)]
-        near = jnp.stack([own] + near)
-        keys = [near]
+        keys = [own] + near
         key_rank = [rank(line, turned(place, s, wide), grp) for s in range(wide)]
         for t in range(1, n_grp):
-            keys.append(permute(near, lambda z, a, g: (z, a, turned(g, t, n_grp))))
-            key_rank += [rank(line, turned(place, s, wide), turned(grp, t, n_grp)) for s in range(wide)]
+            for s in range(wide):
+                keys.append(permute(keys[s], lambda z, a, g: (z, a, turned(g, t, n_grp))))
+                key_rank.append(rank(line, turned(place, s, wide), turned(grp, t, n_grp)))
         vmem = pl.BlockSpec(memory_space=pltpu.VMEM)
         best = pl.pallas_call(
             functools.partial(best_kernel, len(keys), n_clu),

time: 35.6 us -> 33.7 us (0.947)
  waiting for transfers between devices: 14.6 us -> 13.3 us
  other arithmetic: 1.5 us -> 0.52 us
  local copies, waits for them, and re-layouts: 0.09 us -> 1 us
  starting transfers between devices: 15.1 us -> 14.5 us
    ppermute x10 -> x13, waiting for transfers between devices: 14.6 us -> 13.3 us  [permute(): return lax.ppermute(x, ('clu', 'grp'), pairs)]
    another operation x1 -> x0, other arithmetic: 0.98 us -> none  [shards(): near = jnp.stack([own] + near)]
    unnamed x2 -> x4, local copies, waits for them, and re-layouts: 0.01 us -> 0.91 us
    ppermute x10 -> x13, starting transfers between devices: 15.1 us -> 14.5 us  [permute(): return lax.ppermute(x, ('clu', 'grp'), pairs)]
  transfers between devices with their start and end apart: 10 -> 13, of which waited for: 7 -> 11; matrix products, arithmetic and copies ran while one was open for 0% -> 0% of each run, Pallas kernels for 0% -> 0%
where the time goes in v8:
time: 33.7 us; the launch traced here: 33.5 us
  starting transfers between devices  14.5 us (43%)
  waiting for transfers between devices  13.3 us (39%)
  Pallas kernels  4.15 us (12%)
  local copies, waits for them, and re-layouts  1 us (3%)
  other arithmetic  0.52 us (2%)
    ppermute x13, starting transfers between devices, permute(): return lax.ppermute(x, ('clu', 'grp'), pairs)  14.5 us
    ppermute x13, waiting for transfers between devices, permute(): return lax.ppermute(x, ('clu', 'grp'), pairs)  13.3 us
    pallas_call x1, Pallas kernels, shards(): pl.pallas_call(functools.partial(best_kernel, len(keys), n_clu), out_shap...  2.48 us
    pallas_call x1, Pallas kernels, pack(): pl.pallas_call(pack_kernel, out_shape=jax.ShapeDtypeStruct((rows + AUX, w...  1.68 us
    unnamed x4, local copies, waits for them, and re-layouts  0.91 us
  transfers between devices with their start and end apart: 13, of which 11 were waited for; matrix products, arithmetic and copies ran while one was open for 0% of the time, Pallas kernels for 0%

profile of v8, /device:TPU:0, one launch (start us, length us, event | category | flops | bytes accessed | tf_op | source)
XLA Modules:
  0.0 33.5 jit_solution(7630388484902880376)
XLA Ops:
  0.0 1.7 %shard_map.37.refs_0_ = bf16[144,512]{1,0:T(8,128)(2,1)} custom-call(bf16[128,512]{1,0:T(8,128)(2,1)} %emb_ref.1, s32[1,128]{1,0:T(1,128)} %bitcast.16), custom_call_target="tpu_custom_call" | custom-call | tf_op jit(solution)/shard_map/pallas_call | solution.py:30
  1.7 4.0 %collective-permute-start.4 = (bf16[144,512]{1,0:T(8,128)(2,1)}, bf16[144,512]{1,0:T(8,128)(2,1)S(1)}, u32[]{:S(2)}, u32[]{:S(2)}) collective-permute-start(bf16[144,512]{1,0:T(8,128)(2,1)} %shard_map.37.refs_0_), channel_id=1, source_target_pairs={{16,0},{17,1},{18,2},{19,3},{20,4},{21,5},{22,6},{23,7},{24,8},{25... | collective-permute-start | bytes 442376 | tf_op jit(solution)/shard_map/ppermute | solution.py:100
  5.7 1.6 %collective-permute-start.3 = (bf16[144,512]{1,0:T(8,128)(2,1)}, bf16[144,512]{1,0:T(8,128)(2,1)S(1)}, u32[]{:S(2)}, u32[]{:S(2)}) collective-permute-start(bf16[144,512]{1,0:T(8,128)(2,1)} %shard_map.37.refs_0_), channel_id=1, source_target_pairs={{8,0},{9,1},{10,2},{11,3},{12,4},{13,5},{14,6},{15,7},{0,8},{1,9},... | collective-permute-start | bytes 442376 | tf_op jit(solution)/shard_map/ppermute | solution.py:100
  7.3 2.4 %collective-permute-start.2 = (bf16[144,512]{1,0:T(8,128)(2,1)}, bf16[144,512]{1,0:T(8,128)(2,1)S(1)}, u32[]{:S(2)}, u32[]{:S(2)}) collective-permute-start(bf16[144,512]{1,0:T(8,128)(2,1)} %shard_map.37.refs_0_), channel_id=1, source_target_pairs={{6,0},{7,1},{4,2},{5,3},{2,4},{3,5},{0,6},{1,7},{14,8},{15,9},{12,... | collective-permute-start | bytes 442376 | tf_op jit(solution)/shard_map/ppermute | solution.py:100
  9.7 0.5 %collective-permute-start.1 = (bf16[144,512]{1,0:T(8,128)(2,1)}, bf16[144,512]{1,0:T(8,128)(2,1)S(1)}, u32[]{:S(2)}, u32[]{:S(2)}) collective-permute-start(bf16[144,512]{1,0:T(8,128)(2,1)} %shard_map.37.refs_0_), channel_id=1, source_target_pairs={{4,0},{5,1},{6,2},{7,3},{0,4},{1,5},{2,6},{3,7},{12,8},{13,9},{14,... | collective-permute-start | bytes 442376 | tf_op jit(solution)/shard_map/ppermute | solution.py:100
  10.2 0.5 %collective-permute-start = (bf16[144,512]{1,0:T(8,128)(2,1)}, bf16[144,512]{1,0:T(8,128)(2,1)S(1)}, u32[]{:S(2)}, u32[]{:S(2)}) collective-permute-start(bf16[144,512]{1,0:T(8,128)(2,1)} %shard_map.37.refs_0_), channel_id=1, source_target_pairs={{2,0},{3,1},{0,2},{1,3},{6,4},{7,5},{4,6},{5,7},{10,8},{11,9},{8,1... | collective-permute-start | bytes 442376 | tf_op jit(solution)/shard_map/ppermute | solution.py:100
  10.8 2.3 %collective-permute-done.4.refs_9_ = bf16[144,512]{1,0:T(8,128)(2,1)S(1)} collective-permute-done((bf16[144,512]{1,0:T(8,128)(2,1)}, bf16[144,512]{1,0:T(8,128)(2,1)S(1)}, u32[]{:S(2)}, u32[]{:S(2)}) %collective-permute-start.4) | collective-permute-done | bytes 147488 | tf_op jit(solution)/shard_map/ppermute | solution.py:100
  13.0 0.0 collective-permute-start.5
  13.0 0.2 collective-permute-done.3.refs_8_
  13.2 1.2 %collective-permute-done.2.refs_3_ = bf16[144,512]{1,0:T(8,128)(2,1)S(1)} collective-permute-done((bf16[144,512]{1,0:T(8,128)(2,1)}, bf16[144,512]{1,0:T(8,128)(2,1)S(1)}, u32[]{:S(2)}, u32[]{:S(2)}) %collective-permute-start.2) | collective-permute-done | bytes 147488 | tf_op jit(solution)/shard_map/ppermute | solution.py:100
  14.4 2.2 %collective-permute-done.1.refs_2_ = bf16[144,512]{1,0:T(8,128)(2,1)S(1)} collective-permute-done((bf16[144,512]{1,0:T(8,128)(2,1)}, bf16[144,512]{1,0:T(8,128)(2,1)S(1)}, u32[]{:S(2)}, u32[]{:S(2)}) %collective-permute-start.1) | collective-permute-done | bytes 147488 | tf_op jit(solution)/shard_map/ppermute | solution.py:100
  16.6 0.1 collective-permute-done.refs_1_
  16.6 0.0 collective-permute-start.6
  16.6 0.5 %collective-permute-start.7 = (bf16[144,512]{1,0:T(8,128)(2,1)S(1)}, bf16[144,512]{1,0:T(8,128)(2,1)S(1)}, u32[]{:S(2)}, u32[]{:S(2)}) collective-permute-start(bf16[144,512]{1,0:T(8,128)(2,1)S(1)} %collective-permute-done.1.refs_2_), channel_id=1, source_target_pairs={{1,0},{0,1},{3,2},{2,3},{5,4},{4,5},{7,6},{6,7},{9,8},{8,9},{11,10... | collective-permute-start | bytes 442376 | tf_op jit(solution)/shard_map/ppermute | solution.py:100
  17.2 0.0 collective-permute-start.8
  17.2 0.4 %collective-permute-start.9 = (bf16[144,512]{1,0:T(8,128)(2,1)S(1)}, bf16[144,512]{1,0:T(8,128)(2,1)S(1)}, u32[]{:S(2)}, u32[]{:S(2)}) collective-permute-start(bf16[144,512]{1,0:T(8,128)(2,1)S(1)} %collective-permute-done.4.refs_9_), channel_id=1, source_target_pairs={{8,0},{9,1},{10,2},{11,3},{12,4},{13,5},{14,6},{15,7},{0,8},{1,9},... | collective-permute-start | bytes 442376 | tf_op jit(solution)/shard_map/ppermute | solution.py:100
  17.6 0.1 stack.47.rank_ref
  17.7 0.0 copy-start.1
  17.7 0.0 collective-permute-done.5.refs_4_
  17.7 0.3 collective-permute-done.6.refs_5_
  18.0 0.2 collective-permute-done.7.refs_6_
  18.2 0.3 collective-permute-done.8.refs_7_
  18.5 4.9 %collective-permute-done.9.refs_10_ = bf16[144,512]{1,0:T(8,128)(2,1)S(1)} collective-permute-done((bf16[144,512]{1,0:T(8,128)(2,1)S(1)}, bf16[144,512]{1,0:T(8,128)(2,1)S(1)}, u32[]{:S(2)}, u32[]{:S(2)}) %collective-permute-start.9) | collective-permute-done | bytes 147488 | tf_op jit(solution)/shard_map/ppermute | solution.py:100
  23.4 0.0 copy-done.1
  23.4 0.0 copy-start
  23.4 0.9 %copy-done = bf16[144,512]{1,0:T(8,128)(2,1)S(1)} copy-done((bf16[144,512]{1,0:T(8,128)(2,1)S(1)}, bf16[144,512]{1,0:T(8,128)(2,1)}, u32[]{:S(2)}) %copy-start) | copy-done | bytes 147480
  24.3 2.5 %shard_map.38 = (f32[1,128]{1,0:T(1,128)S(1)}, f32[1,128]{1,0:T(1,128)S(1)}, f32[1,128]{1,0:T(1,128)S(1)}, f32[1,128]{1,0:T(1,128)S(1)}) custom-call(s32[11]{0:T(128)S(1)} %stack.47.rank_ref, s32[1,64]{1,0:T(1,128)S(1)} %bitcast.15, bf16[144,512]{1,0:T(8,128)(2,1)S(1)} %copy-done, bf16[144,512]{1,0:T(8,128)(2,1)S(1)} %collective-permute-done.refs_1_, ...), custom_call_target="tpu_custom_call" | custom-call | tf_op jit(solution)/shard_map/pallas_call | solution.py:129
  26.8 0.5 %collective-permute-start.10 = (f32[1,128]{1,0:T(1,128)S(1)}, f32[1,128]{1,0:T(1,128)S(1)}, u32[]{:S(2)}, u32[]{:S(2)}) collective-permute-start(f32[1,128]{1,0:T(1,128)S(1)} %get-tuple-element.20), channel_id=1, source_target_pairs={{8,0},{9,1},{10,2},{11,3},{12,4},{13,5},{14,6},{15,7},{0,8},{1,9},... | collective-permute-start | bytes 1544 | tf_op jit(solution)/shard_map/ppermute | solution.py:100
  27.3 0.3 %collective-permute-start.11 = (f32[1,128]{1,0:T(1,128)S(1)}, f32[1,128]{1,0:T(1,128)S(1)}, u32[]{:S(2)}, u32[]{:S(2)}) collective-permute-start(f32[1,128]{1,0:T(1,128)S(1)} %get-tuple-element.21), channel_id=1, source_target_pairs={{16,0},{17,1},{18,2},{19,3},{20,4},{21,5},{22,6},{23,7},{24,8},{25... | collective-permute-start | bytes 1544 | tf_op jit(solution)/shard_map/ppermute | solution.py:100
  27.7 3.6 %collective-permute-start.12 = (f32[1,128]{1,0:T(1,128)S(1)}, f32[1,128]{1,0:T(1,128)S(1)}, u32[]{:S(2)}, u32[]{:S(2)}) collective-permute-start(f32[1,128]{1,0:T(1,128)S(1)} %get-tuple-element.22), channel_id=1, source_target_pairs={{24,0},{25,1},{26,2},{27,3},{28,4},{29,5},{30,6},{31,7},{16,8},{17... | collective-permute-start | bytes 1544 | tf_op jit(solution)/shard_map/ppermute | solution.py:100
  31.3 0.0 collective-permute-done.10
  31.3 0.5 %collective-permute-done.11 = f32[1,128]{1,0:T(1,128)S(1)} collective-permute-done((f32[1,128]{1,0:T(1,128)S(1)}, f32[1,128]{1,0:T(1,128)S(1)}, u32[]{:S(2)}, u32[]{:S(2)}) %collective-permute-start.11) | collective-permute-done | bytes 544 | tf_op jit(solution)/shard_map/ppermute | solution.py:100
  31.8 1.2 %collective-permute-done.12 = f32[1,128]{1,0:T(1,128)S(1)} collective-permute-done((f32[1,128]{1,0:T(1,128)S(1)}, f32[1,128]{1,0:T(1,128)S(1)}, u32[]{:S(2)}, u32[]{:S(2)}) %collective-permute-start.12) | collective-permute-done | bytes 544 | tf_op jit(solution)/shard_map/ppermute | solution.py:100
  33.0 0.5 %maximum_bitcast_fusion = f32[128]{0:T(128)} fusion(f32[1,128]{1,0:T(1,128)S(1)} %collective-permute-done.12, f32[1,128]{1,0:T(1,128)S(1)} %collective-permute-done.11, f32[1,128]{1,0:T(1,128)S(1)} %get-tuple-element.19, f32[1,128]{1,0:T(1,128)S(1)} %collective-permute-done.10), kind=kLoop, calls=%fused_computation | loop fusion | flops 384 | bytes 2560 | tf_op jit(solution)/shard_map/reshape | solution.py:139
Async XLA Ops:
  1.7 11.4 %collective-permute-start.4 = (bf16[144,512]{1,0:T(8,128)(2,1)}, bf16[144,512]{1,0:T(8,128)(2,1)S(1)}, u32[]{:S(2)}, u32[]{:S(2)}) collective-permute-start(bf16[144,512]{1,0:T(8,128)(2,1)} %shard_map.37.refs_0_), channel_id=1, source_target_pairs={{16,0},{17,1},{18,2},{19,3},{20,4},{21,5},{22,6},{23,7},{24,8},{25... | collective-permute-start | bytes 442376 | tf_op jit(solution)/shard_map/ppermute | solution.py:100
  5.7 7.5 %collective-permute-start.3 = (bf16[144,512]{1,0:T(8,128)(2,1)}, bf16[144,512]{1,0:T(8,128)(2,1)S(1)}, u32[]{:S(2)}, u32[]{:S(2)}) collective-permute-start(bf16[144,512]{1,0:T(8,128)(2,1)} %shard_map.37.refs_0_), channel_id=1, source_target_pairs={{8,0},{9,1},{10,2},{11,3},{12,4},{13,5},{14,6},{15,7},{0,8},{1,9},... | collective-permute-start | bytes 442376 | tf_op jit(solution)/shard_map/ppermute | solution.py:100
  7.3 7.1 %collective-permute-start.2 = (bf16[144,512]{1,0:T(8,128)(2,1)}, bf16[144,512]{1,0:T(8,128)(2,1)S(1)}, u32[]{:S(2)}, u32[]{:S(2)}) collective-permute-start(bf16[144,512]{1,0:T(8,128)(2,1)} %shard_map.37.refs_0_), channel_id=1, source_target_pairs={{6,0},{7,1},{4,2},{5,3},{2,4},{3,5},{0,6},{1,7},{14,8},{15,9},{12,... | collective-permute-start | bytes 442376 | tf_op jit(solution)/shard_map/ppermute | solution.py:100
  9.7 6.8 %collective-permute-start.1 = (bf16[144,512]{1,0:T(8,128)(2,1)}, bf16[144,512]{1,0:T(8,128)(2,1)S(1)}, u32[]{:S(2)}, u32[]{:S(2)}) collective-permute-start(bf16[144,512]{1,0:T(8,128)(2,1)} %shard_map.37.refs_0_), channel_id=1, source_target_pairs={{4,0},{5,1},{6,2},{7,3},{0,4},{1,5},{2,6},{3,7},{12,8},{13,9},{14,... | collective-permute-start | bytes 442376 | tf_op jit(solution)/shard_map/ppermute | solution.py:100
  10.2 6.4 %collective-permute-start = (bf16[144,512]{1,0:T(8,128)(2,1)}, bf16[144,512]{1,0:T(8,128)(2,1)S(1)}, u32[]{:S(2)}, u32[]{:S(2)}) collective-permute-start(bf16[144,512]{1,0:T(8,128)(2,1)} %shard_map.37.refs_0_), channel_id=1, source_target_pairs={{2,0},{3,1},{0,2},{1,3},{6,4},{7,5},{4,6},{5,7},{10,8},{11,9},{8,1... | collective-permute-start | bytes 442376 | tf_op jit(solution)/shard_map/ppermute | solution.py:100
  13.0 4.7 %collective-permute-start.5 = (bf16[144,512]{1,0:T(8,128)(2,1)}, bf16[144,512]{1,0:T(8,128)(2,1)S(1)}, u32[]{:S(2)}, u32[]{:S(2)}) collective-permute-start(bf16[144,512]{1,0:T(8,128)(2,1)} %shard_map.37.refs_0_), channel_id=1, source_target_pairs={{1,0},{0,1},{3,2},{2,3},{5,4},{4,5},{7,6},{6,7},{9,8},{8,9},{11,10... | collective-permute-start | bytes 442376 | tf_op jit(solution)/shard_map/ppermute | solution.py:100
  16.6 1.4 %collective-permute-start.6 = (bf16[144,512]{1,0:T(8,128)(2,1)S(1)}, bf16[144,512]{1,0:T(8,128)(2,1)S(1)}, u32[]{:S(2)}, u32[]{:S(2)}) collective-permute-start(bf16[144,512]{1,0:T(8,128)(2,1)S(1)} %collective-permute-done.refs_1_), channel_id=1, source_target_pairs={{1,0},{0,1},{3,2},{2,3},{5,4},{4,5},{7,6},{6,7},{9,8},{8,9},{11,10... | collective-permute-start | bytes 442376 | tf_op jit(solution)/shard_map/ppermute | solution.py:100
  16.6 1.6 %collective-permute-start.7 = (bf16[144,512]{1,0:T(8,128)(2,1)S(1)}, bf16[144,512]{1,0:T(8,128)(2,1)S(1)}, u32[]{:S(2)}, u32[]{:S(2)}) collective-permute-start(bf16[144,512]{1,0:T(8,128)(2,1)S(1)} %collective-permute-done.1.refs_2_), channel_id=1, source_target_pairs={{1,0},{0,1},{3,2},{2,3},{5,4},{4,5},{7,6},{6,7},{9,8},{8,9},{11,10... | collective-permute-start | bytes 442376 | tf_op jit(solution)/shard_map/ppermute | solution.py:100
  17.2 1.4 %collective-permute-start.8 = (bf16[144,512]{1,0:T(8,128)(2,1)S(1)}, bf16[144,512]{1,0:T(8,128)(2,1)S(1)}, u32[]{:S(2)}, u32[]{:S(2)}) collective-permute-start(bf16[144,512]{1,0:T(8,128)(2,1)S(1)} %collective-permute-done.2.refs_3_), channel_id=1, source_target_pairs={{1,0},{0,1},{3,2},{2,3},{5,4},{4,5},{7,6},{6,7},{9,8},{8,9},{11,10... | collective-permute-start | bytes 442376 | tf_op jit(solution)/shard_map/ppermute | solution.py:100
  17.2 6.3 %collective-permute-start.9 = (bf16[144,512]{1,0:T(8,128)(2,1)S(1)}, bf16[144,512]{1,0:T(8,128)(2,1)S(1)}, u32[]{:S(2)}, u32[]{:S(2)}) collective-permute-start(bf16[144,512]{1,0:T(8,128)(2,1)S(1)} %collective-permute-done.4.refs_9_), channel_id=1, source_target_pairs={{8,0},{9,1},{10,2},{11,3},{12,4},{13,5},{14,6},{15,7},{0,8},{1,9},... | collective-permute-start | bytes 442376 | tf_op jit(solution)/shard_map/ppermute | solution.py:100
  17.7 5.7 %copy-start.1 = (s32[64]{0:T(128)S(1)}, s32[64]{0:T(128)}, u32[]{:S(2)}) copy-start(s32[64]{0:T(128)} %param.5) | copy-start | bytes 772
  23.4 0.9 %copy-start = (bf16[144,512]{1,0:T(8,128)(2,1)S(1)}, bf16[144,512]{1,0:T(8,128)(2,1)}, u32[]{:S(2)}) copy-start(bf16[144,512]{1,0:T(8,128)(2,1)} %shard_map.37.refs_0_) | copy-start | bytes 442372
  26.8 4.5 %collective-permute-start.10 = (f32[1,128]{1,0:T(1,128)S(1)}, f32[1,128]{1,0:T(1,128)S(1)}, u32[]{:S(2)}, u32[]{:S(2)}) collective-permute-start(f32[1,128]{1,0:T(1,128)S(1)} %get-tuple-element.20), channel_id=1, source_target_pairs={{8,0},{9,1},{10,2},{11,3},{12,4},{13,5},{14,6},{15,7},{0,8},{1,9},... | collective-permute-start | bytes 1544 | tf_op jit(solution)/shard_map/ppermute | solution.py:100
  27.3 4.4 %collective-permute-start.11 = (f32[1,128]{1,0:T(1,128)S(1)}, f32[1,128]{1,0:T(1,128)S(1)}, u32[]{:S(2)}, u32[]{:S(2)}) collective-permute-start(f32[1,128]{1,0:T(1,128)S(1)} %get-tuple-element.21), channel_id=1, source_target_pairs={{16,0},{17,1},{18,2},{19,3},{20,4},{21,5},{22,6},{23,7},{24,8},{25... | collective-permute-start | bytes 1544 | tf_op jit(solution)/shard_map/ppermute | solution.py:100
  27.7 5.3 %collective-permute-start.12 = (f32[1,128]{1,0:T(1,128)S(1)}, f32[1,128]{1,0:T(1,128)S(1)}, u32[]{:S(2)}, u32[]{:S(2)}) collective-permute-start(f32[1,128]{1,0:T(1,128)S(1)} %get-tuple-element.22), channel_id=1, source_target_pairs={{24,0},{25,1},{26,2},{27,3},{28,4},{29,5},{30,6},{31,7},{16,8},{17... | collective-permute-start | bytes 1544 | tf_op jit(solution)/shard_map/ppermute | solution.py:100

commit v9 on v8

v9 whole, which is shorter than its diff:
```python
import functools
import math

import jax
import jax.numpy as jnp
from jax import lax
from jax.experimental import pallas as pl
from jax.experimental.pallas import tpu as pltpu
from jax.sharding import PartitionSpec as P

AUX = 16
DIGIT = 256


def pack_kernel(emb_ref, id_ref, *out_refs):
    rows, width = emb_ref.shape
    values = emb_ref[...].astype(jnp.float32)
    scale = lax.rsqrt(jnp.sum(values * values, axis=-1, keepdims=True) + 1e-06)
    unit = (values * scale).astype(jnp.bfloat16)
    ids = jnp.broadcast_to(id_ref[...], (AUX, rows))
    row = lax.broadcasted_iota(jnp.int32, (AUX, rows), 0)
    digits = jnp.where(row == 0, ids % DIGIT, ids // DIGIT)
    if width > rows:
        digits = jnp.concatenate([digits, jnp.zeros((AUX, width - rows), jnp.int32)], axis=1)
    digits = digits.astype(jnp.float32).astype(jnp.bfloat16)
    for ref in out_refs:
        ref[:rows, :] = unit
        ref[rows:, :] = digits


def pack(embeddings, cluster_id):
    rows, width = embeddings.shape
    return pl.pallas_call(
        pack_kernel,
        out_shape=[jax.ShapeDtypeStruct((rows + AUX, width), jnp.bfloat16)] * 2,
    )(embeddings, cluster_id.reshape(1, rows))


def one_hot(digits, clusters):
    number = digits[0:1].astype(jnp.int32) + DIGIT * digits[1:2].astype(jnp.int32)
    index = lax.broadcasted_iota(jnp.int32, (clusters, digits.shape[1]), 0)
    return jnp.where(index == number, 1.0, 0.0).astype(jnp.bfloat16)


def weights_table(group_ref, groups):
    clusters = group_ref.shape[1]
    index = lax.broadcasted_iota(jnp.int32, (groups, clusters), 0)
    member = jnp.where(index == group_ref[...], 1.0, 0.0).astype(jnp.bfloat16)
    same = lax.dot_general(member, member, (((0,), (0,)), ((), ())), preferred_element_type=jnp.float32)
    a = lax.broadcasted_iota(jnp.int32, (clusters, clusters), 0)
    b = lax.broadcasted_iota(jnp.int32, (clusters, clusters), 1)
    return jnp.where(a == b, 1.0, 0.5 * same).astype(jnp.bfloat16)


def best_kernel(jobs, n_blocks, groups, rank_ref, group_ref, *refs):
    blocks, outs = refs[:n_blocks], refs[len(refs) - len(jobs) :]
    before = iter(refs[n_blocks : len(refs) - len(jobs)])
    rows = blocks[0].shape[0] - AUX
    clusters = group_ref.shape[1]
    table = weights_table(group_ref, groups)
    hots = [one_hot(b[rows:, :rows].astype(jnp.float32), clusters) for b in blocks]
    spans = {}
    for _, lo, hi, _ in jobs:
        if (lo, hi) not in spans:
            spans[lo, hi] = (
                jnp.concatenate(hots[lo:hi], axis=1),
                jnp.concatenate([b[:rows, :] for b in blocks[lo:hi]], axis=0),
            )
    for (query, lo, hi, continues), out in zip(jobs, outs):
        key_hot, keys = spans[lo, hi]
        mixed = jnp.dot(table, hots[query], preferred_element_type=jnp.float32).astype(jnp.bfloat16)
        weight = lax.dot_general(key_hot, mixed, (((0,), (0,)), ((), ())), preferred_element_type=jnp.float32)
        sims = lax.dot_general(
            keys, blocks[query][:rows, :], (((1,), (1,)), ((), ())), preferred_element_type=jnp.float32
        )
        score = jnp.where(weight > 0, weight * sims, -1.0)
        best = next(before)[...] if continues else jnp.full((1, rows), -1.0, jnp.float32)
        for i in range(lo, hi):
            part = score[(i - lo) * rows : (i - lo + 1) * rows, :]
            if i == query:
                k = lax.broadcasted_iota(jnp.int32, (rows, rows), 0)
                q = lax.broadcasted_iota(jnp.int32, (rows, rows), 1)
                found = jnp.max(jnp.where(k < q, part, -1.0), axis=0, keepdims=True)
            else:
                found = jnp.max(part, axis=0, keepdims=True)
                found = jnp.where(rank_ref[i] < rank_ref[query], found, -1.0)
            best = jnp.maximum(best, found)
        out[...] = best


def best_of(jobs, blocks, before, cluster_group, groups):
    rows, width = blocks[0][0].shape[0] - AUX, blocks[0][0].shape[1]
    vmem = pl.BlockSpec(memory_space=pltpu.VMEM)
    ranks = jnp.stack([r for _, r in blocks]).astype(jnp.int32)
    pairs = sum(hi - lo for _, lo, hi, _ in jobs) * rows * rows
    return pl.pallas_call(
        functools.partial(best_kernel, jobs, len(blocks), groups),
        out_shape=[jax.ShapeDtypeStruct((1, rows), jnp.float32)] * len(jobs),
        in_specs=[pl.BlockSpec(memory_space=pltpu.SMEM)] + [vmem] * (1 + len(blocks) + len(before)),
        out_specs=[vmem] * len(jobs),
        compiler_params=pltpu.CompilerParams(vmem_limit_bytes=40 * 2**20),
        cost_estimate=pl.CostEstimate(
            flops=2 * pairs * width, bytes_accessed=2 * len(blocks) * rows * width, transcendentals=0
        ),
    )(ranks, cluster_group.reshape(1, -1), *[b for b, _ in blocks], *before)


def solution(mesh):
    n_clu, n_grp = mesh.shape["clu"], mesh.shape["grp"]
    target = math.sqrt(n_clu * n_grp)
    wide = min(a for a in range(1, n_clu + 1) if n_clu % a == 0 and (a * n_grp >= target or a == n_clu))
    length = n_clu // wide

    def permute(x, move):
        pairs = []
        for z in range(length):
            for a in range(wide):
                for g in range(n_grp):
                    at = move(z, a, g)
                    pairs.append(((at[0] * wide + at[1]) * n_grp + at[2], (z * wide + a) * n_grp + g))
        return lax.ppermute(x, ("clu", "grp"), pairs)

    def turned(a, s, n):
        return a ^ abs(s) if n & (n - 1) == 0 else (a + s) % n

    def shards(embeddings, cluster_id, cluster_group):
        rows = embeddings.shape[0]
        own, local = pack(embeddings, cluster_id)
        clu, grp = lax.axis_index("clu"), lax.axis_index("grp")
        line, place = clu // wide, clu % wide

        def rank(z, a, g):
            return g * n_clu + z * wide + a

        def along(x, s):
            return permute(x, lambda z, a, g: (turned(z, s, length), a, g))

        half = length // 2 if length & (length - 1) == 0 else length
        near = [permute(own, lambda z, a, g: (z, turned(a, s, wide), g)) for s in range(1, wide)]
        first = [along(own, s) for s in range(1, min(half + 1, length))]
        near, first = lax.optimization_barrier((near, first))
        last = [along(first[half - 1], s) for s in range(1, length - half)]
        far, far_rank = [], []
        for t in range(1, n_grp):
            for s in range(wide):
                block = near[s - 1] if s else own
                far.append(permute(block, lambda z, a, g: (z, a, turned(g, t, n_grp))))
                far_rank.append(rank(line, turned(place, s, wide), turned(grp, t, n_grp)))
        near = list(zip([local] + near, [rank(line, turned(place, s, wide), grp) for s in range(wide)]))
        far = list(zip(far, far_rank))
        visit_rank = [rank(turned(line, s, length), place, grp) for s in range(1, length)]
        first = list(zip(first, visit_rank))
        last = list(zip(last, visit_rank[len(first) :]))
        jobs = [(0, 0, wide, False)] + [(wide + j, 0, wide, False) for j in range(len(first))]
        best = best_of(jobs, near + first, [], cluster_group, n_clu)
        at, end = len(last), len(last) + wide + len(far)
        jobs = [(at, at + wide, end, True)] + [(end + j, at + wide, end, True) for j in range(len(first))]
        jobs += [(j, at, end, False) for j in range(at)]
        best = best_of(jobs, last + near + far + first, best, cluster_group, n_clu)
        found = [best[0]] + [along(best[s], -s) for s in range(1, length)]
        return functools.reduce(jnp.maximum, found).reshape(rows)

    placed = (P(("clu", "grp"), None), P(("clu", "grp")), P())
    return jax.shard_map(
        shards, mesh=mesh, in_specs=placed, out_specs=P(("clu", "grp")), check_vma=False
    )
```

time: 33.7 us -> 31.6 us (0.938)
  waiting for transfers between devices: 13.3 us -> 9.22 us
  Pallas kernels: 4.15 us -> 5.44 us
  local copies, waits for them, and re-layouts: 1 us -> 1.74 us
    ppermute x13, waiting for transfers between devices: 13.3 us -> 9.22 us  [permute(): return lax.ppermute(x, ('clu', 'grp'), pairs)]
    pallas_call x2 -> x3, Pallas kernels: 4.15 us -> 5.44 us  [the longest x2 3.72 us: best_of(): pl.pallas_call(functools.partial(best_kernel, jobs, len(blocks), groups),...]
    unnamed x4, local copies, waits for them, and re-layouts: 0.91 us -> 1.57 us
  transfers between devices with their start and end apart: 13 -> 13, of which waited for: 11 -> 8; matrix products, arithmetic and copies ran while one was open for 0% -> 1% of each run, Pallas kernels for 0% -> 5%
where the time goes in v9:
time: 31.6 us; the launch traced here: 31.5 us
  starting transfers between devices  14.5 us (46%)
  waiting for transfers between devices  9.22 us (29%)
  Pallas kernels  5.44 us (17%)
  local copies, waits for them, and re-layouts  1.74 us (6%)
  other arithmetic  0.52 us (2%)
    ppermute x13, starting transfers between devices, permute(): return lax.ppermute(x, ('clu', 'grp'), pairs)  14.5 us
    ppermute x13, waiting for transfers between devices, permute(): return lax.ppermute(x, ('clu', 'grp'), pairs)  9.22 us
    pallas_call x2, Pallas kernels, best_of(): pl.pallas_call(functools.partial(best_kernel, jobs, len(blocks), groups),...  3.72 us
    pallas_call x1, Pallas kernels, pack(): pl.pallas_call(pack_kernel, out_shape=[jax.ShapeDtypeStruct((rows + AUX,...  1.73 us
    unnamed x4, local copies, waits for them, and re-layouts  1.57 us
  transfers between devices with their start and end apart: 13, of which 8 were waited for; matrix products, arithmetic and copies ran while one was open for 1% of the time, Pallas kernels for 5%

profile of v9, /device:TPU:0, one launch (start us, length us, event | category | flops | bytes accessed | tf_op | source)
XLA Modules:
  0.0 31.5 jit_solution(4751118682495278861)
XLA Ops:
  0.0 1.7 %shard_map.37 = (bf16[144,512]{1,0:T(8,128)(2,1)}, bf16[144,512]{1,0:T(8,128)(2,1)}) custom-call(bf16[128,512]{1,0:T(8,128)(2,1)} %emb_ref.1, s32[1,128]{1,0:T(1,128)} %bitcast.17), custom_call_target="tpu_custom_call" | custom-call | tf_op jit(solution)/shard_map/pallas_call | solution.py:33
  1.7 4.0 %collective-permute-start.4 = (bf16[144,512]{1,0:T(8,128)(2,1)}, bf16[144,512]{1,0:T(8,128)(2,1)S(1)}, u32[]{:S(2)}, u32[]{:S(2)}) collective-permute-start(bf16[144,512]{1,0:T(8,128)(2,1)} %get-tuple-element.19), channel_id=1, source_target_pairs={{16,0},{17,1},{18,2},{19,3},{20,4},{21,5},{22,6},{23,7},{24,8},{25... | collective-permute-start | bytes 442376 | tf_op jit(solution)/shard_map/ppermute | solution.py:121
  5.8 1.6 %collective-permute-start.3 = (bf16[144,512]{1,0:T(8,128)(2,1)}, bf16[144,512]{1,0:T(8,128)(2,1)S(1)}, u32[]{:S(2)}, u32[]{:S(2)}) collective-permute-start(bf16[144,512]{1,0:T(8,128)(2,1)} %get-tuple-element.19), channel_id=1, source_target_pairs={{8,0},{9,1},{10,2},{11,3},{12,4},{13,5},{14,6},{15,7},{0,8},{1,9},... | collective-permute-start | bytes 442376 | tf_op jit(solution)/shard_map/ppermute | solution.py:121
  7.3 2.4 %collective-permute-start.2 = (bf16[144,512]{1,0:T(8,128)(2,1)}, bf16[144,512]{1,0:T(8,128)(2,1)S(1)}, u32[]{:S(2)}, u32[]{:S(2)}) collective-permute-start(bf16[144,512]{1,0:T(8,128)(2,1)} %get-tuple-element.19), channel_id=1, source_target_pairs={{6,0},{7,1},{4,2},{5,3},{2,4},{3,5},{0,6},{1,7},{14,8},{15,9},{12,... | collective-permute-start | bytes 442376 | tf_op jit(solution)/shard_map/ppermute | solution.py:121
  9.8 0.5 %collective-permute-start.1 = (bf16[144,512]{1,0:T(8,128)(2,1)}, bf16[144,512]{1,0:T(8,128)(2,1)S(1)}, u32[]{:S(2)}, u32[]{:S(2)}) collective-permute-start(bf16[144,512]{1,0:T(8,128)(2,1)} %get-tuple-element.19), channel_id=1, source_target_pairs={{4,0},{5,1},{6,2},{7,3},{0,4},{1,5},{2,6},{3,7},{12,8},{13,9},{14,... | collective-permute-start | bytes 442376 | tf_op jit(solution)/shard_map/ppermute | solution.py:121
  10.3 0.5 %collective-permute-start = (bf16[144,512]{1,0:T(8,128)(2,1)}, bf16[144,512]{1,0:T(8,128)(2,1)S(1)}, u32[]{:S(2)}, u32[]{:S(2)}) collective-permute-start(bf16[144,512]{1,0:T(8,128)(2,1)} %get-tuple-element.19), channel_id=1, source_target_pairs={{2,0},{3,1},{0,2},{1,3},{6,4},{7,5},{4,6},{5,7},{10,8},{11,9},{8,1... | collective-permute-start | bytes 442376 | tf_op jit(solution)/shard_map/ppermute | solution.py:121
  10.8 2.3 %collective-permute-done.4.refs_5_.refs_10_ = bf16[144,512]{1,0:T(8,128)(2,1)S(1)} collective-permute-done((bf16[144,512]{1,0:T(8,128)(2,1)}, bf16[144,512]{1,0:T(8,128)(2,1)S(1)}, u32[]{:S(2)}, u32[]{:S(2)}) %collective-permute-start.4) | collective-permute-done | bytes 147488 | tf_op jit(solution)/shard_map/ppermute | solution.py:121
  13.1 0.0 collective-permute-start.6
  13.1 0.2 collective-permute-done.3.refs_4_.refs_9_
  13.3 1.2 %collective-permute-done.2.refs_3_.refs_4_ = bf16[144,512]{1,0:T(8,128)(2,1)S(1)} collective-permute-done((bf16[144,512]{1,0:T(8,128)(2,1)}, bf16[144,512]{1,0:T(8,128)(2,1)S(1)}, u32[]{:S(2)}, u32[]{:S(2)}) %collective-permute-start.2) | collective-permute-done | bytes 147488 | tf_op jit(solution)/shard_map/ppermute | solution.py:121
  14.5 2.2 %collective-permute-done.1.refs_2_.refs_3_ = bf16[144,512]{1,0:T(8,128)(2,1)S(1)} collective-permute-done((bf16[144,512]{1,0:T(8,128)(2,1)}, bf16[144,512]{1,0:T(8,128)(2,1)S(1)}, u32[]{:S(2)}, u32[]{:S(2)}) %collective-permute-start.1) | collective-permute-done | bytes 147488 | tf_op jit(solution)/shard_map/ppermute | solution.py:121
  16.6 0.1 collective-permute-done.refs_1_.refs_2_
  16.7 0.4 %collective-permute-start.5 = (bf16[144,512]{1,0:T(8,128)(2,1)S(1)}, bf16[144,512]{1,0:T(8,128)(2,1)S(1)}, u32[]{:S(2)}, u32[]{:S(2)}) collective-permute-start(bf16[144,512]{1,0:T(8,128)(2,1)S(1)} %collective-permute-done.4.refs_5_.refs_10_), channel_id=1, source_target_pairs={{8,0},{9,1},{10,2},{11,3},{12,4},{13,5},{14,6},{15,7},{0,8},{1,9},... | collective-permute-start | bytes 442376 | tf_op jit(solution)/shard_map/ppermute | solution.py:121
  17.1 0.0 collective-permute-start.7
  17.1 0.5 %collective-permute-start.8 = (bf16[144,512]{1,0:T(8,128)(2,1)S(1)}, bf16[144,512]{1,0:T(8,128)(2,1)S(1)}, u32[]{:S(2)}, u32[]{:S(2)}) collective-permute-start(bf16[144,512]{1,0:T(8,128)(2,1)S(1)} %collective-permute-done.1.refs_2_.refs_3_), channel_id=1, source_target_pairs={{1,0},{0,1},{3,2},{2,3},{5,4},{4,5},{7,6},{6,7},{9,8},{8,9},{11,10... | collective-permute-start | bytes 442376 | tf_op jit(solution)/shard_map/ppermute | solution.py:121
  17.7 0.0 collective-permute-start.9
  17.7 0.1 stack.57.rank_ref
  17.7 0.1 stack.56.rank_ref
  17.8 0.0 copy-start.1
  17.8 0.7 %copy-done.1 = s32[64]{0:T(128)S(1)} copy-done((s32[64]{0:T(128)S(1)}, s32[64]{0:T(128)}, u32[]{:S(2)}) %copy-start.1) | copy-done | bytes 280
  18.5 0.0 copy-start
  18.5 0.9 %copy-done = bf16[144,512]{1,0:T(8,128)(2,1)S(1)} copy-done((bf16[144,512]{1,0:T(8,128)(2,1)S(1)}, bf16[144,512]{1,0:T(8,128)(2,1)}, u32[]{:S(2)}) %copy-start) | copy-done | bytes 147480
  19.4 1.6 %shard_map.38 = (f32[1,128]{1,0:T(1,128)S(1)}, f32[1,128]{1,0:T(1,128)S(1)}, f32[1,128]{1,0:T(1,128)S(1)}) custom-call(s32[6]{0:T(128)S(1)} %stack.57.rank_ref, s32[1,64]{1,0:T(1,128)S(1)} %bitcast.15, bf16[144,512]{1,0:T(8,128)(2,1)S(1)} %copy-done, bf16[144,512]{1,0:T(8,128)(2,1)S(1)} %collective-permute-done.refs_1_.refs_2_, ...), custom_call_target="tpu_custom_call" | custom-call | flops 201326592 | bytes 786432 | tf_op jit(solution)/shard_map/pallas_call | solution.py:96
  21.0 0.0 collective-permute-done.6.refs_5_
  21.0 0.9 %collective-permute-done.5.refs_0_ = bf16[144,512]{1,0:T(8,128)(2,1)S(1)} collective-permute-done((bf16[144,512]{1,0:T(8,128)(2,1)S(1)}, bf16[144,512]{1,0:T(8,128)(2,1)S(1)}, u32[]{:S(2)}, u32[]{:S(2)}) %collective-permute-start.5) | collective-permute-done | bytes 147488 | tf_op jit(solution)/shard_map/ppermute | solution.py:121
  21.9 0.0 collective-permute-done.7.refs_6_
  21.9 0.0 collective-permute-done.8.refs_7_
  21.9 0.0 collective-permute-done.9.refs_8_
  21.9 2.1 %shard_map.39 = (f32[1,128]{1,0:T(1,128)S(1)}, f32[1,128]{1,0:T(1,128)S(1)}, f32[1,128]{1,0:T(1,128)S(1)}, f32[1,128]{1,0:T(1,128)S(1)}) custom-call(s32[11]{0:T(128)S(1)} %stack.56.rank_ref, s32[1,64]{1,0:T(1,128)S(1)} %bitcast.16, bf16[144,512]{1,0:T(8,128)(2,1)S(1)} %collective-permute-done.5.refs_0_, bf16[144,512]{1,0:T(8,128)(2,1)S(1)} %copy-done, ...), custom_call_target="tpu_custom_call" | custom-call | flops 335544320 | bytes 1441792 | tf_op jit(solution)/shard_map/pallas_call | solution.py:96
  24.0 0.8 %collective-permute-start.10 = (f32[1,128]{1,0:T(1,128)S(1)}, f32[1,128]{1,0:T(1,128)S(1)}, u32[]{:S(2)}, u32[]{:S(2)}) collective-permute-start(f32[1,128]{1,0:T(1,128)S(1)} %get-tuple-element.30), channel_id=1, source_target_pairs={{8,0},{9,1},{10,2},{11,3},{12,4},{13,5},{14,6},{15,7},{0,8},{1,9},... | collective-permute-start | bytes 1544 | tf_op jit(solution)/shard_map/ppermute | solution.py:121
  24.8 0.8 %collective-permute-start.11 = (f32[1,128]{1,0:T(1,128)S(1)}, f32[1,128]{1,0:T(1,128)S(1)}, u32[]{:S(2)}, u32[]{:S(2)}) collective-permute-start(f32[1,128]{1,0:T(1,128)S(1)} %get-tuple-element.31), channel_id=1, source_target_pairs={{16,0},{17,1},{18,2},{19,3},{20,4},{21,5},{22,6},{23,7},{24,8},{25... | collective-permute-start | bytes 1544 | tf_op jit(solution)/shard_map/ppermute | solution.py:121
  25.6 2.9 %collective-permute-start.12 = (f32[1,128]{1,0:T(1,128)S(1)}, f32[1,128]{1,0:T(1,128)S(1)}, u32[]{:S(2)}, u32[]{:S(2)}) collective-permute-start(f32[1,128]{1,0:T(1,128)S(1)} %get-tuple-element.32), channel_id=1, source_target_pairs={{24,0},{25,1},{26,2},{27,3},{28,4},{29,5},{30,6},{31,7},{16,8},{17... | collective-permute-start | bytes 1544 | tf_op jit(solution)/shard_map/ppermute | solution.py:121
  28.5 0.0 collective-permute-done.10
  28.5 0.8 %collective-permute-done.11 = f32[1,128]{1,0:T(1,128)S(1)} collective-permute-done((f32[1,128]{1,0:T(1,128)S(1)}, f32[1,128]{1,0:T(1,128)S(1)}, u32[]{:S(2)}, u32[]{:S(2)}) %collective-permute-start.11) | collective-permute-done | bytes 544 | tf_op jit(solution)/shard_map/ppermute | solution.py:121
  29.3 1.7 %collective-permute-done.12 = f32[1,128]{1,0:T(1,128)S(1)} collective-permute-done((f32[1,128]{1,0:T(1,128)S(1)}, f32[1,128]{1,0:T(1,128)S(1)}, u32[]{:S(2)}, u32[]{:S(2)}) %collective-permute-start.12) | collective-permute-done | bytes 544 | tf_op jit(solution)/shard_map/ppermute | solution.py:121
  31.0 0.5 %maximum_bitcast_fusion = f32[128]{0:T(128)} fusion(f32[1,128]{1,0:T(1,128)S(1)} %collective-permute-done.12, f32[1,128]{1,0:T(1,128)S(1)} %collective-permute-done.11, f32[1,128]{1,0:T(1,128)S(1)} %get-tuple-element.29, f32[1,128]{1,0:T(1,128)S(1)} %collective-permute-done.10), kind=kLoop, calls=%fused_computation | loop fusion | flops 384 | bytes 2560 | tf_op jit(solution)/shard_map/reshape | solution.py:161
Async XLA Ops:
  1.7 11.4 %collective-permute-start.4 = (bf16[144,512]{1,0:T(8,128)(2,1)}, bf16[144,512]{1,0:T(8,128)(2,1)S(1)}, u32[]{:S(2)}, u32[]{:S(2)}) collective-permute-start(bf16[144,512]{1,0:T(8,128)(2,1)} %get-tuple-element.19), channel_id=1, source_target_pairs={{16,0},{17,1},{18,2},{19,3},{20,4},{21,5},{22,6},{23,7},{24,8},{25... | collective-permute-start | bytes 442376 | tf_op jit(solution)/shard_map/ppermute | solution.py:121
  5.8 7.5 %collective-permute-start.3 = (bf16[144,512]{1,0:T(8,128)(2,1)}, bf16[144,512]{1,0:T(8,128)(2,1)S(1)}, u32[]{:S(2)}, u32[]{:S(2)}) collective-permute-start(bf16[144,512]{1,0:T(8,128)(2,1)} %get-tuple-element.19), channel_id=1, source_target_pairs={{8,0},{9,1},{10,2},{11,3},{12,4},{13,5},{14,6},{15,7},{0,8},{1,9},... | collective-permute-start | bytes 442376 | tf_op jit(solution)/shard_map/ppermute | solution.py:121
  7.3 7.1 %collective-permute-start.2 = (bf16[144,512]{1,0:T(8,128)(2,1)}, bf16[144,512]{1,0:T(8,128)(2,1)S(1)}, u32[]{:S(2)}, u32[]{:S(2)}) collective-permute-start(bf16[144,512]{1,0:T(8,128)(2,1)} %get-tuple-element.19), channel_id=1, source_target_pairs={{6,0},{7,1},{4,2},{5,3},{2,4},{3,5},{0,6},{1,7},{14,8},{15,9},{12,... | collective-permute-start | bytes 442376 | tf_op jit(solution)/shard_map/ppermute | solution.py:121
  9.8 6.8 %collective-permute-start.1 = (bf16[144,512]{1,0:T(8,128)(2,1)}, bf16[144,512]{1,0:T(8,128)(2,1)S(1)}, u32[]{:S(2)}, u32[]{:S(2)}) collective-permute-start(bf16[144,512]{1,0:T(8,128)(2,1)} %get-tuple-element.19), channel_id=1, source_target_pairs={{4,0},{5,1},{6,2},{7,3},{0,4},{1,5},{2,6},{3,7},{12,8},{13,9},{14,... | collective-permute-start | bytes 442376 | tf_op jit(solution)/shard_map/ppermute | solution.py:121
  10.3 6.4 %collective-permute-start = (bf16[144,512]{1,0:T(8,128)(2,1)}, bf16[144,512]{1,0:T(8,128)(2,1)S(1)}, u32[]{:S(2)}, u32[]{:S(2)}) collective-permute-start(bf16[144,512]{1,0:T(8,128)(2,1)} %get-tuple-element.19), channel_id=1, source_target_pairs={{2,0},{3,1},{0,2},{1,3},{6,4},{7,5},{4,6},{5,7},{10,8},{11,9},{8,1... | collective-permute-start | bytes 442376 | tf_op jit(solution)/shard_map/ppermute | solution.py:121
  13.1 7.9 %collective-permute-start.6 = (bf16[144,512]{1,0:T(8,128)(2,1)}, bf16[144,512]{1,0:T(8,128)(2,1)S(1)}, u32[]{:S(2)}, u32[]{:S(2)}) collective-permute-start(bf16[144,512]{1,0:T(8,128)(2,1)} %get-tuple-element.19), channel_id=1, source_target_pairs={{1,0},{0,1},{3,2},{2,3},{5,4},{4,5},{7,6},{6,7},{9,8},{8,9},{11,10... | collective-permute-start | bytes 442376 | tf_op jit(solution)/shard_map/ppermute | solution.py:121
  16.7 5.2 %collective-permute-start.5 = (bf16[144,512]{1,0:T(8,128)(2,1)S(1)}, bf16[144,512]{1,0:T(8,128)(2,1)S(1)}, u32[]{:S(2)}, u32[]{:S(2)}) collective-permute-start(bf16[144,512]{1,0:T(8,128)(2,1)S(1)} %collective-permute-done.4.refs_5_.refs_10_), channel_id=1, source_target_pairs={{8,0},{9,1},{10,2},{11,3},{12,4},{13,5},{14,6},{15,7},{0,8},{1,9},... | collective-permute-start | bytes 442376 | tf_op jit(solution)/shard_map/ppermute | solution.py:121
  17.1 4.8 %collective-permute-start.7 = (bf16[144,512]{1,0:T(8,128)(2,1)S(1)}, bf16[144,512]{1,0:T(8,128)(2,1)S(1)}, u32[]{:S(2)}, u32[]{:S(2)}) collective-permute-start(bf16[144,512]{1,0:T(8,128)(2,1)S(1)} %collective-permute-done.refs_1_.refs_2_), channel_id=1, source_target_pairs={{1,0},{0,1},{3,2},{2,3},{5,4},{4,5},{7,6},{6,7},{9,8},{8,9},{11,10... | collective-permute-start | bytes 442376 | tf_op jit(solution)/shard_map/ppermute | solution.py:121
  17.1 4.8 %collective-permute-start.8 = (bf16[144,512]{1,0:T(8,128)(2,1)S(1)}, bf16[144,512]{1,0:T(8,128)(2,1)S(1)}, u32[]{:S(2)}, u32[]{:S(2)}) collective-permute-start(bf16[144,512]{1,0:T(8,128)(2,1)S(1)} %collective-permute-done.1.refs_2_.refs_3_), channel_id=1, source_target_pairs={{1,0},{0,1},{3,2},{2,3},{5,4},{4,5},{7,6},{6,7},{9,8},{8,9},{11,10... | collective-permute-start | bytes 442376 | tf_op jit(solution)/shard_map/ppermute | solution.py:121
  17.7 4.3 %collective-permute-start.9 = (bf16[144,512]{1,0:T(8,128)(2,1)S(1)}, bf16[144,512]{1,0:T(8,128)(2,1)S(1)}, u32[]{:S(2)}, u32[]{:S(2)}) collective-permute-start(bf16[144,512]{1,0:T(8,128)(2,1)S(1)} %collective-permute-done.2.refs_3_.refs_4_), channel_id=1, source_target_pairs={{1,0},{0,1},{3,2},{2,3},{5,4},{4,5},{7,6},{6,7},{9,8},{8,9},{11,10... | collective-permute-start | bytes 442376 | tf_op jit(solution)/shard_map/ppermute | solution.py:121
  17.8 0.7 %copy-start.1 = (s32[64]{0:T(128)S(1)}, s32[64]{0:T(128)}, u32[]{:S(2)}) copy-start(s32[64]{0:T(128)} %param.5) | copy-start | bytes 772
  18.5 0.9 %copy-start = (bf16[144,512]{1,0:T(8,128)(2,1)S(1)}, bf16[144,512]{1,0:T(8,128)(2,1)}, u32[]{:S(2)}) copy-start(bf16[144,512]{1,0:T(8,128)(2,1)} %get-tuple-element.21.refs_0_.refs_1_) | copy-start | bytes 442372
  24.0 4.5 %collective-permute-start.10 = (f32[1,128]{1,0:T(1,128)S(1)}, f32[1,128]{1,0:T(1,128)S(1)}, u32[]{:S(2)}, u32[]{:S(2)}) collective-permute-start(f32[1,128]{1,0:T(1,128)S(1)} %get-tuple-element.30), channel_id=1, source_target_pairs={{8,0},{9,1},{10,2},{11,3},{12,4},{13,5},{14,6},{15,7},{0,8},{1,9},... | collective-permute-start | bytes 1544 | tf_op jit(solution)/shard_map/ppermute | solution.py:121
  24.8 4.4 %collective-permute-start.11 = (f32[1,128]{1,0:T(1,128)S(1)}, f32[1,128]{1,0:T(1,128)S(1)}, u32[]{:S(2)}, u32[]{:S(2)}) collective-permute-start(f32[1,128]{1,0:T(1,128)S(1)} %get-tuple-element.31), channel_id=1, source_target_pairs={{16,0},{17,1},{18,2},{19,3},{20,4},{21,5},{22,6},{23,7},{24,8},{25... | collective-permute-start | bytes 1544 | tf_op jit(solution)/shard_map/ppermute | solution.py:121
  25.6 5.3 %collective-permute-start.12 = (f32[1,128]{1,0:T(1,128)S(1)}, f32[1,128]{1,0:T(1,128)S(1)}, u32[]{:S(2)}, u32[]{:S(2)}) collective-permute-start(f32[1,128]{1,0:T(1,128)S(1)} %get-tuple-element.32), channel_id=1, source_target_pairs={{24,0},{25,1},{26,2},{27,3},{28,4},{29,5},{30,6},{31,7},{16,8},{17... | collective-permute-start | bytes 1544 | tf_op jit(solution)/shard_map/ppermute | solution.py:121

commit v10 on v9

v10 whole, which is shorter than its diff:
```python
import functools
import math

import jax
import jax.numpy as jnp
from jax import lax
from jax.experimental import pallas as pl
from jax.experimental.pallas import tpu as pltpu
from jax.sharding import PartitionSpec as P

AUX = 16
DIGIT = 256


def pack_kernel(groups, emb_ref, id_ref, group_ref, out_ref, table_ref):
    rows, width = emb_ref.shape
    values = emb_ref[...].astype(jnp.float32)
    scale = lax.rsqrt(jnp.sum(values * values, axis=-1, keepdims=True) + 1e-06)
    out_ref[:rows, :] = (values * scale).astype(jnp.bfloat16)
    ids = jnp.broadcast_to(id_ref[...], (AUX, rows))
    row = lax.broadcasted_iota(jnp.int32, (AUX, rows), 0)
    digits = jnp.where(row == 0, ids % DIGIT, ids // DIGIT)
    if width > rows:
        digits = jnp.concatenate([digits, jnp.zeros((AUX, width - rows), jnp.int32)], axis=1)
    out_ref[rows:, :] = digits.astype(jnp.float32).astype(jnp.bfloat16)
    clusters = group_ref.shape[1]
    index = lax.broadcasted_iota(jnp.int32, (groups, clusters), 0)
    member = jnp.where(index == group_ref[...], 1.0, 0.0).astype(jnp.bfloat16)
    same = lax.dot_general(member, member, (((0,), (0,)), ((), ())), preferred_element_type=jnp.float32)
    one = lax.broadcasted_iota(jnp.int32, (clusters, clusters), 0)
    other = lax.broadcasted_iota(jnp.int32, (clusters, clusters), 1)
    table_ref[...] = jnp.where(one == other, 1.0, 0.5 * same).astype(jnp.bfloat16)


def pack(embeddings, cluster_id, cluster_group, groups):
    rows, width = embeddings.shape
    clusters = cluster_group.shape[0]
    return pl.pallas_call(
        functools.partial(pack_kernel, groups),
        out_shape=[pltpu.VMEM((rows + AUX, width), jnp.bfloat16), pltpu.VMEM((clusters, clusters), jnp.bfloat16)],
    )(embeddings, cluster_id.reshape(1, rows), cluster_group.reshape(1, clusters))


def one_hot(digits, clusters):
    number = digits[0:1].astype(jnp.int32) + DIGIT * digits[1:2].astype(jnp.int32)
    index = lax.broadcasted_iota(jnp.int32, (clusters, digits.shape[1]), 0)
    return jnp.where(index == number, 1.0, 0.0).astype(jnp.bfloat16)


def best_kernel(n_keys, own, rank_ref, table_ref, *refs):
    n_queries = (len(refs) - n_keys) // 2
    keys, queries, outs = refs[:n_keys], refs[n_keys : n_keys + n_queries], refs[n_keys + n_queries :]
    rows = keys[0].shape[0] - AUX
    clusters = table_ref.shape[0]

    def hot(block):
        return one_hot(block[rows:, :rows].astype(jnp.float32), clusters)

    key_hot = jnp.concatenate([hot(b) for b in keys], axis=1)
    key_rows = jnp.concatenate([b[:rows, :] for b in keys], axis=0)
    for j in range(n_queries):
        mixed = jnp.dot(table_ref[...], hot(queries[j]), preferred_element_type=jnp.float32).astype(jnp.bfloat16)
        weight = lax.dot_general(key_hot, mixed, (((0,), (0,)), ((), ())), preferred_element_type=jnp.float32)
        sims = lax.dot_general(
            key_rows, queries[j][:rows, :], (((1,), (1,)), ((), ())), preferred_element_type=jnp.float32
        )
        score = jnp.where(weight > 0, weight * sims, -1.0)
        best = jnp.full((1, rows), -1.0, jnp.float32)
        for i in range(n_keys):
            part = score[i * rows : (i + 1) * rows, :]
            if own and i + j == 0:
                k = lax.broadcasted_iota(jnp.int32, (rows, rows), 0)
                q = lax.broadcasted_iota(jnp.int32, (rows, rows), 1)
                found = jnp.max(jnp.where(k < q, part, -1.0), axis=0, keepdims=True)
            else:
                found = jnp.max(part, axis=0, keepdims=True)
                found = jnp.where(rank_ref[i] < rank_ref[n_keys + j], found, -1.0)
            best = jnp.maximum(best, found)
        outs[j][...] = best


def best_of(keys, queries, table, own):
    rows, width = keys[0][0].shape[0] - AUX, keys[0][0].shape[1]
    vmem = pl.BlockSpec(memory_space=pltpu.VMEM)
    ranks = jnp.stack([r for _, r in keys + queries]).astype(jnp.int32)
    pairs = len(keys) * len(queries) * rows * rows
    return pl.pallas_call(
        functools.partial(best_kernel, len(keys), own),
        out_shape=[jax.ShapeDtypeStruct((1, rows), jnp.float32)] * len(queries),
        in_specs=[pl.BlockSpec(memory_space=pltpu.SMEM)] + [vmem] * (1 + len(keys) + len(queries)),
        out_specs=[vmem] * len(queries),
        compiler_params=pltpu.CompilerParams(vmem_limit_bytes=40 * 2**20),
        cost_estimate=pl.CostEstimate(
            flops=2 * pairs * width, bytes_accessed=2 * (len(keys) + len(queries)) * rows * width, transcendentals=0
        ),
    )(ranks, table, *[b for b, _ in keys + queries])


def solution(mesh):
    n_clu, n_grp = mesh.shape["clu"], mesh.shape["grp"]
    target = math.sqrt(n_clu * n_grp)
    wide = min(a for a in range(1, n_clu + 1) if n_clu % a == 0 and (a * n_grp >= target or a == n_clu))
    length = n_clu // wide

    def permute(x, move):
        pairs = []
        for z in range(length):
            for a in range(wide):
                for g in range(n_grp):
                    at = move(z, a, g)
                    pairs.append(((at[0] * wide + at[1]) * n_grp + at[2], (z * wide + a) * n_grp + g))
        return lax.ppermute(x, ("clu", "grp"), pairs)

    def turned(a, s, n):
        return a ^ abs(s) if n & (n - 1) == 0 else (a + s) % n

    def shards(embeddings, cluster_id, cluster_group):
        rows = embeddings.shape[0]
        own, table = pack(embeddings, cluster_id, cluster_group, n_clu)
        clu, grp = lax.axis_index("clu"), lax.axis_index("grp")
        line, place = clu // wide, clu % wide

        def rank(z, a, g):
            return g * n_clu + z * wide + a

        def along(x, s):
            return permute(x, lambda z, a, g: (turned(z, s, length), a, g))

        half = length // 2 if length & (length - 1) == 0 else length
        first = [along(own, s) for s in reversed(range(1, min(half + 1, length)))]
        near = [permute(own, lambda z, a, g: (z, turned(a, s, wide), g)) for s in reversed(range(1, wide))]
        first, near = lax.optimization_barrier((first, near))
        first, near = first[::-1], near[::-1]
        last = [along(first[half - 1], s) for s in range(1, length - half)]
        far, far_rank = [], []
        for t in range(1, n_grp):
            for s in range(wide):
                block = near[s - 1] if s else own
                far.append(permute(block, lambda z, a, g: (z, a, turned(g, t, n_grp))))
                far_rank.append(rank(line, turned(place, s, wide), turned(grp, t, n_grp)))
        near = list(zip([own] + near, [rank(line, turned(place, s, wide), grp) for s in range(wide)]))
        far = list(zip(far, far_rank))
        visit_rank = [rank(turned(line, s, length), place, grp) for s in range(1, length)]
        first = list(zip(first, visit_rank))
        last = list(zip(last, visit_rank[len(first) :]))
        best = best_of(near + far, near[:1] + first, table, True)
        if last:
            best = best + best_of(near + far, last, table, False)
        found = [best[0]] + [along(best[s], -s) for s in range(1, length)]
        return functools.reduce(jnp.maximum, found).reshape(rows)

    placed = (P(("clu", "grp"), None), P(("clu", "grp")), P())
    return jax.shard_map(
        shards, mesh=mesh, in_specs=placed, out_specs=P(("clu", "grp")), check_vma=False
    )
```

time: 31.6 us -> 29.9 us (0.946)
  waiting for transfers between devices: 9.22 us -> 11.8 us
  local copies, waits for them, and re-layouts: 1.74 us -> 0.17 us
  starting transfers between devices: 14.5 us -> 13 us
  Pallas kernels: 5.44 us -> 4.24 us
    ppermute x13, waiting for transfers between devices: 9.22 us -> 11.8 us  [permute(): return lax.ppermute(x, ('clu', 'grp'), pairs)]
    unnamed x4 -> x0, local copies, waits for them, and re-layouts: 1.57 us -> none
    ppermute x13, starting transfers between devices: 14.5 us -> 13 us  [permute(): return lax.ppermute(x, ('clu', 'grp'), pairs)]
    pallas_call x3, Pallas kernels: 5.44 us -> 4.24 us  [the longest x2 3.14 us: best_of(): pl.pallas_call(functools.partial(best_kernel, len(keys), own), out_shape=...]
  transfers between devices with their start and end apart: 13 -> 13, of which waited for: 8 -> 10; matrix products, arithmetic and copies ran while one was open for 1% -> 1% of each run, Pallas kernels for 5% -> 11%
where the time goes in v10:
time: 29.9 us; the launch traced here: 29.8 us
  starting transfers between devices  13 us (43%)
  waiting for transfers between devices  11.8 us (39%)
  Pallas kernels  4.24 us (14%)
  other arithmetic  0.52 us (2%)
    ppermute x13, starting transfers between devices, permute(): return lax.ppermute(x, ('clu', 'grp'), pairs)  13 us
    ppermute x13, waiting for transfers between devices, permute(): return lax.ppermute(x, ('clu', 'grp'), pairs)  11.8 us
    pallas_call x2, Pallas kernels, best_of(): pl.pallas_call(functools.partial(best_kernel, len(keys), own), out_shape=...  3.14 us
    pallas_call x1, Pallas kernels, pack(): pl.pallas_call(functools.partial(pack_kernel, groups), out_shape=[pltpu.V...  1.1 us
  transfers between devices with their start and end apart: 13, of which 10 were waited for; matrix products, arithmetic and copies ran while one was open for 1% of the time, Pallas kernels for 11%

profile of v10, /device:TPU:0, one launch (start us, length us, event | category | flops | bytes accessed | tf_op | source)
XLA Modules:
  0.0 29.8 jit_solution(205198381403663857)
XLA Ops:
  0.0 1.1 %shard_map.37 = (bf16[144,512]{1,0:T(8,128)(2,1)S(1)}, bf16[64,64]{1,0:T(8,128)(2,1)S(1)}) custom-call(bf16[128,512]{1,0:T(8,128)(2,1)} %emb_ref.1, s32[1,128]{1,0:T(1,128)} %bitcast.15, s32[1,64]{1,0:T(1,128)} %bitcast.16), custom_call_target="tpu_custom_call" | custom-call | tf_op jit(solution)/shard_map/pallas_call | solution.py:38
  1.1 4.1 %collective-permute-start = (bf16[144,512]{1,0:T(8,128)(2,1)S(1)}, bf16[144,512]{1,0:T(8,128)(2,1)S(1)}, u32[]{:S(2)}, u32[]{:S(2)}) collective-permute-start(bf16[144,512]{1,0:T(8,128)(2,1)S(1)} %get-tuple-element.16.refs_0_.refs_8_), channel_id=1, source_target_pairs={{16,0},{17,1},{18,2},{19,3},{20,4},{21,5},{22,6},{23,7},{24,8},{25... | collective-permute-start | bytes 442376 | tf_op jit(solution)/shard_map/ppermute | solution.py:112
  5.2 1.6 %collective-permute-start.1 = (bf16[144,512]{1,0:T(8,128)(2,1)S(1)}, bf16[144,512]{1,0:T(8,128)(2,1)S(1)}, u32[]{:S(2)}, u32[]{:S(2)}) collective-permute-start(bf16[144,512]{1,0:T(8,128)(2,1)S(1)} %get-tuple-element.16.refs_0_.refs_8_), channel_id=1, source_target_pairs={{8,0},{9,1},{10,2},{11,3},{12,4},{13,5},{14,6},{15,7},{0,8},{1,9},... | collective-permute-start | bytes 442376 | tf_op jit(solution)/shard_map/ppermute | solution.py:112
  6.8 2.4 %collective-permute-start.2 = (bf16[144,512]{1,0:T(8,128)(2,1)S(1)}, bf16[144,512]{1,0:T(8,128)(2,1)S(1)}, u32[]{:S(2)}, u32[]{:S(2)}) collective-permute-start(bf16[144,512]{1,0:T(8,128)(2,1)S(1)} %get-tuple-element.16.refs_0_.refs_8_), channel_id=1, source_target_pairs={{6,0},{7,1},{4,2},{5,3},{2,4},{3,5},{0,6},{1,7},{14,8},{15,9},{12,... | collective-permute-start | bytes 442376 | tf_op jit(solution)/shard_map/ppermute | solution.py:112
  9.2 0.5 %collective-permute-start.3 = (bf16[144,512]{1,0:T(8,128)(2,1)S(1)}, bf16[144,512]{1,0:T(8,128)(2,1)S(1)}, u32[]{:S(2)}, u32[]{:S(2)}) collective-permute-start(bf16[144,512]{1,0:T(8,128)(2,1)S(1)} %get-tuple-element.16.refs_0_.refs_8_), channel_id=1, source_target_pairs={{4,0},{5,1},{6,2},{7,3},{0,4},{1,5},{2,6},{3,7},{12,8},{13,9},{14,... | collective-permute-start | bytes 442376 | tf_op jit(solution)/shard_map/ppermute | solution.py:112
  9.7 0.5 %collective-permute-start.4 = (bf16[144,512]{1,0:T(8,128)(2,1)S(1)}, bf16[144,512]{1,0:T(8,128)(2,1)S(1)}, u32[]{:S(2)}, u32[]{:S(2)}) collective-permute-start(bf16[144,512]{1,0:T(8,128)(2,1)S(1)} %get-tuple-element.16.refs_0_.refs_8_), channel_id=1, source_target_pairs={{2,0},{3,1},{0,2},{1,3},{6,4},{7,5},{4,6},{5,7},{10,8},{11,9},{8,1... | collective-permute-start | bytes 442376 | tf_op jit(solution)/shard_map/ppermute | solution.py:112
  10.3 2.0 %collective-permute-done.refs_10_ = bf16[144,512]{1,0:T(8,128)(2,1)S(1)} collective-permute-done((bf16[144,512]{1,0:T(8,128)(2,1)S(1)}, bf16[144,512]{1,0:T(8,128)(2,1)S(1)}, u32[]{:S(2)}, u32[]{:S(2)}) %collective-permute-start) | collective-permute-done | bytes 147488 | tf_op jit(solution)/shard_map/ppermute | solution.py:112
  12.3 0.0 collective-permute-start.5
  12.3 0.2 collective-permute-done.1.refs_9_
  12.5 1.2 %collective-permute-done.2.refs_3_ = bf16[144,512]{1,0:T(8,128)(2,1)S(1)} collective-permute-done((bf16[144,512]{1,0:T(8,128)(2,1)S(1)}, bf16[144,512]{1,0:T(8,128)(2,1)S(1)}, u32[]{:S(2)}, u32[]{:S(2)}) %collective-permute-start.2) | collective-permute-done | bytes 147488 | tf_op jit(solution)/shard_map/ppermute | solution.py:112
  13.7 2.2 %collective-permute-done.3.refs_2_ = bf16[144,512]{1,0:T(8,128)(2,1)S(1)} collective-permute-done((bf16[144,512]{1,0:T(8,128)(2,1)S(1)}, bf16[144,512]{1,0:T(8,128)(2,1)S(1)}, u32[]{:S(2)}, u32[]{:S(2)}) %collective-permute-start.3) | collective-permute-done | bytes 147488 | tf_op jit(solution)/shard_map/ppermute | solution.py:112
  15.9 0.1 collective-permute-done.4.refs_1_
  15.9 0.0 collective-permute-start.6
  15.9 0.5 %collective-permute-start.7 = (bf16[144,512]{1,0:T(8,128)(2,1)S(1)}, bf16[144,512]{1,0:T(8,128)(2,1)S(1)}, u32[]{:S(2)}, u32[]{:S(2)}) collective-permute-start(bf16[144,512]{1,0:T(8,128)(2,1)S(1)} %collective-permute-done.3.refs_2_), channel_id=1, source_target_pairs={{1,0},{0,1},{3,2},{2,3},{5,4},{4,5},{7,6},{6,7},{9,8},{8,9},{11,10... | collective-permute-start | bytes 442376 | tf_op jit(solution)/shard_map/ppermute | solution.py:112
  16.4 0.0 collective-permute-start.8
  16.4 0.4 %collective-permute-start.11 = (bf16[144,512]{1,0:T(8,128)(2,1)S(1)}, bf16[144,512]{1,0:T(8,128)(2,1)S(1)}, u32[]{:S(2)}, u32[]{:S(2)}) collective-permute-start(bf16[144,512]{1,0:T(8,128)(2,1)S(1)} %collective-permute-done.refs_10_), channel_id=1, source_target_pairs={{8,0},{9,1},{10,2},{11,3},{12,4},{13,5},{14,6},{15,7},{0,8},{1,9},... | collective-permute-start | bytes 442376 | tf_op jit(solution)/shard_map/ppermute | solution.py:112
  16.9 0.1 stack.60.rank_ref
  17.0 0.1 stack.58.rank_ref
  17.1 0.0 collective-permute-done.5.refs_4_
  17.1 0.2 collective-permute-done.6.refs_5_
  17.3 0.2 collective-permute-done.7.refs_6_
  17.5 0.3 %collective-permute-done.8.refs_7_ = bf16[144,512]{1,0:T(8,128)(2,1)S(1)} collective-permute-done((bf16[144,512]{1,0:T(8,128)(2,1)S(1)}, bf16[144,512]{1,0:T(8,128)(2,1)S(1)}, u32[]{:S(2)}, u32[]{:S(2)}) %collective-permute-start.8) | collective-permute-done | bytes 147488 | tf_op jit(solution)/shard_map/ppermute | solution.py:112
  17.8 2.0 %shard_map.38 = (f32[1,128]{1,0:T(1,128)S(1)}, f32[1,128]{1,0:T(1,128)S(1)}, f32[1,128]{1,0:T(1,128)S(1)}) custom-call(s32[11]{0:T(128)S(1)} %stack.58.rank_ref, bf16[64,64]{1,0:T(8,128)(2,1)S(1)} %get-tuple-element.15.table_ref, bf16[144,512]{1,0:T(8,128)(2,1)S(1)} %get-tuple-element.16.refs_0_.refs_8_, ...), custom_call_target="tpu_custom_call" | custom-call | flops 402653184 | bytes 1441792 | tf_op jit(solution)/shard_map/pallas_call | solution.py:87
  19.8 0.4 %collective-permute-start.10 = (f32[1,128]{1,0:T(1,128)S(1)}, f32[1,128]{1,0:T(1,128)S(1)}, u32[]{:S(2)}, u32[]{:S(2)}) collective-permute-start(f32[1,128]{1,0:T(1,128)S(1)} %get-tuple-element.24), channel_id=1, source_target_pairs={{16,0},{17,1},{18,2},{19,3},{20,4},{21,5},{22,6},{23,7},{24,8},{25... | collective-permute-start | bytes 1544 | tf_op jit(solution)/shard_map/ppermute | solution.py:112
  20.2 0.9 %collective-permute-start.9 = (f32[1,128]{1,0:T(1,128)S(1)}, f32[1,128]{1,0:T(1,128)S(1)}, u32[]{:S(2)}, u32[]{:S(2)}) collective-permute-start(f32[1,128]{1,0:T(1,128)S(1)} %get-tuple-element.23), channel_id=1, source_target_pairs={{8,0},{9,1},{10,2},{11,3},{12,4},{13,5},{14,6},{15,7},{0,8},{1,9},... | collective-permute-start | bytes 1544 | tf_op jit(solution)/shard_map/ppermute | solution.py:112
  21.1 1.6 %collective-permute-done.11.refs_8_ = bf16[144,512]{1,0:T(8,128)(2,1)S(1)} collective-permute-done((bf16[144,512]{1,0:T(8,128)(2,1)S(1)}, bf16[144,512]{1,0:T(8,128)(2,1)S(1)}, u32[]{:S(2)}, u32[]{:S(2)}) %collective-permute-start.11) | collective-permute-done | bytes 147488 | tf_op jit(solution)/shard_map/ppermute | solution.py:112
  22.7 1.2 %shard_map.39 = f32[1,128]{1,0:T(1,128)S(1)} custom-call(s32[9]{0:T(128)S(1)} %stack.60.rank_ref, bf16[64,64]{1,0:T(8,128)(2,1)S(1)} %get-tuple-element.15.table_ref, bf16[144,512]{1,0:T(8,128)(2,1)S(1)} %get-tuple-element.16.refs_0_.refs_8_, bf16[144,512]{1,0:T(8,128)(2,1)S(1)} %collective-permute-done.4.refs_1_, ...), custom_call_target="tpu_custom_call" | custom-call | flops 134217728 | bytes 1179648 | tf_op jit(solution)/shard_map/pallas_call | solution.py:87
  23.9 1.6 %collective-permute-start.12 = (f32[1,128]{1,0:T(1,128)S(1)}, f32[1,128]{1,0:T(1,128)S(1)}, u32[]{:S(2)}, u32[]{:S(2)}) collective-permute-start(f32[1,128]{1,0:T(1,128)S(1)} %shard_map.39), channel_id=1, source_target_pairs={{24,0},{25,1},{26,2},{27,3},{28,4},{29,5},{30,6},{31,7},{16,8},{17... | collective-permute-start | bytes 1544 | tf_op jit(solution)/shard_map/ppermute | solution.py:112
  25.5 0.0 collective-permute-done.10
  25.5 0.0 collective-permute-done.9
  25.5 3.8 %collective-permute-done.12 = f32[1,128]{1,0:T(1,128)S(1)} collective-permute-done((f32[1,128]{1,0:T(1,128)S(1)}, f32[1,128]{1,0:T(1,128)S(1)}, u32[]{:S(2)}, u32[]{:S(2)}) %collective-permute-start.12) | collective-permute-done | bytes 544 | tf_op jit(solution)/shard_map/ppermute | solution.py:112
  29.3 0.5 %maximum_bitcast_fusion = f32[128]{0:T(128)} fusion(f32[1,128]{1,0:T(1,128)S(1)} %collective-permute-done.12, f32[1,128]{1,0:T(1,128)S(1)} %collective-permute-done.10, f32[1,128]{1,0:T(1,128)S(1)} %get-tuple-element.22, f32[1,128]{1,0:T(1,128)S(1)} %collective-permute-done.9), kind=kLoop, calls=%fused_computation | loop fusion | flops 384 | bytes 2560 | tf_op jit(solution)/shard_map/reshape | solution.py:150
Async XLA Ops:
  1.1 11.2 %collective-permute-start = (bf16[144,512]{1,0:T(8,128)(2,1)S(1)}, bf16[144,512]{1,0:T(8,128)(2,1)S(1)}, u32[]{:S(2)}, u32[]{:S(2)}) collective-permute-start(bf16[144,512]{1,0:T(8,128)(2,1)S(1)} %get-tuple-element.16.refs_0_.refs_8_), channel_id=1, source_target_pairs={{16,0},{17,1},{18,2},{19,3},{20,4},{21,5},{22,6},{23,7},{24,8},{25... | collective-permute-start | bytes 442376 | tf_op jit(solution)/shard_map/ppermute | solution.py:112
  5.2 7.3 %collective-permute-start.1 = (bf16[144,512]{1,0:T(8,128)(2,1)S(1)}, bf16[144,512]{1,0:T(8,128)(2,1)S(1)}, u32[]{:S(2)}, u32[]{:S(2)}) collective-permute-start(bf16[144,512]{1,0:T(8,128)(2,1)S(1)} %get-tuple-element.16.refs_0_.refs_8_), channel_id=1, source_target_pairs={{8,0},{9,1},{10,2},{11,3},{12,4},{13,5},{14,6},{15,7},{0,8},{1,9},... | collective-permute-start | bytes 442376 | tf_op jit(solution)/shard_map/ppermute | solution.py:112
  6.8 6.9 %collective-permute-start.2 = (bf16[144,512]{1,0:T(8,128)(2,1)S(1)}, bf16[144,512]{1,0:T(8,128)(2,1)S(1)}, u32[]{:S(2)}, u32[]{:S(2)}) collective-permute-start(bf16[144,512]{1,0:T(8,128)(2,1)S(1)} %get-tuple-element.16.refs_0_.refs_8_), channel_id=1, source_target_pairs={{6,0},{7,1},{4,2},{5,3},{2,4},{3,5},{0,6},{1,7},{14,8},{15,9},{12,... | collective-permute-start | bytes 442376 | tf_op jit(solution)/shard_map/ppermute | solution.py:112
  9.2 6.6 %collective-permute-start.3 = (bf16[144,512]{1,0:T(8,128)(2,1)S(1)}, bf16[144,512]{1,0:T(8,128)(2,1)S(1)}, u32[]{:S(2)}, u32[]{:S(2)}) collective-permute-start(bf16[144,512]{1,0:T(8,128)(2,1)S(1)} %get-tuple-element.16.refs_0_.refs_8_), channel_id=1, source_target_pairs={{4,0},{5,1},{6,2},{7,3},{0,4},{1,5},{2,6},{3,7},{12,8},{13,9},{14,... | collective-permute-start | bytes 442376 | tf_op jit(solution)/shard_map/ppermute | solution.py:112
  9.7 6.2 %collective-permute-start.4 = (bf16[144,512]{1,0:T(8,128)(2,1)S(1)}, bf16[144,512]{1,0:T(8,128)(2,1)S(1)}, u32[]{:S(2)}, u32[]{:S(2)}) collective-permute-start(bf16[144,512]{1,0:T(8,128)(2,1)S(1)} %get-tuple-element.16.refs_0_.refs_8_), channel_id=1, source_target_pairs={{2,0},{3,1},{0,2},{1,3},{6,4},{7,5},{4,6},{5,7},{10,8},{11,9},{8,1... | collective-permute-start | bytes 442376 | tf_op jit(solution)/shard_map/ppermute | solution.py:112
  12.3 4.7 %collective-permute-start.5 = (bf16[144,512]{1,0:T(8,128)(2,1)S(1)}, bf16[144,512]{1,0:T(8,128)(2,1)S(1)}, u32[]{:S(2)}, u32[]{:S(2)}) collective-permute-start(bf16[144,512]{1,0:T(8,128)(2,1)S(1)} %get-tuple-element.16.refs_0_.refs_8_), channel_id=1, source_target_pairs={{1,0},{0,1},{3,2},{2,3},{5,4},{4,5},{7,6},{6,7},{9,8},{8,9},{11,10... | collective-permute-start | bytes 442376 | tf_op jit(solution)/shard_map/ppermute | solution.py:112
  15.9 1.4 %collective-permute-start.6 = (bf16[144,512]{1,0:T(8,128)(2,1)S(1)}, bf16[144,512]{1,0:T(8,128)(2,1)S(1)}, u32[]{:S(2)}, u32[]{:S(2)}) collective-permute-start(bf16[144,512]{1,0:T(8,128)(2,1)S(1)} %collective-permute-done.4.refs_1_), channel_id=1, source_target_pairs={{1,0},{0,1},{3,2},{2,3},{5,4},{4,5},{7,6},{6,7},{9,8},{8,9},{11,10... | collective-permute-start | bytes 442376 | tf_op jit(solution)/shard_map/ppermute | solution.py:112
  15.9 1.6 %collective-permute-start.7 = (bf16[144,512]{1,0:T(8,128)(2,1)S(1)}, bf16[144,512]{1,0:T(8,128)(2,1)S(1)}, u32[]{:S(2)}, u32[]{:S(2)}) collective-permute-start(bf16[144,512]{1,0:T(8,128)(2,1)S(1)} %collective-permute-done.3.refs_2_), channel_id=1, source_target_pairs={{1,0},{0,1},{3,2},{2,3},{5,4},{4,5},{7,6},{6,7},{9,8},{8,9},{11,10... | collective-permute-start | bytes 442376 | tf_op jit(solution)/shard_map/ppermute | solution.py:112
  16.4 1.4 %collective-permute-start.8 = (bf16[144,512]{1,0:T(8,128)(2,1)S(1)}, bf16[144,512]{1,0:T(8,128)(2,1)S(1)}, u32[]{:S(2)}, u32[]{:S(2)}) collective-permute-start(bf16[144,512]{1,0:T(8,128)(2,1)S(1)} %collective-permute-done.2.refs_3_), channel_id=1, source_target_pairs={{1,0},{0,1},{3,2},{2,3},{5,4},{4,5},{7,6},{6,7},{9,8},{8,9},{11,10... | collective-permute-start | bytes 442376 | tf_op jit(solution)/shard_map/ppermute | solution.py:112
  16.4 6.3 %collective-permute-start.11 = (bf16[144,512]{1,0:T(8,128)(2,1)S(1)}, bf16[144,512]{1,0:T(8,128)(2,1)S(1)}, u32[]{:S(2)}, u32[]{:S(2)}) collective-permute-start(bf16[144,512]{1,0:T(8,128)(2,1)S(1)} %collective-permute-done.refs_10_), channel_id=1, source_target_pairs={{8,0},{9,1},{10,2},{11,3},{12,4},{13,5},{14,6},{15,7},{0,8},{1,9},... | collective-permute-start | bytes 442376 | tf_op jit(solution)/shard_map/ppermute | solution.py:112
  19.8 5.7 %collective-permute-start.10 = (f32[1,128]{1,0:T(1,128)S(1)}, f32[1,128]{1,0:T(1,128)S(1)}, u32[]{:S(2)}, u32[]{:S(2)}) collective-permute-start(f32[1,128]{1,0:T(1,128)S(1)} %get-tuple-element.24), channel_id=1, source_target_pairs={{16,0},{17,1},{18,2},{19,3},{20,4},{21,5},{22,6},{23,7},{24,8},{25... | collective-permute-start | bytes 1544 | tf_op jit(solution)/shard_map/ppermute | solution.py:112
  20.2 5.3 %collective-permute-start.9 = (f32[1,128]{1,0:T(1,128)S(1)}, f32[1,128]{1,0:T(1,128)S(1)}, u32[]{:S(2)}, u32[]{:S(2)}) collective-permute-start(f32[1,128]{1,0:T(1,128)S(1)} %get-tuple-element.23), channel_id=1, source_target_pairs={{8,0},{9,1},{10,2},{11,3},{12,4},{13,5},{14,6},{15,7},{0,8},{1,9},... | collective-permute-start | bytes 1544 | tf_op jit(solution)/shard_map/ppermute | solution.py:112
  23.9 5.4 %collective-permute-start.12 = (f32[1,128]{1,0:T(1,128)S(1)}, f32[1,128]{1,0:T(1,128)S(1)}, u32[]{:S(2)}, u32[]{:S(2)}) collective-permute-start(f32[1,128]{1,0:T(1,128)S(1)} %shard_map.39), channel_id=1, source_target_pairs={{24,0},{25,1},{26,2},{27,3},{28,4},{29,5},{30,6},{31,7},{16,8},{17... | collective-permute-start | bytes 1544 | tf_op jit(solution)/shard_map/ppermute | solution.py:112

commit v11 on v10

--- a/solution.py
+++ b/solution.py
@@ -47,11 +47,13 @@
     return jnp.where(index == number, 1.0, 0.0).astype(jnp.bfloat16)
 
 
-def best_kernel(n_keys, own, rank_ref, table_ref, *refs):
+def best_kernel(n_keys, own, ranks, table_ref, *refs):
     n_queries = (len(refs) - n_keys) // 2
     keys, queries, outs = refs[:n_keys], refs[n_keys : n_keys + n_queries], refs[n_keys + n_queries :]
     rows = keys[0].shape[0] - AUX
     clusters = table_ref.shape[0]
+    clu, grp = lax.axis_index("clu"), lax.axis_index("grp")
+    ranks = [rank(clu, grp) for rank in ranks]
 
     def hot(block):
         return one_hot(block[rows:, :rows].astype(jnp.float32), clusters)
@@ -74,7 +76,7 @@
                 found = jnp.max(jnp.where(k < q, part, -1.0), axis=0, keepdims=True)
             else:
                 found = jnp.max(part, axis=0, keepdims=True)
-                found = jnp.where(rank_ref[i] < rank_ref[n_keys + j], found, -1.0)
+                found = jnp.where(ranks[i] < ranks[n_keys + j], found, -1.0)
             best = jnp.maximum(best, found)
         outs[j][...] = best
 
@@ -82,18 +84,18 @@
 def best_of(keys, queries, table, own):
     rows, width = keys[0][0].shape[0] - AUX, keys[0][0].shape[1]
     vmem = pl.BlockSpec(memory_space=pltpu.VMEM)
-    ranks = jnp.stack([r for _, r in keys + queries]).astype(jnp.int32)
+    ranks = [r for _, r in keys + queries]
     pairs = len(keys) * len(queries) * rows * rows
     return pl.pallas_call(
-        functools.partial(best_kernel, len(keys), own),
+        functools.partial(best_kernel, len(keys), own, ranks),
         out_shape=[jax.ShapeDtypeStruct((1, rows), jnp.float32)] * len(queries),
-        in_specs=[pl.BlockSpec(memory_space=pltpu.SMEM)] + [vmem] * (1 + len(keys) + len(queries)),
+        in_specs=[vmem] * (1 + len(keys) + len(queries)),
         out_specs=[vmem] * len(queries),
         compiler_params=pltpu.CompilerParams(vmem_limit_bytes=40 * 2**20),
         cost_estimate=pl.CostEstimate(
             flops=2 * pairs * width, bytes_accessed=2 * (len(keys) + len(queries)) * rows * width, transcendentals=0
         ),
-    )(ranks, table, *[b for b, _ in keys + queries])
+    )(table, *[b for b, _ in keys + queries])
 
 
 def solution(mesh):
@@ -117,11 +119,13 @@
     def shards(embeddings, cluster_id, cluster_group):
         rows = embeddings.shape[0]
         own, table = pack(embeddings, cluster_id, cluster_group, n_clu)
-        clu, grp = lax.axis_index("clu"), lax.axis_index("grp")
-        line, place = clu // wide, clu % wide
 
-        def rank(z, a, g):
-            return g * n_clu + z * wide + a
+        def rank(z=0, a=0, g=0):
+            def of(clu, grp):
+                line, place = turned(clu // wide, z, length), turned(clu % wide, a, wide)
+                return turned(grp, g, n_grp) * n_clu + line * wide + place
+
+            return of
 
         def along(x, s):
             return permute(x, lambda z, a, g: (turned(z, s, length), a, g))
@@ -137,10 +141,10 @@
             for s in range(wide):
                 block = near[s - 1] if s else own
                 far.append(permute(block, lambda z, a, g: (z, a, turned(g, t, n_grp))))
-                far_rank.append(rank(line, turned(place, s, wide), turned(grp, t, n_grp)))
-        near = list(zip([own] + near, [rank(line, turned(place, s, wide), grp) for s in range(wide)]))
+                far_rank.append(rank(a=s, g=t))
+        near = list(zip([own] + near, [rank(a=s) for s in range(wide)]))
         far = list(zip(far, far_rank))
-        visit_rank = [rank(turned(line, s, length), place, grp) for s in range(1, length)]
+        visit_rank = [rank(z=s) for s in range(1, length)]
         first = list(zip(first, visit_rank))
         last = list(zip(last, visit_rank[len(first) :]))
         best = best_of(near + far, near[:1] + first, table, True)

time: 29.9 us -> 29.4 us (0.983)
  waiting for transfers between devices: 11.8 us -> 13.3 us
  Pallas kernels: 4.24 us -> 3.17 us
  starting transfers between devices: 13 us -> 12.3 us
    ppermute x13, waiting for transfers between devices: 11.8 us -> 13.3 us  [permute(): return lax.ppermute(x, ('clu', 'grp'), pairs)]
    pallas_call x2, Pallas kernels: 3.14 us -> 2.06 us  [best_of(): pl.pallas_call(functools.partial(best_kernel, len(keys), own, ranks), out...]
    ppermute x13, starting transfers between devices: 13 us -> 12.3 us  [permute(): return lax.ppermute(x, ('clu', 'grp'), pairs)]
  transfers between devices with their start and end apart: 13 -> 13, of which waited for: 10 -> 10; matrix products, arithmetic and copies ran while one was open for 1% -> 0% of each run, Pallas kernels for 11% -> 7%
where the time goes in v11:
time: 29.4 us; the launch traced here: 29.3 us
  waiting for transfers between devices  13.3 us (45%)
  starting transfers between devices  12.3 us (42%)
  Pallas kernels  3.17 us (11%)
  other arithmetic  0.52 us (2%)
    ppermute x13, waiting for transfers between devices, permute(): return lax.ppermute(x, ('clu', 'grp'), pairs)  13.3 us
    ppermute x13, starting transfers between devices, permute(): return lax.ppermute(x, ('clu', 'grp'), pairs)  12.3 us
    pallas_call x2, Pallas kernels, best_of(): pl.pallas_call(functools.partial(best_kernel, len(keys), own, ranks), out...  2.06 us
    pallas_call x1, Pallas kernels, pack(): pl.pallas_call(functools.partial(pack_kernel, groups), out_shape=[pltpu.V...  1.1 us
  transfers between devices with their start and end apart: 13, of which 10 were waited for; matrix products, arithmetic and copies ran while one was open for 0% of the time, Pallas kernels for 7%

profile of v11, /device:TPU:0, one launch (start us, length us, event | category | flops | bytes accessed | tf_op | source)
XLA Modules:
  0.0 29.3 jit_solution(11429316794740656312)
XLA Ops:
  0.0 1.1 %shard_map.37 = (bf16[144,512]{1,0:T(8,128)(2,1)S(1)}, bf16[64,64]{1,0:T(8,128)(2,1)S(1)}) custom-call(bf16[128,512]{1,0:T(8,128)(2,1)} %emb_ref.1, s32[1,128]{1,0:T(1,128)} %bitcast.4, s32[1,64]{1,0:T(1,128)} %bitcast.5), custom_call_target="tpu_custom_call" | custom-call | tf_op jit(solution)/shard_map/pallas_call | solution.py:38
  1.1 4.1 %collective-permute-start = (bf16[144,512]{1,0:T(8,128)(2,1)S(1)}, bf16[144,512]{1,0:T(8,128)(2,1)S(1)}, u32[]{:S(2)}, u32[]{:S(2)}) collective-permute-start(bf16[144,512]{1,0:T(8,128)(2,1)S(1)} %get-tuple-element.16.refs_0_.refs_8_), channel_id=1, source_target_pairs={{16,0},{17,1},{18,2},{19,3},{20,4},{21,5},{22,6},{23,7},{24,8},{25... | collective-permute-start | bytes 442376 | tf_op jit(solution)/shard_map/ppermute | solution.py:114
  5.2 1.6 %collective-permute-start.1 = (bf16[144,512]{1,0:T(8,128)(2,1)S(1)}, bf16[144,512]{1,0:T(8,128)(2,1)S(1)}, u32[]{:S(2)}, u32[]{:S(2)}) collective-permute-start(bf16[144,512]{1,0:T(8,128)(2,1)S(1)} %get-tuple-element.16.refs_0_.refs_8_), channel_id=1, source_target_pairs={{8,0},{9,1},{10,2},{11,3},{12,4},{13,5},{14,6},{15,7},{0,8},{1,9},... | collective-permute-start | bytes 442376 | tf_op jit(solution)/shard_map/ppermute | solution.py:114
  6.8 2.4 %collective-permute-start.2 = (bf16[144,512]{1,0:T(8,128)(2,1)S(1)}, bf16[144,512]{1,0:T(8,128)(2,1)S(1)}, u32[]{:S(2)}, u32[]{:S(2)}) collective-permute-start(bf16[144,512]{1,0:T(8,128)(2,1)S(1)} %get-tuple-element.16.refs_0_.refs_8_), channel_id=1, source_target_pairs={{6,0},{7,1},{4,2},{5,3},{2,4},{3,5},{0,6},{1,7},{14,8},{15,9},{12,... | collective-permute-start | bytes 442376 | tf_op jit(solution)/shard_map/ppermute | solution.py:114
  9.2 0.5 %collective-permute-start.3 = (bf16[144,512]{1,0:T(8,128)(2,1)S(1)}, bf16[144,512]{1,0:T(8,128)(2,1)S(1)}, u32[]{:S(2)}, u32[]{:S(2)}) collective-permute-start(bf16[144,512]{1,0:T(8,128)(2,1)S(1)} %get-tuple-element.16.refs_0_.refs_8_), channel_id=1, source_target_pairs={{4,0},{5,1},{6,2},{7,3},{0,4},{1,5},{2,6},{3,7},{12,8},{13,9},{14,... | collective-permute-start | bytes 442376 | tf_op jit(solution)/shard_map/ppermute | solution.py:114
  9.7 0.5 %collective-permute-start.4 = (bf16[144,512]{1,0:T(8,128)(2,1)S(1)}, bf16[144,512]{1,0:T(8,128)(2,1)S(1)}, u32[]{:S(2)}, u32[]{:S(2)}) collective-permute-start(bf16[144,512]{1,0:T(8,128)(2,1)S(1)} %get-tuple-element.16.refs_0_.refs_8_), channel_id=1, source_target_pairs={{2,0},{3,1},{0,2},{1,3},{6,4},{7,5},{4,6},{5,7},{10,8},{11,9},{8,1... | collective-permute-start | bytes 442376 | tf_op jit(solution)/shard_map/ppermute | solution.py:114
  10.3 2.0 %collective-permute-done.refs_10_ = bf16[144,512]{1,0:T(8,128)(2,1)S(1)} collective-permute-done((bf16[144,512]{1,0:T(8,128)(2,1)S(1)}, bf16[144,512]{1,0:T(8,128)(2,1)S(1)}, u32[]{:S(2)}, u32[]{:S(2)}) %collective-permute-start) | collective-permute-done | bytes 147488 | tf_op jit(solution)/shard_map/ppermute | solution.py:114
  12.3 0.0 collective-permute-start.5
  12.3 0.2 collective-permute-done.1.refs_9_
  12.5 1.2 %collective-permute-done.2.refs_3_ = bf16[144,512]{1,0:T(8,128)(2,1)S(1)} collective-permute-done((bf16[144,512]{1,0:T(8,128)(2,1)S(1)}, bf16[144,512]{1,0:T(8,128)(2,1)S(1)}, u32[]{:S(2)}, u32[]{:S(2)}) %collective-permute-start.2) | collective-permute-done | bytes 147488 | tf_op jit(solution)/shard_map/ppermute | solution.py:114
  13.7 2.2 %collective-permute-done.3.refs_2_ = bf16[144,512]{1,0:T(8,128)(2,1)S(1)} collective-permute-done((bf16[144,512]{1,0:T(8,128)(2,1)S(1)}, bf16[144,512]{1,0:T(8,128)(2,1)S(1)}, u32[]{:S(2)}, u32[]{:S(2)}) %collective-permute-start.3) | collective-permute-done | bytes 147488 | tf_op jit(solution)/shard_map/ppermute | solution.py:114
  15.9 0.1 collective-permute-done.4.refs_1_
  15.9 0.0 collective-permute-start.6
  15.9 0.5 %collective-permute-start.7 = (bf16[144,512]{1,0:T(8,128)(2,1)S(1)}, bf16[144,512]{1,0:T(8,128)(2,1)S(1)}, u32[]{:S(2)}, u32[]{:S(2)}) collective-permute-start(bf16[144,512]{1,0:T(8,128)(2,1)S(1)} %collective-permute-done.3.refs_2_), channel_id=1, source_target_pairs={{1,0},{0,1},{3,2},{2,3},{5,4},{4,5},{7,6},{6,7},{9,8},{8,9},{11,10... | collective-permute-start | bytes 442376 | tf_op jit(solution)/shard_map/ppermute | solution.py:114
  16.4 0.0 collective-permute-start.8
  16.4 0.4 %collective-permute-start.11 = (bf16[144,512]{1,0:T(8,128)(2,1)S(1)}, bf16[144,512]{1,0:T(8,128)(2,1)S(1)}, u32[]{:S(2)}, u32[]{:S(2)}) collective-permute-start(bf16[144,512]{1,0:T(8,128)(2,1)S(1)} %collective-permute-done.refs_10_), channel_id=1, source_target_pairs={{8,0},{9,1},{10,2},{11,3},{12,4},{13,5},{14,6},{15,7},{0,8},{1,9},... | collective-permute-start | bytes 442376 | tf_op jit(solution)/shard_map/ppermute | solution.py:114
  16.9 0.0 collective-permute-done.5.refs_4_
  16.9 0.4 %collective-permute-done.6.refs_5_ = bf16[144,512]{1,0:T(8,128)(2,1)S(1)} collective-permute-done((bf16[144,512]{1,0:T(8,128)(2,1)S(1)}, bf16[144,512]{1,0:T(8,128)(2,1)S(1)}, u32[]{:S(2)}, u32[]{:S(2)}) %collective-permute-start.6) | collective-permute-done | bytes 147488 | tf_op jit(solution)/shard_map/ppermute | solution.py:114
  17.3 0.2 collective-permute-done.7.refs_6_
  17.5 0.3 %collective-permute-done.8.refs_7_ = bf16[144,512]{1,0:T(8,128)(2,1)S(1)} collective-permute-done((bf16[144,512]{1,0:T(8,128)(2,1)S(1)}, bf16[144,512]{1,0:T(8,128)(2,1)S(1)}, u32[]{:S(2)}, u32[]{:S(2)}) %collective-permute-start.8) | collective-permute-done | bytes 147488 | tf_op jit(solution)/shard_map/ppermute | solution.py:114
  17.8 1.4 %shard_map.38 = (f32[1,128]{1,0:T(1,128)S(1)}, f32[1,128]{1,0:T(1,128)S(1)}, f32[1,128]{1,0:T(1,128)S(1)}) custom-call(bf16[64,64]{1,0:T(8,128)(2,1)S(1)} %get-tuple-element.15.table_ref, bf16[144,512]{1,0:T(8,128)(2,1)S(1)} %get-tuple-element.16.refs_0_.refs_8_, bf16[144,512]{1,0:T(8,128)(2,1)S(1)} %collective-permute-done.4.refs_1_, ...), custom_call_target="tpu_custom_call" | custom-call | flops 402653184 | bytes 1441792 | tf_op jit(solution)/shard_map/pallas_call | solution.py:89
  19.3 0.4 %collective-permute-start.10 = (f32[1,128]{1,0:T(1,128)S(1)}, f32[1,128]{1,0:T(1,128)S(1)}, u32[]{:S(2)}, u32[]{:S(2)}) collective-permute-start(f32[1,128]{1,0:T(1,128)S(1)} %get-tuple-element.24), channel_id=1, source_target_pairs={{16,0},{17,1},{18,2},{19,3},{20,4},{21,5},{22,6},{23,7},{24,8},{25... | collective-permute-start | bytes 1544 | tf_op jit(solution)/shard_map/ppermute | solution.py:114
  19.7 0.7 %collective-permute-start.9 = (f32[1,128]{1,0:T(1,128)S(1)}, f32[1,128]{1,0:T(1,128)S(1)}, u32[]{:S(2)}, u32[]{:S(2)}) collective-permute-start(f32[1,128]{1,0:T(1,128)S(1)} %get-tuple-element.23), channel_id=1, source_target_pairs={{8,0},{9,1},{10,2},{11,3},{12,4},{13,5},{14,6},{15,7},{0,8},{1,9},... | collective-permute-start | bytes 1544 | tf_op jit(solution)/shard_map/ppermute | solution.py:114
  20.4 2.4 %collective-permute-done.11.refs_8_ = bf16[144,512]{1,0:T(8,128)(2,1)S(1)} collective-permute-done((bf16[144,512]{1,0:T(8,128)(2,1)S(1)}, bf16[144,512]{1,0:T(8,128)(2,1)S(1)}, u32[]{:S(2)}, u32[]{:S(2)}) %collective-permute-start.11) | collective-permute-done | bytes 147488 | tf_op jit(solution)/shard_map/ppermute | solution.py:114
  22.7 0.6 %shard_map.39 = f32[1,128]{1,0:T(1,128)S(1)} custom-call(bf16[64,64]{1,0:T(8,128)(2,1)S(1)} %get-tuple-element.15.table_ref, bf16[144,512]{1,0:T(8,128)(2,1)S(1)} %get-tuple-element.16.refs_0_.refs_8_, bf16[144,512]{1,0:T(8,128)(2,1)S(1)} %collective-permute-done.4.refs_1_, bf16[144,512]{1,0:T(8,128)(2,1)S(1)} %collective-permute-done.3.refs_2_, ...), custom_call_target="tpu_custom_call" | custom-call | flops 134217728 | bytes 1179648 | tf_op jit(solution)/shard_map/pallas_call | solution.py:89
  23.3 1.1 %collective-permute-start.12 = (f32[1,128]{1,0:T(1,128)S(1)}, f32[1,128]{1,0:T(1,128)S(1)}, u32[]{:S(2)}, u32[]{:S(2)}) collective-permute-start(f32[1,128]{1,0:T(1,128)S(1)} %shard_map.39), channel_id=1, source_target_pairs={{24,0},{25,1},{26,2},{27,3},{28,4},{29,5},{30,6},{31,7},{16,8},{17... | collective-permute-start | bytes 1544 | tf_op jit(solution)/shard_map/ppermute | solution.py:114
  24.4 0.0 collective-permute-done.10
  24.4 0.0 collective-permute-done.9
  24.4 4.3 %collective-permute-done.12 = f32[1,128]{1,0:T(1,128)S(1)} collective-permute-done((f32[1,128]{1,0:T(1,128)S(1)}, f32[1,128]{1,0:T(1,128)S(1)}, u32[]{:S(2)}, u32[]{:S(2)}) %collective-permute-start.12) | collective-permute-done | bytes 544 | tf_op jit(solution)/shard_map/ppermute | solution.py:114
  28.7 0.5 %maximum_bitcast_fusion = f32[128]{0:T(128)} fusion(f32[1,128]{1,0:T(1,128)S(1)} %collective-permute-done.12, f32[1,128]{1,0:T(1,128)S(1)} %collective-permute-done.10, f32[1,128]{1,0:T(1,128)S(1)} %get-tuple-element.22, f32[1,128]{1,0:T(1,128)S(1)} %collective-permute-done.9), kind=kLoop, calls=%fused_computation | loop fusion | flops 384 | bytes 2560 | tf_op jit(solution)/shard_map/reshape | solution.py:154
Async XLA Ops:
  1.1 11.2 %collective-permute-start = (bf16[144,512]{1,0:T(8,128)(2,1)S(1)}, bf16[144,512]{1,0:T(8,128)(2,1)S(1)}, u32[]{:S(2)}, u32[]{:S(2)}) collective-permute-start(bf16[144,512]{1,0:T(8,128)(2,1)S(1)} %get-tuple-element.16.refs_0_.refs_8_), channel_id=1, source_target_pairs={{16,0},{17,1},{18,2},{19,3},{20,4},{21,5},{22,6},{23,7},{24,8},{25... | collective-permute-start | bytes 442376 | tf_op jit(solution)/shard_map/ppermute | solution.py:114
  5.2 7.3 %collective-permute-start.1 = (bf16[144,512]{1,0:T(8,128)(2,1)S(1)}, bf16[144,512]{1,0:T(8,128)(2,1)S(1)}, u32[]{:S(2)}, u32[]{:S(2)}) collective-permute-start(bf16[144,512]{1,0:T(8,128)(2,1)S(1)} %get-tuple-element.16.refs_0_.refs_8_), channel_id=1, source_target_pairs={{8,0},{9,1},{10,2},{11,3},{12,4},{13,5},{14,6},{15,7},{0,8},{1,9},... | collective-permute-start | bytes 442376 | tf_op jit(solution)/shard_map/ppermute | solution.py:114
  6.8 6.9 %collective-permute-start.2 = (bf16[144,512]{1,0:T(8,128)(2,1)S(1)}, bf16[144,512]{1,0:T(8,128)(2,1)S(1)}, u32[]{:S(2)}, u32[]{:S(2)}) collective-permute-start(bf16[144,512]{1,0:T(8,128)(2,1)S(1)} %get-tuple-element.16.refs_0_.refs_8_), channel_id=1, source_target_pairs={{6,0},{7,1},{4,2},{5,3},{2,4},{3,5},{0,6},{1,7},{14,8},{15,9},{12,... | collective-permute-start | bytes 442376 | tf_op jit(solution)/shard_map/ppermute | solution.py:114
  9.2 6.6 %collective-permute-start.3 = (bf16[144,512]{1,0:T(8,128)(2,1)S(1)}, bf16[144,512]{1,0:T(8,128)(2,1)S(1)}, u32[]{:S(2)}, u32[]{:S(2)}) collective-permute-start(bf16[144,512]{1,0:T(8,128)(2,1)S(1)} %get-tuple-element.16.refs_0_.refs_8_), channel_id=1, source_target_pairs={{4,0},{5,1},{6,2},{7,3},{0,4},{1,5},{2,6},{3,7},{12,8},{13,9},{14,... | collective-permute-start | bytes 442376 | tf_op jit(solution)/shard_map/ppermute | solution.py:114
  9.7 6.2 %collective-permute-start.4 = (bf16[144,512]{1,0:T(8,128)(2,1)S(1)}, bf16[144,512]{1,0:T(8,128)(2,1)S(1)}, u32[]{:S(2)}, u32[]{:S(2)}) collective-permute-start(bf16[144,512]{1,0:T(8,128)(2,1)S(1)} %get-tuple-element.16.refs_0_.refs_8_), channel_id=1, source_target_pairs={{2,0},{3,1},{0,2},{1,3},{6,4},{7,5},{4,6},{5,7},{10,8},{11,9},{8,1... | collective-permute-start | bytes 442376 | tf_op jit(solution)/shard_map/ppermute | solution.py:114
  12.3 4.6 %collective-permute-start.5 = (bf16[144,512]{1,0:T(8,128)(2,1)S(1)}, bf16[144,512]{1,0:T(8,128)(2,1)S(1)}, u32[]{:S(2)}, u32[]{:S(2)}) collective-permute-start(bf16[144,512]{1,0:T(8,128)(2,1)S(1)} %get-tuple-element.16.refs_0_.refs_8_), channel_id=1, source_target_pairs={{1,0},{0,1},{3,2},{2,3},{5,4},{4,5},{7,6},{6,7},{9,8},{8,9},{11,10... | collective-permute-start | bytes 442376 | tf_op jit(solution)/shard_map/ppermute | solution.py:114
  15.9 1.4 %collective-permute-start.6 = (bf16[144,512]{1,0:T(8,128)(2,1)S(1)}, bf16[144,512]{1,0:T(8,128)(2,1)S(1)}, u32[]{:S(2)}, u32[]{:S(2)}) collective-permute-start(bf16[144,512]{1,0:T(8,128)(2,1)S(1)} %collective-permute-done.4.refs_1_), channel_id=1, source_target_pairs={{1,0},{0,1},{3,2},{2,3},{5,4},{4,5},{7,6},{6,7},{9,8},{8,9},{11,10... | collective-permute-start | bytes 442376 | tf_op jit(solution)/shard_map/ppermute | solution.py:114
  15.9 1.6 %collective-permute-start.7 = (bf16[144,512]{1,0:T(8,128)(2,1)S(1)}, bf16[144,512]{1,0:T(8,128)(2,1)S(1)}, u32[]{:S(2)}, u32[]{:S(2)}) collective-permute-start(bf16[144,512]{1,0:T(8,128)(2,1)S(1)} %collective-permute-done.3.refs_2_), channel_id=1, source_target_pairs={{1,0},{0,1},{3,2},{2,3},{5,4},{4,5},{7,6},{6,7},{9,8},{8,9},{11,10... | collective-permute-start | bytes 442376 | tf_op jit(solution)/shard_map/ppermute | solution.py:114
  16.4 1.4 %collective-permute-start.8 = (bf16[144,512]{1,0:T(8,128)(2,1)S(1)}, bf16[144,512]{1,0:T(8,128)(2,1)S(1)}, u32[]{:S(2)}, u32[]{:S(2)}) collective-permute-start(bf16[144,512]{1,0:T(8,128)(2,1)S(1)} %collective-permute-done.2.refs_3_), channel_id=1, source_target_pairs={{1,0},{0,1},{3,2},{2,3},{5,4},{4,5},{7,6},{6,7},{9,8},{8,9},{11,10... | collective-permute-start | bytes 442376 | tf_op jit(solution)/shard_map/ppermute | solution.py:114
  16.4 6.3 %collective-permute-start.11 = (bf16[144,512]{1,0:T(8,128)(2,1)S(1)}, bf16[144,512]{1,0:T(8,128)(2,1)S(1)}, u32[]{:S(2)}, u32[]{:S(2)}) collective-permute-start(bf16[144,512]{1,0:T(8,128)(2,1)S(1)} %collective-permute-done.refs_10_), channel_id=1, source_target_pairs={{8,0},{9,1},{10,2},{11,3},{12,4},{13,5},{14,6},{15,7},{0,8},{1,9},... | collective-permute-start | bytes 442376 | tf_op jit(solution)/shard_map/ppermute | solution.py:114
  19.3 5.2 %collective-permute-start.10 = (f32[1,128]{1,0:T(1,128)S(1)}, f32[1,128]{1,0:T(1,128)S(1)}, u32[]{:S(2)}, u32[]{:S(2)}) collective-permute-start(f32[1,128]{1,0:T(1,128)S(1)} %get-tuple-element.24), channel_id=1, source_target_pairs={{16,0},{17,1},{18,2},{19,3},{20,4},{21,5},{22,6},{23,7},{24,8},{25... | collective-permute-start | bytes 1544 | tf_op jit(solution)/shard_map/ppermute | solution.py:114
  19.7 4.7 %collective-permute-start.9 = (f32[1,128]{1,0:T(1,128)S(1)}, f32[1,128]{1,0:T(1,128)S(1)}, u32[]{:S(2)}, u32[]{:S(2)}) collective-permute-start(f32[1,128]{1,0:T(1,128)S(1)} %get-tuple-element.23), channel_id=1, source_target_pairs={{8,0},{9,1},{10,2},{11,3},{12,4},{13,5},{14,6},{15,7},{0,8},{1,9},... | collective-permute-start | bytes 1544 | tf_op jit(solution)/shard_map/ppermute | solution.py:114
  23.3 5.4 %collective-permute-start.12 = (f32[1,128]{1,0:T(1,128)S(1)}, f32[1,128]{1,0:T(1,128)S(1)}, u32[]{:S(2)}, u32[]{:S(2)}) collective-permute-start(f32[1,128]{1,0:T(1,128)S(1)} %shard_map.39), channel_id=1, source_target_pairs={{24,0},{25,1},{26,2},{27,3},{28,4},{29,5},{30,6},{31,7},{16,8},{17... | collective-permute-start | bytes 1544 | tf_op jit(solution)/shard_map/ppermute | solution.py:114

commit v12 on v11

--- a/solution.py
+++ b/solution.py
@@ -131,10 +131,12 @@
             return permute(x, lambda z, a, g: (turned(z, s, length), a, g))
 
         half = length // 2 if length & (length - 1) == 0 else length
-        first = [along(own, s) for s in reversed(range(1, min(half + 1, length)))]
+        middle = along(own, half) if half < length else None
         near = [permute(own, lambda z, a, g: (z, turned(a, s, wide), g)) for s in reversed(range(1, wide))]
-        first, near = lax.optimization_barrier((first, near))
-        first, near = first[::-1], near[::-1]
+        first = [along(own, s) for s in range(1, half)]
+        middle, near, first = lax.optimization_barrier((middle, near, first))
+        near = near[::-1]
+        first = first if middle is None else first + [middle]
         last = [along(first[half - 1], s) for s in range(1, length - half)]
         far, far_rank = [], []
         for t in range(1, n_grp):

time: 29.4 us -> 28.6 us (0.973)
  waiting for transfers between devices: 13.3 us -> 8.38 us
  starting transfers between devices: 12.3 us -> 16.4 us
    ppermute x13, waiting for transfers between devices: 13.3 us -> 8.38 us  [permute(): return lax.ppermute(x, ('clu', 'grp'), pairs)]
    ppermute x13, starting transfers between devices: 12.3 us -> 16.4 us  [permute(): return lax.ppermute(x, ('clu', 'grp'), pairs)]
  transfers between devices with their start and end apart: 13 -> 13, of which waited for: 10 -> 7; matrix products, arithmetic and copies ran while one was open for 0% -> 0% of each run, Pallas kernels for 7% -> 7%
where the time goes in v12:
time: 28.6 us; the launch traced here: 28.5 us
  starting transfers between devices  16.4 us (57%)
  waiting for transfers between devices  8.38 us (29%)
  Pallas kernels  3.17 us (11%)
  other arithmetic  0.52 us (2%)
    ppermute x13, starting transfers between devices, permute(): return lax.ppermute(x, ('clu', 'grp'), pairs)  16.4 us
    ppermute x13, waiting for transfers between devices, permute(): return lax.ppermute(x, ('clu', 'grp'), pairs)  8.38 us
    pallas_call x2, Pallas kernels, best_of(): pl.pallas_call(functools.partial(best_kernel, len(keys), own, ranks), out...  2.06 us
    pallas_call x1, Pallas kernels, pack(): pl.pallas_call(functools.partial(pack_kernel, groups), out_shape=[pltpu.V...  1.1 us
  transfers between devices with their start and end apart: 13, of which 7 were waited for; matrix products, arithmetic and copies ran while one was open for 0% of the time, Pallas kernels for 7%

profile of v12, /device:TPU:0, one launch (start us, length us, event | category | flops | bytes accessed | tf_op | source)
XLA Modules:
  0.0 28.5 jit_solution(5474939231950219487)
XLA Ops:
  0.0 1.1 %shard_map.37 = (bf16[144,512]{1,0:T(8,128)(2,1)S(1)}, bf16[64,64]{1,0:T(8,128)(2,1)S(1)}) custom-call(bf16[128,512]{1,0:T(8,128)(2,1)} %emb_ref.1, s32[1,128]{1,0:T(1,128)} %bitcast.4, s32[1,64]{1,0:T(1,128)} %bitcast.5), custom_call_target="tpu_custom_call" | custom-call | tf_op jit(solution)/shard_map/pallas_call | solution.py:38
  1.1 4.1 %collective-permute-start = (bf16[144,512]{1,0:T(8,128)(2,1)S(1)}, bf16[144,512]{1,0:T(8,128)(2,1)S(1)}, u32[]{:S(2)}, u32[]{:S(2)}) collective-permute-start(bf16[144,512]{1,0:T(8,128)(2,1)S(1)} %get-tuple-element.16.refs_0_.refs_8_), channel_id=1, source_target_pairs={{16,0},{17,1},{18,2},{19,3},{20,4},{21,5},{22,6},{23,7},{24,8},{25... | collective-permute-start | bytes 442376 | tf_op jit(solution)/shard_map/ppermute | solution.py:114
  5.2 2.4 %collective-permute-start.1 = (bf16[144,512]{1,0:T(8,128)(2,1)S(1)}, bf16[144,512]{1,0:T(8,128)(2,1)S(1)}, u32[]{:S(2)}, u32[]{:S(2)}) collective-permute-start(bf16[144,512]{1,0:T(8,128)(2,1)S(1)} %get-tuple-element.16.refs_0_.refs_8_), channel_id=1, source_target_pairs={{6,0},{7,1},{4,2},{5,3},{2,4},{3,5},{0,6},{1,7},{14,8},{15,9},{12,... | collective-permute-start | bytes 442376 | tf_op jit(solution)/shard_map/ppermute | solution.py:114
  7.7 0.5 %collective-permute-start.2 = (bf16[144,512]{1,0:T(8,128)(2,1)S(1)}, bf16[144,512]{1,0:T(8,128)(2,1)S(1)}, u32[]{:S(2)}, u32[]{:S(2)}) collective-permute-start(bf16[144,512]{1,0:T(8,128)(2,1)S(1)} %get-tuple-element.16.refs_0_.refs_8_), channel_id=1, source_target_pairs={{4,0},{5,1},{6,2},{7,3},{0,4},{1,5},{2,6},{3,7},{12,8},{13,9},{14,... | collective-permute-start | bytes 442376 | tf_op jit(solution)/shard_map/ppermute | solution.py:114
  8.2 0.5 %collective-permute-start.3 = (bf16[144,512]{1,0:T(8,128)(2,1)S(1)}, bf16[144,512]{1,0:T(8,128)(2,1)S(1)}, u32[]{:S(2)}, u32[]{:S(2)}) collective-permute-start(bf16[144,512]{1,0:T(8,128)(2,1)S(1)} %get-tuple-element.16.refs_0_.refs_8_), channel_id=1, source_target_pairs={{2,0},{3,1},{0,2},{1,3},{6,4},{7,5},{4,6},{5,7},{10,8},{11,9},{8,1... | collective-permute-start | bytes 442376 | tf_op jit(solution)/shard_map/ppermute | solution.py:114
  8.7 1.6 %collective-permute-start.4 = (bf16[144,512]{1,0:T(8,128)(2,1)S(1)}, bf16[144,512]{1,0:T(8,128)(2,1)S(1)}, u32[]{:S(2)}, u32[]{:S(2)}) collective-permute-start(bf16[144,512]{1,0:T(8,128)(2,1)S(1)} %get-tuple-element.16.refs_0_.refs_8_), channel_id=1, source_target_pairs={{8,0},{9,1},{10,2},{11,3},{12,4},{13,5},{14,6},{15,7},{0,8},{1,9},... | collective-permute-start | bytes 442376 | tf_op jit(solution)/shard_map/ppermute | solution.py:114
  10.3 2.0 %collective-permute-done.refs_10_ = bf16[144,512]{1,0:T(8,128)(2,1)S(1)} collective-permute-done((bf16[144,512]{1,0:T(8,128)(2,1)S(1)}, bf16[144,512]{1,0:T(8,128)(2,1)S(1)}, u32[]{:S(2)}, u32[]{:S(2)}) %collective-permute-start) | collective-permute-done | bytes 147488 | tf_op jit(solution)/shard_map/ppermute | solution.py:114
  12.3 0.0 collective-permute-start.5
  12.3 0.0 collective-permute-done.1.refs_3_
  12.3 2.2 %collective-permute-done.2.refs_2_ = bf16[144,512]{1,0:T(8,128)(2,1)S(1)} collective-permute-done((bf16[144,512]{1,0:T(8,128)(2,1)S(1)}, bf16[144,512]{1,0:T(8,128)(2,1)S(1)}, u32[]{:S(2)}, u32[]{:S(2)}) %collective-permute-start.2) | collective-permute-done | bytes 147488 | tf_op jit(solution)/shard_map/ppermute | solution.py:114
  14.6 0.1 collective-permute-done.3.refs_1_
  14.6 0.5 %collective-permute-done.4.refs_9_ = bf16[144,512]{1,0:T(8,128)(2,1)S(1)} collective-permute-done((bf16[144,512]{1,0:T(8,128)(2,1)S(1)}, bf16[144,512]{1,0:T(8,128)(2,1)S(1)}, u32[]{:S(2)}, u32[]{:S(2)}) %collective-permute-start.4) | collective-permute-done | bytes 147488 | tf_op jit(solution)/shard_map/ppermute | solution.py:114
  15.1 0.0 collective-permute-start.6
  15.2 0.5 %collective-permute-start.7 = (bf16[144,512]{1,0:T(8,128)(2,1)S(1)}, bf16[144,512]{1,0:T(8,128)(2,1)S(1)}, u32[]{:S(2)}, u32[]{:S(2)}) collective-permute-start(bf16[144,512]{1,0:T(8,128)(2,1)S(1)} %collective-permute-done.2.refs_2_), channel_id=1, source_target_pairs={{1,0},{0,1},{3,2},{2,3},{5,4},{4,5},{7,6},{6,7},{9,8},{8,9},{11,10... | collective-permute-start | bytes 442376 | tf_op jit(solution)/shard_map/ppermute | solution.py:114
  15.7 0.0 collective-permute-start.8
  15.7 1.1 %collective-permute-start.11 = (bf16[144,512]{1,0:T(8,128)(2,1)S(1)}, bf16[144,512]{1,0:T(8,128)(2,1)S(1)}, u32[]{:S(2)}, u32[]{:S(2)}) collective-permute-start(bf16[144,512]{1,0:T(8,128)(2,1)S(1)} %collective-permute-done.refs_10_), channel_id=1, source_target_pairs={{8,0},{9,1},{10,2},{11,3},{12,4},{13,5},{14,6},{15,7},{0,8},{1,9},... | collective-permute-start | bytes 442376 | tf_op jit(solution)/shard_map/ppermute | solution.py:114
  16.8 0.0 collective-permute-done.5.refs_4_
  16.8 0.0 collective-permute-done.6.refs_5_
  16.8 0.0 collective-permute-done.7.refs_6_
  16.8 0.3 collective-permute-done.8.refs_7_
  17.0 1.4 %shard_map.38 = (f32[1,128]{1,0:T(1,128)S(1)}, f32[1,128]{1,0:T(1,128)S(1)}, f32[1,128]{1,0:T(1,128)S(1)}) custom-call(bf16[64,64]{1,0:T(8,128)(2,1)S(1)} %get-tuple-element.15.table_ref, bf16[144,512]{1,0:T(8,128)(2,1)S(1)} %get-tuple-element.16.refs_0_.refs_8_, bf16[144,512]{1,0:T(8,128)(2,1)S(1)} %collective-permute-done.3.refs_1_, ...), custom_call_target="tpu_custom_call" | custom-call | flops 402653184 | bytes 1441792 | tf_op jit(solution)/shard_map/pallas_call | solution.py:89
  18.5 1.7 %collective-permute-start.10 = (f32[1,128]{1,0:T(1,128)S(1)}, f32[1,128]{1,0:T(1,128)S(1)}, u32[]{:S(2)}, u32[]{:S(2)}) collective-permute-start(f32[1,128]{1,0:T(1,128)S(1)} %get-tuple-element.24), channel_id=1, source_target_pairs={{16,0},{17,1},{18,2},{19,3},{20,4},{21,5},{22,6},{23,7},{24,8},{25... | collective-permute-start | bytes 1544 | tf_op jit(solution)/shard_map/ppermute | solution.py:114
  20.2 1.3 %collective-permute-start.9 = (f32[1,128]{1,0:T(1,128)S(1)}, f32[1,128]{1,0:T(1,128)S(1)}, u32[]{:S(2)}, u32[]{:S(2)}) collective-permute-start(f32[1,128]{1,0:T(1,128)S(1)} %get-tuple-element.23), channel_id=1, source_target_pairs={{8,0},{9,1},{10,2},{11,3},{12,4},{13,5},{14,6},{15,7},{0,8},{1,9},... | collective-permute-start | bytes 1544 | tf_op jit(solution)/shard_map/ppermute | solution.py:114
  21.6 0.4 %collective-permute-done.11.refs_8_ = bf16[144,512]{1,0:T(8,128)(2,1)S(1)} collective-permute-done((bf16[144,512]{1,0:T(8,128)(2,1)S(1)}, bf16[144,512]{1,0:T(8,128)(2,1)S(1)}, u32[]{:S(2)}, u32[]{:S(2)}) %collective-permute-start.11) | collective-permute-done | bytes 147488 | tf_op jit(solution)/shard_map/ppermute | solution.py:114
  21.9 0.6 %shard_map.39 = f32[1,128]{1,0:T(1,128)S(1)} custom-call(bf16[64,64]{1,0:T(8,128)(2,1)S(1)} %get-tuple-element.15.table_ref, bf16[144,512]{1,0:T(8,128)(2,1)S(1)} %get-tuple-element.16.refs_0_.refs_8_, bf16[144,512]{1,0:T(8,128)(2,1)S(1)} %collective-permute-done.3.refs_1_, bf16[144,512]{1,0:T(8,128)(2,1)S(1)} %collective-permute-done.2.refs_2_, ...), custom_call_target="tpu_custom_call" | custom-call | flops 134217728 | bytes 1179648 | tf_op jit(solution)/shard_map/pallas_call | solution.py:89
  22.6 2.5 %collective-permute-start.12 = (f32[1,128]{1,0:T(1,128)S(1)}, f32[1,128]{1,0:T(1,128)S(1)}, u32[]{:S(2)}, u32[]{:S(2)}) collective-permute-start(f32[1,128]{1,0:T(1,128)S(1)} %shard_map.39), channel_id=1, source_target_pairs={{24,0},{25,1},{26,2},{27,3},{28,4},{29,5},{30,6},{31,7},{16,8},{17... | collective-permute-start | bytes 1544 | tf_op jit(solution)/shard_map/ppermute | solution.py:114
  25.1 0.0 collective-permute-done.10
  25.1 0.0 collective-permute-done.9
  25.1 2.9 %collective-permute-done.12 = f32[1,128]{1,0:T(1,128)S(1)} collective-permute-done((f32[1,128]{1,0:T(1,128)S(1)}, f32[1,128]{1,0:T(1,128)S(1)}, u32[]{:S(2)}, u32[]{:S(2)}) %collective-permute-start.12) | collective-permute-done | bytes 544 | tf_op jit(solution)/shard_map/ppermute | solution.py:114
  28.0 0.5 %maximum_bitcast_fusion = f32[128]{0:T(128)} fusion(f32[1,128]{1,0:T(1,128)S(1)} %collective-permute-done.12, f32[1,128]{1,0:T(1,128)S(1)} %collective-permute-done.10, f32[1,128]{1,0:T(1,128)S(1)} %get-tuple-element.22, f32[1,128]{1,0:T(1,128)S(1)} %collective-permute-done.9), kind=kLoop, calls=%fused_computation | loop fusion | flops 384 | bytes 2560 | tf_op jit(solution)/shard_map/reshape | solution.py:156
Async XLA Ops:
  1.1 11.2 %collective-permute-start = (bf16[144,512]{1,0:T(8,128)(2,1)S(1)}, bf16[144,512]{1,0:T(8,128)(2,1)S(1)}, u32[]{:S(2)}, u32[]{:S(2)}) collective-permute-start(bf16[144,512]{1,0:T(8,128)(2,1)S(1)} %get-tuple-element.16.refs_0_.refs_8_), channel_id=1, source_target_pairs={{16,0},{17,1},{18,2},{19,3},{20,4},{21,5},{22,6},{23,7},{24,8},{25... | collective-permute-start | bytes 442376 | tf_op jit(solution)/shard_map/ppermute | solution.py:114
  5.2 7.1 %collective-permute-start.1 = (bf16[144,512]{1,0:T(8,128)(2,1)S(1)}, bf16[144,512]{1,0:T(8,128)(2,1)S(1)}, u32[]{:S(2)}, u32[]{:S(2)}) collective-permute-start(bf16[144,512]{1,0:T(8,128)(2,1)S(1)} %get-tuple-element.16.refs_0_.refs_8_), channel_id=1, source_target_pairs={{6,0},{7,1},{4,2},{5,3},{2,4},{3,5},{0,6},{1,7},{14,8},{15,9},{12,... | collective-permute-start | bytes 442376 | tf_op jit(solution)/shard_map/ppermute | solution.py:114
  7.7 6.9 %collective-permute-start.2 = (bf16[144,512]{1,0:T(8,128)(2,1)S(1)}, bf16[144,512]{1,0:T(8,128)(2,1)S(1)}, u32[]{:S(2)}, u32[]{:S(2)}) collective-permute-start(bf16[144,512]{1,0:T(8,128)(2,1)S(1)} %get-tuple-element.16.refs_0_.refs_8_), channel_id=1, source_target_pairs={{4,0},{5,1},{6,2},{7,3},{0,4},{1,5},{2,6},{3,7},{12,8},{13,9},{14,... | collective-permute-start | bytes 442376 | tf_op jit(solution)/shard_map/ppermute | solution.py:114
  8.2 6.5 %collective-permute-start.3 = (bf16[144,512]{1,0:T(8,128)(2,1)S(1)}, bf16[144,512]{1,0:T(8,128)(2,1)S(1)}, u32[]{:S(2)}, u32[]{:S(2)}) collective-permute-start(bf16[144,512]{1,0:T(8,128)(2,1)S(1)} %get-tuple-element.16.refs_0_.refs_8_), channel_id=1, source_target_pairs={{2,0},{3,1},{0,2},{1,3},{6,4},{7,5},{4,6},{5,7},{10,8},{11,9},{8,1... | collective-permute-start | bytes 442376 | tf_op jit(solution)/shard_map/ppermute | solution.py:114
  8.7 6.4 %collective-permute-start.4 = (bf16[144,512]{1,0:T(8,128)(2,1)S(1)}, bf16[144,512]{1,0:T(8,128)(2,1)S(1)}, u32[]{:S(2)}, u32[]{:S(2)}) collective-permute-start(bf16[144,512]{1,0:T(8,128)(2,1)S(1)} %get-tuple-element.16.refs_0_.refs_8_), channel_id=1, source_target_pairs={{8,0},{9,1},{10,2},{11,3},{12,4},{13,5},{14,6},{15,7},{0,8},{1,9},... | collective-permute-start | bytes 442376 | tf_op jit(solution)/shard_map/ppermute | solution.py:114
  12.3 4.4 %collective-permute-start.5 = (bf16[144,512]{1,0:T(8,128)(2,1)S(1)}, bf16[144,512]{1,0:T(8,128)(2,1)S(1)}, u32[]{:S(2)}, u32[]{:S(2)}) collective-permute-start(bf16[144,512]{1,0:T(8,128)(2,1)S(1)} %get-tuple-element.16.refs_0_.refs_8_), channel_id=1, source_target_pairs={{1,0},{0,1},{3,2},{2,3},{5,4},{4,5},{7,6},{6,7},{9,8},{8,9},{11,10... | collective-permute-start | bytes 442376 | tf_op jit(solution)/shard_map/ppermute | solution.py:114
  15.1 1.6 %collective-permute-start.6 = (bf16[144,512]{1,0:T(8,128)(2,1)S(1)}, bf16[144,512]{1,0:T(8,128)(2,1)S(1)}, u32[]{:S(2)}, u32[]{:S(2)}) collective-permute-start(bf16[144,512]{1,0:T(8,128)(2,1)S(1)} %collective-permute-done.3.refs_1_), channel_id=1, source_target_pairs={{1,0},{0,1},{3,2},{2,3},{5,4},{4,5},{7,6},{6,7},{9,8},{8,9},{11,10... | collective-permute-start | bytes 442376 | tf_op jit(solution)/shard_map/ppermute | solution.py:114
  15.2 1.6 %collective-permute-start.7 = (bf16[144,512]{1,0:T(8,128)(2,1)S(1)}, bf16[144,512]{1,0:T(8,128)(2,1)S(1)}, u32[]{:S(2)}, u32[]{:S(2)}) collective-permute-start(bf16[144,512]{1,0:T(8,128)(2,1)S(1)} %collective-permute-done.2.refs_2_), channel_id=1, source_target_pairs={{1,0},{0,1},{3,2},{2,3},{5,4},{4,5},{7,6},{6,7},{9,8},{8,9},{11,10... | collective-permute-start | bytes 442376 | tf_op jit(solution)/shard_map/ppermute | solution.py:114
  15.7 1.4 %collective-permute-start.8 = (bf16[144,512]{1,0:T(8,128)(2,1)S(1)}, bf16[144,512]{1,0:T(8,128)(2,1)S(1)}, u32[]{:S(2)}, u32[]{:S(2)}) collective-permute-start(bf16[144,512]{1,0:T(8,128)(2,1)S(1)} %collective-permute-done.1.refs_3_), channel_id=1, source_target_pairs={{1,0},{0,1},{3,2},{2,3},{5,4},{4,5},{7,6},{6,7},{9,8},{8,9},{11,10... | collective-permute-start | bytes 442376 | tf_op jit(solution)/shard_map/ppermute | solution.py:114
  15.7 6.3 %collective-permute-start.11 = (bf16[144,512]{1,0:T(8,128)(2,1)S(1)}, bf16[144,512]{1,0:T(8,128)(2,1)S(1)}, u32[]{:S(2)}, u32[]{:S(2)}) collective-permute-start(bf16[144,512]{1,0:T(8,128)(2,1)S(1)} %collective-permute-done.refs_10_), channel_id=1, source_target_pairs={{8,0},{9,1},{10,2},{11,3},{12,4},{13,5},{14,6},{15,7},{0,8},{1,9},... | collective-permute-start | bytes 442376 | tf_op jit(solution)/shard_map/ppermute | solution.py:114
  18.5 6.6 %collective-permute-start.10 = (f32[1,128]{1,0:T(1,128)S(1)}, f32[1,128]{1,0:T(1,128)S(1)}, u32[]{:S(2)}, u32[]{:S(2)}) collective-permute-start(f32[1,128]{1,0:T(1,128)S(1)} %get-tuple-element.24), channel_id=1, source_target_pairs={{16,0},{17,1},{18,2},{19,3},{20,4},{21,5},{22,6},{23,7},{24,8},{25... | collective-permute-start | bytes 1544 | tf_op jit(solution)/shard_map/ppermute | solution.py:114
  20.2 4.9 %collective-permute-start.9 = (f32[1,128]{1,0:T(1,128)S(1)}, f32[1,128]{1,0:T(1,128)S(1)}, u32[]{:S(2)}, u32[]{:S(2)}) collective-permute-start(f32[1,128]{1,0:T(1,128)S(1)} %get-tuple-element.23), channel_id=1, source_target_pairs={{8,0},{9,1},{10,2},{11,3},{12,4},{13,5},{14,6},{15,7},{0,8},{1,9},... | collective-permute-start | bytes 1544 | tf_op jit(solution)/shard_map/ppermute | solution.py:114
  22.6 5.4 %collective-permute-start.12 = (f32[1,128]{1,0:T(1,128)S(1)}, f32[1,128]{1,0:T(1,128)S(1)}, u32[]{:S(2)}, u32[]{:S(2)}) collective-permute-start(f32[1,128]{1,0:T(1,128)S(1)} %shard_map.39), channel_id=1, source_target_pairs={{24,0},{25,1},{26,2},{27,3},{28,4},{29,5},{30,6},{31,7},{16,8},{17... | collective-permute-start | bytes 1544 | tf_op jit(solution)/shard_map/ppermute | solution.py:114

commit v13 on v11

--- a/solution.py
+++ b/solution.py
@@ -131,10 +131,8 @@
             return permute(x, lambda z, a, g: (turned(z, s, length), a, g))
 
         half = length // 2 if length & (length - 1) == 0 else length
-        first = [along(own, s) for s in reversed(range(1, min(half + 1, length)))]
-        near = [permute(own, lambda z, a, g: (z, turned(a, s, wide), g)) for s in reversed(range(1, wide))]
-        first, near = lax.optimization_barrier((first, near))
-        first, near = first[::-1], near[::-1]
+        near = [permute(own, lambda z, a, g: (z, turned(a, s, wide), g)) for s in range(1, wide)]
+        first = [along(own, s) for s in range(1, min(half + 1, length))]
         last = [along(first[half - 1], s) for s in range(1, length - half)]
         far, far_rank = [], []
         for t in range(1, n_grp):
@@ -147,9 +145,7 @@
         visit_rank = [rank(z=s) for s in range(1, length)]
         first = list(zip(first, visit_rank))
         last = list(zip(last, visit_rank[len(first) :]))
-        best = best_of(near + far, near[:1] + first, table, True)
-        if last:
-            best = best + best_of(near + far, last, table, False)
+        best = best_of(near + far, near[:1] + first + last, table, True)
         found = [best[0]] + [along(best[s], -s) for s in range(1, length)]
         return functools.reduce(jnp.maximum, found).reshape(rows)
 

time: 29.4 us -> 30.5 us (1.037)
  starting transfers between devices: 12.3 us -> 15.6 us
  waiting for transfers between devices: 13.3 us -> 11.3 us
    ppermute x13, starting transfers between devices: 12.3 us -> 15.6 us  [permute(): return lax.ppermute(x, ('clu', 'grp'), pairs)]
    ppermute x13, waiting for transfers between devices: 13.3 us -> 11.3 us  [permute(): return lax.ppermute(x, ('clu', 'grp'), pairs)]
    pallas_call x2 -> x1, Pallas kernels: 2.06 us -> 1.8 us  [best_of(): pl.pallas_call(functools.partial(best_kernel, len(keys), own, ranks), out...]
  transfers between devices with their start and end apart: 13 -> 13, of which waited for: 10 -> 7; matrix products, arithmetic and copies ran while one was open for 0% -> 0% of each run, Pallas kernels for 7% -> 0%
where the time goes in v13:
time: 30.5 us; the launch traced here: 30.3 us
  starting transfers between devices  15.6 us (51%)
  waiting for transfers between devices  11.3 us (37%)
  Pallas kernels  2.9 us (10%)
  other arithmetic  0.52 us (2%)
    ppermute x13, starting transfers between devices, permute(): return lax.ppermute(x, ('clu', 'grp'), pairs)  15.6 us
    ppermute x13, waiting for transfers between devices, permute(): return lax.ppermute(x, ('clu', 'grp'), pairs)  11.3 us
    pallas_call x1, Pallas kernels, best_of(): pl.pallas_call(functools.partial(best_kernel, len(keys), own, ranks), out...  1.8 us
    pallas_call x1, Pallas kernels, pack(): pl.pallas_call(functools.partial(pack_kernel, groups), out_shape=[pltpu.V...  1.1 us
  transfers between devices with their start and end apart: 13, of which 7 were waited for; matrix products, arithmetic and copies ran while one was open for 0% of the time, Pallas kernels for 0%

profile of v13, /device:TPU:0, one launch (start us, length us, event | category | flops | bytes accessed | tf_op | source)
XLA Modules:
  0.0 30.3 jit_solution(3157164158788337412)
XLA Ops:
  0.0 1.1 %shard_map.37 = (bf16[144,512]{1,0:T(8,128)(2,1)S(1)}, bf16[64,64]{1,0:T(8,128)(2,1)S(1)}) custom-call(bf16[128,512]{1,0:T(8,128)(2,1)} %emb_ref.1, s32[1,128]{1,0:T(1,128)} %bitcast.4, s32[1,64]{1,0:T(1,128)} %bitcast.5), custom_call_target="tpu_custom_call" | custom-call | tf_op jit(solution)/shard_map/pallas_call | solution.py:38
  1.1 4.1 %collective-permute-start.8 = (bf16[144,512]{1,0:T(8,128)(2,1)S(1)}, bf16[144,512]{1,0:T(8,128)(2,1)S(1)}, u32[]{:S(2)}, u32[]{:S(2)}) collective-permute-start(bf16[144,512]{1,0:T(8,128)(2,1)S(1)} %get-tuple-element.12.refs_0_.refs_8_), channel_id=1, source_target_pairs={{16,0},{17,1},{18,2},{19,3},{20,4},{21,5},{22,6},{23,7},{24,8},{25... | collective-permute-start | bytes 442376 | tf_op jit(solution)/shard_map/ppermute | solution.py:114
  5.2 1.6 %collective-permute-start.7 = (bf16[144,512]{1,0:T(8,128)(2,1)S(1)}, bf16[144,512]{1,0:T(8,128)(2,1)S(1)}, u32[]{:S(2)}, u32[]{:S(2)}) collective-permute-start(bf16[144,512]{1,0:T(8,128)(2,1)S(1)} %get-tuple-element.12.refs_0_.refs_8_), channel_id=1, source_target_pairs={{8,0},{9,1},{10,2},{11,3},{12,4},{13,5},{14,6},{15,7},{0,8},{1,9},... | collective-permute-start | bytes 442376 | tf_op jit(solution)/shard_map/ppermute | solution.py:114
  6.8 2.4 %collective-permute-start.2 = (bf16[144,512]{1,0:T(8,128)(2,1)S(1)}, bf16[144,512]{1,0:T(8,128)(2,1)S(1)}, u32[]{:S(2)}, u32[]{:S(2)}) collective-permute-start(bf16[144,512]{1,0:T(8,128)(2,1)S(1)} %get-tuple-element.12.refs_0_.refs_8_), channel_id=1, source_target_pairs={{6,0},{7,1},{4,2},{5,3},{2,4},{3,5},{0,6},{1,7},{14,8},{15,9},{12,... | collective-permute-start | bytes 442376 | tf_op jit(solution)/shard_map/ppermute | solution.py:114
  9.2 0.5 %collective-permute-start.1 = (bf16[144,512]{1,0:T(8,128)(2,1)S(1)}, bf16[144,512]{1,0:T(8,128)(2,1)S(1)}, u32[]{:S(2)}, u32[]{:S(2)}) collective-permute-start(bf16[144,512]{1,0:T(8,128)(2,1)S(1)} %get-tuple-element.12.refs_0_.refs_8_), channel_id=1, source_target_pairs={{4,0},{5,1},{6,2},{7,3},{0,4},{1,5},{2,6},{3,7},{12,8},{13,9},{14,... | collective-permute-start | bytes 442376 | tf_op jit(solution)/shard_map/ppermute | solution.py:114
  9.7 0.5 %collective-permute-start = (bf16[144,512]{1,0:T(8,128)(2,1)S(1)}, bf16[144,512]{1,0:T(8,128)(2,1)S(1)}, u32[]{:S(2)}, u32[]{:S(2)}) collective-permute-start(bf16[144,512]{1,0:T(8,128)(2,1)S(1)} %get-tuple-element.12.refs_0_.refs_8_), channel_id=1, source_target_pairs={{2,0},{3,1},{0,2},{1,3},{6,4},{7,5},{4,6},{5,7},{10,8},{11,9},{8,1... | collective-permute-start | bytes 442376 | tf_op jit(solution)/shard_map/ppermute | solution.py:114
  10.3 2.0 %collective-permute-done.8.refs_10_ = bf16[144,512]{1,0:T(8,128)(2,1)S(1)} collective-permute-done((bf16[144,512]{1,0:T(8,128)(2,1)S(1)}, bf16[144,512]{1,0:T(8,128)(2,1)S(1)}, u32[]{:S(2)}, u32[]{:S(2)}) %collective-permute-start.8) | collective-permute-done | bytes 147488 | tf_op jit(solution)/shard_map/ppermute | solution.py:114
  12.3 0.0 collective-permute-start.3
  12.3 0.2 collective-permute-done.7.refs_9_
  12.5 1.5 %collective-permute-start.9 = (bf16[144,512]{1,0:T(8,128)(2,1)S(1)}, bf16[144,512]{1,0:T(8,128)(2,1)S(1)}, u32[]{:S(2)}, u32[]{:S(2)}) collective-permute-start(bf16[144,512]{1,0:T(8,128)(2,1)S(1)} %collective-permute-done.8.refs_10_), channel_id=1, source_target_pairs={{8,0},{9,1},{10,2},{11,3},{12,4},{13,5},{14,6},{15,7},{0,8},{1,9},... | collective-permute-start | bytes 442376 | tf_op jit(solution)/shard_map/ppermute | solution.py:114
  14.0 0.0 collective-permute-done.2.refs_3_
  14.0 0.0 collective-permute-start.6
  14.0 1.9 %collective-permute-done.1.refs_2_ = bf16[144,512]{1,0:T(8,128)(2,1)S(1)} collective-permute-done((bf16[144,512]{1,0:T(8,128)(2,1)S(1)}, bf16[144,512]{1,0:T(8,128)(2,1)S(1)}, u32[]{:S(2)}, u32[]{:S(2)}) %collective-permute-start.1) | collective-permute-done | bytes 147488 | tf_op jit(solution)/shard_map/ppermute | solution.py:114
  15.9 0.0 collective-permute-start.5
  15.9 0.1 collective-permute-done.refs_1_
  15.9 0.5 %collective-permute-start.4 = (bf16[144,512]{1,0:T(8,128)(2,1)S(1)}, bf16[144,512]{1,0:T(8,128)(2,1)S(1)}, u32[]{:S(2)}, u32[]{:S(2)}) collective-permute-start(bf16[144,512]{1,0:T(8,128)(2,1)S(1)} %collective-permute-done.refs_1_), channel_id=1, source_target_pairs={{1,0},{0,1},{3,2},{2,3},{5,4},{4,5},{7,6},{6,7},{9,8},{8,9},{11,10... | collective-permute-start | bytes 442376 | tf_op jit(solution)/shard_map/ppermute | solution.py:114
  16.4 0.0 collective-permute-done.3.refs_4_
  16.4 2.2 %collective-permute-done.9.refs_11_ = bf16[144,512]{1,0:T(8,128)(2,1)S(1)} collective-permute-done((bf16[144,512]{1,0:T(8,128)(2,1)S(1)}, bf16[144,512]{1,0:T(8,128)(2,1)S(1)}, u32[]{:S(2)}, u32[]{:S(2)}) %collective-permute-start.9) | collective-permute-done | bytes 147488 | tf_op jit(solution)/shard_map/ppermute | solution.py:114
  18.6 0.0 collective-permute-done.6.refs_7_
  18.6 0.0 collective-permute-done.5.refs_6_
  18.6 0.0 collective-permute-done.4.refs_5_
  18.6 1.8 %shard_map.38 = (f32[1,128]{1,0:T(1,128)S(1)}, f32[1,128]{1,0:T(1,128)S(1)}, f32[1,128]{1,0:T(1,128)S(1)}, f32[1,128]{1,0:T(1,128)S(1)}) custom-call(bf16[64,64]{1,0:T(8,128)(2,1)S(1)} %get-tuple-element.11.table_ref, bf16[144,512]{1,0:T(8,128)(2,1)S(1)} %get-tuple-element.12.refs_0_.refs_8_, bf16[144,512]{1,0:T(8,128)(2,1)S(1)} %collective-permute-done.refs_1_, ...), custom_call_target="tpu_custom_call" | custom-call | flops 536870912 | bytes 1572864 | tf_op jit(solution)/shard_map/pallas_call | solution.py:89
  20.4 0.7 %collective-permute-start.10 = (f32[1,128]{1,0:T(1,128)S(1)}, f32[1,128]{1,0:T(1,128)S(1)}, u32[]{:S(2)}, u32[]{:S(2)}) collective-permute-start(f32[1,128]{1,0:T(1,128)S(1)} %get-tuple-element.14), channel_id=1, source_target_pairs={{8,0},{9,1},{10,2},{11,3},{12,4},{13,5},{14,6},{15,7},{0,8},{1,9},... | collective-permute-start | bytes 1544 | tf_op jit(solution)/shard_map/ppermute | solution.py:114
  21.1 3.4 %collective-permute-start.11 = (f32[1,128]{1,0:T(1,128)S(1)}, f32[1,128]{1,0:T(1,128)S(1)}, u32[]{:S(2)}, u32[]{:S(2)}) collective-permute-start(f32[1,128]{1,0:T(1,128)S(1)} %get-tuple-element.15), channel_id=1, source_target_pairs={{16,0},{17,1},{18,2},{19,3},{20,4},{21,5},{22,6},{23,7},{24,8},{25... | collective-permute-start | bytes 1544 | tf_op jit(solution)/shard_map/ppermute | solution.py:114
  24.5 0.4 %collective-permute-start.12 = (f32[1,128]{1,0:T(1,128)S(1)}, f32[1,128]{1,0:T(1,128)S(1)}, u32[]{:S(2)}, u32[]{:S(2)}) collective-permute-start(f32[1,128]{1,0:T(1,128)S(1)} %get-tuple-element.16), channel_id=1, source_target_pairs={{24,0},{25,1},{26,2},{27,3},{28,4},{29,5},{30,6},{31,7},{16,8},{17... | collective-permute-start | bytes 1544 | tf_op jit(solution)/shard_map/ppermute | solution.py:114
  24.9 0.0 collective-permute-done.10
  24.9 1.1 %collective-permute-done.11 = f32[1,128]{1,0:T(1,128)S(1)} collective-permute-done((f32[1,128]{1,0:T(1,128)S(1)}, f32[1,128]{1,0:T(1,128)S(1)}, u32[]{:S(2)}, u32[]{:S(2)}) %collective-permute-start.11) | collective-permute-done | bytes 544 | tf_op jit(solution)/shard_map/ppermute | solution.py:114
  26.0 3.8 %collective-permute-done.12 = f32[1,128]{1,0:T(1,128)S(1)} collective-permute-done((f32[1,128]{1,0:T(1,128)S(1)}, f32[1,128]{1,0:T(1,128)S(1)}, u32[]{:S(2)}, u32[]{:S(2)}) %collective-permute-start.12) | collective-permute-done | bytes 544 | tf_op jit(solution)/shard_map/ppermute | solution.py:114
  29.8 0.5 %maximum_bitcast_fusion = f32[128]{0:T(128)} fusion(f32[1,128]{1,0:T(1,128)S(1)} %collective-permute-done.12, f32[1,128]{1,0:T(1,128)S(1)} %collective-permute-done.11, f32[1,128]{1,0:T(1,128)S(1)} %get-tuple-element.13, f32[1,128]{1,0:T(1,128)S(1)} %collective-permute-done.10), kind=kLoop, calls=%fused_computation | loop fusion | flops 384 | bytes 2560 | tf_op jit(solution)/shard_map/reshape | solution.py:150
Async XLA Ops:
  1.1 11.2 %collective-permute-start.8 = (bf16[144,512]{1,0:T(8,128)(2,1)S(1)}, bf16[144,512]{1,0:T(8,128)(2,1)S(1)}, u32[]{:S(2)}, u32[]{:S(2)}) collective-permute-start(bf16[144,512]{1,0:T(8,128)(2,1)S(1)} %get-tuple-element.12.refs_0_.refs_8_), channel_id=1, source_target_pairs={{16,0},{17,1},{18,2},{19,3},{20,4},{21,5},{22,6},{23,7},{24,8},{25... | collective-permute-start | bytes 442376 | tf_op jit(solution)/shard_map/ppermute | solution.py:114
  5.2 7.3 %collective-permute-start.7 = (bf16[144,512]{1,0:T(8,128)(2,1)S(1)}, bf16[144,512]{1,0:T(8,128)(2,1)S(1)}, u32[]{:S(2)}, u32[]{:S(2)}) collective-permute-start(bf16[144,512]{1,0:T(8,128)(2,1)S(1)} %get-tuple-element.12.refs_0_.refs_8_), channel_id=1, source_target_pairs={{8,0},{9,1},{10,2},{11,3},{12,4},{13,5},{14,6},{15,7},{0,8},{1,9},... | collective-permute-start | bytes 442376 | tf_op jit(solution)/shard_map/ppermute | solution.py:114
  6.8 7.2 %collective-permute-start.2 = (bf16[144,512]{1,0:T(8,128)(2,1)S(1)}, bf16[144,512]{1,0:T(8,128)(2,1)S(1)}, u32[]{:S(2)}, u32[]{:S(2)}) collective-permute-start(bf16[144,512]{1,0:T(8,128)(2,1)S(1)} %get-tuple-element.12.refs_0_.refs_8_), channel_id=1, source_target_pairs={{6,0},{7,1},{4,2},{5,3},{2,4},{3,5},{0,6},{1,7},{14,8},{15,9},{12,... | collective-permute-start | bytes 442376 | tf_op jit(solution)/shard_map/ppermute | solution.py:114
  9.2 6.6 %collective-permute-start.1 = (bf16[144,512]{1,0:T(8,128)(2,1)S(1)}, bf16[144,512]{1,0:T(8,128)(2,1)S(1)}, u32[]{:S(2)}, u32[]{:S(2)}) collective-permute-start(bf16[144,512]{1,0:T(8,128)(2,1)S(1)} %get-tuple-element.12.refs_0_.refs_8_), channel_id=1, source_target_pairs={{4,0},{5,1},{6,2},{7,3},{0,4},{1,5},{2,6},{3,7},{12,8},{13,9},{14,... | collective-permute-start | bytes 442376 | tf_op jit(solution)/shard_map/ppermute | solution.py:114
  9.7 6.2 %collective-permute-start = (bf16[144,512]{1,0:T(8,128)(2,1)S(1)}, bf16[144,512]{1,0:T(8,128)(2,1)S(1)}, u32[]{:S(2)}, u32[]{:S(2)}) collective-permute-start(bf16[144,512]{1,0:T(8,128)(2,1)S(1)} %get-tuple-element.12.refs_0_.refs_8_), channel_id=1, source_target_pairs={{2,0},{3,1},{0,2},{1,3},{6,4},{7,5},{4,6},{5,7},{10,8},{11,9},{8,1... | collective-permute-start | bytes 442376 | tf_op jit(solution)/shard_map/ppermute | solution.py:114
  12.3 4.1 %collective-permute-start.3 = (bf16[144,512]{1,0:T(8,128)(2,1)S(1)}, bf16[144,512]{1,0:T(8,128)(2,1)S(1)}, u32[]{:S(2)}, u32[]{:S(2)}) collective-permute-start(bf16[144,512]{1,0:T(8,128)(2,1)S(1)} %get-tuple-element.12.refs_0_.refs_8_), channel_id=1, source_target_pairs={{1,0},{0,1},{3,2},{2,3},{5,4},{4,5},{7,6},{6,7},{9,8},{8,9},{11,10... | collective-permute-start | bytes 442376 | tf_op jit(solution)/shard_map/ppermute | solution.py:114
  12.5 6.1 %collective-permute-start.9 = (bf16[144,512]{1,0:T(8,128)(2,1)S(1)}, bf16[144,512]{1,0:T(8,128)(2,1)S(1)}, u32[]{:S(2)}, u32[]{:S(2)}) collective-permute-start(bf16[144,512]{1,0:T(8,128)(2,1)S(1)} %collective-permute-done.8.refs_10_), channel_id=1, source_target_pairs={{8,0},{9,1},{10,2},{11,3},{12,4},{13,5},{14,6},{15,7},{0,8},{1,9},... | collective-permute-start | bytes 442376 | tf_op jit(solution)/shard_map/ppermute | solution.py:114
  14.0 4.6 %collective-permute-start.6 = (bf16[144,512]{1,0:T(8,128)(2,1)S(1)}, bf16[144,512]{1,0:T(8,128)(2,1)S(1)}, u32[]{:S(2)}, u32[]{:S(2)}) collective-permute-start(bf16[144,512]{1,0:T(8,128)(2,1)S(1)} %collective-permute-done.2.refs_3_), channel_id=1, source_target_pairs={{1,0},{0,1},{3,2},{2,3},{5,4},{4,5},{7,6},{6,7},{9,8},{8,9},{11,10... | collective-permute-start | bytes 442376 | tf_op jit(solution)/shard_map/ppermute | solution.py:114
  15.9 2.7 %collective-permute-start.5 = (bf16[144,512]{1,0:T(8,128)(2,1)S(1)}, bf16[144,512]{1,0:T(8,128)(2,1)S(1)}, u32[]{:S(2)}, u32[]{:S(2)}) collective-permute-start(bf16[144,512]{1,0:T(8,128)(2,1)S(1)} %collective-permute-done.1.refs_2_), channel_id=1, source_target_pairs={{1,0},{0,1},{3,2},{2,3},{5,4},{4,5},{7,6},{6,7},{9,8},{8,9},{11,10... | collective-permute-start | bytes 442376 | tf_op jit(solution)/shard_map/ppermute | solution.py:114
  15.9 2.7 %collective-permute-start.4 = (bf16[144,512]{1,0:T(8,128)(2,1)S(1)}, bf16[144,512]{1,0:T(8,128)(2,1)S(1)}, u32[]{:S(2)}, u32[]{:S(2)}) collective-permute-start(bf16[144,512]{1,0:T(8,128)(2,1)S(1)} %collective-permute-done.refs_1_), channel_id=1, source_target_pairs={{1,0},{0,1},{3,2},{2,3},{5,4},{4,5},{7,6},{6,7},{9,8},{8,9},{11,10... | collective-permute-start | bytes 442376 | tf_op jit(solution)/shard_map/ppermute | solution.py:114
  20.4 4.5 %collective-permute-start.10 = (f32[1,128]{1,0:T(1,128)S(1)}, f32[1,128]{1,0:T(1,128)S(1)}, u32[]{:S(2)}, u32[]{:S(2)}) collective-permute-start(f32[1,128]{1,0:T(1,128)S(1)} %get-tuple-element.14), channel_id=1, source_target_pairs={{8,0},{9,1},{10,2},{11,3},{12,4},{13,5},{14,6},{15,7},{0,8},{1,9},... | collective-permute-start | bytes 1544 | tf_op jit(solution)/shard_map/ppermute | solution.py:114
  21.1 4.9 %collective-permute-start.11 = (f32[1,128]{1,0:T(1,128)S(1)}, f32[1,128]{1,0:T(1,128)S(1)}, u32[]{:S(2)}, u32[]{:S(2)}) collective-permute-start(f32[1,128]{1,0:T(1,128)S(1)} %get-tuple-element.15), channel_id=1, source_target_pairs={{16,0},{17,1},{18,2},{19,3},{20,4},{21,5},{22,6},{23,7},{24,8},{25... | collective-permute-start | bytes 1544 | tf_op jit(solution)/shard_map/ppermute | solution.py:114
  24.5 5.3 %collective-permute-start.12 = (f32[1,128]{1,0:T(1,128)S(1)}, f32[1,128]{1,0:T(1,128)S(1)}, u32[]{:S(2)}, u32[]{:S(2)}) collective-permute-start(f32[1,128]{1,0:T(1,128)S(1)} %get-tuple-element.16), channel_id=1, source_target_pairs={{24,0},{25,1},{26,2},{27,3},{28,4},{29,5},{30,6},{31,7},{16,8},{17... | collective-permute-start | bytes 1544 | tf_op jit(solution)/shard_map/ppermute | solution.py:114

commit v14 on v13

--- a/solution.py
+++ b/solution.py
@@ -146,7 +146,7 @@
         first = list(zip(first, visit_rank))
         last = list(zip(last, visit_rank[len(first) :]))
         best = best_of(near + far, near[:1] + first + last, table, True)
-        found = [best[0]] + [along(best[s], -s) for s in range(1, length)]
+        found = [along(best[s], -s) for s in reversed(range(1, length))] + [best[0]]
         return functools.reduce(jnp.maximum, found).reshape(rows)
 
     placed = (P(("clu", "grp"), None), P(("clu", "grp")), P())

time: 30.5 us -> 29 us (0.951)
  waiting for transfers between devices: 11.3 us -> 9.86 us
    ppermute x13, waiting for transfers between devices: 11.3 us -> 9.86 us  [permute(): return lax.ppermute(x, ('clu', 'grp'), pairs)]
where the time goes in v14:
time: 29 us; the launch traced here: 28.9 us
  starting transfers between devices  15.6 us (54%)
  waiting for transfers between devices  9.86 us (34%)
  Pallas kernels  2.9 us (10%)
  other arithmetic  0.52 us (2%)
    ppermute x13, starting transfers between devices, permute(): return lax.ppermute(x, ('clu', 'grp'), pairs)  15.6 us
    ppermute x13, waiting for transfers between devices, permute(): return lax.ppermute(x, ('clu', 'grp'), pairs)  9.86 us
    pallas_call x1, Pallas kernels, best_of(): pl.pallas_call(functools.partial(best_kernel, len(keys), own, ranks), out...  1.8 us
    pallas_call x1, Pallas kernels, pack(): pl.pallas_call(functools.partial(pack_kernel, groups), out_shape=[pltpu.V...  1.1 us
  transfers between devices with their start and end apart: 13, of which 7 were waited for; matrix products, arithmetic and copies ran while one was open for 0% of the time, Pallas kernels for 0%

profile of v14, /device:TPU:0, one launch (start us, length us, event | category | flops | bytes accessed | tf_op | source)
XLA Modules:
  0.0 28.9 jit_solution(13452057815227560076)
XLA Ops:
  0.0 1.1 %shard_map.37 = (bf16[144,512]{1,0:T(8,128)(2,1)S(1)}, bf16[64,64]{1,0:T(8,128)(2,1)S(1)}) custom-call(bf16[128,512]{1,0:T(8,128)(2,1)} %emb_ref.1, s32[1,128]{1,0:T(1,128)} %bitcast.4, s32[1,64]{1,0:T(1,128)} %bitcast.5), custom_call_target="tpu_custom_call" | custom-call | tf_op jit(solution)/shard_map/pallas_call | solution.py:38
  1.1 4.1 %collective-permute-start.8 = (bf16[144,512]{1,0:T(8,128)(2,1)S(1)}, bf16[144,512]{1,0:T(8,128)(2,1)S(1)}, u32[]{:S(2)}, u32[]{:S(2)}) collective-permute-start(bf16[144,512]{1,0:T(8,128)(2,1)S(1)} %get-tuple-element.12.refs_0_.refs_8_), channel_id=1, source_target_pairs={{16,0},{17,1},{18,2},{19,3},{20,4},{21,5},{22,6},{23,7},{24,8},{25... | collective-permute-start | bytes 442376 | tf_op jit(solution)/shard_map/ppermute | solution.py:114
  5.2 1.6 %collective-permute-start.7 = (bf16[144,512]{1,0:T(8,128)(2,1)S(1)}, bf16[144,512]{1,0:T(8,128)(2,1)S(1)}, u32[]{:S(2)}, u32[]{:S(2)}) collective-permute-start(bf16[144,512]{1,0:T(8,128)(2,1)S(1)} %get-tuple-element.12.refs_0_.refs_8_), channel_id=1, source_target_pairs={{8,0},{9,1},{10,2},{11,3},{12,4},{13,5},{14,6},{15,7},{0,8},{1,9},... | collective-permute-start | bytes 442376 | tf_op jit(solution)/shard_map/ppermute | solution.py:114
  6.8 2.4 %collective-permute-start.2 = (bf16[144,512]{1,0:T(8,128)(2,1)S(1)}, bf16[144,512]{1,0:T(8,128)(2,1)S(1)}, u32[]{:S(2)}, u32[]{:S(2)}) collective-permute-start(bf16[144,512]{1,0:T(8,128)(2,1)S(1)} %get-tuple-element.12.refs_0_.refs_8_), channel_id=1, source_target_pairs={{6,0},{7,1},{4,2},{5,3},{2,4},{3,5},{0,6},{1,7},{14,8},{15,9},{12,... | collective-permute-start | bytes 442376 | tf_op jit(solution)/shard_map/ppermute | solution.py:114
  9.2 0.5 %collective-permute-start.1 = (bf16[144,512]{1,0:T(8,128)(2,1)S(1)}, bf16[144,512]{1,0:T(8,128)(2,1)S(1)}, u32[]{:S(2)}, u32[]{:S(2)}) collective-permute-start(bf16[144,512]{1,0:T(8,128)(2,1)S(1)} %get-tuple-element.12.refs_0_.refs_8_), channel_id=1, source_target_pairs={{4,0},{5,1},{6,2},{7,3},{0,4},{1,5},{2,6},{3,7},{12,8},{13,9},{14,... | collective-permute-start | bytes 442376 | tf_op jit(solution)/shard_map/ppermute | solution.py:114
  9.7 0.5 %collective-permute-start = (bf16[144,512]{1,0:T(8,128)(2,1)S(1)}, bf16[144,512]{1,0:T(8,128)(2,1)S(1)}, u32[]{:S(2)}, u32[]{:S(2)}) collective-permute-start(bf16[144,512]{1,0:T(8,128)(2,1)S(1)} %get-tuple-element.12.refs_0_.refs_8_), channel_id=1, source_target_pairs={{2,0},{3,1},{0,2},{1,3},{6,4},{7,5},{4,6},{5,7},{10,8},{11,9},{8,1... | collective-permute-start | bytes 442376 | tf_op jit(solution)/shard_map/ppermute | solution.py:114
  10.3 2.0 %collective-permute-done.8.refs_10_ = bf16[144,512]{1,0:T(8,128)(2,1)S(1)} collective-permute-done((bf16[144,512]{1,0:T(8,128)(2,1)S(1)}, bf16[144,512]{1,0:T(8,128)(2,1)S(1)}, u32[]{:S(2)}, u32[]{:S(2)}) %collective-permute-start.8) | collective-permute-done | bytes 147488 | tf_op jit(solution)/shard_map/ppermute | solution.py:114
  12.3 0.0 collective-permute-start.3
  12.3 0.2 collective-permute-done.7.refs_9_
  12.5 1.5 %collective-permute-start.9 = (bf16[144,512]{1,0:T(8,128)(2,1)S(1)}, bf16[144,512]{1,0:T(8,128)(2,1)S(1)}, u32[]{:S(2)}, u32[]{:S(2)}) collective-permute-start(bf16[144,512]{1,0:T(8,128)(2,1)S(1)} %collective-permute-done.8.refs_10_), channel_id=1, source_target_pairs={{8,0},{9,1},{10,2},{11,3},{12,4},{13,5},{14,6},{15,7},{0,8},{1,9},... | collective-permute-start | bytes 442376 | tf_op jit(solution)/shard_map/ppermute | solution.py:114
  14.0 0.0 collective-permute-done.2.refs_3_
  14.0 0.0 collective-permute-start.6
  14.0 1.9 %collective-permute-done.1.refs_2_ = bf16[144,512]{1,0:T(8,128)(2,1)S(1)} collective-permute-done((bf16[144,512]{1,0:T(8,128)(2,1)S(1)}, bf16[144,512]{1,0:T(8,128)(2,1)S(1)}, u32[]{:S(2)}, u32[]{:S(2)}) %collective-permute-start.1) | collective-permute-done | bytes 147488 | tf_op jit(solution)/shard_map/ppermute | solution.py:114
  15.9 0.0 collective-permute-start.5
  15.9 0.1 collective-permute-done.refs_1_
  15.9 0.5 %collective-permute-start.4 = (bf16[144,512]{1,0:T(8,128)(2,1)S(1)}, bf16[144,512]{1,0:T(8,128)(2,1)S(1)}, u32[]{:S(2)}, u32[]{:S(2)}) collective-permute-start(bf16[144,512]{1,0:T(8,128)(2,1)S(1)} %collective-permute-done.refs_1_), channel_id=1, source_target_pairs={{1,0},{0,1},{3,2},{2,3},{5,4},{4,5},{7,6},{6,7},{9,8},{8,9},{11,10... | collective-permute-start | bytes 442376 | tf_op jit(solution)/shard_map/ppermute | solution.py:114
  16.4 0.0 collective-permute-done.3.refs_4_
  16.4 2.2 %collective-permute-done.9.refs_11_ = bf16[144,512]{1,0:T(8,128)(2,1)S(1)} collective-permute-done((bf16[144,512]{1,0:T(8,128)(2,1)S(1)}, bf16[144,512]{1,0:T(8,128)(2,1)S(1)}, u32[]{:S(2)}, u32[]{:S(2)}) %collective-permute-start.9) | collective-permute-done | bytes 147488 | tf_op jit(solution)/shard_map/ppermute | solution.py:114
  18.6 0.0 collective-permute-done.6.refs_7_
  18.6 0.0 collective-permute-done.5.refs_6_
  18.6 0.0 collective-permute-done.4.refs_5_
  18.6 1.8 %shard_map.38 = (f32[1,128]{1,0:T(1,128)S(1)}, f32[1,128]{1,0:T(1,128)S(1)}, f32[1,128]{1,0:T(1,128)S(1)}, f32[1,128]{1,0:T(1,128)S(1)}) custom-call(bf16[64,64]{1,0:T(8,128)(2,1)S(1)} %get-tuple-element.11.table_ref, bf16[144,512]{1,0:T(8,128)(2,1)S(1)} %get-tuple-element.12.refs_0_.refs_8_, bf16[144,512]{1,0:T(8,128)(2,1)S(1)} %collective-permute-done.refs_1_, ...), custom_call_target="tpu_custom_call" | custom-call | flops 536870912 | bytes 1572864 | tf_op jit(solution)/shard_map/pallas_call | solution.py:89
  20.4 3.5 %collective-permute-start.10 = (f32[1,128]{1,0:T(1,128)S(1)}, f32[1,128]{1,0:T(1,128)S(1)}, u32[]{:S(2)}, u32[]{:S(2)}) collective-permute-start(f32[1,128]{1,0:T(1,128)S(1)} %get-tuple-element.13), channel_id=1, source_target_pairs={{24,0},{25,1},{26,2},{27,3},{28,4},{29,5},{30,6},{31,7},{16,8},{17... | collective-permute-start | bytes 1544 | tf_op jit(solution)/shard_map/ppermute | solution.py:114
  23.9 0.0 collective-permute-start.11
  23.9 0.9 %collective-permute-start.12 = (f32[1,128]{1,0:T(1,128)S(1)}, f32[1,128]{1,0:T(1,128)S(1)}, u32[]{:S(2)}, u32[]{:S(2)}) collective-permute-start(f32[1,128]{1,0:T(1,128)S(1)} %get-tuple-element.15), channel_id=1, source_target_pairs={{8,0},{9,1},{10,2},{11,3},{12,4},{13,5},{14,6},{15,7},{0,8},{1,9},... | collective-permute-start | bytes 1544 | tf_op jit(solution)/shard_map/ppermute | solution.py:114
  24.9 0.9 %collective-permute-done.10 = f32[1,128]{1,0:T(1,128)S(1)} collective-permute-done((f32[1,128]{1,0:T(1,128)S(1)}, f32[1,128]{1,0:T(1,128)S(1)}, u32[]{:S(2)}, u32[]{:S(2)}) %collective-permute-start.10) | collective-permute-done | bytes 544 | tf_op jit(solution)/shard_map/ppermute | solution.py:114
  25.8 2.5 %collective-permute-done.11 = f32[1,128]{1,0:T(1,128)S(1)} collective-permute-done((f32[1,128]{1,0:T(1,128)S(1)}, f32[1,128]{1,0:T(1,128)S(1)}, u32[]{:S(2)}, u32[]{:S(2)}) %collective-permute-start.11) | collective-permute-done | bytes 544 | tf_op jit(solution)/shard_map/ppermute | solution.py:114
  28.3 0.0 collective-permute-done.12
  28.4 0.5 %maximum_bitcast_fusion = f32[128]{0:T(128)} fusion(f32[1,128]{1,0:T(1,128)S(1)} %get-tuple-element.16, f32[1,128]{1,0:T(1,128)S(1)} %collective-permute-done.12, f32[1,128]{1,0:T(1,128)S(1)} %collective-permute-done.10, f32[1,128]{1,0:T(1,128)S(1)} %collective-permute-done.11), kind=kLoop, calls=%fused_computation | loop fusion | flops 384 | bytes 2560 | tf_op jit(solution)/shard_map/reshape | solution.py:150
Async XLA Ops:
  1.1 11.2 %collective-permute-start.8 = (bf16[144,512]{1,0:T(8,128)(2,1)S(1)}, bf16[144,512]{1,0:T(8,128)(2,1)S(1)}, u32[]{:S(2)}, u32[]{:S(2)}) collective-permute-start(bf16[144,512]{1,0:T(8,128)(2,1)S(1)} %get-tuple-element.12.refs_0_.refs_8_), channel_id=1, source_target_pairs={{16,0},{17,1},{18,2},{19,3},{20,4},{21,5},{22,6},{23,7},{24,8},{25... | collective-permute-start | bytes 442376 | tf_op jit(solution)/shard_map/ppermute | solution.py:114
  5.2 7.3 %collective-permute-start.7 = (bf16[144,512]{1,0:T(8,128)(2,1)S(1)}, bf16[144,512]{1,0:T(8,128)(2,1)S(1)}, u32[]{:S(2)}, u32[]{:S(2)}) collective-permute-start(bf16[144,512]{1,0:T(8,128)(2,1)S(1)} %get-tuple-element.12.refs_0_.refs_8_), channel_id=1, source_target_pairs={{8,0},{9,1},{10,2},{11,3},{12,4},{13,5},{14,6},{15,7},{0,8},{1,9},... | collective-permute-start | bytes 442376 | tf_op jit(solution)/shard_map/ppermute | solution.py:114
  6.8 7.2 %collective-permute-start.2 = (bf16[144,512]{1,0:T(8,128)(2,1)S(1)}, bf16[144,512]{1,0:T(8,128)(2,1)S(1)}, u32[]{:S(2)}, u32[]{:S(2)}) collective-permute-start(bf16[144,512]{1,0:T(8,128)(2,1)S(1)} %get-tuple-element.12.refs_0_.refs_8_), channel_id=1, source_target_pairs={{6,0},{7,1},{4,2},{5,3},{2,4},{3,5},{0,6},{1,7},{14,8},{15,9},{12,... | collective-permute-start | bytes 442376 | tf_op jit(solution)/shard_map/ppermute | solution.py:114
  9.2 6.6 %collective-permute-start.1 = (bf16[144,512]{1,0:T(8,128)(2,1)S(1)}, bf16[144,512]{1,0:T(8,128)(2,1)S(1)}, u32[]{:S(2)}, u32[]{:S(2)}) collective-permute-start(bf16[144,512]{1,0:T(8,128)(2,1)S(1)} %get-tuple-element.12.refs_0_.refs_8_), channel_id=1, source_target_pairs={{4,0},{5,1},{6,2},{7,3},{0,4},{1,5},{2,6},{3,7},{12,8},{13,9},{14,... | collective-permute-start | bytes 442376 | tf_op jit(solution)/shard_map/ppermute | solution.py:114
  9.7 6.2 %collective-permute-start = (bf16[144,512]{1,0:T(8,128)(2,1)S(1)}, bf16[144,512]{1,0:T(8,128)(2,1)S(1)}, u32[]{:S(2)}, u32[]{:S(2)}) collective-permute-start(bf16[144,512]{1,0:T(8,128)(2,1)S(1)} %get-tuple-element.12.refs_0_.refs_8_), channel_id=1, source_target_pairs={{2,0},{3,1},{0,2},{1,3},{6,4},{7,5},{4,6},{5,7},{10,8},{11,9},{8,1... | collective-permute-start | bytes 442376 | tf_op jit(solution)/shard_map/ppermute | solution.py:114
  12.3 4.1 %collective-permute-start.3 = (bf16[144,512]{1,0:T(8,128)(2,1)S(1)}, bf16[144,512]{1,0:T(8,128)(2,1)S(1)}, u32[]{:S(2)}, u32[]{:S(2)}) collective-permute-start(bf16[144,512]{1,0:T(8,128)(2,1)S(1)} %get-tuple-element.12.refs_0_.refs_8_), channel_id=1, source_target_pairs={{1,0},{0,1},{3,2},{2,3},{5,4},{4,5},{7,6},{6,7},{9,8},{8,9},{11,10... | collective-permute-start | bytes 442376 | tf_op jit(solution)/shard_map/ppermute | solution.py:114
  12.5 6.1 %collective-permute-start.9 = (bf16[144,512]{1,0:T(8,128)(2,1)S(1)}, bf16[144,512]{1,0:T(8,128)(2,1)S(1)}, u32[]{:S(2)}, u32[]{:S(2)}) collective-permute-start(bf16[144,512]{1,0:T(8,128)(2,1)S(1)} %collective-permute-done.8.refs_10_), channel_id=1, source_target_pairs={{8,0},{9,1},{10,2},{11,3},{12,4},{13,5},{14,6},{15,7},{0,8},{1,9},... | collective-permute-start | bytes 442376 | tf_op jit(solution)/shard_map/ppermute | solution.py:114
  14.0 4.6 %collective-permute-start.6 = (bf16[144,512]{1,0:T(8,128)(2,1)S(1)}, bf16[144,512]{1,0:T(8,128)(2,1)S(1)}, u32[]{:S(2)}, u32[]{:S(2)}) collective-permute-start(bf16[144,512]{1,0:T(8,128)(2,1)S(1)} %collective-permute-done.2.refs_3_), channel_id=1, source_target_pairs={{1,0},{0,1},{3,2},{2,3},{5,4},{4,5},{7,6},{6,7},{9,8},{8,9},{11,10... | collective-permute-start | bytes 442376 | tf_op jit(solution)/shard_map/ppermute | solution.py:114
  15.9 2.7 %collective-permute-start.5 = (bf16[144,512]{1,0:T(8,128)(2,1)S(1)}, bf16[144,512]{1,0:T(8,128)(2,1)S(1)}, u32[]{:S(2)}, u32[]{:S(2)}) collective-permute-start(bf16[144,512]{1,0:T(8,128)(2,1)S(1)} %collective-permute-done.1.refs_2_), channel_id=1, source_target_pairs={{1,0},{0,1},{3,2},{2,3},{5,4},{4,5},{7,6},{6,7},{9,8},{8,9},{11,10... | collective-permute-start | bytes 442376 | tf_op jit(solution)/shard_map/ppermute | solution.py:114
  15.9 2.7 %collective-permute-start.4 = (bf16[144,512]{1,0:T(8,128)(2,1)S(1)}, bf16[144,512]{1,0:T(8,128)(2,1)S(1)}, u32[]{:S(2)}, u32[]{:S(2)}) collective-permute-start(bf16[144,512]{1,0:T(8,128)(2,1)S(1)} %collective-permute-done.refs_1_), channel_id=1, source_target_pairs={{1,0},{0,1},{3,2},{2,3},{5,4},{4,5},{7,6},{6,7},{9,8},{8,9},{11,10... | collective-permute-start | bytes 442376 | tf_op jit(solution)/shard_map/ppermute | solution.py:114
  20.4 5.4 %collective-permute-start.10 = (f32[1,128]{1,0:T(1,128)S(1)}, f32[1,128]{1,0:T(1,128)S(1)}, u32[]{:S(2)}, u32[]{:S(2)}) collective-permute-start(f32[1,128]{1,0:T(1,128)S(1)} %get-tuple-element.13), channel_id=1, source_target_pairs={{24,0},{25,1},{26,2},{27,3},{28,4},{29,5},{30,6},{31,7},{16,8},{17... | collective-permute-start | bytes 1544 | tf_op jit(solution)/shard_map/ppermute | solution.py:114
  23.9 4.4 %collective-permute-start.11 = (f32[1,128]{1,0:T(1,128)S(1)}, f32[1,128]{1,0:T(1,128)S(1)}, u32[]{:S(2)}, u32[]{:S(2)}) collective-permute-start(f32[1,128]{1,0:T(1,128)S(1)} %get-tuple-element.14), channel_id=1, source_target_pairs={{16,0},{17,1},{18,2},{19,3},{20,4},{21,5},{22,6},{23,7},{24,8},{25... | collective-permute-start | bytes 1544 | tf_op jit(solution)/shard_map/ppermute | solution.py:114
  23.9 4.4 %collective-permute-start.12 = (f32[1,128]{1,0:T(1,128)S(1)}, f32[1,128]{1,0:T(1,128)S(1)}, u32[]{:S(2)}, u32[]{:S(2)}) collective-permute-start(f32[1,128]{1,0:T(1,128)S(1)} %get-tuple-element.15), channel_id=1, source_target_pairs={{8,0},{9,1},{10,2},{11,3},{12,4},{13,5},{14,6},{15,7},{0,8},{1,9},... | collective-permute-start | bytes 1544 | tf_op jit(solution)/shard_map/ppermute | solution.py:114

commit v15 on v12

--- a/solution.py
+++ b/solution.py
@@ -131,13 +131,16 @@
             return permute(x, lambda z, a, g: (turned(z, s, length), a, g))
 
         half = length // 2 if length & (length - 1) == 0 else length
-        middle = along(own, half) if half < length else None
+        middle = along(own, length - 1) if half < length else None
         near = [permute(own, lambda z, a, g: (z, turned(a, s, wide), g)) for s in reversed(range(1, wide))]
         first = [along(own, s) for s in range(1, half)]
         middle, near, first = lax.optimization_barrier((middle, near, first))
         near = near[::-1]
-        first = first if middle is None else first + [middle]
-        last = [along(first[half - 1], s) for s in range(1, length - half)]
+        last = [along(middle, s) for s in range(1, half)] if half < length else []
+        offsets = list(range(1, half))
+        if half < length:
+            first = first + [middle]
+            offsets += [length - 1] + [(length - 1) ^ s for s in range(1, half)]
         far, far_rank = [], []
         for t in range(1, n_grp):
             for s in range(wide):
@@ -146,13 +149,13 @@
                 far_rank.append(rank(a=s, g=t))
         near = list(zip([own] + near, [rank(a=s) for s in range(wide)]))
         far = list(zip(far, far_rank))
-        visit_rank = [rank(z=s) for s in range(1, length)]
+        visit_rank = [rank(z=s) for s in offsets]
         first = list(zip(first, visit_rank))
         last = list(zip(last, visit_rank[len(first) :]))
         best = best_of(near + far, near[:1] + first, table, True)
         if last:
             best = best + best_of(near + far, last, table, False)
-        found = [best[0]] + [along(best[s], -s) for s in range(1, length)]
+        found = [best[0]] + [along(b, -s) for b, s in zip(best[1:], offsets)]
         return functools.reduce(jnp.maximum, found).reshape(rows)
 
     placed = (P(("clu", "grp"), None), P(("clu", "grp")), P())

time: 28.6 us -> 28.2 us (0.986)
  starting transfers between devices: 16.4 us -> 11.5 us
  waiting for transfers between devices: 8.38 us -> 12.9 us
    ppermute x13, starting transfers between devices: 16.4 us -> 11.5 us  [permute(): return lax.ppermute(x, ('clu', 'grp'), pairs)]
    ppermute x13, waiting for transfers between devices: 8.38 us -> 12.9 us  [permute(): return lax.ppermute(x, ('clu', 'grp'), pairs)]
  transfers between devices with their start and end apart: 13 -> 13, of which waited for: 7 -> 10; matrix products, arithmetic and copies ran while one was open for 0% -> 0% of each run, Pallas kernels for 7% -> 7%
where the time goes in v15:
time: 28.2 us; the launch traced here: 28.1 us
  waiting for transfers between devices  12.9 us (46%)
  starting transfers between devices  11.5 us (41%)
  Pallas kernels  3.17 us (11%)
  other arithmetic  0.52 us (2%)
    ppermute x13, waiting for transfers between devices, permute(): return lax.ppermute(x, ('clu', 'grp'), pairs)  12.9 us
    ppermute x13, starting transfers between devices, permute(): return lax.ppermute(x, ('clu', 'grp'), pairs)  11.5 us
    pallas_call x2, Pallas kernels, best_of(): pl.pallas_call(functools.partial(best_kernel, len(keys), own, ranks), out...  2.06 us
    pallas_call x1, Pallas kernels, pack(): pl.pallas_call(functools.partial(pack_kernel, groups), out_shape=[pltpu.V...  1.1 us
  transfers between devices with their start and end apart: 13, of which 10 were waited for; matrix products, arithmetic and copies ran while one was open for 0% of the time, Pallas kernels for 7%

profile of v15, /device:TPU:0, one launch (start us, length us, event | category | flops | bytes accessed | tf_op | source)
XLA Modules:
  0.0 28.1 jit_solution(7498403343385648867)
XLA Ops:
  0.0 1.1 %shard_map.37 = (bf16[144,512]{1,0:T(8,128)(2,1)S(1)}, bf16[64,64]{1,0:T(8,128)(2,1)S(1)}) custom-call(bf16[128,512]{1,0:T(8,128)(2,1)} %emb_ref.1, s32[1,128]{1,0:T(1,128)} %bitcast.4, s32[1,64]{1,0:T(1,128)} %bitcast.5), custom_call_target="tpu_custom_call" | custom-call | tf_op jit(solution)/shard_map/pallas_call | solution.py:38
  1.1 5.1 %collective-permute-start = (bf16[144,512]{1,0:T(8,128)(2,1)S(1)}, bf16[144,512]{1,0:T(8,128)(2,1)S(1)}, u32[]{:S(2)}, u32[]{:S(2)}) collective-permute-start(bf16[144,512]{1,0:T(8,128)(2,1)S(1)} %get-tuple-element.16.refs_0_.refs_8_), channel_id=1, source_target_pairs={{24,0},{25,1},{26,2},{27,3},{28,4},{29,5},{30,6},{31,7},{16,8},{17... | collective-permute-start | bytes 442376 | tf_op jit(solution)/shard_map/ppermute | solution.py:114
  6.2 2.4 %collective-permute-start.1 = (bf16[144,512]{1,0:T(8,128)(2,1)S(1)}, bf16[144,512]{1,0:T(8,128)(2,1)S(1)}, u32[]{:S(2)}, u32[]{:S(2)}) collective-permute-start(bf16[144,512]{1,0:T(8,128)(2,1)S(1)} %get-tuple-element.16.refs_0_.refs_8_), channel_id=1, source_target_pairs={{6,0},{7,1},{4,2},{5,3},{2,4},{3,5},{0,6},{1,7},{14,8},{15,9},{12,... | collective-permute-start | bytes 442376 | tf_op jit(solution)/shard_map/ppermute | solution.py:114
  8.7 0.5 %collective-permute-start.2 = (bf16[144,512]{1,0:T(8,128)(2,1)S(1)}, bf16[144,512]{1,0:T(8,128)(2,1)S(1)}, u32[]{:S(2)}, u32[]{:S(2)}) collective-permute-start(bf16[144,512]{1,0:T(8,128)(2,1)S(1)} %get-tuple-element.16.refs_0_.refs_8_), channel_id=1, source_target_pairs={{4,0},{5,1},{6,2},{7,3},{0,4},{1,5},{2,6},{3,7},{12,8},{13,9},{14,... | collective-permute-start | bytes 442376 | tf_op jit(solution)/shard_map/ppermute | solution.py:114
  9.2 0.5 %collective-permute-start.3 = (bf16[144,512]{1,0:T(8,128)(2,1)S(1)}, bf16[144,512]{1,0:T(8,128)(2,1)S(1)}, u32[]{:S(2)}, u32[]{:S(2)}) collective-permute-start(bf16[144,512]{1,0:T(8,128)(2,1)S(1)} %get-tuple-element.16.refs_0_.refs_8_), channel_id=1, source_target_pairs={{2,0},{3,1},{0,2},{1,3},{6,4},{7,5},{4,6},{5,7},{10,8},{11,9},{8,1... | collective-permute-start | bytes 442376 | tf_op jit(solution)/shard_map/ppermute | solution.py:114
  9.7 0.0 collective-permute-start.4
  9.7 0.6 %collective-permute-done.refs_10_ = bf16[144,512]{1,0:T(8,128)(2,1)S(1)} collective-permute-done((bf16[144,512]{1,0:T(8,128)(2,1)S(1)}, bf16[144,512]{1,0:T(8,128)(2,1)S(1)}, u32[]{:S(2)}, u32[]{:S(2)}) %collective-permute-start) | collective-permute-done | bytes 147488 | tf_op jit(solution)/shard_map/ppermute | solution.py:114
  10.3 0.0 collective-permute-start.5
  10.3 2.9 %collective-permute-done.1.refs_3_ = bf16[144,512]{1,0:T(8,128)(2,1)S(1)} collective-permute-done((bf16[144,512]{1,0:T(8,128)(2,1)S(1)}, bf16[144,512]{1,0:T(8,128)(2,1)S(1)}, u32[]{:S(2)}, u32[]{:S(2)}) %collective-permute-start.1) | collective-permute-done | bytes 147488 | tf_op jit(solution)/shard_map/ppermute | solution.py:114
  13.1 2.5 %collective-permute-done.2.refs_2_ = bf16[144,512]{1,0:T(8,128)(2,1)S(1)} collective-permute-done((bf16[144,512]{1,0:T(8,128)(2,1)S(1)}, bf16[144,512]{1,0:T(8,128)(2,1)S(1)}, u32[]{:S(2)}, u32[]{:S(2)}) %collective-permute-start.2) | collective-permute-done | bytes 147488 | tf_op jit(solution)/shard_map/ppermute | solution.py:114
  15.6 0.1 collective-permute-done.3.refs_1_
  15.6 0.0 collective-permute-done.4.refs_9_
  15.7 0.0 collective-permute-start.6
  15.7 0.5 %collective-permute-start.7 = (bf16[144,512]{1,0:T(8,128)(2,1)S(1)}, bf16[144,512]{1,0:T(8,128)(2,1)S(1)}, u32[]{:S(2)}, u32[]{:S(2)}) collective-permute-start(bf16[144,512]{1,0:T(8,128)(2,1)S(1)} %collective-permute-done.2.refs_2_), channel_id=1, source_target_pairs={{1,0},{0,1},{3,2},{2,3},{5,4},{4,5},{7,6},{6,7},{9,8},{8,9},{11,10... | collective-permute-start | bytes 442376 | tf_op jit(solution)/shard_map/ppermute | solution.py:114
  16.2 0.0 collective-permute-start.8
  16.2 0.0 collective-permute-start.11
  16.2 0.0 collective-permute-done.5.refs_4_
  16.2 0.8 %collective-permute-done.6.refs_5_ = bf16[144,512]{1,0:T(8,128)(2,1)S(1)} collective-permute-done((bf16[144,512]{1,0:T(8,128)(2,1)S(1)}, bf16[144,512]{1,0:T(8,128)(2,1)S(1)}, u32[]{:S(2)}, u32[]{:S(2)}) %collective-permute-start.6) | collective-permute-done | bytes 147488 | tf_op jit(solution)/shard_map/ppermute | solution.py:114
  17.0 0.2 collective-permute-done.7.refs_6_
  17.2 0.3 %collective-permute-done.8.refs_7_ = bf16[144,512]{1,0:T(8,128)(2,1)S(1)} collective-permute-done((bf16[144,512]{1,0:T(8,128)(2,1)S(1)}, bf16[144,512]{1,0:T(8,128)(2,1)S(1)}, u32[]{:S(2)}, u32[]{:S(2)}) %collective-permute-start.8) | collective-permute-done | bytes 147488 | tf_op jit(solution)/shard_map/ppermute | solution.py:114
  17.5 1.4 %shard_map.38 = (f32[1,128]{1,0:T(1,128)S(1)}, f32[1,128]{1,0:T(1,128)S(1)}, f32[1,128]{1,0:T(1,128)S(1)}) custom-call(bf16[64,64]{1,0:T(8,128)(2,1)S(1)} %get-tuple-element.15.table_ref, bf16[144,512]{1,0:T(8,128)(2,1)S(1)} %get-tuple-element.16.refs_0_.refs_8_, bf16[144,512]{1,0:T(8,128)(2,1)S(1)} %collective-permute-done.3.refs_1_, ...), custom_call_target="tpu_custom_call" | custom-call | flops 402653184 | bytes 1441792 | tf_op jit(solution)/shard_map/pallas_call | solution.py:89
  19.0 1.3 %collective-permute-start.10 = (f32[1,128]{1,0:T(1,128)S(1)}, f32[1,128]{1,0:T(1,128)S(1)}, u32[]{:S(2)}, u32[]{:S(2)}) collective-permute-start(f32[1,128]{1,0:T(1,128)S(1)} %get-tuple-element.24), channel_id=1, source_target_pairs={{24,0},{25,1},{26,2},{27,3},{28,4},{29,5},{30,6},{31,7},{16,8},{17... | collective-permute-start | bytes 1544 | tf_op jit(solution)/shard_map/ppermute | solution.py:114
  20.3 0.0 collective-permute-start.9
  20.3 2.2 %collective-permute-done.11.refs_8_ = bf16[144,512]{1,0:T(8,128)(2,1)S(1)} collective-permute-done((bf16[144,512]{1,0:T(8,128)(2,1)S(1)}, bf16[144,512]{1,0:T(8,128)(2,1)S(1)}, u32[]{:S(2)}, u32[]{:S(2)}) %collective-permute-start.11) | collective-permute-done | bytes 147488 | tf_op jit(solution)/shard_map/ppermute | solution.py:114
  22.4 0.6 %shard_map.39 = f32[1,128]{1,0:T(1,128)S(1)} custom-call(bf16[64,64]{1,0:T(8,128)(2,1)S(1)} %get-tuple-element.15.table_ref, bf16[144,512]{1,0:T(8,128)(2,1)S(1)} %get-tuple-element.16.refs_0_.refs_8_, bf16[144,512]{1,0:T(8,128)(2,1)S(1)} %collective-permute-done.3.refs_1_, bf16[144,512]{1,0:T(8,128)(2,1)S(1)} %collective-permute-done.2.refs_2_, ...), custom_call_target="tpu_custom_call" | custom-call | flops 134217728 | bytes 1179648 | tf_op jit(solution)/shard_map/pallas_call | solution.py:89
  23.1 1.1 %collective-permute-start.12 = (f32[1,128]{1,0:T(1,128)S(1)}, f32[1,128]{1,0:T(1,128)S(1)}, u32[]{:S(2)}, u32[]{:S(2)}) collective-permute-start(f32[1,128]{1,0:T(1,128)S(1)} %shard_map.39), channel_id=1, source_target_pairs={{16,0},{17,1},{18,2},{19,3},{20,4},{21,5},{22,6},{23,7},{24,8},{25... | collective-permute-start | bytes 1544 | tf_op jit(solution)/shard_map/ppermute | solution.py:114
  24.1 0.2 collective-permute-done.10
  24.4 0.0 collective-permute-done.9
  24.4 3.2 %collective-permute-done.12 = f32[1,128]{1,0:T(1,128)S(1)} collective-permute-done((f32[1,128]{1,0:T(1,128)S(1)}, f32[1,128]{1,0:T(1,128)S(1)}, u32[]{:S(2)}, u32[]{:S(2)}) %collective-permute-start.12) | collective-permute-done | bytes 544 | tf_op jit(solution)/shard_map/ppermute | solution.py:114
  27.6 0.5 %maximum_bitcast_fusion = f32[128]{0:T(128)} fusion(f32[1,128]{1,0:T(1,128)S(1)} %collective-permute-done.12, f32[1,128]{1,0:T(1,128)S(1)} %collective-permute-done.10, f32[1,128]{1,0:T(1,128)S(1)} %get-tuple-element.22, f32[1,128]{1,0:T(1,128)S(1)} %collective-permute-done.9), kind=kLoop, calls=%fused_computation | loop fusion | flops 384 | bytes 2560 | tf_op jit(solution)/shard_map/reshape | solution.py:159
Async XLA Ops:
  1.1 9.2 %collective-permute-start = (bf16[144,512]{1,0:T(8,128)(2,1)S(1)}, bf16[144,512]{1,0:T(8,128)(2,1)S(1)}, u32[]{:S(2)}, u32[]{:S(2)}) collective-permute-start(bf16[144,512]{1,0:T(8,128)(2,1)S(1)} %get-tuple-element.16.refs_0_.refs_8_), channel_id=1, source_target_pairs={{24,0},{25,1},{26,2},{27,3},{28,4},{29,5},{30,6},{31,7},{16,8},{17... | collective-permute-start | bytes 442376 | tf_op jit(solution)/shard_map/ppermute | solution.py:114
  6.2 6.9 %collective-permute-start.1 = (bf16[144,512]{1,0:T(8,128)(2,1)S(1)}, bf16[144,512]{1,0:T(8,128)(2,1)S(1)}, u32[]{:S(2)}, u32[]{:S(2)}) collective-permute-start(bf16[144,512]{1,0:T(8,128)(2,1)S(1)} %get-tuple-element.16.refs_0_.refs_8_), channel_id=1, source_target_pairs={{6,0},{7,1},{4,2},{5,3},{2,4},{3,5},{0,6},{1,7},{14,8},{15,9},{12,... | collective-permute-start | bytes 442376 | tf_op jit(solution)/shard_map/ppermute | solution.py:114
  8.7 6.9 %collective-permute-start.2 = (bf16[144,512]{1,0:T(8,128)(2,1)S(1)}, bf16[144,512]{1,0:T(8,128)(2,1)S(1)}, u32[]{:S(2)}, u32[]{:S(2)}) collective-permute-start(bf16[144,512]{1,0:T(8,128)(2,1)S(1)} %get-tuple-element.16.refs_0_.refs_8_), channel_id=1, source_target_pairs={{4,0},{5,1},{6,2},{7,3},{0,4},{1,5},{2,6},{3,7},{12,8},{13,9},{14,... | collective-permute-start | bytes 442376 | tf_op jit(solution)/shard_map/ppermute | solution.py:114
  9.2 6.5 %collective-permute-start.3 = (bf16[144,512]{1,0:T(8,128)(2,1)S(1)}, bf16[144,512]{1,0:T(8,128)(2,1)S(1)}, u32[]{:S(2)}, u32[]{:S(2)}) collective-permute-start(bf16[144,512]{1,0:T(8,128)(2,1)S(1)} %get-tuple-element.16.refs_0_.refs_8_), channel_id=1, source_target_pairs={{2,0},{3,1},{0,2},{1,3},{6,4},{7,5},{4,6},{5,7},{10,8},{11,9},{8,1... | collective-permute-start | bytes 442376 | tf_op jit(solution)/shard_map/ppermute | solution.py:114
  9.7 5.9 %collective-permute-start.4 = (bf16[144,512]{1,0:T(8,128)(2,1)S(1)}, bf16[144,512]{1,0:T(8,128)(2,1)S(1)}, u32[]{:S(2)}, u32[]{:S(2)}) collective-permute-start(bf16[144,512]{1,0:T(8,128)(2,1)S(1)} %get-tuple-element.16.refs_0_.refs_8_), channel_id=1, source_target_pairs={{8,0},{9,1},{10,2},{11,3},{12,4},{13,5},{14,6},{15,7},{0,8},{1,9},... | collective-permute-start | bytes 442376 | tf_op jit(solution)/shard_map/ppermute | solution.py:114
  10.3 5.9 %collective-permute-start.5 = (bf16[144,512]{1,0:T(8,128)(2,1)S(1)}, bf16[144,512]{1,0:T(8,128)(2,1)S(1)}, u32[]{:S(2)}, u32[]{:S(2)}) collective-permute-start(bf16[144,512]{1,0:T(8,128)(2,1)S(1)} %get-tuple-element.16.refs_0_.refs_8_), channel_id=1, source_target_pairs={{1,0},{0,1},{3,2},{2,3},{5,4},{4,5},{7,6},{6,7},{9,8},{8,9},{11,10... | collective-permute-start | bytes 442376 | tf_op jit(solution)/shard_map/ppermute | solution.py:114
  15.7 1.4 %collective-permute-start.6 = (bf16[144,512]{1,0:T(8,128)(2,1)S(1)}, bf16[144,512]{1,0:T(8,128)(2,1)S(1)}, u32[]{:S(2)}, u32[]{:S(2)}) collective-permute-start(bf16[144,512]{1,0:T(8,128)(2,1)S(1)} %collective-permute-done.3.refs_1_), channel_id=1, source_target_pairs={{1,0},{0,1},{3,2},{2,3},{5,4},{4,5},{7,6},{6,7},{9,8},{8,9},{11,10... | collective-permute-start | bytes 442376 | tf_op jit(solution)/shard_map/ppermute | solution.py:114
  15.7 1.6 %collective-permute-start.7 = (bf16[144,512]{1,0:T(8,128)(2,1)S(1)}, bf16[144,512]{1,0:T(8,128)(2,1)S(1)}, u32[]{:S(2)}, u32[]{:S(2)}) collective-permute-start(bf16[144,512]{1,0:T(8,128)(2,1)S(1)} %collective-permute-done.2.refs_2_), channel_id=1, source_target_pairs={{1,0},{0,1},{3,2},{2,3},{5,4},{4,5},{7,6},{6,7},{9,8},{8,9},{11,10... | collective-permute-start | bytes 442376 | tf_op jit(solution)/shard_map/ppermute | solution.py:114
  16.2 1.4 %collective-permute-start.8 = (bf16[144,512]{1,0:T(8,128)(2,1)S(1)}, bf16[144,512]{1,0:T(8,128)(2,1)S(1)}, u32[]{:S(2)}, u32[]{:S(2)}) collective-permute-start(bf16[144,512]{1,0:T(8,128)(2,1)S(1)} %collective-permute-done.1.refs_3_), channel_id=1, source_target_pairs={{1,0},{0,1},{3,2},{2,3},{5,4},{4,5},{7,6},{6,7},{9,8},{8,9},{11,10... | collective-permute-start | bytes 442376 | tf_op jit(solution)/shard_map/ppermute | solution.py:114
  16.2 6.2 %collective-permute-start.11 = (bf16[144,512]{1,0:T(8,128)(2,1)S(1)}, bf16[144,512]{1,0:T(8,128)(2,1)S(1)}, u32[]{:S(2)}, u32[]{:S(2)}) collective-permute-start(bf16[144,512]{1,0:T(8,128)(2,1)S(1)} %collective-permute-done.refs_10_), channel_id=1, source_target_pairs={{8,0},{9,1},{10,2},{11,3},{12,4},{13,5},{14,6},{15,7},{0,8},{1,9},... | collective-permute-start | bytes 442376 | tf_op jit(solution)/shard_map/ppermute | solution.py:114
  19.0 5.4 %collective-permute-start.10 = (f32[1,128]{1,0:T(1,128)S(1)}, f32[1,128]{1,0:T(1,128)S(1)}, u32[]{:S(2)}, u32[]{:S(2)}) collective-permute-start(f32[1,128]{1,0:T(1,128)S(1)} %get-tuple-element.24), channel_id=1, source_target_pairs={{24,0},{25,1},{26,2},{27,3},{28,4},{29,5},{30,6},{31,7},{16,8},{17... | collective-permute-start | bytes 1544 | tf_op jit(solution)/shard_map/ppermute | solution.py:114
  20.3 4.1 %collective-permute-start.9 = (f32[1,128]{1,0:T(1,128)S(1)}, f32[1,128]{1,0:T(1,128)S(1)}, u32[]{:S(2)}, u32[]{:S(2)}) collective-permute-start(f32[1,128]{1,0:T(1,128)S(1)} %get-tuple-element.23), channel_id=1, source_target_pairs={{8,0},{9,1},{10,2},{11,3},{12,4},{13,5},{14,6},{15,7},{0,8},{1,9},... | collective-permute-start | bytes 1544 | tf_op jit(solution)/shard_map/ppermute | solution.py:114
  23.1 4.5 %collective-permute-start.12 = (f32[1,128]{1,0:T(1,128)S(1)}, f32[1,128]{1,0:T(1,128)S(1)}, u32[]{:S(2)}, u32[]{:S(2)}) collective-permute-start(f32[1,128]{1,0:T(1,128)S(1)} %shard_map.39), channel_id=1, source_target_pairs={{16,0},{17,1},{18,2},{19,3},{20,4},{21,5},{22,6},{23,7},{24,8},{25... | collective-permute-start | bytes 1544 | tf_op jit(solution)/shard_map/ppermute | solution.py:114

commit v16 on v15

--- a/solution.py
+++ b/solution.py
@@ -8,7 +8,7 @@
 from jax.experimental.pallas import tpu as pltpu
 from jax.sharding import PartitionSpec as P
 
-AUX = 16
+AUX = 8
 DIGIT = 256
 
 

time: 28.2 us -> 27.7 us (0.982)
  waiting for transfers between devices: 12.9 us -> 12.2 us
    ppermute x13, waiting for transfers between devices: 12.9 us -> 12.2 us  [permute(): return lax.ppermute(x, ('clu', 'grp'), pairs)]
where the time goes in v16:
time: 27.7 us; the launch traced here: 27.6 us
  waiting for transfers between devices  12.2 us (44%)
  starting transfers between devices  11.7 us (42%)
  Pallas kernels  3.17 us (11%)
  other arithmetic  0.52 us (2%)
    ppermute x13, waiting for transfers between devices, permute(): return lax.ppermute(x, ('clu', 'grp'), pairs)  12.2 us
    ppermute x13, starting transfers between devices, permute(): return lax.ppermute(x, ('clu', 'grp'), pairs)  11.7 us
    pallas_call x2, Pallas kernels, best_of(): pl.pallas_call(functools.partial(best_kernel, len(keys), own, ranks), out...  2.06 us
    pallas_call x1, Pallas kernels, pack(): pl.pallas_call(functools.partial(pack_kernel, groups), out_shape=[pltpu.V...  1.1 us
  transfers between devices with their start and end apart: 13, of which 10 were waited for; matrix products, arithmetic and copies ran while one was open for 0% of the time, Pallas kernels for 7%

profile of v16, /device:TPU:0, one launch (start us, length us, event | category | flops | bytes accessed | tf_op | source)
XLA Modules:
  0.0 27.6 jit_solution(17540429434571196277)
XLA Ops:
  0.0 1.1 %shard_map.37 = (bf16[136,512]{1,0:T(8,128)(2,1)S(1)}, bf16[64,64]{1,0:T(8,128)(2,1)S(1)}) custom-call(bf16[128,512]{1,0:T(8,128)(2,1)} %emb_ref.1, s32[1,128]{1,0:T(1,128)} %bitcast.4, s32[1,64]{1,0:T(1,128)} %bitcast.5), custom_call_target="tpu_custom_call" | custom-call | tf_op jit(solution)/shard_map/pallas_call | solution.py:38
  1.1 5.1 %collective-permute-start = (bf16[136,512]{1,0:T(8,128)(2,1)S(1)}, bf16[136,512]{1,0:T(8,128)(2,1)S(1)}, u32[]{:S(2)}, u32[]{:S(2)}) collective-permute-start(bf16[136,512]{1,0:T(8,128)(2,1)S(1)} %get-tuple-element.16.refs_0_.refs_8_), channel_id=1, source_target_pairs={{24,0},{25,1},{26,2},{27,3},{28,4},{29,5},{30,6},{31,7},{16,8},{17... | collective-permute-start | bytes 417800 | tf_op jit(solution)/shard_map/ppermute | solution.py:114
  6.2 2.4 %collective-permute-start.1 = (bf16[136,512]{1,0:T(8,128)(2,1)S(1)}, bf16[136,512]{1,0:T(8,128)(2,1)S(1)}, u32[]{:S(2)}, u32[]{:S(2)}) collective-permute-start(bf16[136,512]{1,0:T(8,128)(2,1)S(1)} %get-tuple-element.16.refs_0_.refs_8_), channel_id=1, source_target_pairs={{6,0},{7,1},{4,2},{5,3},{2,4},{3,5},{0,6},{1,7},{14,8},{15,9},{12,... | collective-permute-start | bytes 417800 | tf_op jit(solution)/shard_map/ppermute | solution.py:114
  8.7 0.5 %collective-permute-start.2 = (bf16[136,512]{1,0:T(8,128)(2,1)S(1)}, bf16[136,512]{1,0:T(8,128)(2,1)S(1)}, u32[]{:S(2)}, u32[]{:S(2)}) collective-permute-start(bf16[136,512]{1,0:T(8,128)(2,1)S(1)} %get-tuple-element.16.refs_0_.refs_8_), channel_id=1, source_target_pairs={{4,0},{5,1},{6,2},{7,3},{0,4},{1,5},{2,6},{3,7},{12,8},{13,9},{14,... | collective-permute-start | bytes 417800 | tf_op jit(solution)/shard_map/ppermute | solution.py:114
  9.2 0.5 %collective-permute-start.3 = (bf16[136,512]{1,0:T(8,128)(2,1)S(1)}, bf16[136,512]{1,0:T(8,128)(2,1)S(1)}, u32[]{:S(2)}, u32[]{:S(2)}) collective-permute-start(bf16[136,512]{1,0:T(8,128)(2,1)S(1)} %get-tuple-element.16.refs_0_.refs_8_), channel_id=1, source_target_pairs={{2,0},{3,1},{0,2},{1,3},{6,4},{7,5},{4,6},{5,7},{10,8},{11,9},{8,1... | collective-permute-start | bytes 417800 | tf_op jit(solution)/shard_map/ppermute | solution.py:114
  9.7 0.0 collective-permute-start.4
  9.7 0.3 %collective-permute-done.refs_10_ = bf16[136,512]{1,0:T(8,128)(2,1)S(1)} collective-permute-done((bf16[136,512]{1,0:T(8,128)(2,1)S(1)}, bf16[136,512]{1,0:T(8,128)(2,1)S(1)}, u32[]{:S(2)}, u32[]{:S(2)}) %collective-permute-start) | collective-permute-done | bytes 139296 | tf_op jit(solution)/shard_map/ppermute | solution.py:114
  10.0 0.0 collective-permute-start.5
  10.0 2.8 %collective-permute-done.1.refs_3_ = bf16[136,512]{1,0:T(8,128)(2,1)S(1)} collective-permute-done((bf16[136,512]{1,0:T(8,128)(2,1)S(1)}, bf16[136,512]{1,0:T(8,128)(2,1)S(1)}, u32[]{:S(2)}, u32[]{:S(2)}) %collective-permute-start.1) | collective-permute-done | bytes 139296 | tf_op jit(solution)/shard_map/ppermute | solution.py:114
  12.8 2.5 %collective-permute-done.2.refs_2_ = bf16[136,512]{1,0:T(8,128)(2,1)S(1)} collective-permute-done((bf16[136,512]{1,0:T(8,128)(2,1)S(1)}, bf16[136,512]{1,0:T(8,128)(2,1)S(1)}, u32[]{:S(2)}, u32[]{:S(2)}) %collective-permute-start.2) | collective-permute-done | bytes 139296 | tf_op jit(solution)/shard_map/ppermute | solution.py:114
  15.2 0.1 collective-permute-done.3.refs_1_
  15.3 0.0 collective-permute-done.4.refs_9_
  15.3 0.0 collective-permute-start.6
  15.3 0.5 %collective-permute-start.7 = (bf16[136,512]{1,0:T(8,128)(2,1)S(1)}, bf16[136,512]{1,0:T(8,128)(2,1)S(1)}, u32[]{:S(2)}, u32[]{:S(2)}) collective-permute-start(bf16[136,512]{1,0:T(8,128)(2,1)S(1)} %collective-permute-done.2.refs_2_), channel_id=1, source_target_pairs={{1,0},{0,1},{3,2},{2,3},{5,4},{4,5},{7,6},{6,7},{9,8},{8,9},{11,10... | collective-permute-start | bytes 417800 | tf_op jit(solution)/shard_map/ppermute | solution.py:114
  15.8 0.0 collective-permute-start.8
  15.9 0.0 collective-permute-start.11
  15.9 0.0 collective-permute-done.5.refs_4_
  15.9 0.8 %collective-permute-done.6.refs_5_ = bf16[136,512]{1,0:T(8,128)(2,1)S(1)} collective-permute-done((bf16[136,512]{1,0:T(8,128)(2,1)S(1)}, bf16[136,512]{1,0:T(8,128)(2,1)S(1)}, u32[]{:S(2)}, u32[]{:S(2)}) %collective-permute-start.6) | collective-permute-done | bytes 139296 | tf_op jit(solution)/shard_map/ppermute | solution.py:114
  16.7 0.2 collective-permute-done.7.refs_6_
  16.9 0.3 %collective-permute-done.8.refs_7_ = bf16[136,512]{1,0:T(8,128)(2,1)S(1)} collective-permute-done((bf16[136,512]{1,0:T(8,128)(2,1)S(1)}, bf16[136,512]{1,0:T(8,128)(2,1)S(1)}, u32[]{:S(2)}, u32[]{:S(2)}) %collective-permute-start.8) | collective-permute-done | bytes 139296 | tf_op jit(solution)/shard_map/ppermute | solution.py:114
  17.2 1.4 %shard_map.38 = (f32[1,128]{1,0:T(1,128)S(1)}, f32[1,128]{1,0:T(1,128)S(1)}, f32[1,128]{1,0:T(1,128)S(1)}) custom-call(bf16[64,64]{1,0:T(8,128)(2,1)S(1)} %get-tuple-element.15.table_ref, bf16[136,512]{1,0:T(8,128)(2,1)S(1)} %get-tuple-element.16.refs_0_.refs_8_, bf16[136,512]{1,0:T(8,128)(2,1)S(1)} %collective-permute-done.3.refs_1_, ...), custom_call_target="tpu_custom_call" | custom-call | flops 402653184 | bytes 1441792 | tf_op jit(solution)/shard_map/pallas_call | solution.py:89
  18.6 1.3 %collective-permute-start.10 = (f32[1,128]{1,0:T(1,128)S(1)}, f32[1,128]{1,0:T(1,128)S(1)}, u32[]{:S(2)}, u32[]{:S(2)}) collective-permute-start(f32[1,128]{1,0:T(1,128)S(1)} %get-tuple-element.24), channel_id=1, source_target_pairs={{24,0},{25,1},{26,2},{27,3},{28,4},{29,5},{30,6},{31,7},{16,8},{17... | collective-permute-start | bytes 1544 | tf_op jit(solution)/shard_map/ppermute | solution.py:114
  19.9 0.0 collective-permute-start.9
  19.9 2.0 %collective-permute-done.11.refs_8_ = bf16[136,512]{1,0:T(8,128)(2,1)S(1)} collective-permute-done((bf16[136,512]{1,0:T(8,128)(2,1)S(1)}, bf16[136,512]{1,0:T(8,128)(2,1)S(1)}, u32[]{:S(2)}, u32[]{:S(2)}) %collective-permute-start.11) | collective-permute-done | bytes 139296 | tf_op jit(solution)/shard_map/ppermute | solution.py:114
  21.9 0.6 %shard_map.39 = f32[1,128]{1,0:T(1,128)S(1)} custom-call(bf16[64,64]{1,0:T(8,128)(2,1)S(1)} %get-tuple-element.15.table_ref, bf16[136,512]{1,0:T(8,128)(2,1)S(1)} %get-tuple-element.16.refs_0_.refs_8_, bf16[136,512]{1,0:T(8,128)(2,1)S(1)} %collective-permute-done.3.refs_1_, bf16[136,512]{1,0:T(8,128)(2,1)S(1)} %collective-permute-done.2.refs_2_, ...), custom_call_target="tpu_custom_call" | custom-call | flops 134217728 | bytes 1179648 | tf_op jit(solution)/shard_map/pallas_call | solution.py:89
  22.5 1.2 %collective-permute-start.12 = (f32[1,128]{1,0:T(1,128)S(1)}, f32[1,128]{1,0:T(1,128)S(1)}, u32[]{:S(2)}, u32[]{:S(2)}) collective-permute-start(f32[1,128]{1,0:T(1,128)S(1)} %shard_map.39), channel_id=1, source_target_pairs={{16,0},{17,1},{18,2},{19,3},{20,4},{21,5},{22,6},{23,7},{24,8},{25... | collective-permute-start | bytes 1544 | tf_op jit(solution)/shard_map/ppermute | solution.py:114
  23.8 0.2 collective-permute-done.10
  24.0 0.0 collective-permute-done.9
  24.0 3.0 %collective-permute-done.12 = f32[1,128]{1,0:T(1,128)S(1)} collective-permute-done((f32[1,128]{1,0:T(1,128)S(1)}, f32[1,128]{1,0:T(1,128)S(1)}, u32[]{:S(2)}, u32[]{:S(2)}) %collective-permute-start.12) | collective-permute-done | bytes 544 | tf_op jit(solution)/shard_map/ppermute | solution.py:114
  27.0 0.5 %maximum_bitcast_fusion = f32[128]{0:T(128)} fusion(f32[1,128]{1,0:T(1,128)S(1)} %collective-permute-done.12, f32[1,128]{1,0:T(1,128)S(1)} %collective-permute-done.10, f32[1,128]{1,0:T(1,128)S(1)} %get-tuple-element.22, f32[1,128]{1,0:T(1,128)S(1)} %collective-permute-done.9), kind=kLoop, calls=%fused_computation | loop fusion | flops 384 | bytes 2560 | tf_op jit(solution)/shard_map/reshape | solution.py:159
Async XLA Ops:
  1.1 8.9 %collective-permute-start = (bf16[136,512]{1,0:T(8,128)(2,1)S(1)}, bf16[136,512]{1,0:T(8,128)(2,1)S(1)}, u32[]{:S(2)}, u32[]{:S(2)}) collective-permute-start(bf16[136,512]{1,0:T(8,128)(2,1)S(1)} %get-tuple-element.16.refs_0_.refs_8_), channel_id=1, source_target_pairs={{24,0},{25,1},{26,2},{27,3},{28,4},{29,5},{30,6},{31,7},{16,8},{17... | collective-permute-start | bytes 417800 | tf_op jit(solution)/shard_map/ppermute | solution.py:114
  6.2 6.6 %collective-permute-start.1 = (bf16[136,512]{1,0:T(8,128)(2,1)S(1)}, bf16[136,512]{1,0:T(8,128)(2,1)S(1)}, u32[]{:S(2)}, u32[]{:S(2)}) collective-permute-start(bf16[136,512]{1,0:T(8,128)(2,1)S(1)} %get-tuple-element.16.refs_0_.refs_8_), channel_id=1, source_target_pairs={{6,0},{7,1},{4,2},{5,3},{2,4},{3,5},{0,6},{1,7},{14,8},{15,9},{12,... | collective-permute-start | bytes 417800 | tf_op jit(solution)/shard_map/ppermute | solution.py:114
  8.7 6.6 %collective-permute-start.2 = (bf16[136,512]{1,0:T(8,128)(2,1)S(1)}, bf16[136,512]{1,0:T(8,128)(2,1)S(1)}, u32[]{:S(2)}, u32[]{:S(2)}) collective-permute-start(bf16[136,512]{1,0:T(8,128)(2,1)S(1)} %get-tuple-element.16.refs_0_.refs_8_), channel_id=1, source_target_pairs={{4,0},{5,1},{6,2},{7,3},{0,4},{1,5},{2,6},{3,7},{12,8},{13,9},{14,... | collective-permute-start | bytes 417800 | tf_op jit(solution)/shard_map/ppermute | solution.py:114
  9.2 6.1 %collective-permute-start.3 = (bf16[136,512]{1,0:T(8,128)(2,1)S(1)}, bf16[136,512]{1,0:T(8,128)(2,1)S(1)}, u32[]{:S(2)}, u32[]{:S(2)}) collective-permute-start(bf16[136,512]{1,0:T(8,128)(2,1)S(1)} %get-tuple-element.16.refs_0_.refs_8_), channel_id=1, source_target_pairs={{2,0},{3,1},{0,2},{1,3},{6,4},{7,5},{4,6},{5,7},{10,8},{11,9},{8,1... | collective-permute-start | bytes 417800 | tf_op jit(solution)/shard_map/ppermute | solution.py:114
  9.7 5.6 %collective-permute-start.4 = (bf16[136,512]{1,0:T(8,128)(2,1)S(1)}, bf16[136,512]{1,0:T(8,128)(2,1)S(1)}, u32[]{:S(2)}, u32[]{:S(2)}) collective-permute-start(bf16[136,512]{1,0:T(8,128)(2,1)S(1)} %get-tuple-element.16.refs_0_.refs_8_), channel_id=1, source_target_pairs={{8,0},{9,1},{10,2},{11,3},{12,4},{13,5},{14,6},{15,7},{0,8},{1,9},... | collective-permute-start | bytes 417800 | tf_op jit(solution)/shard_map/ppermute | solution.py:114
  10.0 5.9 %collective-permute-start.5 = (bf16[136,512]{1,0:T(8,128)(2,1)S(1)}, bf16[136,512]{1,0:T(8,128)(2,1)S(1)}, u32[]{:S(2)}, u32[]{:S(2)}) collective-permute-start(bf16[136,512]{1,0:T(8,128)(2,1)S(1)} %get-tuple-element.16.refs_0_.refs_8_), channel_id=1, source_target_pairs={{1,0},{0,1},{3,2},{2,3},{5,4},{4,5},{7,6},{6,7},{9,8},{8,9},{11,10... | collective-permute-start | bytes 417800 | tf_op jit(solution)/shard_map/ppermute | solution.py:114
  15.3 1.4 %collective-permute-start.6 = (bf16[136,512]{1,0:T(8,128)(2,1)S(1)}, bf16[136,512]{1,0:T(8,128)(2,1)S(1)}, u32[]{:S(2)}, u32[]{:S(2)}) collective-permute-start(bf16[136,512]{1,0:T(8,128)(2,1)S(1)} %collective-permute-done.3.refs_1_), channel_id=1, source_target_pairs={{1,0},{0,1},{3,2},{2,3},{5,4},{4,5},{7,6},{6,7},{9,8},{8,9},{11,10... | collective-permute-start | bytes 417800 | tf_op jit(solution)/shard_map/ppermute | solution.py:114
  15.3 1.6 %collective-permute-start.7 = (bf16[136,512]{1,0:T(8,128)(2,1)S(1)}, bf16[136,512]{1,0:T(8,128)(2,1)S(1)}, u32[]{:S(2)}, u32[]{:S(2)}) collective-permute-start(bf16[136,512]{1,0:T(8,128)(2,1)S(1)} %collective-permute-done.2.refs_2_), channel_id=1, source_target_pairs={{1,0},{0,1},{3,2},{2,3},{5,4},{4,5},{7,6},{6,7},{9,8},{8,9},{11,10... | collective-permute-start | bytes 417800 | tf_op jit(solution)/shard_map/ppermute | solution.py:114
  15.8 1.4 %collective-permute-start.8 = (bf16[136,512]{1,0:T(8,128)(2,1)S(1)}, bf16[136,512]{1,0:T(8,128)(2,1)S(1)}, u32[]{:S(2)}, u32[]{:S(2)}) collective-permute-start(bf16[136,512]{1,0:T(8,128)(2,1)S(1)} %collective-permute-done.1.refs_3_), channel_id=1, source_target_pairs={{1,0},{0,1},{3,2},{2,3},{5,4},{4,5},{7,6},{6,7},{9,8},{8,9},{11,10... | collective-permute-start | bytes 417800 | tf_op jit(solution)/shard_map/ppermute | solution.py:114
  15.9 6.0 %collective-permute-start.11 = (bf16[136,512]{1,0:T(8,128)(2,1)S(1)}, bf16[136,512]{1,0:T(8,128)(2,1)S(1)}, u32[]{:S(2)}, u32[]{:S(2)}) collective-permute-start(bf16[136,512]{1,0:T(8,128)(2,1)S(1)} %collective-permute-done.refs_10_), channel_id=1, source_target_pairs={{8,0},{9,1},{10,2},{11,3},{12,4},{13,5},{14,6},{15,7},{0,8},{1,9},... | collective-permute-start | bytes 417800 | tf_op jit(solution)/shard_map/ppermute | solution.py:114
  18.6 5.4 %collective-permute-start.10 = (f32[1,128]{1,0:T(1,128)S(1)}, f32[1,128]{1,0:T(1,128)S(1)}, u32[]{:S(2)}, u32[]{:S(2)}) collective-permute-start(f32[1,128]{1,0:T(1,128)S(1)} %get-tuple-element.24), channel_id=1, source_target_pairs={{24,0},{25,1},{26,2},{27,3},{28,4},{29,5},{30,6},{31,7},{16,8},{17... | collective-permute-start | bytes 1544 | tf_op jit(solution)/shard_map/ppermute | solution.py:114
  19.9 4.1 %collective-permute-start.9 = (f32[1,128]{1,0:T(1,128)S(1)}, f32[1,128]{1,0:T(1,128)S(1)}, u32[]{:S(2)}, u32[]{:S(2)}) collective-permute-start(f32[1,128]{1,0:T(1,128)S(1)} %get-tuple-element.23), channel_id=1, source_target_pairs={{8,0},{9,1},{10,2},{11,3},{12,4},{13,5},{14,6},{15,7},{0,8},{1,9},... | collective-permute-start | bytes 1544 | tf_op jit(solution)/shard_map/ppermute | solution.py:114
  22.5 4.5 %collective-permute-start.12 = (f32[1,128]{1,0:T(1,128)S(1)}, f32[1,128]{1,0:T(1,128)S(1)}, u32[]{:S(2)}, u32[]{:S(2)}) collective-permute-start(f32[1,128]{1,0:T(1,128)S(1)} %shard_map.39), channel_id=1, source_target_pairs={{16,0},{17,1},{18,2},{19,3},{20,4},{21,5},{22,6},{23,7},{24,8},{25... | collective-permute-start | bytes 1544 | tf_op jit(solution)/shard_map/ppermute | solution.py:114

commit v17 on v14

--- a/solution.py
+++ b/solution.py
@@ -8,7 +8,7 @@
 from jax.experimental.pallas import tpu as pltpu
 from jax.sharding import PartitionSpec as P
 
-AUX = 16
+AUX = 8
 DIGIT = 256
 
 
@@ -131,9 +131,12 @@
             return permute(x, lambda z, a, g: (turned(z, s, length), a, g))
 
         half = length // 2 if length & (length - 1) == 0 else length
+        direct = list(range(1, half)) + ([length - 1] if half < length else [])
+        onward = [s for s in range(1, half) if half < length]
+        offsets = direct + [(length - 1) ^ s for s in onward]
         near = [permute(own, lambda z, a, g: (z, turned(a, s, wide), g)) for s in range(1, wide)]
-        first = [along(own, s) for s in range(1, min(half + 1, length))]
-        last = [along(first[half - 1], s) for s in range(1, length - half)]
+        first = [along(own, s) for s in direct]
+        last = [along(first[-1], s) for s in onward]
         far, far_rank = [], []
         for t in range(1, n_grp):
             for s in range(wide):
@@ -142,11 +145,12 @@
                 far_rank.append(rank(a=s, g=t))
         near = list(zip([own] + near, [rank(a=s) for s in range(wide)]))
         far = list(zip(far, far_rank))
-        visit_rank = [rank(z=s) for s in range(1, length)]
+        visit_rank = [rank(z=s) for s in offsets]
         first = list(zip(first, visit_rank))
         last = list(zip(last, visit_rank[len(first) :]))
         best = best_of(near + far, near[:1] + first + last, table, True)
-        found = [along(best[s], -s) for s in reversed(range(1, length))] + [best[0]]
+        back = sorted(zip(offsets, best[1:]), key=lambda pair: -pair[0])
+        found = [along(b, -s) for s, b in back] + [best[0]]
         return functools.reduce(jnp.maximum, found).reshape(rows)
 
     placed = (P(("clu", "grp"), None), P(("clu", "grp")), P())

time: 29 us -> 27.7 us (0.955)
  waiting for transfers between devices: 9.86 us -> 8.89 us
  starting transfers between devices: 15.6 us -> 15.2 us
    ppermute x13, waiting for transfers between devices: 9.86 us -> 8.89 us  [permute(): return lax.ppermute(x, ('clu', 'grp'), pairs)]
    ppermute x13, starting transfers between devices: 15.6 us -> 15.2 us  [permute(): return lax.ppermute(x, ('clu', 'grp'), pairs)]
where the time goes in v17:
time: 27.7 us; the launch traced here: 27.5 us
  starting transfers between devices  15.2 us (55%)
  waiting for transfers between devices  8.89 us (32%)
  Pallas kernels  2.9 us (10%)
  other arithmetic  0.52 us (2%)
    ppermute x13, starting transfers between devices, permute(): return lax.ppermute(x, ('clu', 'grp'), pairs)  15.2 us
    ppermute x13, waiting for transfers between devices, permute(): return lax.ppermute(x, ('clu', 'grp'), pairs)  8.89 us
    pallas_call x1, Pallas kernels, best_of(): pl.pallas_call(functools.partial(best_kernel, len(keys), own, ranks), out...  1.8 us
    pallas_call x1, Pallas kernels, pack(): pl.pallas_call(functools.partial(pack_kernel, groups), out_shape=[pltpu.V...  1.1 us
  transfers between devices with their start and end apart: 13, of which 7 were waited for; matrix products, arithmetic and copies ran while one was open for 0% of the time, Pallas kernels for 0%

profile of v17, /device:TPU:0, one launch (start us, length us, event | category | flops | bytes accessed | tf_op | source)
XLA Modules:
  0.0 27.5 jit_solution(1558469763324672108)
XLA Ops:
  0.0 1.1 %shard_map.37 = (bf16[136,512]{1,0:T(8,128)(2,1)S(1)}, bf16[64,64]{1,0:T(8,128)(2,1)S(1)}) custom-call(bf16[128,512]{1,0:T(8,128)(2,1)} %emb_ref.1, s32[1,128]{1,0:T(1,128)} %bitcast.4, s32[1,64]{1,0:T(1,128)} %bitcast.5), custom_call_target="tpu_custom_call" | custom-call | tf_op jit(solution)/shard_map/pallas_call | solution.py:38
  1.1 5.1 %collective-permute-start.8 = (bf16[136,512]{1,0:T(8,128)(2,1)S(1)}, bf16[136,512]{1,0:T(8,128)(2,1)S(1)}, u32[]{:S(2)}, u32[]{:S(2)}) collective-permute-start(bf16[136,512]{1,0:T(8,128)(2,1)S(1)} %get-tuple-element.12.refs_0_.refs_8_), channel_id=1, source_target_pairs={{24,0},{25,1},{26,2},{27,3},{28,4},{29,5},{30,6},{31,7},{16,8},{17... | collective-permute-start | bytes 417800 | tf_op jit(solution)/shard_map/ppermute | solution.py:114
  6.2 0.0 collective-permute-start.7
  6.2 2.4 %collective-permute-start.2 = (bf16[136,512]{1,0:T(8,128)(2,1)S(1)}, bf16[136,512]{1,0:T(8,128)(2,1)S(1)}, u32[]{:S(2)}, u32[]{:S(2)}) collective-permute-start(bf16[136,512]{1,0:T(8,128)(2,1)S(1)} %get-tuple-element.12.refs_0_.refs_8_), channel_id=1, source_target_pairs={{6,0},{7,1},{4,2},{5,3},{2,4},{3,5},{0,6},{1,7},{14,8},{15,9},{12,... | collective-permute-start | bytes 417800 | tf_op jit(solution)/shard_map/ppermute | solution.py:114
  8.7 0.5 %collective-permute-start.1 = (bf16[136,512]{1,0:T(8,128)(2,1)S(1)}, bf16[136,512]{1,0:T(8,128)(2,1)S(1)}, u32[]{:S(2)}, u32[]{:S(2)}) collective-permute-start(bf16[136,512]{1,0:T(8,128)(2,1)S(1)} %get-tuple-element.12.refs_0_.refs_8_), channel_id=1, source_target_pairs={{4,0},{5,1},{6,2},{7,3},{0,4},{1,5},{2,6},{3,7},{12,8},{13,9},{14,... | collective-permute-start | bytes 417800 | tf_op jit(solution)/shard_map/ppermute | solution.py:114
  9.2 0.5 %collective-permute-start = (bf16[136,512]{1,0:T(8,128)(2,1)S(1)}, bf16[136,512]{1,0:T(8,128)(2,1)S(1)}, u32[]{:S(2)}, u32[]{:S(2)}) collective-permute-start(bf16[136,512]{1,0:T(8,128)(2,1)S(1)} %get-tuple-element.12.refs_0_.refs_8_), channel_id=1, source_target_pairs={{2,0},{3,1},{0,2},{1,3},{6,4},{7,5},{4,6},{5,7},{10,8},{11,9},{8,1... | collective-permute-start | bytes 417800 | tf_op jit(solution)/shard_map/ppermute | solution.py:114
  9.7 1.1 %collective-permute-done.8.refs_10_ = bf16[136,512]{1,0:T(8,128)(2,1)S(1)} collective-permute-done((bf16[136,512]{1,0:T(8,128)(2,1)S(1)}, bf16[136,512]{1,0:T(8,128)(2,1)S(1)}, u32[]{:S(2)}, u32[]{:S(2)}) %collective-permute-start.8) | collective-permute-done | bytes 139296 | tf_op jit(solution)/shard_map/ppermute | solution.py:114
  10.8 0.0 collective-permute-start.3
  10.8 2.2 %collective-permute-done.7.refs_9_ = bf16[136,512]{1,0:T(8,128)(2,1)S(1)} collective-permute-done((bf16[136,512]{1,0:T(8,128)(2,1)S(1)}, bf16[136,512]{1,0:T(8,128)(2,1)S(1)}, u32[]{:S(2)}, u32[]{:S(2)}) %collective-permute-start.7) | collective-permute-done | bytes 139296 | tf_op jit(solution)/shard_map/ppermute | solution.py:114
  13.0 1.7 %collective-permute-start.9 = (bf16[136,512]{1,0:T(8,128)(2,1)S(1)}, bf16[136,512]{1,0:T(8,128)(2,1)S(1)}, u32[]{:S(2)}, u32[]{:S(2)}) collective-permute-start(bf16[136,512]{1,0:T(8,128)(2,1)S(1)} %collective-permute-done.8.refs_10_), channel_id=1, source_target_pairs={{8,0},{9,1},{10,2},{11,3},{12,4},{13,5},{14,6},{15,7},{0,8},{1,9},... | collective-permute-start | bytes 417800 | tf_op jit(solution)/shard_map/ppermute | solution.py:114
  14.7 0.0 collective-permute-done.2.refs_3_
  14.7 0.0 collective-permute-start.6
  14.7 0.6 %collective-permute-done.1.refs_2_ = bf16[136,512]{1,0:T(8,128)(2,1)S(1)} collective-permute-done((bf16[136,512]{1,0:T(8,128)(2,1)S(1)}, bf16[136,512]{1,0:T(8,128)(2,1)S(1)}, u32[]{:S(2)}, u32[]{:S(2)}) %collective-permute-start.1) | collective-permute-done | bytes 139296 | tf_op jit(solution)/shard_map/ppermute | solution.py:114
  15.2 0.0 collective-permute-start.5
  15.2 0.1 collective-permute-done.refs_1_
  15.3 0.5 %collective-permute-start.4 = (bf16[136,512]{1,0:T(8,128)(2,1)S(1)}, bf16[136,512]{1,0:T(8,128)(2,1)S(1)}, u32[]{:S(2)}, u32[]{:S(2)}) collective-permute-start(bf16[136,512]{1,0:T(8,128)(2,1)S(1)} %collective-permute-done.refs_1_), channel_id=1, source_target_pairs={{1,0},{0,1},{3,2},{2,3},{5,4},{4,5},{7,6},{6,7},{9,8},{8,9},{11,10... | collective-permute-start | bytes 417800 | tf_op jit(solution)/shard_map/ppermute | solution.py:114
  15.8 0.0 collective-permute-done.3.refs_4_
  15.8 2.6 %collective-permute-done.9.refs_11_ = bf16[136,512]{1,0:T(8,128)(2,1)S(1)} collective-permute-done((bf16[136,512]{1,0:T(8,128)(2,1)S(1)}, bf16[136,512]{1,0:T(8,128)(2,1)S(1)}, u32[]{:S(2)}, u32[]{:S(2)}) %collective-permute-start.9) | collective-permute-done | bytes 139296 | tf_op jit(solution)/shard_map/ppermute | solution.py:114
  18.4 0.0 collective-permute-done.6.refs_7_
  18.4 0.0 collective-permute-done.5.refs_6_
  18.4 0.0 collective-permute-done.4.refs_5_
  18.4 1.8 %shard_map.38 = (f32[1,128]{1,0:T(1,128)S(1)}, f32[1,128]{1,0:T(1,128)S(1)}, f32[1,128]{1,0:T(1,128)S(1)}, f32[1,128]{1,0:T(1,128)S(1)}) custom-call(bf16[64,64]{1,0:T(8,128)(2,1)S(1)} %get-tuple-element.11.table_ref, bf16[136,512]{1,0:T(8,128)(2,1)S(1)} %get-tuple-element.12.refs_0_.refs_8_, bf16[136,512]{1,0:T(8,128)(2,1)S(1)} %collective-permute-done.refs_1_, ...), custom_call_target="tpu_custom_call" | custom-call | flops 536870912 | bytes 1572864 | tf_op jit(solution)/shard_map/pallas_call | solution.py:89
  20.2 2.4 %collective-permute-start.10 = (f32[1,128]{1,0:T(1,128)S(1)}, f32[1,128]{1,0:T(1,128)S(1)}, u32[]{:S(2)}, u32[]{:S(2)}) collective-permute-start(f32[1,128]{1,0:T(1,128)S(1)} %get-tuple-element.13), channel_id=1, source_target_pairs={{24,0},{25,1},{26,2},{27,3},{28,4},{29,5},{30,6},{31,7},{16,8},{17... | collective-permute-start | bytes 1544 | tf_op jit(solution)/shard_map/ppermute | solution.py:114
  22.6 0.5 %collective-permute-start.11 = (f32[1,128]{1,0:T(1,128)S(1)}, f32[1,128]{1,0:T(1,128)S(1)}, u32[]{:S(2)}, u32[]{:S(2)}) collective-permute-start(f32[1,128]{1,0:T(1,128)S(1)} %get-tuple-element.14), channel_id=1, source_target_pairs={{16,0},{17,1},{18,2},{19,3},{20,4},{21,5},{22,6},{23,7},{24,8},{25... | collective-permute-start | bytes 1544 | tf_op jit(solution)/shard_map/ppermute | solution.py:114
  23.1 1.6 %collective-permute-start.12 = (f32[1,128]{1,0:T(1,128)S(1)}, f32[1,128]{1,0:T(1,128)S(1)}, u32[]{:S(2)}, u32[]{:S(2)}) collective-permute-start(f32[1,128]{1,0:T(1,128)S(1)} %get-tuple-element.15), channel_id=1, source_target_pairs={{8,0},{9,1},{10,2},{11,3},{12,4},{13,5},{14,6},{15,7},{0,8},{1,9},... | collective-permute-start | bytes 1544 | tf_op jit(solution)/shard_map/ppermute | solution.py:114
  24.7 0.9 %collective-permute-done.10 = f32[1,128]{1,0:T(1,128)S(1)} collective-permute-done((f32[1,128]{1,0:T(1,128)S(1)}, f32[1,128]{1,0:T(1,128)S(1)}, u32[]{:S(2)}, u32[]{:S(2)}) %collective-permute-start.10) | collective-permute-done | bytes 544 | tf_op jit(solution)/shard_map/ppermute | solution.py:114
  25.6 1.4 %collective-permute-done.11 = f32[1,128]{1,0:T(1,128)S(1)} collective-permute-done((f32[1,128]{1,0:T(1,128)S(1)}, f32[1,128]{1,0:T(1,128)S(1)}, u32[]{:S(2)}, u32[]{:S(2)}) %collective-permute-start.11) | collective-permute-done | bytes 544 | tf_op jit(solution)/shard_map/ppermute | solution.py:114
  27.0 0.0 collective-permute-done.12
  27.0 0.5 %maximum_bitcast_fusion = f32[128]{0:T(128)} fusion(f32[1,128]{1,0:T(1,128)S(1)} %get-tuple-element.16, f32[1,128]{1,0:T(1,128)S(1)} %collective-permute-done.12, f32[1,128]{1,0:T(1,128)S(1)} %collective-permute-done.10, f32[1,128]{1,0:T(1,128)S(1)} %collective-permute-done.11), kind=kLoop, calls=%fused_computation | loop fusion | flops 384 | bytes 2560 | tf_op jit(solution)/shard_map/reshape | solution.py:154
Async XLA Ops:
  1.1 9.7 %collective-permute-start.8 = (bf16[136,512]{1,0:T(8,128)(2,1)S(1)}, bf16[136,512]{1,0:T(8,128)(2,1)S(1)}, u32[]{:S(2)}, u32[]{:S(2)}) collective-permute-start(bf16[136,512]{1,0:T(8,128)(2,1)S(1)} %get-tuple-element.12.refs_0_.refs_8_), channel_id=1, source_target_pairs={{24,0},{25,1},{26,2},{27,3},{28,4},{29,5},{30,6},{31,7},{16,8},{17... | collective-permute-start | bytes 417800 | tf_op jit(solution)/shard_map/ppermute | solution.py:114
  6.2 6.8 %collective-permute-start.7 = (bf16[136,512]{1,0:T(8,128)(2,1)S(1)}, bf16[136,512]{1,0:T(8,128)(2,1)S(1)}, u32[]{:S(2)}, u32[]{:S(2)}) collective-permute-start(bf16[136,512]{1,0:T(8,128)(2,1)S(1)} %get-tuple-element.12.refs_0_.refs_8_), channel_id=1, source_target_pairs={{8,0},{9,1},{10,2},{11,3},{12,4},{13,5},{14,6},{15,7},{0,8},{1,9},... | collective-permute-start | bytes 417800 | tf_op jit(solution)/shard_map/ppermute | solution.py:114
  6.2 8.4 %collective-permute-start.2 = (bf16[136,512]{1,0:T(8,128)(2,1)S(1)}, bf16[136,512]{1,0:T(8,128)(2,1)S(1)}, u32[]{:S(2)}, u32[]{:S(2)}) collective-permute-start(bf16[136,512]{1,0:T(8,128)(2,1)S(1)} %get-tuple-element.12.refs_0_.refs_8_), channel_id=1, source_target_pairs={{6,0},{7,1},{4,2},{5,3},{2,4},{3,5},{0,6},{1,7},{14,8},{15,9},{12,... | collective-permute-start | bytes 417800 | tf_op jit(solution)/shard_map/ppermute | solution.py:114
  8.7 6.6 %collective-permute-start.1 = (bf16[136,512]{1,0:T(8,128)(2,1)S(1)}, bf16[136,512]{1,0:T(8,128)(2,1)S(1)}, u32[]{:S(2)}, u32[]{:S(2)}) collective-permute-start(bf16[136,512]{1,0:T(8,128)(2,1)S(1)} %get-tuple-element.12.refs_0_.refs_8_), channel_id=1, source_target_pairs={{4,0},{5,1},{6,2},{7,3},{0,4},{1,5},{2,6},{3,7},{12,8},{13,9},{14,... | collective-permute-start | bytes 417800 | tf_op jit(solution)/shard_map/ppermute | solution.py:114
  9.2 6.1 %collective-permute-start = (bf16[136,512]{1,0:T(8,128)(2,1)S(1)}, bf16[136,512]{1,0:T(8,128)(2,1)S(1)}, u32[]{:S(2)}, u32[]{:S(2)}) collective-permute-start(bf16[136,512]{1,0:T(8,128)(2,1)S(1)} %get-tuple-element.12.refs_0_.refs_8_), channel_id=1, source_target_pairs={{2,0},{3,1},{0,2},{1,3},{6,4},{7,5},{4,6},{5,7},{10,8},{11,9},{8,1... | collective-permute-start | bytes 417800 | tf_op jit(solution)/shard_map/ppermute | solution.py:114
  10.8 5.0 %collective-permute-start.3 = (bf16[136,512]{1,0:T(8,128)(2,1)S(1)}, bf16[136,512]{1,0:T(8,128)(2,1)S(1)}, u32[]{:S(2)}, u32[]{:S(2)}) collective-permute-start(bf16[136,512]{1,0:T(8,128)(2,1)S(1)} %get-tuple-element.12.refs_0_.refs_8_), channel_id=1, source_target_pairs={{1,0},{0,1},{3,2},{2,3},{5,4},{4,5},{7,6},{6,7},{9,8},{8,9},{11,10... | collective-permute-start | bytes 417800 | tf_op jit(solution)/shard_map/ppermute | solution.py:114
  13.0 5.4 %collective-permute-start.9 = (bf16[136,512]{1,0:T(8,128)(2,1)S(1)}, bf16[136,512]{1,0:T(8,128)(2,1)S(1)}, u32[]{:S(2)}, u32[]{:S(2)}) collective-permute-start(bf16[136,512]{1,0:T(8,128)(2,1)S(1)} %collective-permute-done.8.refs_10_), channel_id=1, source_target_pairs={{8,0},{9,1},{10,2},{11,3},{12,4},{13,5},{14,6},{15,7},{0,8},{1,9},... | collective-permute-start | bytes 417800 | tf_op jit(solution)/shard_map/ppermute | solution.py:114
  14.7 3.7 %collective-permute-start.6 = (bf16[136,512]{1,0:T(8,128)(2,1)S(1)}, bf16[136,512]{1,0:T(8,128)(2,1)S(1)}, u32[]{:S(2)}, u32[]{:S(2)}) collective-permute-start(bf16[136,512]{1,0:T(8,128)(2,1)S(1)} %collective-permute-done.2.refs_3_), channel_id=1, source_target_pairs={{1,0},{0,1},{3,2},{2,3},{5,4},{4,5},{7,6},{6,7},{9,8},{8,9},{11,10... | collective-permute-start | bytes 417800 | tf_op jit(solution)/shard_map/ppermute | solution.py:114
  15.2 3.2 %collective-permute-start.5 = (bf16[136,512]{1,0:T(8,128)(2,1)S(1)}, bf16[136,512]{1,0:T(8,128)(2,1)S(1)}, u32[]{:S(2)}, u32[]{:S(2)}) collective-permute-start(bf16[136,512]{1,0:T(8,128)(2,1)S(1)} %collective-permute-done.1.refs_2_), channel_id=1, source_target_pairs={{1,0},{0,1},{3,2},{2,3},{5,4},{4,5},{7,6},{6,7},{9,8},{8,9},{11,10... | collective-permute-start | bytes 417800 | tf_op jit(solution)/shard_map/ppermute | solution.py:114
  15.3 3.1 %collective-permute-start.4 = (bf16[136,512]{1,0:T(8,128)(2,1)S(1)}, bf16[136,512]{1,0:T(8,128)(2,1)S(1)}, u32[]{:S(2)}, u32[]{:S(2)}) collective-permute-start(bf16[136,512]{1,0:T(8,128)(2,1)S(1)} %collective-permute-done.refs_1_), channel_id=1, source_target_pairs={{1,0},{0,1},{3,2},{2,3},{5,4},{4,5},{7,6},{6,7},{9,8},{8,9},{11,10... | collective-permute-start | bytes 417800 | tf_op jit(solution)/shard_map/ppermute | solution.py:114
  20.2 5.4 %collective-permute-start.10 = (f32[1,128]{1,0:T(1,128)S(1)}, f32[1,128]{1,0:T(1,128)S(1)}, u32[]{:S(2)}, u32[]{:S(2)}) collective-permute-start(f32[1,128]{1,0:T(1,128)S(1)} %get-tuple-element.13), channel_id=1, source_target_pairs={{24,0},{25,1},{26,2},{27,3},{28,4},{29,5},{30,6},{31,7},{16,8},{17... | collective-permute-start | bytes 1544 | tf_op jit(solution)/shard_map/ppermute | solution.py:114
  22.6 4.4 %collective-permute-start.11 = (f32[1,128]{1,0:T(1,128)S(1)}, f32[1,128]{1,0:T(1,128)S(1)}, u32[]{:S(2)}, u32[]{:S(2)}) collective-permute-start(f32[1,128]{1,0:T(1,128)S(1)} %get-tuple-element.14), channel_id=1, source_target_pairs={{16,0},{17,1},{18,2},{19,3},{20,4},{21,5},{22,6},{23,7},{24,8},{25... | collective-permute-start | bytes 1544 | tf_op jit(solution)/shard_map/ppermute | solution.py:114
  23.1 4.0 %collective-permute-start.12 = (f32[1,128]{1,0:T(1,128)S(1)}, f32[1,128]{1,0:T(1,128)S(1)}, u32[]{:S(2)}, u32[]{:S(2)}) collective-permute-start(f32[1,128]{1,0:T(1,128)S(1)} %get-tuple-element.15), channel_id=1, source_target_pairs={{8,0},{9,1},{10,2},{11,3},{12,4},{13,5},{14,6},{15,7},{0,8},{1,9},... | collective-permute-start | bytes 1544 | tf_op jit(solution)/shard_map/ppermute | solution.py:114

commit v18 on v17

--- a/solution.py
+++ b/solution.py
@@ -137,10 +137,11 @@
         near = [permute(own, lambda z, a, g: (z, turned(a, s, wide), g)) for s in range(1, wide)]
         first = [along(own, s) for s in direct]
         last = [along(first[-1], s) for s in onward]
+        near[0], mine = lax.optimization_barrier((near[0], own))
         far, far_rank = [], []
         for t in range(1, n_grp):
             for s in range(wide):
-                block = near[s - 1] if s else own
+                block = near[s - 1] if s else mine
                 far.append(permute(block, lambda z, a, g: (z, a, turned(g, t, n_grp))))
                 far_rank.append(rank(a=s, g=t))
         near = list(zip([own] + near, [rank(a=s) for s in range(wide)]))

time: 27.7 us -> 28.2 us (1.018)
  waiting for transfers between devices: 8.89 us -> 9.61 us
    ppermute x13, waiting for transfers between devices: 8.89 us -> 9.61 us  [permute(): return lax.ppermute(x, ('clu', 'grp'), pairs)]
where the time goes in v18:
time: 28.2 us; the launch traced here: 28 us
  starting transfers between devices  15 us (53%)
  waiting for transfers between devices  9.61 us (34%)
  Pallas kernels  2.9 us (10%)
  other arithmetic  0.52 us (2%)
    ppermute x13, starting transfers between devices, permute(): return lax.ppermute(x, ('clu', 'grp'), pairs)  15 us
    ppermute x13, waiting for transfers between devices, permute(): return lax.ppermute(x, ('clu', 'grp'), pairs)  9.61 us
    pallas_call x1, Pallas kernels, best_of(): pl.pallas_call(functools.partial(best_kernel, len(keys), own, ranks), out...  1.79 us
    pallas_call x1, Pallas kernels, pack(): pl.pallas_call(functools.partial(pack_kernel, groups), out_shape=[pltpu.V...  1.1 us
  transfers between devices with their start and end apart: 13, of which 7 were waited for; matrix products, arithmetic and copies ran while one was open for 0% of the time, Pallas kernels for 0%

profile of v18, /device:TPU:0, one launch (start us, length us, event | category | flops | bytes accessed | tf_op | source)
XLA Modules:
  0.0 28.0 jit_solution(9390299362969286093)
XLA Ops:
  0.0 1.1 %shard_map.37 = (bf16[136,512]{1,0:T(8,128)(2,1)S(1)}, bf16[64,64]{1,0:T(8,128)(2,1)S(1)}) custom-call(bf16[128,512]{1,0:T(8,128)(2,1)} %emb_ref.1, s32[1,128]{1,0:T(1,128)} %bitcast.4, s32[1,64]{1,0:T(1,128)} %bitcast.5), custom_call_target="tpu_custom_call" | custom-call | tf_op jit(solution)/shard_map/pallas_call | solution.py:38
  1.1 3.0 %collective-permute-start = (bf16[136,512]{1,0:T(8,128)(2,1)S(1)}, bf16[136,512]{1,0:T(8,128)(2,1)S(1)}, u32[]{:S(2)}, u32[]{:S(2)}) collective-permute-start(bf16[136,512]{1,0:T(8,128)(2,1)S(1)} %get-tuple-element.16.refs_0_.refs_8_), channel_id=1, source_target_pairs={{2,0},{3,1},{0,2},{1,3},{6,4},{7,5},{4,6},{5,7},{10,8},{11,9},{8,1... | collective-permute-start | bytes 417800 | tf_op jit(solution)/shard_map/ppermute | solution.py:114
  4.1 3.6 %collective-permute-start.8 = (bf16[136,512]{1,0:T(8,128)(2,1)S(1)}, bf16[136,512]{1,0:T(8,128)(2,1)S(1)}, u32[]{:S(2)}, u32[]{:S(2)}) collective-permute-start(bf16[136,512]{1,0:T(8,128)(2,1)S(1)} %get-tuple-element.16.refs_0_.refs_8_), channel_id=1, source_target_pairs={{24,0},{25,1},{26,2},{27,3},{28,4},{29,5},{30,6},{31,7},{16,8},{17... | collective-permute-start | bytes 417800 | tf_op jit(solution)/shard_map/ppermute | solution.py:114
  7.7 1.5 %collective-permute-start.2 = (bf16[136,512]{1,0:T(8,128)(2,1)S(1)}, bf16[136,512]{1,0:T(8,128)(2,1)S(1)}, u32[]{:S(2)}, u32[]{:S(2)}) collective-permute-start(bf16[136,512]{1,0:T(8,128)(2,1)S(1)} %get-tuple-element.16.refs_0_.refs_8_), channel_id=1, source_target_pairs={{6,0},{7,1},{4,2},{5,3},{2,4},{3,5},{0,6},{1,7},{14,8},{15,9},{12,... | collective-permute-start | bytes 417800 | tf_op jit(solution)/shard_map/ppermute | solution.py:114
  9.2 0.5 %collective-permute-start.1 = (bf16[136,512]{1,0:T(8,128)(2,1)S(1)}, bf16[136,512]{1,0:T(8,128)(2,1)S(1)}, u32[]{:S(2)}, u32[]{:S(2)}) collective-permute-start(bf16[136,512]{1,0:T(8,128)(2,1)S(1)} %get-tuple-element.16.refs_0_.refs_8_), channel_id=1, source_target_pairs={{4,0},{5,1},{6,2},{7,3},{0,4},{1,5},{2,6},{3,7},{12,8},{13,9},{14,... | collective-permute-start | bytes 417800 | tf_op jit(solution)/shard_map/ppermute | solution.py:114
  9.7 0.0 collective-permute-start.7
  9.7 0.0 collective-permute-done.refs_1_
  9.7 0.0 collective-permute-start.3
  9.7 2.7 %collective-permute-done.8.refs_10_ = bf16[136,512]{1,0:T(8,128)(2,1)S(1)} collective-permute-done((bf16[136,512]{1,0:T(8,128)(2,1)S(1)}, bf16[136,512]{1,0:T(8,128)(2,1)S(1)}, u32[]{:S(2)}, u32[]{:S(2)}) %collective-permute-start.8) | collective-permute-done | bytes 139296 | tf_op jit(solution)/shard_map/ppermute | solution.py:114
  12.4 1.4 %collective-permute-start.9 = (bf16[136,512]{1,0:T(8,128)(2,1)S(1)}, bf16[136,512]{1,0:T(8,128)(2,1)S(1)}, u32[]{:S(2)}, u32[]{:S(2)}) collective-permute-start(bf16[136,512]{1,0:T(8,128)(2,1)S(1)} %collective-permute-done.8.refs_10_), channel_id=1, source_target_pairs={{8,0},{9,1},{10,2},{11,3},{12,4},{13,5},{14,6},{15,7},{0,8},{1,9},... | collective-permute-start | bytes 417800 | tf_op jit(solution)/shard_map/ppermute | solution.py:114
  13.8 0.0 collective-permute-done.2.refs_3_
  13.8 0.0 collective-permute-start.6
  13.8 2.6 %collective-permute-done.1.refs_2_ = bf16[136,512]{1,0:T(8,128)(2,1)S(1)} collective-permute-done((bf16[136,512]{1,0:T(8,128)(2,1)S(1)}, bf16[136,512]{1,0:T(8,128)(2,1)S(1)}, u32[]{:S(2)}, u32[]{:S(2)}) %collective-permute-start.1) | collective-permute-done | bytes 139296 | tf_op jit(solution)/shard_map/ppermute | solution.py:114
  16.5 0.0 collective-permute-start.5
  16.5 0.0 collective-permute-done.7.refs_9_
  16.5 0.5 %collective-permute-start.4 = (bf16[136,512]{1,0:T(8,128)(2,1)S(1)}, bf16[136,512]{1,0:T(8,128)(2,1)S(1)}, u32[]{:S(2)}, u32[]{:S(2)}) collective-permute-start(bf16[136,512]{1,0:T(8,128)(2,1)S(1)} %collective-permute-done.refs_1_), channel_id=1, source_target_pairs={{1,0},{0,1},{3,2},{2,3},{5,4},{4,5},{7,6},{6,7},{9,8},{8,9},{11,10... | collective-permute-start | bytes 417800 | tf_op jit(solution)/shard_map/ppermute | solution.py:114
  17.0 0.8 %collective-permute-done.9.refs_11_ = bf16[136,512]{1,0:T(8,128)(2,1)S(1)} collective-permute-done((bf16[136,512]{1,0:T(8,128)(2,1)S(1)}, bf16[136,512]{1,0:T(8,128)(2,1)S(1)}, u32[]{:S(2)}, u32[]{:S(2)}) %collective-permute-start.9) | collective-permute-done | bytes 139296 | tf_op jit(solution)/shard_map/ppermute | solution.py:114
  17.8 0.0 collective-permute-done.6.refs_7_
  17.8 0.1 collective-permute-done.5.refs_6_
  17.8 0.0 collective-permute-done.3.refs_4_
  17.8 0.2 collective-permute-done.4.refs_5_
  18.0 1.8 %shard_map.38 = (f32[1,128]{1,0:T(1,128)S(1)}, f32[1,128]{1,0:T(1,128)S(1)}, f32[1,128]{1,0:T(1,128)S(1)}, f32[1,128]{1,0:T(1,128)S(1)}) custom-call(bf16[64,64]{1,0:T(8,128)(2,1)S(1)} %get-tuple-element.13.table_ref, bf16[136,512]{1,0:T(8,128)(2,1)S(1)} %get-tuple-element.16.refs_0_.refs_8_, bf16[136,512]{1,0:T(8,128)(2,1)S(1)} %collective-permute-done.refs_1_, ...), custom_call_target="tpu_custom_call" | custom-call | flops 536870912 | bytes 1572864 | tf_op jit(solution)/shard_map/pallas_call | solution.py:89
  19.8 3.3 %collective-permute-start.10 = (f32[1,128]{1,0:T(1,128)S(1)}, f32[1,128]{1,0:T(1,128)S(1)}, u32[]{:S(2)}, u32[]{:S(2)}) collective-permute-start(f32[1,128]{1,0:T(1,128)S(1)} %get-tuple-element.17), channel_id=1, source_target_pairs={{24,0},{25,1},{26,2},{27,3},{28,4},{29,5},{30,6},{31,7},{16,8},{17... | collective-permute-start | bytes 1544 | tf_op jit(solution)/shard_map/ppermute | solution.py:114
  23.1 0.0 collective-permute-start.11
  23.1 1.2 %collective-permute-start.12 = (f32[1,128]{1,0:T(1,128)S(1)}, f32[1,128]{1,0:T(1,128)S(1)}, u32[]{:S(2)}, u32[]{:S(2)}) collective-permute-start(f32[1,128]{1,0:T(1,128)S(1)} %get-tuple-element.19), channel_id=1, source_target_pairs={{8,0},{9,1},{10,2},{11,3},{12,4},{13,5},{14,6},{15,7},{0,8},{1,9},... | collective-permute-start | bytes 1544 | tf_op jit(solution)/shard_map/ppermute | solution.py:114
  24.3 0.9 %collective-permute-done.10 = f32[1,128]{1,0:T(1,128)S(1)} collective-permute-done((f32[1,128]{1,0:T(1,128)S(1)}, f32[1,128]{1,0:T(1,128)S(1)}, u32[]{:S(2)}, u32[]{:S(2)}) %collective-permute-start.10) | collective-permute-done | bytes 544 | tf_op jit(solution)/shard_map/ppermute | solution.py:114
  25.2 2.3 %collective-permute-done.11 = f32[1,128]{1,0:T(1,128)S(1)} collective-permute-done((f32[1,128]{1,0:T(1,128)S(1)}, f32[1,128]{1,0:T(1,128)S(1)}, u32[]{:S(2)}, u32[]{:S(2)}) %collective-permute-start.11) | collective-permute-done | bytes 544 | tf_op jit(solution)/shard_map/ppermute | solution.py:114
  27.5 0.0 collective-permute-done.12
  27.5 0.5 %maximum_bitcast_fusion = f32[128]{0:T(128)} fusion(f32[1,128]{1,0:T(1,128)S(1)} %get-tuple-element.20, f32[1,128]{1,0:T(1,128)S(1)} %collective-permute-done.12, f32[1,128]{1,0:T(1,128)S(1)} %collective-permute-done.10, f32[1,128]{1,0:T(1,128)S(1)} %collective-permute-done.11), kind=kLoop, calls=%fused_computation | loop fusion | flops 384 | bytes 2560 | tf_op jit(solution)/shard_map/reshape | solution.py:155
Async XLA Ops:
  1.1 8.6 %collective-permute-start = (bf16[136,512]{1,0:T(8,128)(2,1)S(1)}, bf16[136,512]{1,0:T(8,128)(2,1)S(1)}, u32[]{:S(2)}, u32[]{:S(2)}) collective-permute-start(bf16[136,512]{1,0:T(8,128)(2,1)S(1)} %get-tuple-element.16.refs_0_.refs_8_), channel_id=1, source_target_pairs={{2,0},{3,1},{0,2},{1,3},{6,4},{7,5},{4,6},{5,7},{10,8},{11,9},{8,1... | collective-permute-start | bytes 417800 | tf_op jit(solution)/shard_map/ppermute | solution.py:114
  4.1 8.3 %collective-permute-start.8 = (bf16[136,512]{1,0:T(8,128)(2,1)S(1)}, bf16[136,512]{1,0:T(8,128)(2,1)S(1)}, u32[]{:S(2)}, u32[]{:S(2)}) collective-permute-start(bf16[136,512]{1,0:T(8,128)(2,1)S(1)} %get-tuple-element.16.refs_0_.refs_8_), channel_id=1, source_target_pairs={{24,0},{25,1},{26,2},{27,3},{28,4},{29,5},{30,6},{31,7},{16,8},{17... | collective-permute-start | bytes 417800 | tf_op jit(solution)/shard_map/ppermute | solution.py:114
  7.7 6.1 %collective-permute-start.2 = (bf16[136,512]{1,0:T(8,128)(2,1)S(1)}, bf16[136,512]{1,0:T(8,128)(2,1)S(1)}, u32[]{:S(2)}, u32[]{:S(2)}) collective-permute-start(bf16[136,512]{1,0:T(8,128)(2,1)S(1)} %get-tuple-element.16.refs_0_.refs_8_), channel_id=1, source_target_pairs={{6,0},{7,1},{4,2},{5,3},{2,4},{3,5},{0,6},{1,7},{14,8},{15,9},{12,... | collective-permute-start | bytes 417800 | tf_op jit(solution)/shard_map/ppermute | solution.py:114
  9.2 7.2 %collective-permute-start.1 = (bf16[136,512]{1,0:T(8,128)(2,1)S(1)}, bf16[136,512]{1,0:T(8,128)(2,1)S(1)}, u32[]{:S(2)}, u32[]{:S(2)}) collective-permute-start(bf16[136,512]{1,0:T(8,128)(2,1)S(1)} %get-tuple-element.16.refs_0_.refs_8_), channel_id=1, source_target_pairs={{4,0},{5,1},{6,2},{7,3},{0,4},{1,5},{2,6},{3,7},{12,8},{13,9},{14,... | collective-permute-start | bytes 417800 | tf_op jit(solution)/shard_map/ppermute | solution.py:114
  9.7 6.7 %collective-permute-start.7 = (bf16[136,512]{1,0:T(8,128)(2,1)S(1)}, bf16[136,512]{1,0:T(8,128)(2,1)S(1)}, u32[]{:S(2)}, u32[]{:S(2)}) collective-permute-start(bf16[136,512]{1,0:T(8,128)(2,1)S(1)} %get-tuple-element.16.refs_0_.refs_8_), channel_id=1, source_target_pairs={{8,0},{9,1},{10,2},{11,3},{12,4},{13,5},{14,6},{15,7},{0,8},{1,9},... | collective-permute-start | bytes 417800 | tf_op jit(solution)/shard_map/ppermute | solution.py:114
  9.7 8.1 %collective-permute-start.3 = (bf16[136,512]{1,0:T(8,128)(2,1)S(1)}, bf16[136,512]{1,0:T(8,128)(2,1)S(1)}, u32[]{:S(2)}, u32[]{:S(2)}) collective-permute-start(bf16[136,512]{1,0:T(8,128)(2,1)S(1)} %get-tuple-element.16.refs_0_.refs_8_), channel_id=1, source_target_pairs={{1,0},{0,1},{3,2},{2,3},{5,4},{4,5},{7,6},{6,7},{9,8},{8,9},{11,10... | collective-permute-start | bytes 417800 | tf_op jit(solution)/shard_map/ppermute | solution.py:114
  12.4 5.3 %collective-permute-start.9 = (bf16[136,512]{1,0:T(8,128)(2,1)S(1)}, bf16[136,512]{1,0:T(8,128)(2,1)S(1)}, u32[]{:S(2)}, u32[]{:S(2)}) collective-permute-start(bf16[136,512]{1,0:T(8,128)(2,1)S(1)} %collective-permute-done.8.refs_10_), channel_id=1, source_target_pairs={{8,0},{9,1},{10,2},{11,3},{12,4},{13,5},{14,6},{15,7},{0,8},{1,9},... | collective-permute-start | bytes 417800 | tf_op jit(solution)/shard_map/ppermute | solution.py:114
  13.8 3.9 %collective-permute-start.6 = (bf16[136,512]{1,0:T(8,128)(2,1)S(1)}, bf16[136,512]{1,0:T(8,128)(2,1)S(1)}, u32[]{:S(2)}, u32[]{:S(2)}) collective-permute-start(bf16[136,512]{1,0:T(8,128)(2,1)S(1)} %collective-permute-done.2.refs_3_), channel_id=1, source_target_pairs={{1,0},{0,1},{3,2},{2,3},{5,4},{4,5},{7,6},{6,7},{9,8},{8,9},{11,10... | collective-permute-start | bytes 417800 | tf_op jit(solution)/shard_map/ppermute | solution.py:114
  16.5 1.4 %collective-permute-start.5 = (bf16[136,512]{1,0:T(8,128)(2,1)S(1)}, bf16[136,512]{1,0:T(8,128)(2,1)S(1)}, u32[]{:S(2)}, u32[]{:S(2)}) collective-permute-start(bf16[136,512]{1,0:T(8,128)(2,1)S(1)} %collective-permute-done.1.refs_2_), channel_id=1, source_target_pairs={{1,0},{0,1},{3,2},{2,3},{5,4},{4,5},{7,6},{6,7},{9,8},{8,9},{11,10... | collective-permute-start | bytes 417800 | tf_op jit(solution)/shard_map/ppermute | solution.py:114
  16.5 1.6 %collective-permute-start.4 = (bf16[136,512]{1,0:T(8,128)(2,1)S(1)}, bf16[136,512]{1,0:T(8,128)(2,1)S(1)}, u32[]{:S(2)}, u32[]{:S(2)}) collective-permute-start(bf16[136,512]{1,0:T(8,128)(2,1)S(1)} %collective-permute-done.refs_1_), channel_id=1, source_target_pairs={{1,0},{0,1},{3,2},{2,3},{5,4},{4,5},{7,6},{6,7},{9,8},{8,9},{11,10... | collective-permute-start | bytes 417800 | tf_op jit(solution)/shard_map/ppermute | solution.py:114
  19.8 5.4 %collective-permute-start.10 = (f32[1,128]{1,0:T(1,128)S(1)}, f32[1,128]{1,0:T(1,128)S(1)}, u32[]{:S(2)}, u32[]{:S(2)}) collective-permute-start(f32[1,128]{1,0:T(1,128)S(1)} %get-tuple-element.17), channel_id=1, source_target_pairs={{24,0},{25,1},{26,2},{27,3},{28,4},{29,5},{30,6},{31,7},{16,8},{17... | collective-permute-start | bytes 1544 | tf_op jit(solution)/shard_map/ppermute | solution.py:114
  23.1 4.4 %collective-permute-start.11 = (f32[1,128]{1,0:T(1,128)S(1)}, f32[1,128]{1,0:T(1,128)S(1)}, u32[]{:S(2)}, u32[]{:S(2)}) collective-permute-start(f32[1,128]{1,0:T(1,128)S(1)} %get-tuple-element.18), channel_id=1, source_target_pairs={{16,0},{17,1},{18,2},{19,3},{20,4},{21,5},{22,6},{23,7},{24,8},{25... | collective-permute-start | bytes 1544 | tf_op jit(solution)/shard_map/ppermute | solution.py:114
  23.1 4.4 %collective-permute-start.12 = (f32[1,128]{1,0:T(1,128)S(1)}, f32[1,128]{1,0:T(1,128)S(1)}, u32[]{:S(2)}, u32[]{:S(2)}) collective-permute-start(f32[1,128]{1,0:T(1,128)S(1)} %get-tuple-element.19), channel_id=1, source_target_pairs={{8,0},{9,1},{10,2},{11,3},{12,4},{13,5},{14,6},{15,7},{0,8},{1,9},... | collective-permute-start | bytes 1544 | tf_op jit(solution)/shard_map/ppermute | solution.py:114

commit v19 on v18

--- a/solution.py
+++ b/solution.py
@@ -136,7 +136,9 @@
         offsets = direct + [(length - 1) ^ s for s in onward]
         near = [permute(own, lambda z, a, g: (z, turned(a, s, wide), g)) for s in range(1, wide)]
         first = [along(own, s) for s in direct]
-        last = [along(first[-1], s) for s in onward]
+        last = [
+            permute(first[-1], lambda z, a, g: (turned(z, s, length) if g or z < half else z, a, g)) for s in onward
+        ]
         near[0], mine = lax.optimization_barrier((near[0], own))
         far, far_rank = [], []
         for t in range(1, n_grp):

time: 28.2 us -> 28.3 us (level)
  starting transfers between devices: 15 us -> 16.9 us
  waiting for transfers between devices: 9.61 us -> 7.74 us
    ppermute x13, starting transfers between devices: 15 us -> 16.9 us  [permute(): return lax.ppermute(x, ('clu', 'grp'), pairs)]
    ppermute x13, waiting for transfers between devices: 9.61 us -> 7.74 us  [permute(): return lax.ppermute(x, ('clu', 'grp'), pairs)]
  transfers between devices with their start and end apart: 13 -> 13, of which waited for: 7 -> 5; matrix products, arithmetic and copies ran while one was open for 0% -> 0% of each run, Pallas kernels for 0% -> 0%
where the time goes in v19:
time: 28.3 us; the launch traced here: 28.2 us
  starting transfers between devices  16.9 us (60%)
  waiting for transfers between devices  7.74 us (27%)
  Pallas kernels  2.9 us (10%)
  other arithmetic  0.52 us (2%)
    ppermute x13, starting transfers between devices, permute(): return lax.ppermute(x, ('clu', 'grp'), pairs)  16.9 us
    ppermute x13, waiting for transfers between devices, permute(): return lax.ppermute(x, ('clu', 'grp'), pairs)  7.74 us
    pallas_call x1, Pallas kernels, best_of(): pl.pallas_call(functools.partial(best_kernel, len(keys), own, ranks), out...  1.79 us
    pallas_call x1, Pallas kernels, pack(): pl.pallas_call(functools.partial(pack_kernel, groups), out_shape=[pltpu.V...  1.1 us
  transfers between devices with their start and end apart: 13, of which 5 were waited for; matrix products, arithmetic and copies ran while one was open for 0% of the time, Pallas kernels for 0%

profile of v19, /device:TPU:0, one launch (start us, length us, event | category | flops | bytes accessed | tf_op | source)
XLA Modules:
  0.0 28.2 jit_solution(17690669921117100616)
XLA Ops:
  0.0 1.1 %shard_map.37 = (bf16[136,512]{1,0:T(8,128)(2,1)S(1)}, bf16[64,64]{1,0:T(8,128)(2,1)S(1)}) custom-call(bf16[128,512]{1,0:T(8,128)(2,1)} %emb_ref.1, s32[1,128]{1,0:T(1,128)} %bitcast.4, s32[1,64]{1,0:T(1,128)} %bitcast.5), custom_call_target="tpu_custom_call" | custom-call | tf_op jit(solution)/shard_map/pallas_call | solution.py:38
  1.1 3.0 %collective-permute-start = (bf16[136,512]{1,0:T(8,128)(2,1)S(1)}, bf16[136,512]{1,0:T(8,128)(2,1)S(1)}, u32[]{:S(2)}, u32[]{:S(2)}) collective-permute-start(bf16[136,512]{1,0:T(8,128)(2,1)S(1)} %get-tuple-element.16.refs_0_.refs_8_), channel_id=1, source_target_pairs={{2,0},{3,1},{0,2},{1,3},{6,4},{7,5},{4,6},{5,7},{10,8},{11,9},{8,1... | collective-permute-start | bytes 417800 | tf_op jit(solution)/shard_map/ppermute | solution.py:114
  4.1 3.6 %collective-permute-start.8 = (bf16[136,512]{1,0:T(8,128)(2,1)S(1)}, bf16[136,512]{1,0:T(8,128)(2,1)S(1)}, u32[]{:S(2)}, u32[]{:S(2)}) collective-permute-start(bf16[136,512]{1,0:T(8,128)(2,1)S(1)} %get-tuple-element.16.refs_0_.refs_8_), channel_id=1, source_target_pairs={{24,0},{25,1},{26,2},{27,3},{28,4},{29,5},{30,6},{31,7},{16,8},{17... | collective-permute-start | bytes 417800 | tf_op jit(solution)/shard_map/ppermute | solution.py:114
  7.7 1.5 %collective-permute-start.2 = (bf16[136,512]{1,0:T(8,128)(2,1)S(1)}, bf16[136,512]{1,0:T(8,128)(2,1)S(1)}, u32[]{:S(2)}, u32[]{:S(2)}) collective-permute-start(bf16[136,512]{1,0:T(8,128)(2,1)S(1)} %get-tuple-element.16.refs_0_.refs_8_), channel_id=1, source_target_pairs={{6,0},{7,1},{4,2},{5,3},{2,4},{3,5},{0,6},{1,7},{14,8},{15,9},{12,... | collective-permute-start | bytes 417800 | tf_op jit(solution)/shard_map/ppermute | solution.py:114
  9.2 0.5 %collective-permute-start.1 = (bf16[136,512]{1,0:T(8,128)(2,1)S(1)}, bf16[136,512]{1,0:T(8,128)(2,1)S(1)}, u32[]{:S(2)}, u32[]{:S(2)}) collective-permute-start(bf16[136,512]{1,0:T(8,128)(2,1)S(1)} %get-tuple-element.16.refs_0_.refs_8_), channel_id=1, source_target_pairs={{4,0},{5,1},{6,2},{7,3},{0,4},{1,5},{2,6},{3,7},{12,8},{13,9},{14,... | collective-permute-start | bytes 417800 | tf_op jit(solution)/shard_map/ppermute | solution.py:114
  9.7 0.0 collective-permute-start.7
  9.7 0.0 collective-permute-done.refs_1_
  9.7 0.0 collective-permute-start.3
  9.7 2.7 %collective-permute-done.8.refs_10_ = bf16[136,512]{1,0:T(8,128)(2,1)S(1)} collective-permute-done((bf16[136,512]{1,0:T(8,128)(2,1)S(1)}, bf16[136,512]{1,0:T(8,128)(2,1)S(1)}, u32[]{:S(2)}, u32[]{:S(2)}) %collective-permute-start.8) | collective-permute-done | bytes 139296 | tf_op jit(solution)/shard_map/ppermute | solution.py:114
  12.4 3.3 %collective-permute-start.9 = (bf16[136,512]{1,0:T(8,128)(2,1)S(1)}, bf16[136,512]{1,0:T(8,128)(2,1)S(1)}, u32[]{:S(2)}, u32[]{:S(2)}) collective-permute-start(bf16[136,512]{1,0:T(8,128)(2,1)S(1)} %collective-permute-done.8.refs_10_), channel_id=1, source_target_pairs={{8,0},{9,1},{10,2},{11,3},{12,4},{13,5},{14,6},{15,7},{0,8},{1,9},... | collective-permute-start | bytes 417800 | tf_op jit(solution)/shard_map/ppermute | solution.py:114
  15.7 0.0 collective-permute-done.2.refs_3_
  15.7 0.1 collective-permute-start.6
  15.8 0.7 %collective-permute-done.1.refs_2_ = bf16[136,512]{1,0:T(8,128)(2,1)S(1)} collective-permute-done((bf16[136,512]{1,0:T(8,128)(2,1)S(1)}, bf16[136,512]{1,0:T(8,128)(2,1)S(1)}, u32[]{:S(2)}, u32[]{:S(2)}) %collective-permute-start.1) | collective-permute-done | bytes 139296 | tf_op jit(solution)/shard_map/ppermute | solution.py:114
  16.5 0.0 collective-permute-start.5
  16.5 0.0 collective-permute-done.7.refs_9_
  16.5 0.5 %collective-permute-start.4 = (bf16[136,512]{1,0:T(8,128)(2,1)S(1)}, bf16[136,512]{1,0:T(8,128)(2,1)S(1)}, u32[]{:S(2)}, u32[]{:S(2)}) collective-permute-start(bf16[136,512]{1,0:T(8,128)(2,1)S(1)} %collective-permute-done.refs_1_), channel_id=1, source_target_pairs={{1,0},{0,1},{3,2},{2,3},{5,4},{4,5},{7,6},{6,7},{9,8},{8,9},{11,10... | collective-permute-start | bytes 417800 | tf_op jit(solution)/shard_map/ppermute | solution.py:114
  17.0 2.4 %collective-permute-done.9.refs_11_ = bf16[136,512]{1,0:T(8,128)(2,1)S(1)} collective-permute-done((bf16[136,512]{1,0:T(8,128)(2,1)S(1)}, bf16[136,512]{1,0:T(8,128)(2,1)S(1)}, u32[]{:S(2)}, u32[]{:S(2)}) %collective-permute-start.9) | collective-permute-done | bytes 139296 | tf_op jit(solution)/shard_map/ppermute | solution.py:114
  19.3 0.0 collective-permute-done.6.refs_7_
  19.4 0.0 collective-permute-done.5.refs_6_
  19.4 0.0 collective-permute-done.3.refs_4_
  19.4 0.0 collective-permute-done.4.refs_5_
  19.4 1.8 %shard_map.38 = (f32[1,128]{1,0:T(1,128)S(1)}, f32[1,128]{1,0:T(1,128)S(1)}, f32[1,128]{1,0:T(1,128)S(1)}, f32[1,128]{1,0:T(1,128)S(1)}) custom-call(bf16[64,64]{1,0:T(8,128)(2,1)S(1)} %get-tuple-element.13.table_ref, bf16[136,512]{1,0:T(8,128)(2,1)S(1)} %get-tuple-element.16.refs_0_.refs_8_, bf16[136,512]{1,0:T(8,128)(2,1)S(1)} %collective-permute-done.refs_1_, ...), custom_call_target="tpu_custom_call" | custom-call | flops 536870912 | bytes 1572864 | tf_op jit(solution)/shard_map/pallas_call | solution.py:89
  21.2 0.1 collective-permute-start.10
  21.3 2.9 %collective-permute-start.11 = (f32[1,128]{1,0:T(1,128)S(1)}, f32[1,128]{1,0:T(1,128)S(1)}, u32[]{:S(2)}, u32[]{:S(2)}) collective-permute-start(f32[1,128]{1,0:T(1,128)S(1)} %get-tuple-element.18), channel_id=1, source_target_pairs={{16,0},{17,1},{18,2},{19,3},{20,4},{21,5},{22,6},{23,7},{24,8},{25... | collective-permute-start | bytes 1544 | tf_op jit(solution)/shard_map/ppermute | solution.py:114
  24.1 1.5 %collective-permute-start.12 = (f32[1,128]{1,0:T(1,128)S(1)}, f32[1,128]{1,0:T(1,128)S(1)}, u32[]{:S(2)}, u32[]{:S(2)}) collective-permute-start(f32[1,128]{1,0:T(1,128)S(1)} %get-tuple-element.19), channel_id=1, source_target_pairs={{8,0},{9,1},{10,2},{11,3},{12,4},{13,5},{14,6},{15,7},{0,8},{1,9},... | collective-permute-start | bytes 1544 | tf_op jit(solution)/shard_map/ppermute | solution.py:114
  25.6 0.9 %collective-permute-done.10 = f32[1,128]{1,0:T(1,128)S(1)} collective-permute-done((f32[1,128]{1,0:T(1,128)S(1)}, f32[1,128]{1,0:T(1,128)S(1)}, u32[]{:S(2)}, u32[]{:S(2)}) %collective-permute-start.10) | collective-permute-done | bytes 544 | tf_op jit(solution)/shard_map/ppermute | solution.py:114
  26.6 0.0 collective-permute-done.11
  26.6 1.1 %collective-permute-done.12 = f32[1,128]{1,0:T(1,128)S(1)} collective-permute-done((f32[1,128]{1,0:T(1,128)S(1)}, f32[1,128]{1,0:T(1,128)S(1)}, u32[]{:S(2)}, u32[]{:S(2)}) %collective-permute-start.12) | collective-permute-done | bytes 544 | tf_op jit(solution)/shard_map/ppermute | solution.py:114
  27.6 0.5 %maximum_bitcast_fusion = f32[128]{0:T(128)} fusion(f32[1,128]{1,0:T(1,128)S(1)} %get-tuple-element.20, f32[1,128]{1,0:T(1,128)S(1)} %collective-permute-done.12, f32[1,128]{1,0:T(1,128)S(1)} %collective-permute-done.10, f32[1,128]{1,0:T(1,128)S(1)} %collective-permute-done.11), kind=kLoop, calls=%fused_computation | loop fusion | flops 384 | bytes 2560 | tf_op jit(solution)/shard_map/reshape | solution.py:157
Async XLA Ops:
  1.1 8.6 %collective-permute-start = (bf16[136,512]{1,0:T(8,128)(2,1)S(1)}, bf16[136,512]{1,0:T(8,128)(2,1)S(1)}, u32[]{:S(2)}, u32[]{:S(2)}) collective-permute-start(bf16[136,512]{1,0:T(8,128)(2,1)S(1)} %get-tuple-element.16.refs_0_.refs_8_), channel_id=1, source_target_pairs={{2,0},{3,1},{0,2},{1,3},{6,4},{7,5},{4,6},{5,7},{10,8},{11,9},{8,1... | collective-permute-start | bytes 417800 | tf_op jit(solution)/shard_map/ppermute | solution.py:114
  4.1 8.3 %collective-permute-start.8 = (bf16[136,512]{1,0:T(8,128)(2,1)S(1)}, bf16[136,512]{1,0:T(8,128)(2,1)S(1)}, u32[]{:S(2)}, u32[]{:S(2)}) collective-permute-start(bf16[136,512]{1,0:T(8,128)(2,1)S(1)} %get-tuple-element.16.refs_0_.refs_8_), channel_id=1, source_target_pairs={{24,0},{25,1},{26,2},{27,3},{28,4},{29,5},{30,6},{31,7},{16,8},{17... | collective-permute-start | bytes 417800 | tf_op jit(solution)/shard_map/ppermute | solution.py:114
  7.7 8.0 %collective-permute-start.2 = (bf16[136,512]{1,0:T(8,128)(2,1)S(1)}, bf16[136,512]{1,0:T(8,128)(2,1)S(1)}, u32[]{:S(2)}, u32[]{:S(2)}) collective-permute-start(bf16[136,512]{1,0:T(8,128)(2,1)S(1)} %get-tuple-element.16.refs_0_.refs_8_), channel_id=1, source_target_pairs={{6,0},{7,1},{4,2},{5,3},{2,4},{3,5},{0,6},{1,7},{14,8},{15,9},{12,... | collective-permute-start | bytes 417800 | tf_op jit(solution)/shard_map/ppermute | solution.py:114
  9.2 7.2 %collective-permute-start.1 = (bf16[136,512]{1,0:T(8,128)(2,1)S(1)}, bf16[136,512]{1,0:T(8,128)(2,1)S(1)}, u32[]{:S(2)}, u32[]{:S(2)}) collective-permute-start(bf16[136,512]{1,0:T(8,128)(2,1)S(1)} %get-tuple-element.16.refs_0_.refs_8_), channel_id=1, source_target_pairs={{4,0},{5,1},{6,2},{7,3},{0,4},{1,5},{2,6},{3,7},{12,8},{13,9},{14,... | collective-permute-start | bytes 417800 | tf_op jit(solution)/shard_map/ppermute | solution.py:114
  9.7 6.7 %collective-permute-start.7 = (bf16[136,512]{1,0:T(8,128)(2,1)S(1)}, bf16[136,512]{1,0:T(8,128)(2,1)S(1)}, u32[]{:S(2)}, u32[]{:S(2)}) collective-permute-start(bf16[136,512]{1,0:T(8,128)(2,1)S(1)} %get-tuple-element.16.refs_0_.refs_8_), channel_id=1, source_target_pairs={{8,0},{9,1},{10,2},{11,3},{12,4},{13,5},{14,6},{15,7},{0,8},{1,9},... | collective-permute-start | bytes 417800 | tf_op jit(solution)/shard_map/ppermute | solution.py:114
  9.7 9.6 %collective-permute-start.3 = (bf16[136,512]{1,0:T(8,128)(2,1)S(1)}, bf16[136,512]{1,0:T(8,128)(2,1)S(1)}, u32[]{:S(2)}, u32[]{:S(2)}) collective-permute-start(bf16[136,512]{1,0:T(8,128)(2,1)S(1)} %get-tuple-element.16.refs_0_.refs_8_), channel_id=1, source_target_pairs={{1,0},{0,1},{3,2},{2,3},{5,4},{4,5},{7,6},{6,7},{9,8},{8,9},{11,10... | collective-permute-start | bytes 417800 | tf_op jit(solution)/shard_map/ppermute | solution.py:114
  12.4 6.9 %collective-permute-start.9 = (bf16[136,512]{1,0:T(8,128)(2,1)S(1)}, bf16[136,512]{1,0:T(8,128)(2,1)S(1)}, u32[]{:S(2)}, u32[]{:S(2)}) collective-permute-start(bf16[136,512]{1,0:T(8,128)(2,1)S(1)} %collective-permute-done.8.refs_10_), channel_id=1, source_target_pairs={{8,0},{9,1},{10,2},{11,3},{12,4},{13,5},{14,6},{15,7},{0,8},{1,9},... | collective-permute-start | bytes 417800 | tf_op jit(solution)/shard_map/ppermute | solution.py:114
  15.7 3.6 %collective-permute-start.6 = (bf16[136,512]{1,0:T(8,128)(2,1)S(1)}, bf16[136,512]{1,0:T(8,128)(2,1)S(1)}, u32[]{:S(2)}, u32[]{:S(2)}) collective-permute-start(bf16[136,512]{1,0:T(8,128)(2,1)S(1)} %collective-permute-done.2.refs_3_), channel_id=1, source_target_pairs={{1,0},{0,1},{3,2},{2,3},{5,4},{4,5},{7,6},{6,7},{9,8},{8,9},{11,10... | collective-permute-start | bytes 417800 | tf_op jit(solution)/shard_map/ppermute | solution.py:114
  16.5 2.9 %collective-permute-start.5 = (bf16[136,512]{1,0:T(8,128)(2,1)S(1)}, bf16[136,512]{1,0:T(8,128)(2,1)S(1)}, u32[]{:S(2)}, u32[]{:S(2)}) collective-permute-start(bf16[136,512]{1,0:T(8,128)(2,1)S(1)} %collective-permute-done.1.refs_2_), channel_id=1, source_target_pairs={{1,0},{0,1},{3,2},{2,3},{5,4},{4,5},{7,6},{6,7},{9,8},{8,9},{11,10... | collective-permute-start | bytes 417800 | tf_op jit(solution)/shard_map/ppermute | solution.py:114
  16.5 2.9 %collective-permute-start.4 = (bf16[136,512]{1,0:T(8,128)(2,1)S(1)}, bf16[136,512]{1,0:T(8,128)(2,1)S(1)}, u32[]{:S(2)}, u32[]{:S(2)}) collective-permute-start(bf16[136,512]{1,0:T(8,128)(2,1)S(1)} %collective-permute-done.refs_1_), channel_id=1, source_target_pairs={{1,0},{0,1},{3,2},{2,3},{5,4},{4,5},{7,6},{6,7},{9,8},{8,9},{11,10... | collective-permute-start | bytes 417800 | tf_op jit(solution)/shard_map/ppermute | solution.py:114
  21.2 5.4 %collective-permute-start.10 = (f32[1,128]{1,0:T(1,128)S(1)}, f32[1,128]{1,0:T(1,128)S(1)}, u32[]{:S(2)}, u32[]{:S(2)}) collective-permute-start(f32[1,128]{1,0:T(1,128)S(1)} %get-tuple-element.17), channel_id=1, source_target_pairs={{24,0},{25,1},{26,2},{27,3},{28,4},{29,5},{30,6},{31,7},{16,8},{17... | collective-permute-start | bytes 1544 | tf_op jit(solution)/shard_map/ppermute | solution.py:114
  21.3 5.3 %collective-permute-start.11 = (f32[1,128]{1,0:T(1,128)S(1)}, f32[1,128]{1,0:T(1,128)S(1)}, u32[]{:S(2)}, u32[]{:S(2)}) collective-permute-start(f32[1,128]{1,0:T(1,128)S(1)} %get-tuple-element.18), channel_id=1, source_target_pairs={{16,0},{17,1},{18,2},{19,3},{20,4},{21,5},{22,6},{23,7},{24,8},{25... | collective-permute-start | bytes 1544 | tf_op jit(solution)/shard_map/ppermute | solution.py:114
  24.1 3.5 %collective-permute-start.12 = (f32[1,128]{1,0:T(1,128)S(1)}, f32[1,128]{1,0:T(1,128)S(1)}, u32[]{:S(2)}, u32[]{:S(2)}) collective-permute-start(f32[1,128]{1,0:T(1,128)S(1)} %get-tuple-element.19), channel_id=1, source_target_pairs={{8,0},{9,1},{10,2},{11,3},{12,4},{13,5},{14,6},{15,7},{0,8},{1,9},... | collective-permute-start | bytes 1544 | tf_op jit(solution)/shard_map/ppermute | solution.py:114

commit v20 on v16

--- a/solution.py
+++ b/solution.py
@@ -131,10 +131,10 @@
             return permute(x, lambda z, a, g: (turned(z, s, length), a, g))
 
         half = length // 2 if length & (length - 1) == 0 else length
+        near = [permute(own, lambda z, a, g: (z, turned(a, s, wide), g)) for s in reversed(range(1, wide))]
         middle = along(own, length - 1) if half < length else None
-        near = [permute(own, lambda z, a, g: (z, turned(a, s, wide), g)) for s in reversed(range(1, wide))]
         first = [along(own, s) for s in range(1, half)]
-        middle, near, first = lax.optimization_barrier((middle, near, first))
+        near, middle, first = lax.optimization_barrier((near, middle, first))
         near = near[::-1]
         last = [along(middle, s) for s in range(1, half)] if half < length else []
         offsets = list(range(1, half))

time: 27.7 us -> 28 us (1.011)
  starting transfers between devices: 11.7 us -> 14 us
  waiting for transfers between devices: 12.2 us -> 10.1 us
    ppermute x13, starting transfers between devices: 11.7 us -> 14 us  [permute(): return lax.ppermute(x, ('clu', 'grp'), pairs)]
    ppermute x13, waiting for transfers between devices: 12.2 us -> 10.1 us  [permute(): return lax.ppermute(x, ('clu', 'grp'), pairs)]
  transfers between devices with their start and end apart: 13 -> 13, of which waited for: 10 -> 7; matrix products, arithmetic and copies ran while one was open for 0% -> 0% of each run, Pallas kernels for 7% -> 7%
where the time goes in v20:
time: 28 us; the launch traced here: 27.9 us
  starting transfers between devices  14 us (50%)
  waiting for transfers between devices  10.1 us (36%)
  Pallas kernels  3.17 us (11%)
  other arithmetic  0.52 us (2%)
    ppermute x13, starting transfers between devices, permute(): return lax.ppermute(x, ('clu', 'grp'), pairs)  14 us
    ppermute x13, waiting for transfers between devices, permute(): return lax.ppermute(x, ('clu', 'grp'), pairs)  10.1 us
    pallas_call x2, Pallas kernels, best_of(): pl.pallas_call(functools.partial(best_kernel, len(keys), own, ranks), out...  2.07 us
    pallas_call x1, Pallas kernels, pack(): pl.pallas_call(functools.partial(pack_kernel, groups), out_shape=[pltpu.V...  1.1 us
  transfers between devices with their start and end apart: 13, of which 7 were waited for; matrix products, arithmetic and copies ran while one was open for 0% of the time, Pallas kernels for 7%

profile of v20, /device:TPU:0, one launch (start us, length us, event | category | flops | bytes accessed | tf_op | source)
XLA Modules:
  0.0 27.9 jit_solution(15386758015468915121)
XLA Ops:
  0.0 1.1 %shard_map.37 = (bf16[136,512]{1,0:T(8,128)(2,1)S(1)}, bf16[64,64]{1,0:T(8,128)(2,1)S(1)}) custom-call(bf16[128,512]{1,0:T(8,128)(2,1)} %emb_ref.1, s32[1,128]{1,0:T(1,128)} %bitcast.4, s32[1,64]{1,0:T(1,128)} %bitcast.5), custom_call_target="tpu_custom_call" | custom-call | tf_op jit(solution)/shard_map/pallas_call | solution.py:38
  1.1 4.0 %collective-permute-start = (bf16[136,512]{1,0:T(8,128)(2,1)S(1)}, bf16[136,512]{1,0:T(8,128)(2,1)S(1)}, u32[]{:S(2)}, u32[]{:S(2)}) collective-permute-start(bf16[136,512]{1,0:T(8,128)(2,1)S(1)} %get-tuple-element.16.refs_0_.refs_8_), channel_id=1, source_target_pairs={{6,0},{7,1},{4,2},{5,3},{2,4},{3,5},{0,6},{1,7},{14,8},{15,9},{12,... | collective-permute-start | bytes 417800 | tf_op jit(solution)/shard_map/ppermute | solution.py:114
  5.1 0.5 %collective-permute-start.1 = (bf16[136,512]{1,0:T(8,128)(2,1)S(1)}, bf16[136,512]{1,0:T(8,128)(2,1)S(1)}, u32[]{:S(2)}, u32[]{:S(2)}) collective-permute-start(bf16[136,512]{1,0:T(8,128)(2,1)S(1)} %get-tuple-element.16.refs_0_.refs_8_), channel_id=1, source_target_pairs={{4,0},{5,1},{6,2},{7,3},{0,4},{1,5},{2,6},{3,7},{12,8},{13,9},{14,... | collective-permute-start | bytes 417800 | tf_op jit(solution)/shard_map/ppermute | solution.py:114
  5.6 0.1 collective-permute-start.2
  5.7 4.0 %collective-permute-start.3 = (bf16[136,512]{1,0:T(8,128)(2,1)S(1)}, bf16[136,512]{1,0:T(8,128)(2,1)S(1)}, u32[]{:S(2)}, u32[]{:S(2)}) collective-permute-start(bf16[136,512]{1,0:T(8,128)(2,1)S(1)} %get-tuple-element.16.refs_0_.refs_8_), channel_id=1, source_target_pairs={{24,0},{25,1},{26,2},{27,3},{28,4},{29,5},{30,6},{31,7},{16,8},{17... | collective-permute-start | bytes 417800 | tf_op jit(solution)/shard_map/ppermute | solution.py:114
  9.7 0.0 collective-permute-start.4
  9.7 0.0 collective-permute-done.refs_3_
  9.7 0.0 collective-permute-start.5
  9.7 2.0 %collective-permute-done.1.refs_2_ = bf16[136,512]{1,0:T(8,128)(2,1)S(1)} collective-permute-done((bf16[136,512]{1,0:T(8,128)(2,1)S(1)}, bf16[136,512]{1,0:T(8,128)(2,1)S(1)}, u32[]{:S(2)}, u32[]{:S(2)}) %collective-permute-start.1) | collective-permute-done | bytes 139296 | tf_op jit(solution)/shard_map/ppermute | solution.py:114
  11.7 0.3 collective-permute-done.2.refs_1_
  12.0 2.1 %collective-permute-done.3.refs_10_ = bf16[136,512]{1,0:T(8,128)(2,1)S(1)} collective-permute-done((bf16[136,512]{1,0:T(8,128)(2,1)S(1)}, bf16[136,512]{1,0:T(8,128)(2,1)S(1)}, u32[]{:S(2)}, u32[]{:S(2)}) %collective-permute-start.3) | collective-permute-done | bytes 139296 | tf_op jit(solution)/shard_map/ppermute | solution.py:114
  14.1 1.5 %collective-permute-done.4.refs_9_ = bf16[136,512]{1,0:T(8,128)(2,1)S(1)} collective-permute-done((bf16[136,512]{1,0:T(8,128)(2,1)S(1)}, bf16[136,512]{1,0:T(8,128)(2,1)S(1)}, u32[]{:S(2)}, u32[]{:S(2)}) %collective-permute-start.4) | collective-permute-done | bytes 139296 | tf_op jit(solution)/shard_map/ppermute | solution.py:114
  15.6 0.0 collective-permute-start.6
  15.6 0.5 %collective-permute-start.7 = (bf16[136,512]{1,0:T(8,128)(2,1)S(1)}, bf16[136,512]{1,0:T(8,128)(2,1)S(1)}, u32[]{:S(2)}, u32[]{:S(2)}) collective-permute-start(bf16[136,512]{1,0:T(8,128)(2,1)S(1)} %collective-permute-done.1.refs_2_), channel_id=1, source_target_pairs={{1,0},{0,1},{3,2},{2,3},{5,4},{4,5},{7,6},{6,7},{9,8},{8,9},{11,10... | collective-permute-start | bytes 417800 | tf_op jit(solution)/shard_map/ppermute | solution.py:114
  16.1 0.0 collective-permute-start.8
  16.1 1.6 %collective-permute-start.11 = (bf16[136,512]{1,0:T(8,128)(2,1)S(1)}, bf16[136,512]{1,0:T(8,128)(2,1)S(1)}, u32[]{:S(2)}, u32[]{:S(2)}) collective-permute-start(bf16[136,512]{1,0:T(8,128)(2,1)S(1)} %collective-permute-done.3.refs_10_), channel_id=1, source_target_pairs={{8,0},{9,1},{10,2},{11,3},{12,4},{13,5},{14,6},{15,7},{0,8},{1,9},... | collective-permute-start | bytes 417800 | tf_op jit(solution)/shard_map/ppermute | solution.py:114
  17.8 0.0 collective-permute-done.5.refs_4_
  17.8 0.0 collective-permute-done.6.refs_5_
  17.8 0.0 collective-permute-done.7.refs_6_
  17.8 0.0 collective-permute-done.8.refs_7_
  17.8 1.4 %shard_map.38 = (f32[1,128]{1,0:T(1,128)S(1)}, f32[1,128]{1,0:T(1,128)S(1)}, f32[1,128]{1,0:T(1,128)S(1)}) custom-call(bf16[64,64]{1,0:T(8,128)(2,1)S(1)} %get-tuple-element.15.table_ref, bf16[136,512]{1,0:T(8,128)(2,1)S(1)} %get-tuple-element.16.refs_0_.refs_8_, bf16[136,512]{1,0:T(8,128)(2,1)S(1)} %collective-permute-done.2.refs_1_, ...), custom_call_target="tpu_custom_call" | custom-call | flops 402653184 | bytes 1441792 | tf_op jit(solution)/shard_map/pallas_call | solution.py:89
  19.2 1.7 %collective-permute-start.10 = (f32[1,128]{1,0:T(1,128)S(1)}, f32[1,128]{1,0:T(1,128)S(1)}, u32[]{:S(2)}, u32[]{:S(2)}) collective-permute-start(f32[1,128]{1,0:T(1,128)S(1)} %get-tuple-element.24), channel_id=1, source_target_pairs={{24,0},{25,1},{26,2},{27,3},{28,4},{29,5},{30,6},{31,7},{16,8},{17... | collective-permute-start | bytes 1544 | tf_op jit(solution)/shard_map/ppermute | solution.py:114
  21.0 0.0 collective-permute-start.9
  21.0 1.3 %collective-permute-done.11.refs_8_ = bf16[136,512]{1,0:T(8,128)(2,1)S(1)} collective-permute-done((bf16[136,512]{1,0:T(8,128)(2,1)S(1)}, bf16[136,512]{1,0:T(8,128)(2,1)S(1)}, u32[]{:S(2)}, u32[]{:S(2)}) %collective-permute-start.11) | collective-permute-done | bytes 139296 | tf_op jit(solution)/shard_map/ppermute | solution.py:114
  22.2 0.6 %shard_map.39 = f32[1,128]{1,0:T(1,128)S(1)} custom-call(bf16[64,64]{1,0:T(8,128)(2,1)S(1)} %get-tuple-element.15.table_ref, bf16[136,512]{1,0:T(8,128)(2,1)S(1)} %get-tuple-element.16.refs_0_.refs_8_, bf16[136,512]{1,0:T(8,128)(2,1)S(1)} %collective-permute-done.2.refs_1_, bf16[136,512]{1,0:T(8,128)(2,1)S(1)} %collective-permute-done.1.refs_2_, ...), custom_call_target="tpu_custom_call" | custom-call | flops 134217728 | bytes 1179648 | tf_op jit(solution)/shard_map/pallas_call | solution.py:89
  22.9 1.5 %collective-permute-start.12 = (f32[1,128]{1,0:T(1,128)S(1)}, f32[1,128]{1,0:T(1,128)S(1)}, u32[]{:S(2)}, u32[]{:S(2)}) collective-permute-start(f32[1,128]{1,0:T(1,128)S(1)} %shard_map.39), channel_id=1, source_target_pairs={{16,0},{17,1},{18,2},{19,3},{20,4},{21,5},{22,6},{23,7},{24,8},{25... | collective-permute-start | bytes 1544 | tf_op jit(solution)/shard_map/ppermute | solution.py:114
  24.4 0.2 collective-permute-done.10
  24.7 0.0 collective-permute-done.9
  24.7 2.7 %collective-permute-done.12 = f32[1,128]{1,0:T(1,128)S(1)} collective-permute-done((f32[1,128]{1,0:T(1,128)S(1)}, f32[1,128]{1,0:T(1,128)S(1)}, u32[]{:S(2)}, u32[]{:S(2)}) %collective-permute-start.12) | collective-permute-done | bytes 544 | tf_op jit(solution)/shard_map/ppermute | solution.py:114
  27.4 0.5 %maximum_bitcast_fusion = f32[128]{0:T(128)} fusion(f32[1,128]{1,0:T(1,128)S(1)} %collective-permute-done.12, f32[1,128]{1,0:T(1,128)S(1)} %collective-permute-done.10, f32[1,128]{1,0:T(1,128)S(1)} %get-tuple-element.22, f32[1,128]{1,0:T(1,128)S(1)} %collective-permute-done.9), kind=kLoop, calls=%fused_computation | loop fusion | flops 384 | bytes 2560 | tf_op jit(solution)/shard_map/reshape | solution.py:159
Async XLA Ops:
  1.1 8.6 %collective-permute-start = (bf16[136,512]{1,0:T(8,128)(2,1)S(1)}, bf16[136,512]{1,0:T(8,128)(2,1)S(1)}, u32[]{:S(2)}, u32[]{:S(2)}) collective-permute-start(bf16[136,512]{1,0:T(8,128)(2,1)S(1)} %get-tuple-element.16.refs_0_.refs_8_), channel_id=1, source_target_pairs={{6,0},{7,1},{4,2},{5,3},{2,4},{3,5},{0,6},{1,7},{14,8},{15,9},{12,... | collective-permute-start | bytes 417800 | tf_op jit(solution)/shard_map/ppermute | solution.py:114
  5.1 6.7 %collective-permute-start.1 = (bf16[136,512]{1,0:T(8,128)(2,1)S(1)}, bf16[136,512]{1,0:T(8,128)(2,1)S(1)}, u32[]{:S(2)}, u32[]{:S(2)}) collective-permute-start(bf16[136,512]{1,0:T(8,128)(2,1)S(1)} %get-tuple-element.16.refs_0_.refs_8_), channel_id=1, source_target_pairs={{4,0},{5,1},{6,2},{7,3},{0,4},{1,5},{2,6},{3,7},{12,8},{13,9},{14,... | collective-permute-start | bytes 417800 | tf_op jit(solution)/shard_map/ppermute | solution.py:114
  5.6 6.4 %collective-permute-start.2 = (bf16[136,512]{1,0:T(8,128)(2,1)S(1)}, bf16[136,512]{1,0:T(8,128)(2,1)S(1)}, u32[]{:S(2)}, u32[]{:S(2)}) collective-permute-start(bf16[136,512]{1,0:T(8,128)(2,1)S(1)} %get-tuple-element.16.refs_0_.refs_8_), channel_id=1, source_target_pairs={{2,0},{3,1},{0,2},{1,3},{6,4},{7,5},{4,6},{5,7},{10,8},{11,9},{8,1... | collective-permute-start | bytes 417800 | tf_op jit(solution)/shard_map/ppermute | solution.py:114
  5.7 8.4 %collective-permute-start.3 = (bf16[136,512]{1,0:T(8,128)(2,1)S(1)}, bf16[136,512]{1,0:T(8,128)(2,1)S(1)}, u32[]{:S(2)}, u32[]{:S(2)}) collective-permute-start(bf16[136,512]{1,0:T(8,128)(2,1)S(1)} %get-tuple-element.16.refs_0_.refs_8_), channel_id=1, source_target_pairs={{24,0},{25,1},{26,2},{27,3},{28,4},{29,5},{30,6},{31,7},{16,8},{17... | collective-permute-start | bytes 417800 | tf_op jit(solution)/shard_map/ppermute | solution.py:114
  9.7 5.9 %collective-permute-start.4 = (bf16[136,512]{1,0:T(8,128)(2,1)S(1)}, bf16[136,512]{1,0:T(8,128)(2,1)S(1)}, u32[]{:S(2)}, u32[]{:S(2)}) collective-permute-start(bf16[136,512]{1,0:T(8,128)(2,1)S(1)} %get-tuple-element.16.refs_0_.refs_8_), channel_id=1, source_target_pairs={{8,0},{9,1},{10,2},{11,3},{12,4},{13,5},{14,6},{15,7},{0,8},{1,9},... | collective-permute-start | bytes 417800 | tf_op jit(solution)/shard_map/ppermute | solution.py:114
  9.7 8.1 %collective-permute-start.5 = (bf16[136,512]{1,0:T(8,128)(2,1)S(1)}, bf16[136,512]{1,0:T(8,128)(2,1)S(1)}, u32[]{:S(2)}, u32[]{:S(2)}) collective-permute-start(bf16[136,512]{1,0:T(8,128)(2,1)S(1)} %get-tuple-element.16.refs_0_.refs_8_), channel_id=1, source_target_pairs={{1,0},{0,1},{3,2},{2,3},{5,4},{4,5},{7,6},{6,7},{9,8},{8,9},{11,10... | collective-permute-start | bytes 417800 | tf_op jit(solution)/shard_map/ppermute | solution.py:114
  15.6 2.2 %collective-permute-start.6 = (bf16[136,512]{1,0:T(8,128)(2,1)S(1)}, bf16[136,512]{1,0:T(8,128)(2,1)S(1)}, u32[]{:S(2)}, u32[]{:S(2)}) collective-permute-start(bf16[136,512]{1,0:T(8,128)(2,1)S(1)} %collective-permute-done.2.refs_1_), channel_id=1, source_target_pairs={{1,0},{0,1},{3,2},{2,3},{5,4},{4,5},{7,6},{6,7},{9,8},{8,9},{11,10... | collective-permute-start | bytes 417800 | tf_op jit(solution)/shard_map/ppermute | solution.py:114
  15.6 2.2 %collective-permute-start.7 = (bf16[136,512]{1,0:T(8,128)(2,1)S(1)}, bf16[136,512]{1,0:T(8,128)(2,1)S(1)}, u32[]{:S(2)}, u32[]{:S(2)}) collective-permute-start(bf16[136,512]{1,0:T(8,128)(2,1)S(1)} %collective-permute-done.1.refs_2_), channel_id=1, source_target_pairs={{1,0},{0,1},{3,2},{2,3},{5,4},{4,5},{7,6},{6,7},{9,8},{8,9},{11,10... | collective-permute-start | bytes 417800 | tf_op jit(solution)/shard_map/ppermute | solution.py:114
  16.1 1.7 %collective-permute-start.8 = (bf16[136,512]{1,0:T(8,128)(2,1)S(1)}, bf16[136,512]{1,0:T(8,128)(2,1)S(1)}, u32[]{:S(2)}, u32[]{:S(2)}) collective-permute-start(bf16[136,512]{1,0:T(8,128)(2,1)S(1)} %collective-permute-done.refs_3_), channel_id=1, source_target_pairs={{1,0},{0,1},{3,2},{2,3},{5,4},{4,5},{7,6},{6,7},{9,8},{8,9},{11,10... | collective-permute-start | bytes 417800 | tf_op jit(solution)/shard_map/ppermute | solution.py:114
  16.1 6.1 %collective-permute-start.11 = (bf16[136,512]{1,0:T(8,128)(2,1)S(1)}, bf16[136,512]{1,0:T(8,128)(2,1)S(1)}, u32[]{:S(2)}, u32[]{:S(2)}) collective-permute-start(bf16[136,512]{1,0:T(8,128)(2,1)S(1)} %collective-permute-done.3.refs_10_), channel_id=1, source_target_pairs={{8,0},{9,1},{10,2},{11,3},{12,4},{13,5},{14,6},{15,7},{0,8},{1,9},... | collective-permute-start | bytes 417800 | tf_op jit(solution)/shard_map/ppermute | solution.py:114
  19.2 5.4 %collective-permute-start.10 = (f32[1,128]{1,0:T(1,128)S(1)}, f32[1,128]{1,0:T(1,128)S(1)}, u32[]{:S(2)}, u32[]{:S(2)}) collective-permute-start(f32[1,128]{1,0:T(1,128)S(1)} %get-tuple-element.24), channel_id=1, source_target_pairs={{24,0},{25,1},{26,2},{27,3},{28,4},{29,5},{30,6},{31,7},{16,8},{17... | collective-permute-start | bytes 1544 | tf_op jit(solution)/shard_map/ppermute | solution.py:114
  21.0 3.7 %collective-permute-start.9 = (f32[1,128]{1,0:T(1,128)S(1)}, f32[1,128]{1,0:T(1,128)S(1)}, u32[]{:S(2)}, u32[]{:S(2)}) collective-permute-start(f32[1,128]{1,0:T(1,128)S(1)} %get-tuple-element.23), channel_id=1, source_target_pairs={{8,0},{9,1},{10,2},{11,3},{12,4},{13,5},{14,6},{15,7},{0,8},{1,9},... | collective-permute-start | bytes 1544 | tf_op jit(solution)/shard_map/ppermute | solution.py:114
  22.9 4.5 %collective-permute-start.12 = (f32[1,128]{1,0:T(1,128)S(1)}, f32[1,128]{1,0:T(1,128)S(1)}, u32[]{:S(2)}, u32[]{:S(2)}) collective-permute-start(f32[1,128]{1,0:T(1,128)S(1)} %shard_map.39), channel_id=1, source_target_pairs={{16,0},{17,1},{18,2},{19,3},{20,4},{21,5},{22,6},{23,7},{24,8},{25... | collective-permute-start | bytes 1544 | tf_op jit(solution)/shard_map/ppermute | solution.py:114

commit v21 on v20

--- a/solution.py
+++ b/solution.py
@@ -132,9 +132,9 @@
 
         half = length // 2 if length & (length - 1) == 0 else length
         near = [permute(own, lambda z, a, g: (z, turned(a, s, wide), g)) for s in reversed(range(1, wide))]
+        first = [along(own, s) for s in range(1, half)]
         middle = along(own, length - 1) if half < length else None
-        first = [along(own, s) for s in range(1, half)]
-        near, middle, first = lax.optimization_barrier((near, middle, first))
+        near, first = lax.optimization_barrier((near, first))
         near = near[::-1]
         last = [along(middle, s) for s in range(1, half)] if half < length else []
         offsets = list(range(1, half))

time: 28 us -> 26.9 us (0.961)
  waiting for transfers between devices: 10.1 us -> 7.52 us
  starting transfers between devices: 14 us -> 15.5 us
    ppermute x13, waiting for transfers between devices: 10.1 us -> 7.52 us  [permute(): return lax.ppermute(x, ('clu', 'grp'), pairs)]
    ppermute x13, starting transfers between devices: 14 us -> 15.5 us  [permute(): return lax.ppermute(x, ('clu', 'grp'), pairs)]
  transfers between devices with their start and end apart: 13 -> 13, of which waited for: 7 -> 5; matrix products, arithmetic and copies ran while one was open for 0% -> 0% of each run, Pallas kernels for 7% -> 8%
where the time goes in v21:
time: 26.9 us; the launch traced here: 26.8 us
  starting transfers between devices  15.5 us (58%)
  waiting for transfers between devices  7.52 us (28%)
  Pallas kernels  3.17 us (12%)
  other arithmetic  0.52 us (2%)
    ppermute x13, starting transfers between devices, permute(): return lax.ppermute(x, ('clu', 'grp'), pairs)  15.5 us
    ppermute x13, waiting for transfers between devices, permute(): return lax.ppermute(x, ('clu', 'grp'), pairs)  7.52 us
    pallas_call x2, Pallas kernels, best_of(): pl.pallas_call(functools.partial(best_kernel, len(keys), own, ranks), out...  2.07 us
    pallas_call x1, Pallas kernels, pack(): pl.pallas_call(functools.partial(pack_kernel, groups), out_shape=[pltpu.V...  1.1 us
  transfers between devices with their start and end apart: 13, of which 5 were waited for; matrix products, arithmetic and copies ran while one was open for 0% of the time, Pallas kernels for 8%

profile of v21, /device:TPU:0, one launch (start us, length us, event | category | flops | bytes accessed | tf_op | source)
XLA Modules:
  0.0 26.8 jit_solution(1672436690635980731)
XLA Ops:
  0.0 1.1 %shard_map.37 = (bf16[136,512]{1,0:T(8,128)(2,1)S(1)}, bf16[64,64]{1,0:T(8,128)(2,1)S(1)}) custom-call(bf16[128,512]{1,0:T(8,128)(2,1)} %emb_ref.1, s32[1,128]{1,0:T(1,128)} %bitcast.4, s32[1,64]{1,0:T(1,128)} %bitcast.5), custom_call_target="tpu_custom_call" | custom-call | tf_op jit(solution)/shard_map/pallas_call | solution.py:38
  1.1 4.0 %collective-permute-start = (bf16[136,512]{1,0:T(8,128)(2,1)S(1)}, bf16[136,512]{1,0:T(8,128)(2,1)S(1)}, u32[]{:S(2)}, u32[]{:S(2)}) collective-permute-start(bf16[136,512]{1,0:T(8,128)(2,1)S(1)} %get-tuple-element.15.refs_0_.refs_8_), channel_id=1, source_target_pairs={{6,0},{7,1},{4,2},{5,3},{2,4},{3,5},{0,6},{1,7},{14,8},{15,9},{12,... | collective-permute-start | bytes 417800 | tf_op jit(solution)/shard_map/ppermute | solution.py:114
  5.1 0.5 %collective-permute-start.1 = (bf16[136,512]{1,0:T(8,128)(2,1)S(1)}, bf16[136,512]{1,0:T(8,128)(2,1)S(1)}, u32[]{:S(2)}, u32[]{:S(2)}) collective-permute-start(bf16[136,512]{1,0:T(8,128)(2,1)S(1)} %get-tuple-element.15.refs_0_.refs_8_), channel_id=1, source_target_pairs={{4,0},{5,1},{6,2},{7,3},{0,4},{1,5},{2,6},{3,7},{12,8},{13,9},{14,... | collective-permute-start | bytes 417800 | tf_op jit(solution)/shard_map/ppermute | solution.py:114
  5.6 0.1 collective-permute-start.2
  5.7 2.0 %collective-permute-start.3 = (bf16[136,512]{1,0:T(8,128)(2,1)S(1)}, bf16[136,512]{1,0:T(8,128)(2,1)S(1)}, u32[]{:S(2)}, u32[]{:S(2)}) collective-permute-start(bf16[136,512]{1,0:T(8,128)(2,1)S(1)} %get-tuple-element.15.refs_0_.refs_8_), channel_id=1, source_target_pairs={{8,0},{9,1},{10,2},{11,3},{12,4},{13,5},{14,6},{15,7},{0,8},{1,9},... | collective-permute-start | bytes 417800 | tf_op jit(solution)/shard_map/ppermute | solution.py:114
  7.7 2.5 %collective-permute-start.8 = (bf16[136,512]{1,0:T(8,128)(2,1)S(1)}, bf16[136,512]{1,0:T(8,128)(2,1)S(1)}, u32[]{:S(2)}, u32[]{:S(2)}) collective-permute-start(bf16[136,512]{1,0:T(8,128)(2,1)S(1)} %get-tuple-element.15.refs_0_.refs_8_), channel_id=1, source_target_pairs={{24,0},{25,1},{26,2},{27,3},{28,4},{29,5},{30,6},{31,7},{16,8},{17... | collective-permute-start | bytes 417800 | tf_op jit(solution)/shard_map/ppermute | solution.py:114
  10.2 0.0 collective-permute-done.refs_3_
  10.2 0.0 collective-permute-start.4
  10.2 1.6 %collective-permute-done.1.refs_2_ = bf16[136,512]{1,0:T(8,128)(2,1)S(1)} collective-permute-done((bf16[136,512]{1,0:T(8,128)(2,1)S(1)}, bf16[136,512]{1,0:T(8,128)(2,1)S(1)}, u32[]{:S(2)}, u32[]{:S(2)}) %collective-permute-start.1) | collective-permute-done | bytes 139296 | tf_op jit(solution)/shard_map/ppermute | solution.py:114
  11.7 0.3 collective-permute-done.2.refs_1_
  12.0 0.0 collective-permute-done.3.refs_9_
  12.0 0.0 collective-permute-start.5
  12.0 0.5 %collective-permute-start.6 = (bf16[136,512]{1,0:T(8,128)(2,1)S(1)}, bf16[136,512]{1,0:T(8,128)(2,1)S(1)}, u32[]{:S(2)}, u32[]{:S(2)}) collective-permute-start(bf16[136,512]{1,0:T(8,128)(2,1)S(1)} %collective-permute-done.1.refs_2_), channel_id=1, source_target_pairs={{1,0},{0,1},{3,2},{2,3},{5,4},{4,5},{7,6},{6,7},{9,8},{8,9},{11,10... | collective-permute-start | bytes 417800 | tf_op jit(solution)/shard_map/ppermute | solution.py:114
  12.5 0.0 collective-permute-start.7
  12.5 3.3 %collective-permute-done.8.refs_10_ = bf16[136,512]{1,0:T(8,128)(2,1)S(1)} collective-permute-done((bf16[136,512]{1,0:T(8,128)(2,1)S(1)}, bf16[136,512]{1,0:T(8,128)(2,1)S(1)}, u32[]{:S(2)}, u32[]{:S(2)}) %collective-permute-start.8) | collective-permute-done | bytes 139296 | tf_op jit(solution)/shard_map/ppermute | solution.py:114
  15.8 0.6 %collective-permute-start.11 = (bf16[136,512]{1,0:T(8,128)(2,1)S(1)}, bf16[136,512]{1,0:T(8,128)(2,1)S(1)}, u32[]{:S(2)}, u32[]{:S(2)}) collective-permute-start(bf16[136,512]{1,0:T(8,128)(2,1)S(1)} %collective-permute-done.8.refs_10_), channel_id=1, source_target_pairs={{8,0},{9,1},{10,2},{11,3},{12,4},{13,5},{14,6},{15,7},{0,8},{1,9},... | collective-permute-start | bytes 417800 | tf_op jit(solution)/shard_map/ppermute | solution.py:114
  16.4 0.0 collective-permute-done.4.refs_4_
  16.4 0.0 collective-permute-done.5.refs_5_
  16.4 0.0 collective-permute-done.6.refs_6_
  16.4 0.0 collective-permute-done.7.refs_7_
  16.4 1.4 %shard_map.38 = (f32[1,128]{1,0:T(1,128)S(1)}, f32[1,128]{1,0:T(1,128)S(1)}, f32[1,128]{1,0:T(1,128)S(1)}) custom-call(bf16[64,64]{1,0:T(8,128)(2,1)S(1)} %get-tuple-element.14.table_ref, bf16[136,512]{1,0:T(8,128)(2,1)S(1)} %get-tuple-element.15.refs_0_.refs_8_, bf16[136,512]{1,0:T(8,128)(2,1)S(1)} %collective-permute-done.2.refs_1_, ...), custom_call_target="tpu_custom_call" | custom-call | flops 402653184 | bytes 1441792 | tf_op jit(solution)/shard_map/pallas_call | solution.py:89
  17.8 3.3 %collective-permute-start.10 = (f32[1,128]{1,0:T(1,128)S(1)}, f32[1,128]{1,0:T(1,128)S(1)}, u32[]{:S(2)}, u32[]{:S(2)}) collective-permute-start(f32[1,128]{1,0:T(1,128)S(1)} %get-tuple-element.22), channel_id=1, source_target_pairs={{24,0},{25,1},{26,2},{27,3},{28,4},{29,5},{30,6},{31,7},{16,8},{17... | collective-permute-start | bytes 1544 | tf_op jit(solution)/shard_map/ppermute | solution.py:114
  21.1 0.0 collective-permute-start.9
  21.1 0.0 collective-permute-done.11.refs_8_
  21.1 0.6 %shard_map.39 = f32[1,128]{1,0:T(1,128)S(1)} custom-call(bf16[64,64]{1,0:T(8,128)(2,1)S(1)} %get-tuple-element.14.table_ref, bf16[136,512]{1,0:T(8,128)(2,1)S(1)} %get-tuple-element.15.refs_0_.refs_8_, bf16[136,512]{1,0:T(8,128)(2,1)S(1)} %collective-permute-done.2.refs_1_, bf16[136,512]{1,0:T(8,128)(2,1)S(1)} %collective-permute-done.1.refs_2_, ...), custom_call_target="tpu_custom_call" | custom-call | flops 134217728 | bytes 1179648 | tf_op jit(solution)/shard_map/pallas_call | solution.py:89
  21.8 2.1 %collective-permute-start.12 = (f32[1,128]{1,0:T(1,128)S(1)}, f32[1,128]{1,0:T(1,128)S(1)}, u32[]{:S(2)}, u32[]{:S(2)}) collective-permute-start(f32[1,128]{1,0:T(1,128)S(1)} %shard_map.39), channel_id=1, source_target_pairs={{16,0},{17,1},{18,2},{19,3},{20,4},{21,5},{22,6},{23,7},{24,8},{25... | collective-permute-start | bytes 1544 | tf_op jit(solution)/shard_map/ppermute | solution.py:114
  23.9 0.0 collective-permute-done.10
  23.9 0.8 %collective-permute-done.9 = f32[1,128]{1,0:T(1,128)S(1)} collective-permute-done((f32[1,128]{1,0:T(1,128)S(1)}, f32[1,128]{1,0:T(1,128)S(1)}, u32[]{:S(2)}, u32[]{:S(2)}) %collective-permute-start.9) | collective-permute-done | bytes 544 | tf_op jit(solution)/shard_map/ppermute | solution.py:114
  24.7 1.6 %collective-permute-done.12 = f32[1,128]{1,0:T(1,128)S(1)} collective-permute-done((f32[1,128]{1,0:T(1,128)S(1)}, f32[1,128]{1,0:T(1,128)S(1)}, u32[]{:S(2)}, u32[]{:S(2)}) %collective-permute-start.12) | collective-permute-done | bytes 544 | tf_op jit(solution)/shard_map/ppermute | solution.py:114
  26.3 0.5 %maximum_bitcast_fusion = f32[128]{0:T(128)} fusion(f32[1,128]{1,0:T(1,128)S(1)} %collective-permute-done.12, f32[1,128]{1,0:T(1,128)S(1)} %collective-permute-done.10, f32[1,128]{1,0:T(1,128)S(1)} %get-tuple-element.20, f32[1,128]{1,0:T(1,128)S(1)} %collective-permute-done.9), kind=kLoop, calls=%fused_computation | loop fusion | flops 384 | bytes 2560 | tf_op jit(solution)/shard_map/reshape | solution.py:159
Async XLA Ops:
  1.1 9.1 %collective-permute-start = (bf16[136,512]{1,0:T(8,128)(2,1)S(1)}, bf16[136,512]{1,0:T(8,128)(2,1)S(1)}, u32[]{:S(2)}, u32[]{:S(2)}) collective-permute-start(bf16[136,512]{1,0:T(8,128)(2,1)S(1)} %get-tuple-element.15.refs_0_.refs_8_), channel_id=1, source_target_pairs={{6,0},{7,1},{4,2},{5,3},{2,4},{3,5},{0,6},{1,7},{14,8},{15,9},{12,... | collective-permute-start | bytes 417800 | tf_op jit(solution)/shard_map/ppermute | solution.py:114
  5.1 6.7 %collective-permute-start.1 = (bf16[136,512]{1,0:T(8,128)(2,1)S(1)}, bf16[136,512]{1,0:T(8,128)(2,1)S(1)}, u32[]{:S(2)}, u32[]{:S(2)}) collective-permute-start(bf16[136,512]{1,0:T(8,128)(2,1)S(1)} %get-tuple-element.15.refs_0_.refs_8_), channel_id=1, source_target_pairs={{4,0},{5,1},{6,2},{7,3},{0,4},{1,5},{2,6},{3,7},{12,8},{13,9},{14,... | collective-permute-start | bytes 417800 | tf_op jit(solution)/shard_map/ppermute | solution.py:114
  5.6 6.4 %collective-permute-start.2 = (bf16[136,512]{1,0:T(8,128)(2,1)S(1)}, bf16[136,512]{1,0:T(8,128)(2,1)S(1)}, u32[]{:S(2)}, u32[]{:S(2)}) collective-permute-start(bf16[136,512]{1,0:T(8,128)(2,1)S(1)} %get-tuple-element.15.refs_0_.refs_8_), channel_id=1, source_target_pairs={{2,0},{3,1},{0,2},{1,3},{6,4},{7,5},{4,6},{5,7},{10,8},{11,9},{8,1... | collective-permute-start | bytes 417800 | tf_op jit(solution)/shard_map/ppermute | solution.py:114
  5.7 6.3 %collective-permute-start.3 = (bf16[136,512]{1,0:T(8,128)(2,1)S(1)}, bf16[136,512]{1,0:T(8,128)(2,1)S(1)}, u32[]{:S(2)}, u32[]{:S(2)}) collective-permute-start(bf16[136,512]{1,0:T(8,128)(2,1)S(1)} %get-tuple-element.15.refs_0_.refs_8_), channel_id=1, source_target_pairs={{8,0},{9,1},{10,2},{11,3},{12,4},{13,5},{14,6},{15,7},{0,8},{1,9},... | collective-permute-start | bytes 417800 | tf_op jit(solution)/shard_map/ppermute | solution.py:114
  7.7 8.1 %collective-permute-start.8 = (bf16[136,512]{1,0:T(8,128)(2,1)S(1)}, bf16[136,512]{1,0:T(8,128)(2,1)S(1)}, u32[]{:S(2)}, u32[]{:S(2)}) collective-permute-start(bf16[136,512]{1,0:T(8,128)(2,1)S(1)} %get-tuple-element.15.refs_0_.refs_8_), channel_id=1, source_target_pairs={{24,0},{25,1},{26,2},{27,3},{28,4},{29,5},{30,6},{31,7},{16,8},{17... | collective-permute-start | bytes 417800 | tf_op jit(solution)/shard_map/ppermute | solution.py:114
  10.2 6.2 %collective-permute-start.4 = (bf16[136,512]{1,0:T(8,128)(2,1)S(1)}, bf16[136,512]{1,0:T(8,128)(2,1)S(1)}, u32[]{:S(2)}, u32[]{:S(2)}) collective-permute-start(bf16[136,512]{1,0:T(8,128)(2,1)S(1)} %get-tuple-element.15.refs_0_.refs_8_), channel_id=1, source_target_pairs={{1,0},{0,1},{3,2},{2,3},{5,4},{4,5},{7,6},{6,7},{9,8},{8,9},{11,10... | collective-permute-start | bytes 417800 | tf_op jit(solution)/shard_map/ppermute | solution.py:114
  12.0 4.4 %collective-permute-start.5 = (bf16[136,512]{1,0:T(8,128)(2,1)S(1)}, bf16[136,512]{1,0:T(8,128)(2,1)S(1)}, u32[]{:S(2)}, u32[]{:S(2)}) collective-permute-start(bf16[136,512]{1,0:T(8,128)(2,1)S(1)} %collective-permute-done.2.refs_1_), channel_id=1, source_target_pairs={{1,0},{0,1},{3,2},{2,3},{5,4},{4,5},{7,6},{6,7},{9,8},{8,9},{11,10... | collective-permute-start | bytes 417800 | tf_op jit(solution)/shard_map/ppermute | solution.py:114
  12.0 4.4 %collective-permute-start.6 = (bf16[136,512]{1,0:T(8,128)(2,1)S(1)}, bf16[136,512]{1,0:T(8,128)(2,1)S(1)}, u32[]{:S(2)}, u32[]{:S(2)}) collective-permute-start(bf16[136,512]{1,0:T(8,128)(2,1)S(1)} %collective-permute-done.1.refs_2_), channel_id=1, source_target_pairs={{1,0},{0,1},{3,2},{2,3},{5,4},{4,5},{7,6},{6,7},{9,8},{8,9},{11,10... | collective-permute-start | bytes 417800 | tf_op jit(solution)/shard_map/ppermute | solution.py:114
  12.5 3.9 %collective-permute-start.7 = (bf16[136,512]{1,0:T(8,128)(2,1)S(1)}, bf16[136,512]{1,0:T(8,128)(2,1)S(1)}, u32[]{:S(2)}, u32[]{:S(2)}) collective-permute-start(bf16[136,512]{1,0:T(8,128)(2,1)S(1)} %collective-permute-done.refs_3_), channel_id=1, source_target_pairs={{1,0},{0,1},{3,2},{2,3},{5,4},{4,5},{7,6},{6,7},{9,8},{8,9},{11,10... | collective-permute-start | bytes 417800 | tf_op jit(solution)/shard_map/ppermute | solution.py:114
  15.8 5.3 %collective-permute-start.11 = (bf16[136,512]{1,0:T(8,128)(2,1)S(1)}, bf16[136,512]{1,0:T(8,128)(2,1)S(1)}, u32[]{:S(2)}, u32[]{:S(2)}) collective-permute-start(bf16[136,512]{1,0:T(8,128)(2,1)S(1)} %collective-permute-done.8.refs_10_), channel_id=1, source_target_pairs={{8,0},{9,1},{10,2},{11,3},{12,4},{13,5},{14,6},{15,7},{0,8},{1,9},... | collective-permute-start | bytes 417800 | tf_op jit(solution)/shard_map/ppermute | solution.py:114
  17.8 6.0 %collective-permute-start.10 = (f32[1,128]{1,0:T(1,128)S(1)}, f32[1,128]{1,0:T(1,128)S(1)}, u32[]{:S(2)}, u32[]{:S(2)}) collective-permute-start(f32[1,128]{1,0:T(1,128)S(1)} %get-tuple-element.22), channel_id=1, source_target_pairs={{24,0},{25,1},{26,2},{27,3},{28,4},{29,5},{30,6},{31,7},{16,8},{17... | collective-permute-start | bytes 1544 | tf_op jit(solution)/shard_map/ppermute | solution.py:114
  21.1 3.5 %collective-permute-start.9 = (f32[1,128]{1,0:T(1,128)S(1)}, f32[1,128]{1,0:T(1,128)S(1)}, u32[]{:S(2)}, u32[]{:S(2)}) collective-permute-start(f32[1,128]{1,0:T(1,128)S(1)} %get-tuple-element.21), channel_id=1, source_target_pairs={{8,0},{9,1},{10,2},{11,3},{12,4},{13,5},{14,6},{15,7},{0,8},{1,9},... | collective-permute-start | bytes 1544 | tf_op jit(solution)/shard_map/ppermute | solution.py:114
  21.8 4.5 %collective-permute-start.12 = (f32[1,128]{1,0:T(1,128)S(1)}, f32[1,128]{1,0:T(1,128)S(1)}, u32[]{:S(2)}, u32[]{:S(2)}) collective-permute-start(f32[1,128]{1,0:T(1,128)S(1)} %shard_map.39), channel_id=1, source_target_pairs={{16,0},{17,1},{18,2},{19,3},{20,4},{21,5},{22,6},{23,7},{24,8},{25... | collective-permute-start | bytes 1544 | tf_op jit(solution)/shard_map/ppermute | solution.py:114

commit v22 on v20

--- a/solution.py
+++ b/solution.py
@@ -134,7 +134,8 @@
         near = [permute(own, lambda z, a, g: (z, turned(a, s, wide), g)) for s in reversed(range(1, wide))]
         middle = along(own, length - 1) if half < length else None
         first = [along(own, s) for s in range(1, half)]
-        near, middle, first = lax.optimization_barrier((near, middle, first))
+        near = lax.optimization_barrier(near)
+        middle, first = lax.optimization_barrier((middle, first))
         near = near[::-1]
         last = [along(middle, s) for s in range(1, half)] if half < length else []
         offsets = list(range(1, half))

time: 28 us -> 26.5 us (0.946)
  waiting for transfers between devices: 10.1 us -> 7.57 us
  starting transfers between devices: 14 us -> 15 us
    ppermute x13, waiting for transfers between devices: 10.1 us -> 7.57 us  [permute(): return lax.ppermute(x, ('clu', 'grp'), pairs)]
    ppermute x13, starting transfers between devices: 14 us -> 15 us  [permute(): return lax.ppermute(x, ('clu', 'grp'), pairs)]
  transfers between devices with their start and end apart: 13 -> 13, of which waited for: 7 -> 7; matrix products, arithmetic and copies ran while one was open for 0% -> 0% of each run, Pallas kernels for 7% -> 8%
where the time goes in v22:
time: 26.5 us; the launch traced here: 26.3 us
  starting transfers between devices  15 us (57%)
  waiting for transfers between devices  7.57 us (29%)
  Pallas kernels  3.17 us (12%)
  other arithmetic  0.52 us (2%)
    ppermute x13, starting transfers between devices, permute(): return lax.ppermute(x, ('clu', 'grp'), pairs)  15 us
    ppermute x13, waiting for transfers between devices, permute(): return lax.ppermute(x, ('clu', 'grp'), pairs)  7.57 us
    pallas_call x2, Pallas kernels, best_of(): pl.pallas_call(functools.partial(best_kernel, len(keys), own, ranks), out...  2.07 us
    pallas_call x1, Pallas kernels, pack(): pl.pallas_call(functools.partial(pack_kernel, groups), out_shape=[pltpu.V...  1.1 us
  transfers between devices with their start and end apart: 13, of which 7 were waited for; matrix products, arithmetic and copies ran while one was open for 0% of the time, Pallas kernels for 8%

profile of v22, /device:TPU:0, one launch (start us, length us, event | category | flops | bytes accessed | tf_op | source)
XLA Modules:
  0.0 26.3 jit_solution(6111381095179418782)
XLA Ops:
  0.0 1.1 %shard_map.37 = (bf16[136,512]{1,0:T(8,128)(2,1)S(1)}, bf16[64,64]{1,0:T(8,128)(2,1)S(1)}) custom-call(bf16[128,512]{1,0:T(8,128)(2,1)} %emb_ref.1, s32[1,128]{1,0:T(1,128)} %bitcast.4, s32[1,64]{1,0:T(1,128)} %bitcast.5), custom_call_target="tpu_custom_call" | custom-call | tf_op jit(solution)/shard_map/pallas_call | solution.py:38
  1.1 4.0 %collective-permute-start = (bf16[136,512]{1,0:T(8,128)(2,1)S(1)}, bf16[136,512]{1,0:T(8,128)(2,1)S(1)}, u32[]{:S(2)}, u32[]{:S(2)}) collective-permute-start(bf16[136,512]{1,0:T(8,128)(2,1)S(1)} %get-tuple-element.16.refs_0_.refs_8_), channel_id=1, source_target_pairs={{6,0},{7,1},{4,2},{5,3},{2,4},{3,5},{0,6},{1,7},{14,8},{15,9},{12,... | collective-permute-start | bytes 417800 | tf_op jit(solution)/shard_map/ppermute | solution.py:114
  5.1 0.5 %collective-permute-start.1 = (bf16[136,512]{1,0:T(8,128)(2,1)S(1)}, bf16[136,512]{1,0:T(8,128)(2,1)S(1)}, u32[]{:S(2)}, u32[]{:S(2)}) collective-permute-start(bf16[136,512]{1,0:T(8,128)(2,1)S(1)} %get-tuple-element.16.refs_0_.refs_8_), channel_id=1, source_target_pairs={{4,0},{5,1},{6,2},{7,3},{0,4},{1,5},{2,6},{3,7},{12,8},{13,9},{14,... | collective-permute-start | bytes 417800 | tf_op jit(solution)/shard_map/ppermute | solution.py:114
  5.6 0.1 collective-permute-start.2
  5.7 4.0 %collective-permute-start.7 = (bf16[136,512]{1,0:T(8,128)(2,1)S(1)}, bf16[136,512]{1,0:T(8,128)(2,1)S(1)}, u32[]{:S(2)}, u32[]{:S(2)}) collective-permute-start(bf16[136,512]{1,0:T(8,128)(2,1)S(1)} %get-tuple-element.16.refs_0_.refs_8_), channel_id=1, source_target_pairs={{24,0},{25,1},{26,2},{27,3},{28,4},{29,5},{30,6},{31,7},{16,8},{17... | collective-permute-start | bytes 417800 | tf_op jit(solution)/shard_map/ppermute | solution.py:114
  9.7 0.0 collective-permute-start.8
  9.7 0.0 collective-permute-done.refs_3_
  9.7 0.0 collective-permute-start.3
  9.7 2.0 %collective-permute-done.1.refs_2_ = bf16[136,512]{1,0:T(8,128)(2,1)S(1)} collective-permute-done((bf16[136,512]{1,0:T(8,128)(2,1)S(1)}, bf16[136,512]{1,0:T(8,128)(2,1)S(1)}, u32[]{:S(2)}, u32[]{:S(2)}) %collective-permute-start.1) | collective-permute-done | bytes 139296 | tf_op jit(solution)/shard_map/ppermute | solution.py:114
  11.7 0.3 collective-permute-done.2.refs_1_
  12.0 0.0 collective-permute-start.4
  12.0 0.5 %collective-permute-start.5 = (bf16[136,512]{1,0:T(8,128)(2,1)S(1)}, bf16[136,512]{1,0:T(8,128)(2,1)S(1)}, u32[]{:S(2)}, u32[]{:S(2)}) collective-permute-start(bf16[136,512]{1,0:T(8,128)(2,1)S(1)} %collective-permute-done.1.refs_2_), channel_id=1, source_target_pairs={{1,0},{0,1},{3,2},{2,3},{5,4},{4,5},{7,6},{6,7},{9,8},{8,9},{11,10... | collective-permute-start | bytes 417800 | tf_op jit(solution)/shard_map/ppermute | solution.py:114
  12.5 1.6 %collective-permute-done.7.refs_10_ = bf16[136,512]{1,0:T(8,128)(2,1)S(1)} collective-permute-done((bf16[136,512]{1,0:T(8,128)(2,1)S(1)}, bf16[136,512]{1,0:T(8,128)(2,1)S(1)}, u32[]{:S(2)}, u32[]{:S(2)}) %collective-permute-start.7) | collective-permute-done | bytes 139296 | tf_op jit(solution)/shard_map/ppermute | solution.py:114
  14.1 0.0 collective-permute-start.6
  14.1 1.5 %collective-permute-done.8.refs_9_ = bf16[136,512]{1,0:T(8,128)(2,1)S(1)} collective-permute-done((bf16[136,512]{1,0:T(8,128)(2,1)S(1)}, bf16[136,512]{1,0:T(8,128)(2,1)S(1)}, u32[]{:S(2)}, u32[]{:S(2)}) %collective-permute-start.8) | collective-permute-done | bytes 139296 | tf_op jit(solution)/shard_map/ppermute | solution.py:114
  15.6 1.6 %collective-permute-start.11 = (bf16[136,512]{1,0:T(8,128)(2,1)S(1)}, bf16[136,512]{1,0:T(8,128)(2,1)S(1)}, u32[]{:S(2)}, u32[]{:S(2)}) collective-permute-start(bf16[136,512]{1,0:T(8,128)(2,1)S(1)} %collective-permute-done.7.refs_10_), channel_id=1, source_target_pairs={{8,0},{9,1},{10,2},{11,3},{12,4},{13,5},{14,6},{15,7},{0,8},{1,9},... | collective-permute-start | bytes 417800 | tf_op jit(solution)/shard_map/ppermute | solution.py:114
  17.3 0.0 collective-permute-done.3.refs_4_
  17.3 0.0 collective-permute-done.4.refs_5_
  17.3 0.0 collective-permute-done.5.refs_6_
  17.3 0.0 collective-permute-done.6.refs_7_
  17.3 1.4 %shard_map.38 = (f32[1,128]{1,0:T(1,128)S(1)}, f32[1,128]{1,0:T(1,128)S(1)}, f32[1,128]{1,0:T(1,128)S(1)}) custom-call(bf16[64,64]{1,0:T(8,128)(2,1)S(1)} %get-tuple-element.15.table_ref, bf16[136,512]{1,0:T(8,128)(2,1)S(1)} %get-tuple-element.16.refs_0_.refs_8_, bf16[136,512]{1,0:T(8,128)(2,1)S(1)} %collective-permute-done.2.refs_1_, ...), custom_call_target="tpu_custom_call" | custom-call | flops 402653184 | bytes 1441792 | tf_op jit(solution)/shard_map/pallas_call | solution.py:89
  18.7 1.7 %collective-permute-start.10 = (f32[1,128]{1,0:T(1,128)S(1)}, f32[1,128]{1,0:T(1,128)S(1)}, u32[]{:S(2)}, u32[]{:S(2)}) collective-permute-start(f32[1,128]{1,0:T(1,128)S(1)} %get-tuple-element.24), channel_id=1, source_target_pairs={{24,0},{25,1},{26,2},{27,3},{28,4},{29,5},{30,6},{31,7},{16,8},{17... | collective-permute-start | bytes 1544 | tf_op jit(solution)/shard_map/ppermute | solution.py:114
  20.4 0.0 collective-permute-start.9
  20.5 0.2 collective-permute-done.11.refs_8_
  20.7 0.6 %shard_map.39 = f32[1,128]{1,0:T(1,128)S(1)} custom-call(bf16[64,64]{1,0:T(8,128)(2,1)S(1)} %get-tuple-element.15.table_ref, bf16[136,512]{1,0:T(8,128)(2,1)S(1)} %get-tuple-element.16.refs_0_.refs_8_, bf16[136,512]{1,0:T(8,128)(2,1)S(1)} %collective-permute-done.2.refs_1_, bf16[136,512]{1,0:T(8,128)(2,1)S(1)} %collective-permute-done.1.refs_2_, ...), custom_call_target="tpu_custom_call" | custom-call | flops 134217728 | bytes 1179648 | tf_op jit(solution)/shard_map/pallas_call | solution.py:89
  21.3 2.6 %collective-permute-start.12 = (f32[1,128]{1,0:T(1,128)S(1)}, f32[1,128]{1,0:T(1,128)S(1)}, u32[]{:S(2)}, u32[]{:S(2)}) collective-permute-start(f32[1,128]{1,0:T(1,128)S(1)} %shard_map.39), channel_id=1, source_target_pairs={{16,0},{17,1},{18,2},{19,3},{20,4},{21,5},{22,6},{23,7},{24,8},{25... | collective-permute-start | bytes 1544 | tf_op jit(solution)/shard_map/ppermute | solution.py:114
  23.9 0.2 collective-permute-done.10
  24.1 0.0 collective-permute-done.9
  24.1 1.7 %collective-permute-done.12 = f32[1,128]{1,0:T(1,128)S(1)} collective-permute-done((f32[1,128]{1,0:T(1,128)S(1)}, f32[1,128]{1,0:T(1,128)S(1)}, u32[]{:S(2)}, u32[]{:S(2)}) %collective-permute-start.12) | collective-permute-done | bytes 544 | tf_op jit(solution)/shard_map/ppermute | solution.py:114
  25.8 0.5 %maximum_bitcast_fusion = f32[128]{0:T(128)} fusion(f32[1,128]{1,0:T(1,128)S(1)} %collective-permute-done.12, f32[1,128]{1,0:T(1,128)S(1)} %collective-permute-done.10, f32[1,128]{1,0:T(1,128)S(1)} %get-tuple-element.22, f32[1,128]{1,0:T(1,128)S(1)} %collective-permute-done.9), kind=kLoop, calls=%fused_computation | loop fusion | flops 384 | bytes 2560 | tf_op jit(solution)/shard_map/reshape | solution.py:160
Async XLA Ops:
  1.1 8.6 %collective-permute-start = (bf16[136,512]{1,0:T(8,128)(2,1)S(1)}, bf16[136,512]{1,0:T(8,128)(2,1)S(1)}, u32[]{:S(2)}, u32[]{:S(2)}) collective-permute-start(bf16[136,512]{1,0:T(8,128)(2,1)S(1)} %get-tuple-element.16.refs_0_.refs_8_), channel_id=1, source_target_pairs={{6,0},{7,1},{4,2},{5,3},{2,4},{3,5},{0,6},{1,7},{14,8},{15,9},{12,... | collective-permute-start | bytes 417800 | tf_op jit(solution)/shard_map/ppermute | solution.py:114
  5.1 6.7 %collective-permute-start.1 = (bf16[136,512]{1,0:T(8,128)(2,1)S(1)}, bf16[136,512]{1,0:T(8,128)(2,1)S(1)}, u32[]{:S(2)}, u32[]{:S(2)}) collective-permute-start(bf16[136,512]{1,0:T(8,128)(2,1)S(1)} %get-tuple-element.16.refs_0_.refs_8_), channel_id=1, source_target_pairs={{4,0},{5,1},{6,2},{7,3},{0,4},{1,5},{2,6},{3,7},{12,8},{13,9},{14,... | collective-permute-start | bytes 417800 | tf_op jit(solution)/shard_map/ppermute | solution.py:114
  5.6 6.4 %collective-permute-start.2 = (bf16[136,512]{1,0:T(8,128)(2,1)S(1)}, bf16[136,512]{1,0:T(8,128)(2,1)S(1)}, u32[]{:S(2)}, u32[]{:S(2)}) collective-permute-start(bf16[136,512]{1,0:T(8,128)(2,1)S(1)} %get-tuple-element.16.refs_0_.refs_8_), channel_id=1, source_target_pairs={{2,0},{3,1},{0,2},{1,3},{6,4},{7,5},{4,6},{5,7},{10,8},{11,9},{8,1... | collective-permute-start | bytes 417800 | tf_op jit(solution)/shard_map/ppermute | solution.py:114
  5.7 8.4 %collective-permute-start.7 = (bf16[136,512]{1,0:T(8,128)(2,1)S(1)}, bf16[136,512]{1,0:T(8,128)(2,1)S(1)}, u32[]{:S(2)}, u32[]{:S(2)}) collective-permute-start(bf16[136,512]{1,0:T(8,128)(2,1)S(1)} %get-tuple-element.16.refs_0_.refs_8_), channel_id=1, source_target_pairs={{24,0},{25,1},{26,2},{27,3},{28,4},{29,5},{30,6},{31,7},{16,8},{17... | collective-permute-start | bytes 417800 | tf_op jit(solution)/shard_map/ppermute | solution.py:114
  9.7 5.9 %collective-permute-start.8 = (bf16[136,512]{1,0:T(8,128)(2,1)S(1)}, bf16[136,512]{1,0:T(8,128)(2,1)S(1)}, u32[]{:S(2)}, u32[]{:S(2)}) collective-permute-start(bf16[136,512]{1,0:T(8,128)(2,1)S(1)} %get-tuple-element.16.refs_0_.refs_8_), channel_id=1, source_target_pairs={{8,0},{9,1},{10,2},{11,3},{12,4},{13,5},{14,6},{15,7},{0,8},{1,9},... | collective-permute-start | bytes 417800 | tf_op jit(solution)/shard_map/ppermute | solution.py:114
  9.7 7.6 %collective-permute-start.3 = (bf16[136,512]{1,0:T(8,128)(2,1)S(1)}, bf16[136,512]{1,0:T(8,128)(2,1)S(1)}, u32[]{:S(2)}, u32[]{:S(2)}) collective-permute-start(bf16[136,512]{1,0:T(8,128)(2,1)S(1)} %get-tuple-element.16.refs_0_.refs_8_), channel_id=1, source_target_pairs={{1,0},{0,1},{3,2},{2,3},{5,4},{4,5},{7,6},{6,7},{9,8},{8,9},{11,10... | collective-permute-start | bytes 417800 | tf_op jit(solution)/shard_map/ppermute | solution.py:114
  12.0 5.3 %collective-permute-start.4 = (bf16[136,512]{1,0:T(8,128)(2,1)S(1)}, bf16[136,512]{1,0:T(8,128)(2,1)S(1)}, u32[]{:S(2)}, u32[]{:S(2)}) collective-permute-start(bf16[136,512]{1,0:T(8,128)(2,1)S(1)} %collective-permute-done.2.refs_1_), channel_id=1, source_target_pairs={{1,0},{0,1},{3,2},{2,3},{5,4},{4,5},{7,6},{6,7},{9,8},{8,9},{11,10... | collective-permute-start | bytes 417800 | tf_op jit(solution)/shard_map/ppermute | solution.py:114
  12.0 5.3 %collective-permute-start.5 = (bf16[136,512]{1,0:T(8,128)(2,1)S(1)}, bf16[136,512]{1,0:T(8,128)(2,1)S(1)}, u32[]{:S(2)}, u32[]{:S(2)}) collective-permute-start(bf16[136,512]{1,0:T(8,128)(2,1)S(1)} %collective-permute-done.1.refs_2_), channel_id=1, source_target_pairs={{1,0},{0,1},{3,2},{2,3},{5,4},{4,5},{7,6},{6,7},{9,8},{8,9},{11,10... | collective-permute-start | bytes 417800 | tf_op jit(solution)/shard_map/ppermute | solution.py:114
  14.1 3.2 %collective-permute-start.6 = (bf16[136,512]{1,0:T(8,128)(2,1)S(1)}, bf16[136,512]{1,0:T(8,128)(2,1)S(1)}, u32[]{:S(2)}, u32[]{:S(2)}) collective-permute-start(bf16[136,512]{1,0:T(8,128)(2,1)S(1)} %collective-permute-done.refs_3_), channel_id=1, source_target_pairs={{1,0},{0,1},{3,2},{2,3},{5,4},{4,5},{7,6},{6,7},{9,8},{8,9},{11,10... | collective-permute-start | bytes 417800 | tf_op jit(solution)/shard_map/ppermute | solution.py:114
  15.6 5.1 %collective-permute-start.11 = (bf16[136,512]{1,0:T(8,128)(2,1)S(1)}, bf16[136,512]{1,0:T(8,128)(2,1)S(1)}, u32[]{:S(2)}, u32[]{:S(2)}) collective-permute-start(bf16[136,512]{1,0:T(8,128)(2,1)S(1)} %collective-permute-done.7.refs_10_), channel_id=1, source_target_pairs={{8,0},{9,1},{10,2},{11,3},{12,4},{13,5},{14,6},{15,7},{0,8},{1,9},... | collective-permute-start | bytes 417800 | tf_op jit(solution)/shard_map/ppermute | solution.py:114
  18.7 5.4 %collective-permute-start.10 = (f32[1,128]{1,0:T(1,128)S(1)}, f32[1,128]{1,0:T(1,128)S(1)}, u32[]{:S(2)}, u32[]{:S(2)}) collective-permute-start(f32[1,128]{1,0:T(1,128)S(1)} %get-tuple-element.24), channel_id=1, source_target_pairs={{24,0},{25,1},{26,2},{27,3},{28,4},{29,5},{30,6},{31,7},{16,8},{17... | collective-permute-start | bytes 1544 | tf_op jit(solution)/shard_map/ppermute | solution.py:114
  20.4 3.7 %collective-permute-start.9 = (f32[1,128]{1,0:T(1,128)S(1)}, f32[1,128]{1,0:T(1,128)S(1)}, u32[]{:S(2)}, u32[]{:S(2)}) collective-permute-start(f32[1,128]{1,0:T(1,128)S(1)} %get-tuple-element.23), channel_id=1, source_target_pairs={{8,0},{9,1},{10,2},{11,3},{12,4},{13,5},{14,6},{15,7},{0,8},{1,9},... | collective-permute-start | bytes 1544 | tf_op jit(solution)/shard_map/ppermute | solution.py:114
  21.3 4.5 %collective-permute-start.12 = (f32[1,128]{1,0:T(1,128)S(1)}, f32[1,128]{1,0:T(1,128)S(1)}, u32[]{:S(2)}, u32[]{:S(2)}) collective-permute-start(f32[1,128]{1,0:T(1,128)S(1)} %shard_map.39), channel_id=1, source_target_pairs={{16,0},{17,1},{18,2},{19,3},{20,4},{21,5},{22,6},{23,7},{24,8},{25... | collective-permute-start | bytes 1544 | tf_op jit(solution)/shard_map/ppermute | solution.py:114

commit v23 on v22

--- a/solution.py
+++ b/solution.py
@@ -47,7 +47,7 @@
     return jnp.where(index == number, 1.0, 0.0).astype(jnp.bfloat16)
 
 
-def best_kernel(n_keys, own, ranks, table_ref, *refs):
+def best_kernel(n_keys, n_spans, own, ranks, table_ref, *refs):
     n_queries = (len(refs) - n_keys) // 2
     keys, queries, outs = refs[:n_keys], refs[n_keys : n_keys + n_queries], refs[n_keys + n_queries :]
     rows = keys[0].shape[0] - AUX
@@ -58,36 +58,50 @@
     def hot(block):
         return one_hot(block[rows:, :rows].astype(jnp.float32), clusters)
 
-    key_hot = jnp.concatenate([hot(b) for b in keys], axis=1)
-    key_rows = jnp.concatenate([b[:rows, :] for b in keys], axis=0)
-    for j in range(n_queries):
-        mixed = jnp.dot(table_ref[...], hot(queries[j]), preferred_element_type=jnp.float32).astype(jnp.bfloat16)
-        weight = lax.dot_general(key_hot, mixed, (((0,), (0,)), ((), ())), preferred_element_type=jnp.float32)
-        sims = lax.dot_general(
-            key_rows, queries[j][:rows, :], (((1,), (1,)), ((), ())), preferred_element_type=jnp.float32
-        )
-        score = jnp.where(weight > 0, weight * sims, -1.0)
-        best = jnp.full((1, rows), -1.0, jnp.float32)
-        for i in range(n_keys):
-            part = score[i * rows : (i + 1) * rows, :]
-            if own and i + j == 0:
-                k = lax.broadcasted_iota(jnp.int32, (rows, rows), 0)
-                q = lax.broadcasted_iota(jnp.int32, (rows, rows), 1)
-                found = jnp.max(jnp.where(k < q, part, -1.0), axis=0, keepdims=True)
-            else:
-                found = jnp.max(part, axis=0, keepdims=True)
-                found = jnp.where(ranks[i] < ranks[n_keys + j], found, -1.0)
-            best = jnp.maximum(best, found)
-        outs[j][...] = best
+    mixed = [
+        jnp.dot(table_ref[...], hot(query), preferred_element_type=jnp.float32).astype(jnp.bfloat16)
+        for query in queries
+    ]
+
+    def search(span, first):
+        key_hot = jnp.concatenate([hot(keys[i]) for i in span], axis=1)
+        key_rows = jnp.concatenate([keys[i][:rows, :] for i in span], axis=0)
+        for j in range(n_queries):
+            weight = lax.dot_general(
+                key_hot, mixed[j], (((0,), (0,)), ((), ())), preferred_element_type=jnp.float32
+            )
+            sims = lax.dot_general(
+                key_rows, queries[j][:rows, :], (((1,), (1,)), ((), ())), preferred_element_type=jnp.float32
+            )
+            score = jnp.where(weight > 0, weight * sims, -1.0)
+            best = jnp.full((1, rows), -1.0, jnp.float32) if first else outs[j][...]
+            for at, i in enumerate(span):
+                part = score[at * rows : (at + 1) * rows, :]
+                if own and i + j == 0:
+                    k = lax.broadcasted_iota(jnp.int32, (rows, rows), 0)
+                    q = lax.broadcasted_iota(jnp.int32, (rows, rows), 1)
+                    found = jnp.max(jnp.where(k < q, part, -1.0), axis=0, keepdims=True)
+                else:
+                    found = jnp.max(part, axis=0, keepdims=True)
+                    found = jnp.where(ranks[i] < ranks[n_keys + j], found, -1.0)
+                best = jnp.maximum(best, found)
+            outs[j][...] = best
+
+    width = n_keys // n_spans
+    search(range(width), True)
+    for t in range(1, n_spans):
+        @pl.when(ranks[t * width] < ranks[0])
+        def _():
+            search(range(t * width, (t + 1) * width), False)
 
 
-def best_of(keys, queries, table, own):
+def best_of(keys, n_spans, queries, table, own):
     rows, width = keys[0][0].shape[0] - AUX, keys[0][0].shape[1]
     vmem = pl.BlockSpec(memory_space=pltpu.VMEM)
     ranks = [r for _, r in keys + queries]
     pairs = len(keys) * len(queries) * rows * rows
     return pl.pallas_call(
-        functools.partial(best_kernel, len(keys), own, ranks),
+        functools.partial(best_kernel, len(keys), n_spans, own, ranks),
         out_shape=[jax.ShapeDtypeStruct((1, rows), jnp.float32)] * len(queries),
         in_specs=[vmem] * (1 + len(keys) + len(queries)),
         out_specs=[vmem] * len(queries),
@@ -153,9 +167,9 @@
         visit_rank = [rank(z=s) for s in offsets]
         first = list(zip(first, visit_rank))
         last = list(zip(last, visit_rank[len(first) :]))
-        best = best_of(near + far, near[:1] + first, table, True)
+        best = best_of(near + far, n_grp, near[:1] + first, table, True)
         if last:
-            best = best + best_of(near + far, last, table, False)
+            best = best + best_of(near + far, n_grp, last, table, False)
         found = [best[0]] + [along(b, -s) for b, s in zip(best[1:], offsets)]
         return functools.reduce(jnp.maximum, found).reshape(rows)
 

time: 26.5 us -> 26.3 us (level)
  waiting for transfers between devices: 7.57 us -> 8.82 us
  Pallas kernels: 3.17 us -> 2.37 us
  starting transfers between devices: 15 us -> 14.4 us
    ppermute x13, waiting for transfers between devices: 7.57 us -> 8.82 us  [permute(): return lax.ppermute(x, ('clu', 'grp'), pairs)]
    pallas_call x2, Pallas kernels: 2.07 us -> 1.26 us  [best_of(): pl.pallas_call(functools.partial(best_kernel, len(keys), n_spans, own, ra...]
    ppermute x13, starting transfers between devices: 15 us -> 14.4 us  [permute(): return lax.ppermute(x, ('clu', 'grp'), pairs)]
  transfers between devices with their start and end apart: 13 -> 13, of which waited for: 7 -> 7; matrix products, arithmetic and copies ran while one was open for 0% -> 0% of each run, Pallas kernels for 8% -> 5%
where the time goes in v23:
time: 26.3 us; the launch traced here: 26.2 us
  starting transfers between devices  14.4 us (55%)
  waiting for transfers between devices  8.82 us (34%)
  Pallas kernels  2.37 us (9%)
  other arithmetic  0.52 us (2%)
    ppermute x13, starting transfers between devices, permute(): return lax.ppermute(x, ('clu', 'grp'), pairs)  14.4 us
    ppermute x13, waiting for transfers between devices, permute(): return lax.ppermute(x, ('clu', 'grp'), pairs)  8.82 us
    pallas_call x2, Pallas kernels, best_of(): pl.pallas_call(functools.partial(best_kernel, len(keys), n_spans, own, ra...  1.26 us
    pallas_call x1, Pallas kernels, pack(): pl.pallas_call(functools.partial(pack_kernel, groups), out_shape=[pltpu.V...  1.1 us
  transfers between devices with their start and end apart: 13, of which 7 were waited for; matrix products, arithmetic and copies ran while one was open for 0% of the time, Pallas kernels for 5%

profile of v23, /device:TPU:0, one launch (start us, length us, event | category | flops | bytes accessed | tf_op | source)
XLA Modules:
  0.0 26.2 jit_solution(16489962012878986404)
XLA Ops:
  0.0 1.1 %shard_map.37 = (bf16[136,512]{1,0:T(8,128)(2,1)S(1)}, bf16[64,64]{1,0:T(8,128)(2,1)S(1)}) custom-call(bf16[128,512]{1,0:T(8,128)(2,1)} %emb_ref.1, s32[1,128]{1,0:T(1,128)} %bitcast.4, s32[1,64]{1,0:T(1,128)} %bitcast.5), custom_call_target="tpu_custom_call" | custom-call | tf_op jit(solution)/shard_map/pallas_call | solution.py:38
  1.1 4.0 %collective-permute-start = (bf16[136,512]{1,0:T(8,128)(2,1)S(1)}, bf16[136,512]{1,0:T(8,128)(2,1)S(1)}, u32[]{:S(2)}, u32[]{:S(2)}) collective-permute-start(bf16[136,512]{1,0:T(8,128)(2,1)S(1)} %get-tuple-element.16.refs_0_.refs_8_), channel_id=1, source_target_pairs={{6,0},{7,1},{4,2},{5,3},{2,4},{3,5},{0,6},{1,7},{14,8},{15,9},{12,... | collective-permute-start | bytes 417800 | tf_op jit(solution)/shard_map/ppermute | solution.py:128
  5.1 0.5 %collective-permute-start.1 = (bf16[136,512]{1,0:T(8,128)(2,1)S(1)}, bf16[136,512]{1,0:T(8,128)(2,1)S(1)}, u32[]{:S(2)}, u32[]{:S(2)}) collective-permute-start(bf16[136,512]{1,0:T(8,128)(2,1)S(1)} %get-tuple-element.16.refs_0_.refs_8_), channel_id=1, source_target_pairs={{4,0},{5,1},{6,2},{7,3},{0,4},{1,5},{2,6},{3,7},{12,8},{13,9},{14,... | collective-permute-start | bytes 417800 | tf_op jit(solution)/shard_map/ppermute | solution.py:128
  5.6 0.1 collective-permute-start.2
  5.7 4.0 %collective-permute-start.7 = (bf16[136,512]{1,0:T(8,128)(2,1)S(1)}, bf16[136,512]{1,0:T(8,128)(2,1)S(1)}, u32[]{:S(2)}, u32[]{:S(2)}) collective-permute-start(bf16[136,512]{1,0:T(8,128)(2,1)S(1)} %get-tuple-element.16.refs_0_.refs_8_), channel_id=1, source_target_pairs={{24,0},{25,1},{26,2},{27,3},{28,4},{29,5},{30,6},{31,7},{16,8},{17... | collective-permute-start | bytes 417800 | tf_op jit(solution)/shard_map/ppermute | solution.py:128
  9.7 0.0 collective-permute-start.8
  9.7 0.0 collective-permute-done.refs_3_
  9.7 0.0 collective-permute-start.3
  9.7 2.0 %collective-permute-done.1.refs_2_ = bf16[136,512]{1,0:T(8,128)(2,1)S(1)} collective-permute-done((bf16[136,512]{1,0:T(8,128)(2,1)S(1)}, bf16[136,512]{1,0:T(8,128)(2,1)S(1)}, u32[]{:S(2)}, u32[]{:S(2)}) %collective-permute-start.1) | collective-permute-done | bytes 139296 | tf_op jit(solution)/shard_map/ppermute | solution.py:128
  11.7 0.3 collective-permute-done.2.refs_1_
  12.0 0.0 collective-permute-start.4
  12.0 0.5 %collective-permute-start.5 = (bf16[136,512]{1,0:T(8,128)(2,1)S(1)}, bf16[136,512]{1,0:T(8,128)(2,1)S(1)}, u32[]{:S(2)}, u32[]{:S(2)}) collective-permute-start(bf16[136,512]{1,0:T(8,128)(2,1)S(1)} %collective-permute-done.1.refs_2_), channel_id=1, source_target_pairs={{1,0},{0,1},{3,2},{2,3},{5,4},{4,5},{7,6},{6,7},{9,8},{8,9},{11,10... | collective-permute-start | bytes 417800 | tf_op jit(solution)/shard_map/ppermute | solution.py:128
  12.5 1.6 %collective-permute-done.7.refs_10_ = bf16[136,512]{1,0:T(8,128)(2,1)S(1)} collective-permute-done((bf16[136,512]{1,0:T(8,128)(2,1)S(1)}, bf16[136,512]{1,0:T(8,128)(2,1)S(1)}, u32[]{:S(2)}, u32[]{:S(2)}) %collective-permute-start.7) | collective-permute-done | bytes 139296 | tf_op jit(solution)/shard_map/ppermute | solution.py:128
  14.1 0.0 collective-permute-start.6
  14.1 1.5 %collective-permute-done.8.refs_9_ = bf16[136,512]{1,0:T(8,128)(2,1)S(1)} collective-permute-done((bf16[136,512]{1,0:T(8,128)(2,1)S(1)}, bf16[136,512]{1,0:T(8,128)(2,1)S(1)}, u32[]{:S(2)}, u32[]{:S(2)}) %collective-permute-start.8) | collective-permute-done | bytes 139296 | tf_op jit(solution)/shard_map/ppermute | solution.py:128
  15.6 1.6 %collective-permute-start.11 = (bf16[136,512]{1,0:T(8,128)(2,1)S(1)}, bf16[136,512]{1,0:T(8,128)(2,1)S(1)}, u32[]{:S(2)}, u32[]{:S(2)}) collective-permute-start(bf16[136,512]{1,0:T(8,128)(2,1)S(1)} %collective-permute-done.7.refs_10_), channel_id=1, source_target_pairs={{8,0},{9,1},{10,2},{11,3},{12,4},{13,5},{14,6},{15,7},{0,8},{1,9},... | collective-permute-start | bytes 417800 | tf_op jit(solution)/shard_map/ppermute | solution.py:128
  17.3 0.0 collective-permute-done.3.refs_4_
  17.3 0.0 collective-permute-done.4.refs_5_
  17.3 0.0 collective-permute-done.5.refs_6_
  17.3 0.0 collective-permute-done.6.refs_7_
  17.3 0.8 %shard_map.38 = (f32[1,128]{1,0:T(1,128)S(1)}, f32[1,128]{1,0:T(1,128)S(1)}, f32[1,128]{1,0:T(1,128)S(1)}) custom-call(bf16[64,64]{1,0:T(8,128)(2,1)S(1)} %get-tuple-element.15.table_ref, bf16[136,512]{1,0:T(8,128)(2,1)S(1)} %get-tuple-element.16.refs_0_.refs_8_, bf16[136,512]{1,0:T(8,128)(2,1)S(1)} %collective-permute-done.2.refs_1_, ...), custom_call_target="tpu_custom_call" | custom-call | flops 402653184 | bytes 1441792 | tf_op jit(solution)/shard_map/pallas_call | solution.py:103
  18.1 1.7 %collective-permute-start.10 = (f32[1,128]{1,0:T(1,128)S(1)}, f32[1,128]{1,0:T(1,128)S(1)}, u32[]{:S(2)}, u32[]{:S(2)}) collective-permute-start(f32[1,128]{1,0:T(1,128)S(1)} %get-tuple-element.24), channel_id=1, source_target_pairs={{24,0},{25,1},{26,2},{27,3},{28,4},{29,5},{30,6},{31,7},{16,8},{17... | collective-permute-start | bytes 1544 | tf_op jit(solution)/shard_map/ppermute | solution.py:128
  19.8 0.0 collective-permute-start.9
  19.8 0.9 %collective-permute-done.11.refs_8_ = bf16[136,512]{1,0:T(8,128)(2,1)S(1)} collective-permute-done((bf16[136,512]{1,0:T(8,128)(2,1)S(1)}, bf16[136,512]{1,0:T(8,128)(2,1)S(1)}, u32[]{:S(2)}, u32[]{:S(2)}) %collective-permute-start.11) | collective-permute-done | bytes 139296 | tf_op jit(solution)/shard_map/ppermute | solution.py:128
  20.7 0.5 %shard_map.39 = f32[1,128]{1,0:T(1,128)S(1)} custom-call(bf16[64,64]{1,0:T(8,128)(2,1)S(1)} %get-tuple-element.15.table_ref, bf16[136,512]{1,0:T(8,128)(2,1)S(1)} %get-tuple-element.16.refs_0_.refs_8_, bf16[136,512]{1,0:T(8,128)(2,1)S(1)} %collective-permute-done.2.refs_1_, bf16[136,512]{1,0:T(8,128)(2,1)S(1)} %collective-permute-done.1.refs_2_, ...), custom_call_target="tpu_custom_call" | custom-call | flops 134217728 | bytes 1179648 | tf_op jit(solution)/shard_map/pallas_call | solution.py:103
  21.1 1.9 %collective-permute-start.12 = (f32[1,128]{1,0:T(1,128)S(1)}, f32[1,128]{1,0:T(1,128)S(1)}, u32[]{:S(2)}, u32[]{:S(2)}) collective-permute-start(f32[1,128]{1,0:T(1,128)S(1)} %shard_map.39), channel_id=1, source_target_pairs={{16,0},{17,1},{18,2},{19,3},{20,4},{21,5},{22,6},{23,7},{24,8},{25... | collective-permute-start | bytes 1544 | tf_op jit(solution)/shard_map/ppermute | solution.py:128
  23.1 0.4 %collective-permute-done.10 = f32[1,128]{1,0:T(1,128)S(1)} collective-permute-done((f32[1,128]{1,0:T(1,128)S(1)}, f32[1,128]{1,0:T(1,128)S(1)}, u32[]{:S(2)}, u32[]{:S(2)}) %collective-permute-start.10) | collective-permute-done | bytes 544 | tf_op jit(solution)/shard_map/ppermute | solution.py:128
  23.5 0.0 collective-permute-done.9
  23.5 2.1 %collective-permute-done.12 = f32[1,128]{1,0:T(1,128)S(1)} collective-permute-done((f32[1,128]{1,0:T(1,128)S(1)}, f32[1,128]{1,0:T(1,128)S(1)}, u32[]{:S(2)}, u32[]{:S(2)}) %collective-permute-start.12) | collective-permute-done | bytes 544 | tf_op jit(solution)/shard_map/ppermute | solution.py:128
  25.7 0.5 %maximum_bitcast_fusion = f32[128]{0:T(128)} fusion(f32[1,128]{1,0:T(1,128)S(1)} %collective-permute-done.12, f32[1,128]{1,0:T(1,128)S(1)} %collective-permute-done.10, f32[1,128]{1,0:T(1,128)S(1)} %get-tuple-element.22, f32[1,128]{1,0:T(1,128)S(1)} %collective-permute-done.9), kind=kLoop, calls=%fused_computation | loop fusion | flops 384 | bytes 2560 | tf_op jit(solution)/shard_map/reshape | solution.py:174
Async XLA Ops:
  1.1 8.6 %collective-permute-start = (bf16[136,512]{1,0:T(8,128)(2,1)S(1)}, bf16[136,512]{1,0:T(8,128)(2,1)S(1)}, u32[]{:S(2)}, u32[]{:S(2)}) collective-permute-start(bf16[136,512]{1,0:T(8,128)(2,1)S(1)} %get-tuple-element.16.refs_0_.refs_8_), channel_id=1, source_target_pairs={{6,0},{7,1},{4,2},{5,3},{2,4},{3,5},{0,6},{1,7},{14,8},{15,9},{12,... | collective-permute-start | bytes 417800 | tf_op jit(solution)/shard_map/ppermute | solution.py:128
  5.1 6.7 %collective-permute-start.1 = (bf16[136,512]{1,0:T(8,128)(2,1)S(1)}, bf16[136,512]{1,0:T(8,128)(2,1)S(1)}, u32[]{:S(2)}, u32[]{:S(2)}) collective-permute-start(bf16[136,512]{1,0:T(8,128)(2,1)S(1)} %get-tuple-element.16.refs_0_.refs_8_), channel_id=1, source_target_pairs={{4,0},{5,1},{6,2},{7,3},{0,4},{1,5},{2,6},{3,7},{12,8},{13,9},{14,... | collective-permute-start | bytes 417800 | tf_op jit(solution)/shard_map/ppermute | solution.py:128
  5.6 6.4 %collective-permute-start.2 = (bf16[136,512]{1,0:T(8,128)(2,1)S(1)}, bf16[136,512]{1,0:T(8,128)(2,1)S(1)}, u32[]{:S(2)}, u32[]{:S(2)}) collective-permute-start(bf16[136,512]{1,0:T(8,128)(2,1)S(1)} %get-tuple-element.16.refs_0_.refs_8_), channel_id=1, source_target_pairs={{2,0},{3,1},{0,2},{1,3},{6,4},{7,5},{4,6},{5,7},{10,8},{11,9},{8,1... | collective-permute-start | bytes 417800 | tf_op jit(solution)/shard_map/ppermute | solution.py:128
  5.7 8.4 %collective-permute-start.7 = (bf16[136,512]{1,0:T(8,128)(2,1)S(1)}, bf16[136,512]{1,0:T(8,128)(2,1)S(1)}, u32[]{:S(2)}, u32[]{:S(2)}) collective-permute-start(bf16[136,512]{1,0:T(8,128)(2,1)S(1)} %get-tuple-element.16.refs_0_.refs_8_), channel_id=1, source_target_pairs={{24,0},{25,1},{26,2},{27,3},{28,4},{29,5},{30,6},{31,7},{16,8},{17... | collective-permute-start | bytes 417800 | tf_op jit(solution)/shard_map/ppermute | solution.py:128
  9.7 5.9 %collective-permute-start.8 = (bf16[136,512]{1,0:T(8,128)(2,1)S(1)}, bf16[136,512]{1,0:T(8,128)(2,1)S(1)}, u32[]{:S(2)}, u32[]{:S(2)}) collective-permute-start(bf16[136,512]{1,0:T(8,128)(2,1)S(1)} %get-tuple-element.16.refs_0_.refs_8_), channel_id=1, source_target_pairs={{8,0},{9,1},{10,2},{11,3},{12,4},{13,5},{14,6},{15,7},{0,8},{1,9},... | collective-permute-start | bytes 417800 | tf_op jit(solution)/shard_map/ppermute | solution.py:128
  9.7 7.6 %collective-permute-start.3 = (bf16[136,512]{1,0:T(8,128)(2,1)S(1)}, bf16[136,512]{1,0:T(8,128)(2,1)S(1)}, u32[]{:S(2)}, u32[]{:S(2)}) collective-permute-start(bf16[136,512]{1,0:T(8,128)(2,1)S(1)} %get-tuple-element.16.refs_0_.refs_8_), channel_id=1, source_target_pairs={{1,0},{0,1},{3,2},{2,3},{5,4},{4,5},{7,6},{6,7},{9,8},{8,9},{11,10... | collective-permute-start | bytes 417800 | tf_op jit(solution)/shard_map/ppermute | solution.py:128
  12.0 5.3 %collective-permute-start.4 = (bf16[136,512]{1,0:T(8,128)(2,1)S(1)}, bf16[136,512]{1,0:T(8,128)(2,1)S(1)}, u32[]{:S(2)}, u32[]{:S(2)}) collective-permute-start(bf16[136,512]{1,0:T(8,128)(2,1)S(1)} %collective-permute-done.2.refs_1_), channel_id=1, source_target_pairs={{1,0},{0,1},{3,2},{2,3},{5,4},{4,5},{7,6},{6,7},{9,8},{8,9},{11,10... | collective-permute-start | bytes 417800 | tf_op jit(solution)/shard_map/ppermute | solution.py:128
  12.0 5.3 %collective-permute-start.5 = (bf16[136,512]{1,0:T(8,128)(2,1)S(1)}, bf16[136,512]{1,0:T(8,128)(2,1)S(1)}, u32[]{:S(2)}, u32[]{:S(2)}) collective-permute-start(bf16[136,512]{1,0:T(8,128)(2,1)S(1)} %collective-permute-done.1.refs_2_), channel_id=1, source_target_pairs={{1,0},{0,1},{3,2},{2,3},{5,4},{4,5},{7,6},{6,7},{9,8},{8,9},{11,10... | collective-permute-start | bytes 417800 | tf_op jit(solution)/shard_map/ppermute | solution.py:128
  14.1 3.2 %collective-permute-start.6 = (bf16[136,512]{1,0:T(8,128)(2,1)S(1)}, bf16[136,512]{1,0:T(8,128)(2,1)S(1)}, u32[]{:S(2)}, u32[]{:S(2)}) collective-permute-start(bf16[136,512]{1,0:T(8,128)(2,1)S(1)} %collective-permute-done.refs_3_), channel_id=1, source_target_pairs={{1,0},{0,1},{3,2},{2,3},{5,4},{4,5},{7,6},{6,7},{9,8},{8,9},{11,10... | collective-permute-start | bytes 417800 | tf_op jit(solution)/shard_map/ppermute | solution.py:128
  15.6 5.1 %collective-permute-start.11 = (bf16[136,512]{1,0:T(8,128)(2,1)S(1)}, bf16[136,512]{1,0:T(8,128)(2,1)S(1)}, u32[]{:S(2)}, u32[]{:S(2)}) collective-permute-start(bf16[136,512]{1,0:T(8,128)(2,1)S(1)} %collective-permute-done.7.refs_10_), channel_id=1, source_target_pairs={{8,0},{9,1},{10,2},{11,3},{12,4},{13,5},{14,6},{15,7},{0,8},{1,9},... | collective-permute-start | bytes 417800 | tf_op jit(solution)/shard_map/ppermute | solution.py:128
  18.1 5.4 %collective-permute-start.10 = (f32[1,128]{1,0:T(1,128)S(1)}, f32[1,128]{1,0:T(1,128)S(1)}, u32[]{:S(2)}, u32[]{:S(2)}) collective-permute-start(f32[1,128]{1,0:T(1,128)S(1)} %get-tuple-element.24), channel_id=1, source_target_pairs={{24,0},{25,1},{26,2},{27,3},{28,4},{29,5},{30,6},{31,7},{16,8},{17... | collective-permute-start | bytes 1544 | tf_op jit(solution)/shard_map/ppermute | solution.py:128
  19.8 3.7 %collective-permute-start.9 = (f32[1,128]{1,0:T(1,128)S(1)}, f32[1,128]{1,0:T(1,128)S(1)}, u32[]{:S(2)}, u32[]{:S(2)}) collective-permute-start(f32[1,128]{1,0:T(1,128)S(1)} %get-tuple-element.23), channel_id=1, source_target_pairs={{8,0},{9,1},{10,2},{11,3},{12,4},{13,5},{14,6},{15,7},{0,8},{1,9},... | collective-permute-start | bytes 1544 | tf_op jit(solution)/shard_map/ppermute | solution.py:128
  21.1 4.5 %collective-permute-start.12 = (f32[1,128]{1,0:T(1,128)S(1)}, f32[1,128]{1,0:T(1,128)S(1)}, u32[]{:S(2)}, u32[]{:S(2)}) collective-permute-start(f32[1,128]{1,0:T(1,128)S(1)} %shard_map.39), channel_id=1, source_target_pairs={{16,0},{17,1},{18,2},{19,3},{20,4},{21,5},{22,6},{23,7},{24,8},{25... | collective-permute-start | bytes 1544 | tf_op jit(solution)/shard_map/ppermute | solution.py:128

commit v24 on v23

--- a/solution.py
+++ b/solution.py
@@ -148,8 +148,9 @@
         near = [permute(own, lambda z, a, g: (z, turned(a, s, wide), g)) for s in reversed(range(1, wide))]
         middle = along(own, length - 1) if half < length else None
         first = [along(own, s) for s in range(1, half)]
-        near = lax.optimization_barrier(near)
-        middle, first = lax.optimization_barrier((middle, first))
+        early, middle = lax.optimization_barrier((near[:-1], middle))
+        late, first = lax.optimization_barrier((near[-1:], first))
+        near = early + late
         near = near[::-1]
         last = [along(middle, s) for s in range(1, half)] if half < length else []
         offsets = list(range(1, half))

time: 26.3 us -> 27.2 us (1.034)
  waiting for transfers between devices: 8.82 us -> 9.89 us
    ppermute x13, waiting for transfers between devices: 8.82 us -> 9.89 us  [permute(): return lax.ppermute(x, ('clu', 'grp'), pairs)]
  transfers between devices with their start and end apart: 13 -> 13, of which waited for: 7 -> 6; matrix products, arithmetic and copies ran while one was open for 0% -> 0% of each run, Pallas kernels for 5% -> 5%
where the time goes in v24:
time: 27.2 us; the launch traced here: 27.1 us
  starting transfers between devices  14.2 us (52%)
  waiting for transfers between devices  9.89 us (36%)
  Pallas kernels  2.37 us (9%)
  other arithmetic  0.52 us (2%)
    ppermute x13, starting transfers between devices, permute(): return lax.ppermute(x, ('clu', 'grp'), pairs)  14.2 us
    ppermute x13, waiting for transfers between devices, permute(): return lax.ppermute(x, ('clu', 'grp'), pairs)  9.89 us
    pallas_call x2, Pallas kernels, best_of(): pl.pallas_call(functools.partial(best_kernel, len(keys), n_spans, own, ra...  1.27 us
    pallas_call x1, Pallas kernels, pack(): pl.pallas_call(functools.partial(pack_kernel, groups), out_shape=[pltpu.V...  1.1 us
  transfers between devices with their start and end apart: 13, of which 6 were waited for; matrix products, arithmetic and copies ran while one was open for 0% of the time, Pallas kernels for 5%

profile of v24, /device:TPU:0, one launch (start us, length us, event | category | flops | bytes accessed | tf_op | source)
XLA Modules:
  0.0 27.1 jit_solution(17888897812979134367)
XLA Ops:
  0.0 1.1 %shard_map.37 = (bf16[136,512]{1,0:T(8,128)(2,1)S(1)}, bf16[64,64]{1,0:T(8,128)(2,1)S(1)}) custom-call(bf16[128,512]{1,0:T(8,128)(2,1)} %emb_ref.1, s32[1,128]{1,0:T(1,128)} %bitcast.4, s32[1,64]{1,0:T(1,128)} %bitcast.5), custom_call_target="tpu_custom_call" | custom-call | tf_op jit(solution)/shard_map/pallas_call | solution.py:38
  1.1 4.0 %collective-permute-start.2 = (bf16[136,512]{1,0:T(8,128)(2,1)S(1)}, bf16[136,512]{1,0:T(8,128)(2,1)S(1)}, u32[]{:S(2)}, u32[]{:S(2)}) collective-permute-start(bf16[136,512]{1,0:T(8,128)(2,1)S(1)} %get-tuple-element.16.refs_0_.refs_8_), channel_id=1, source_target_pairs={{6,0},{7,1},{4,2},{5,3},{2,4},{3,5},{0,6},{1,7},{14,8},{15,9},{12,... | collective-permute-start | bytes 417800 | tf_op jit(solution)/shard_map/ppermute | solution.py:128
  5.1 0.5 %collective-permute-start.3 = (bf16[136,512]{1,0:T(8,128)(2,1)S(1)}, bf16[136,512]{1,0:T(8,128)(2,1)S(1)}, u32[]{:S(2)}, u32[]{:S(2)}) collective-permute-start(bf16[136,512]{1,0:T(8,128)(2,1)S(1)} %get-tuple-element.16.refs_0_.refs_8_), channel_id=1, source_target_pairs={{4,0},{5,1},{6,2},{7,3},{0,4},{1,5},{2,6},{3,7},{12,8},{13,9},{14,... | collective-permute-start | bytes 417800 | tf_op jit(solution)/shard_map/ppermute | solution.py:128
  5.6 3.6 %collective-permute-start.4 = (bf16[136,512]{1,0:T(8,128)(2,1)S(1)}, bf16[136,512]{1,0:T(8,128)(2,1)S(1)}, u32[]{:S(2)}, u32[]{:S(2)}) collective-permute-start(bf16[136,512]{1,0:T(8,128)(2,1)S(1)} %get-tuple-element.16.refs_0_.refs_8_), channel_id=1, source_target_pairs={{24,0},{25,1},{26,2},{27,3},{28,4},{29,5},{30,6},{31,7},{16,8},{17... | collective-permute-start | bytes 417800 | tf_op jit(solution)/shard_map/ppermute | solution.py:128
  9.2 0.5 %collective-permute-start = (bf16[136,512]{1,0:T(8,128)(2,1)S(1)}, bf16[136,512]{1,0:T(8,128)(2,1)S(1)}, u32[]{:S(2)}, u32[]{:S(2)}) collective-permute-start(bf16[136,512]{1,0:T(8,128)(2,1)S(1)} %get-tuple-element.16.refs_0_.refs_8_), channel_id=1, source_target_pairs={{2,0},{3,1},{0,2},{1,3},{6,4},{7,5},{4,6},{5,7},{10,8},{11,9},{8,1... | collective-permute-start | bytes 417800 | tf_op jit(solution)/shard_map/ppermute | solution.py:128
  9.7 0.0 collective-permute-start.1
  9.7 0.0 collective-permute-done.2.refs_3_
  9.7 0.0 collective-permute-start.5
  9.7 2.0 %collective-permute-done.3.refs_2_ = bf16[136,512]{1,0:T(8,128)(2,1)S(1)} collective-permute-done((bf16[136,512]{1,0:T(8,128)(2,1)S(1)}, bf16[136,512]{1,0:T(8,128)(2,1)S(1)}, u32[]{:S(2)}, u32[]{:S(2)}) %collective-permute-start.3) | collective-permute-done | bytes 139296 | tf_op jit(solution)/shard_map/ppermute | solution.py:128
  11.7 2.2 %collective-permute-done.4.refs_10_ = bf16[136,512]{1,0:T(8,128)(2,1)S(1)} collective-permute-done((bf16[136,512]{1,0:T(8,128)(2,1)S(1)}, bf16[136,512]{1,0:T(8,128)(2,1)S(1)}, u32[]{:S(2)}, u32[]{:S(2)}) %collective-permute-start.4) | collective-permute-done | bytes 139296 | tf_op jit(solution)/shard_map/ppermute | solution.py:128
  13.9 0.0 collective-permute-start.7
  13.9 0.5 %collective-permute-start.8 = (bf16[136,512]{1,0:T(8,128)(2,1)S(1)}, bf16[136,512]{1,0:T(8,128)(2,1)S(1)}, u32[]{:S(2)}, u32[]{:S(2)}) collective-permute-start(bf16[136,512]{1,0:T(8,128)(2,1)S(1)} %collective-permute-done.2.refs_3_), channel_id=1, source_target_pairs={{1,0},{0,1},{3,2},{2,3},{5,4},{4,5},{7,6},{6,7},{9,8},{8,9},{11,10... | collective-permute-start | bytes 417800 | tf_op jit(solution)/shard_map/ppermute | solution.py:128
  14.4 0.0 collective-permute-done.refs_1_
  14.4 1.0 %collective-permute-done.1.refs_9_ = bf16[136,512]{1,0:T(8,128)(2,1)S(1)} collective-permute-done((bf16[136,512]{1,0:T(8,128)(2,1)S(1)}, bf16[136,512]{1,0:T(8,128)(2,1)S(1)}, u32[]{:S(2)}, u32[]{:S(2)}) %collective-permute-start.1) | collective-permute-done | bytes 139296 | tf_op jit(solution)/shard_map/ppermute | solution.py:128
  15.5 0.0 collective-permute-start.6
  15.5 1.6 %collective-permute-start.11 = (bf16[136,512]{1,0:T(8,128)(2,1)S(1)}, bf16[136,512]{1,0:T(8,128)(2,1)S(1)}, u32[]{:S(2)}, u32[]{:S(2)}) collective-permute-start(bf16[136,512]{1,0:T(8,128)(2,1)S(1)} %collective-permute-done.4.refs_10_), channel_id=1, source_target_pairs={{8,0},{9,1},{10,2},{11,3},{12,4},{13,5},{14,6},{15,7},{0,8},{1,9},... | collective-permute-start | bytes 417800 | tf_op jit(solution)/shard_map/ppermute | solution.py:128
  17.1 0.0 collective-permute-done.5.refs_4_
  17.1 0.0 collective-permute-done.7.refs_6_
  17.1 0.0 collective-permute-done.8.refs_7_
  17.1 0.0 collective-permute-done.6.refs_5_
  17.1 0.8 %shard_map.38 = (f32[1,128]{1,0:T(1,128)S(1)}, f32[1,128]{1,0:T(1,128)S(1)}, f32[1,128]{1,0:T(1,128)S(1)}) custom-call(bf16[64,64]{1,0:T(8,128)(2,1)S(1)} %get-tuple-element.15.table_ref, bf16[136,512]{1,0:T(8,128)(2,1)S(1)} %get-tuple-element.16.refs_0_.refs_8_, bf16[136,512]{1,0:T(8,128)(2,1)S(1)} %collective-permute-done.refs_1_, ...), custom_call_target="tpu_custom_call" | custom-call | flops 402653184 | bytes 1441792 | tf_op jit(solution)/shard_map/pallas_call | solution.py:103
  17.9 2.2 %collective-permute-start.10 = (f32[1,128]{1,0:T(1,128)S(1)}, f32[1,128]{1,0:T(1,128)S(1)}, u32[]{:S(2)}, u32[]{:S(2)}) collective-permute-start(f32[1,128]{1,0:T(1,128)S(1)} %get-tuple-element.24), channel_id=1, source_target_pairs={{24,0},{25,1},{26,2},{27,3},{28,4},{29,5},{30,6},{31,7},{16,8},{17... | collective-permute-start | bytes 1544 | tf_op jit(solution)/shard_map/ppermute | solution.py:128
  20.1 0.0 collective-permute-start.9
  20.1 1.4 %collective-permute-done.11.refs_8_ = bf16[136,512]{1,0:T(8,128)(2,1)S(1)} collective-permute-done((bf16[136,512]{1,0:T(8,128)(2,1)S(1)}, bf16[136,512]{1,0:T(8,128)(2,1)S(1)}, u32[]{:S(2)}, u32[]{:S(2)}) %collective-permute-start.11) | collective-permute-done | bytes 139296 | tf_op jit(solution)/shard_map/ppermute | solution.py:128
  21.6 0.5 %shard_map.39 = f32[1,128]{1,0:T(1,128)S(1)} custom-call(bf16[64,64]{1,0:T(8,128)(2,1)S(1)} %get-tuple-element.15.table_ref, bf16[136,512]{1,0:T(8,128)(2,1)S(1)} %get-tuple-element.16.refs_0_.refs_8_, bf16[136,512]{1,0:T(8,128)(2,1)S(1)} %collective-permute-done.refs_1_, bf16[136,512]{1,0:T(8,128)(2,1)S(1)} %collective-permute-done.3.refs_2_, ...), custom_call_target="tpu_custom_call" | custom-call | flops 134217728 | bytes 1179648 | tf_op jit(solution)/shard_map/pallas_call | solution.py:103
  22.0 1.3 %collective-permute-start.12 = (f32[1,128]{1,0:T(1,128)S(1)}, f32[1,128]{1,0:T(1,128)S(1)}, u32[]{:S(2)}, u32[]{:S(2)}) collective-permute-start(f32[1,128]{1,0:T(1,128)S(1)} %shard_map.39), channel_id=1, source_target_pairs={{16,0},{17,1},{18,2},{19,3},{20,4},{21,5},{22,6},{23,7},{24,8},{25... | collective-permute-start | bytes 1544 | tf_op jit(solution)/shard_map/ppermute | solution.py:128
  23.3 0.0 collective-permute-done.10
  23.3 0.3 %collective-permute-done.9 = f32[1,128]{1,0:T(1,128)S(1)} collective-permute-done((f32[1,128]{1,0:T(1,128)S(1)}, f32[1,128]{1,0:T(1,128)S(1)}, u32[]{:S(2)}, u32[]{:S(2)}) %collective-permute-start.9) | collective-permute-done | bytes 544 | tf_op jit(solution)/shard_map/ppermute | solution.py:128
  23.7 2.9 %collective-permute-done.12 = f32[1,128]{1,0:T(1,128)S(1)} collective-permute-done((f32[1,128]{1,0:T(1,128)S(1)}, f32[1,128]{1,0:T(1,128)S(1)}, u32[]{:S(2)}, u32[]{:S(2)}) %collective-permute-start.12) | collective-permute-done | bytes 544 | tf_op jit(solution)/shard_map/ppermute | solution.py:128
  26.5 0.5 %maximum_bitcast_fusion = f32[128]{0:T(128)} fusion(f32[1,128]{1,0:T(1,128)S(1)} %collective-permute-done.12, f32[1,128]{1,0:T(1,128)S(1)} %collective-permute-done.10, f32[1,128]{1,0:T(1,128)S(1)} %get-tuple-element.22, f32[1,128]{1,0:T(1,128)S(1)} %collective-permute-done.9), kind=kLoop, calls=%fused_computation | loop fusion | flops 384 | bytes 2560 | tf_op jit(solution)/shard_map/reshape | solution.py:175
Async XLA Ops:
  1.1 8.6 %collective-permute-start.2 = (bf16[136,512]{1,0:T(8,128)(2,1)S(1)}, bf16[136,512]{1,0:T(8,128)(2,1)S(1)}, u32[]{:S(2)}, u32[]{:S(2)}) collective-permute-start(bf16[136,512]{1,0:T(8,128)(2,1)S(1)} %get-tuple-element.16.refs_0_.refs_8_), channel_id=1, source_target_pairs={{6,0},{7,1},{4,2},{5,3},{2,4},{3,5},{0,6},{1,7},{14,8},{15,9},{12,... | collective-permute-start | bytes 417800 | tf_op jit(solution)/shard_map/ppermute | solution.py:128
  5.1 6.7 %collective-permute-start.3 = (bf16[136,512]{1,0:T(8,128)(2,1)S(1)}, bf16[136,512]{1,0:T(8,128)(2,1)S(1)}, u32[]{:S(2)}, u32[]{:S(2)}) collective-permute-start(bf16[136,512]{1,0:T(8,128)(2,1)S(1)} %get-tuple-element.16.refs_0_.refs_8_), channel_id=1, source_target_pairs={{4,0},{5,1},{6,2},{7,3},{0,4},{1,5},{2,6},{3,7},{12,8},{13,9},{14,... | collective-permute-start | bytes 417800 | tf_op jit(solution)/shard_map/ppermute | solution.py:128
  5.6 8.4 %collective-permute-start.4 = (bf16[136,512]{1,0:T(8,128)(2,1)S(1)}, bf16[136,512]{1,0:T(8,128)(2,1)S(1)}, u32[]{:S(2)}, u32[]{:S(2)}) collective-permute-start(bf16[136,512]{1,0:T(8,128)(2,1)S(1)} %get-tuple-element.16.refs_0_.refs_8_), channel_id=1, source_target_pairs={{24,0},{25,1},{26,2},{27,3},{28,4},{29,5},{30,6},{31,7},{16,8},{17... | collective-permute-start | bytes 417800 | tf_op jit(solution)/shard_map/ppermute | solution.py:128
  9.2 5.3 %collective-permute-start = (bf16[136,512]{1,0:T(8,128)(2,1)S(1)}, bf16[136,512]{1,0:T(8,128)(2,1)S(1)}, u32[]{:S(2)}, u32[]{:S(2)}) collective-permute-start(bf16[136,512]{1,0:T(8,128)(2,1)S(1)} %get-tuple-element.16.refs_0_.refs_8_), channel_id=1, source_target_pairs={{2,0},{3,1},{0,2},{1,3},{6,4},{7,5},{4,6},{5,7},{10,8},{11,9},{8,1... | collective-permute-start | bytes 417800 | tf_op jit(solution)/shard_map/ppermute | solution.py:128
  9.7 5.8 %collective-permute-start.1 = (bf16[136,512]{1,0:T(8,128)(2,1)S(1)}, bf16[136,512]{1,0:T(8,128)(2,1)S(1)}, u32[]{:S(2)}, u32[]{:S(2)}) collective-permute-start(bf16[136,512]{1,0:T(8,128)(2,1)S(1)} %get-tuple-element.16.refs_0_.refs_8_), channel_id=1, source_target_pairs={{8,0},{9,1},{10,2},{11,3},{12,4},{13,5},{14,6},{15,7},{0,8},{1,9},... | collective-permute-start | bytes 417800 | tf_op jit(solution)/shard_map/ppermute | solution.py:128
  9.7 7.3 %collective-permute-start.5 = (bf16[136,512]{1,0:T(8,128)(2,1)S(1)}, bf16[136,512]{1,0:T(8,128)(2,1)S(1)}, u32[]{:S(2)}, u32[]{:S(2)}) collective-permute-start(bf16[136,512]{1,0:T(8,128)(2,1)S(1)} %get-tuple-element.16.refs_0_.refs_8_), channel_id=1, source_target_pairs={{1,0},{0,1},{3,2},{2,3},{5,4},{4,5},{7,6},{6,7},{9,8},{8,9},{11,10... | collective-permute-start | bytes 417800 | tf_op jit(solution)/shard_map/ppermute | solution.py:128
  13.9 3.1 %collective-permute-start.7 = (bf16[136,512]{1,0:T(8,128)(2,1)S(1)}, bf16[136,512]{1,0:T(8,128)(2,1)S(1)}, u32[]{:S(2)}, u32[]{:S(2)}) collective-permute-start(bf16[136,512]{1,0:T(8,128)(2,1)S(1)} %collective-permute-done.3.refs_2_), channel_id=1, source_target_pairs={{1,0},{0,1},{3,2},{2,3},{5,4},{4,5},{7,6},{6,7},{9,8},{8,9},{11,10... | collective-permute-start | bytes 417800 | tf_op jit(solution)/shard_map/ppermute | solution.py:128
  13.9 3.1 %collective-permute-start.8 = (bf16[136,512]{1,0:T(8,128)(2,1)S(1)}, bf16[136,512]{1,0:T(8,128)(2,1)S(1)}, u32[]{:S(2)}, u32[]{:S(2)}) collective-permute-start(bf16[136,512]{1,0:T(8,128)(2,1)S(1)} %collective-permute-done.2.refs_3_), channel_id=1, source_target_pairs={{1,0},{0,1},{3,2},{2,3},{5,4},{4,5},{7,6},{6,7},{9,8},{8,9},{11,10... | collective-permute-start | bytes 417800 | tf_op jit(solution)/shard_map/ppermute | solution.py:128
  15.5 1.6 %collective-permute-start.6 = (bf16[136,512]{1,0:T(8,128)(2,1)S(1)}, bf16[136,512]{1,0:T(8,128)(2,1)S(1)}, u32[]{:S(2)}, u32[]{:S(2)}) collective-permute-start(bf16[136,512]{1,0:T(8,128)(2,1)S(1)} %collective-permute-done.refs_1_), channel_id=1, source_target_pairs={{1,0},{0,1},{3,2},{2,3},{5,4},{4,5},{7,6},{6,7},{9,8},{8,9},{11,10... | collective-permute-start | bytes 417800 | tf_op jit(solution)/shard_map/ppermute | solution.py:128
  15.5 6.1 %collective-permute-start.11 = (bf16[136,512]{1,0:T(8,128)(2,1)S(1)}, bf16[136,512]{1,0:T(8,128)(2,1)S(1)}, u32[]{:S(2)}, u32[]{:S(2)}) collective-permute-start(bf16[136,512]{1,0:T(8,128)(2,1)S(1)} %collective-permute-done.4.refs_10_), channel_id=1, source_target_pairs={{8,0},{9,1},{10,2},{11,3},{12,4},{13,5},{14,6},{15,7},{0,8},{1,9},... | collective-permute-start | bytes 417800 | tf_op jit(solution)/shard_map/ppermute | solution.py:128
  17.9 5.4 %collective-permute-start.10 = (f32[1,128]{1,0:T(1,128)S(1)}, f32[1,128]{1,0:T(1,128)S(1)}, u32[]{:S(2)}, u32[]{:S(2)}) collective-permute-start(f32[1,128]{1,0:T(1,128)S(1)} %get-tuple-element.24), channel_id=1, source_target_pairs={{24,0},{25,1},{26,2},{27,3},{28,4},{29,5},{30,6},{31,7},{16,8},{17... | collective-permute-start | bytes 1544 | tf_op jit(solution)/shard_map/ppermute | solution.py:128
  20.1 3.5 %collective-permute-start.9 = (f32[1,128]{1,0:T(1,128)S(1)}, f32[1,128]{1,0:T(1,128)S(1)}, u32[]{:S(2)}, u32[]{:S(2)}) collective-permute-start(f32[1,128]{1,0:T(1,128)S(1)} %get-tuple-element.23), channel_id=1, source_target_pairs={{8,0},{9,1},{10,2},{11,3},{12,4},{13,5},{14,6},{15,7},{0,8},{1,9},... | collective-permute-start | bytes 1544 | tf_op jit(solution)/shard_map/ppermute | solution.py:128
  22.0 4.5 %collective-permute-start.12 = (f32[1,128]{1,0:T(1,128)S(1)}, f32[1,128]{1,0:T(1,128)S(1)}, u32[]{:S(2)}, u32[]{:S(2)}) collective-permute-start(f32[1,128]{1,0:T(1,128)S(1)} %shard_map.39), channel_id=1, source_target_pairs={{16,0},{17,1},{18,2},{19,3},{20,4},{21,5},{22,6},{23,7},{24,8},{25... | collective-permute-start | bytes 1544 | tf_op jit(solution)/shard_map/ppermute | solution.py:128

commit v25 on v23

--- a/solution.py
+++ b/solution.py
@@ -148,7 +148,6 @@
         near = [permute(own, lambda z, a, g: (z, turned(a, s, wide), g)) for s in reversed(range(1, wide))]
         middle = along(own, length - 1) if half < length else None
         first = [along(own, s) for s in range(1, half)]
-        near = lax.optimization_barrier(near)
         middle, first = lax.optimization_barrier((middle, first))
         near = near[::-1]
         last = [along(middle, s) for s in range(1, half)] if half < length else []

time: 26.3 us -> 27.5 us (1.046)
  waiting for transfers between devices: 8.82 us -> 13.5 us
  starting transfers between devices: 14.4 us -> 11 us
    ppermute x13, waiting for transfers between devices: 8.82 us -> 13.5 us  [permute(): return lax.ppermute(x, ('clu', 'grp'), pairs)]
    ppermute x13, starting transfers between devices: 14.4 us -> 11 us  [permute(): return lax.ppermute(x, ('clu', 'grp'), pairs)]
  transfers between devices with their start and end apart: 13 -> 13, of which waited for: 7 -> 8; matrix products, arithmetic and copies ran while one was open for 0% -> 0% of each run, Pallas kernels for 5% -> 5%
where the time goes in v25:
time: 27.5 us; the launch traced here: 27.4 us
  waiting for transfers between devices  13.5 us (49%)
  starting transfers between devices  11 us (40%)
  Pallas kernels  2.37 us (9%)
  other arithmetic  0.52 us (2%)
    ppermute x13, waiting for transfers between devices, permute(): return lax.ppermute(x, ('clu', 'grp'), pairs)  13.5 us
    ppermute x13, starting transfers between devices, permute(): return lax.ppermute(x, ('clu', 'grp'), pairs)  11 us
    pallas_call x2, Pallas kernels, best_of(): pl.pallas_call(functools.partial(best_kernel, len(keys), n_spans, own, ra...  1.26 us
    pallas_call x1, Pallas kernels, pack(): pl.pallas_call(functools.partial(pack_kernel, groups), out_shape=[pltpu.V...  1.1 us
  transfers between devices with their start and end apart: 13, of which 8 were waited for; matrix products, arithmetic and copies ran while one was open for 0% of the time, Pallas kernels for 5%

profile of v25, /device:TPU:0, one launch (start us, length us, event | category | flops | bytes accessed | tf_op | source)
XLA Modules:
  0.0 27.4 jit_solution(8913024714478416297)
XLA Ops:
  0.0 1.1 %shard_map.37 = (bf16[136,512]{1,0:T(8,128)(2,1)S(1)}, bf16[64,64]{1,0:T(8,128)(2,1)S(1)}) custom-call(bf16[128,512]{1,0:T(8,128)(2,1)} %emb_ref.1, s32[1,128]{1,0:T(1,128)} %bitcast.4, s32[1,64]{1,0:T(1,128)} %bitcast.5), custom_call_target="tpu_custom_call" | custom-call | tf_op jit(solution)/shard_map/pallas_call | solution.py:38
  1.1 5.1 %collective-permute-start.7 = (bf16[136,512]{1,0:T(8,128)(2,1)S(1)}, bf16[136,512]{1,0:T(8,128)(2,1)S(1)}, u32[]{:S(2)}, u32[]{:S(2)}) collective-permute-start(bf16[136,512]{1,0:T(8,128)(2,1)S(1)} %get-tuple-element.13.refs_0_.refs_8_), channel_id=1, source_target_pairs={{24,0},{25,1},{26,2},{27,3},{28,4},{29,5},{30,6},{31,7},{16,8},{17... | collective-permute-start | bytes 417800 | tf_op jit(solution)/shard_map/ppermute | solution.py:128
  6.2 1.5 %collective-permute-start = (bf16[136,512]{1,0:T(8,128)(2,1)S(1)}, bf16[136,512]{1,0:T(8,128)(2,1)S(1)}, u32[]{:S(2)}, u32[]{:S(2)}) collective-permute-start(bf16[136,512]{1,0:T(8,128)(2,1)S(1)} %get-tuple-element.13.refs_0_.refs_8_), channel_id=1, source_target_pairs={{2,0},{3,1},{0,2},{1,3},{6,4},{7,5},{4,6},{5,7},{10,8},{11,9},{8,1... | collective-permute-start | bytes 417800 | tf_op jit(solution)/shard_map/ppermute | solution.py:128
  7.7 1.5 %collective-permute-start.1 = (bf16[136,512]{1,0:T(8,128)(2,1)S(1)}, bf16[136,512]{1,0:T(8,128)(2,1)S(1)}, u32[]{:S(2)}, u32[]{:S(2)}) collective-permute-start(bf16[136,512]{1,0:T(8,128)(2,1)S(1)} %get-tuple-element.13.refs_0_.refs_8_), channel_id=1, source_target_pairs={{4,0},{5,1},{6,2},{7,3},{0,4},{1,5},{2,6},{3,7},{12,8},{13,9},{14,... | collective-permute-start | bytes 417800 | tf_op jit(solution)/shard_map/ppermute | solution.py:128
  9.2 0.5 %collective-permute-start.2 = (bf16[136,512]{1,0:T(8,128)(2,1)S(1)}, bf16[136,512]{1,0:T(8,128)(2,1)S(1)}, u32[]{:S(2)}, u32[]{:S(2)}) collective-permute-start(bf16[136,512]{1,0:T(8,128)(2,1)S(1)} %get-tuple-element.13.refs_0_.refs_8_), channel_id=1, source_target_pairs={{6,0},{7,1},{4,2},{5,3},{2,4},{3,5},{0,6},{1,7},{14,8},{15,9},{12,... | collective-permute-start | bytes 417800 | tf_op jit(solution)/shard_map/ppermute | solution.py:128
  9.7 0.0 collective-permute-start.8
  9.7 0.3 %collective-permute-done.7.refs_10_ = bf16[136,512]{1,0:T(8,128)(2,1)S(1)} collective-permute-done((bf16[136,512]{1,0:T(8,128)(2,1)S(1)}, bf16[136,512]{1,0:T(8,128)(2,1)S(1)}, u32[]{:S(2)}, u32[]{:S(2)}) %collective-permute-start.7) | collective-permute-done | bytes 139296 | tf_op jit(solution)/shard_map/ppermute | solution.py:128
  10.0 0.0 collective-permute-start.3
  10.0 1.9 %collective-permute-done.refs_1_ = bf16[136,512]{1,0:T(8,128)(2,1)S(1)} collective-permute-done((bf16[136,512]{1,0:T(8,128)(2,1)S(1)}, bf16[136,512]{1,0:T(8,128)(2,1)S(1)}, u32[]{:S(2)}, u32[]{:S(2)}) %collective-permute-start) | collective-permute-done | bytes 139296 | tf_op jit(solution)/shard_map/ppermute | solution.py:128
  11.9 0.0 collective-permute-start.4
  12.0 3.8 %collective-permute-done.1.refs_2_ = bf16[136,512]{1,0:T(8,128)(2,1)S(1)} collective-permute-done((bf16[136,512]{1,0:T(8,128)(2,1)S(1)}, bf16[136,512]{1,0:T(8,128)(2,1)S(1)}, u32[]{:S(2)}, u32[]{:S(2)}) %collective-permute-start.1) | collective-permute-done | bytes 139296 | tf_op jit(solution)/shard_map/ppermute | solution.py:128
  15.8 0.0 collective-permute-start.5
  15.8 0.0 collective-permute-done.2.refs_3_
  15.8 0.5 %collective-permute-start.6 = (bf16[136,512]{1,0:T(8,128)(2,1)S(1)}, bf16[136,512]{1,0:T(8,128)(2,1)S(1)}, u32[]{:S(2)}, u32[]{:S(2)}) collective-permute-start(bf16[136,512]{1,0:T(8,128)(2,1)S(1)} %collective-permute-done.2.refs_3_), channel_id=1, source_target_pairs={{1,0},{0,1},{3,2},{2,3},{5,4},{4,5},{7,6},{6,7},{9,8},{8,9},{11,10... | collective-permute-start | bytes 417800 | tf_op jit(solution)/shard_map/ppermute | solution.py:128
  16.3 0.0 collective-permute-done.8.refs_9_
  16.3 0.0 collective-permute-start.11
  16.3 0.0 collective-permute-done.3.refs_4_
  16.3 0.0 collective-permute-done.4.refs_5_
  16.3 0.8 %collective-permute-done.5.refs_6_ = bf16[136,512]{1,0:T(8,128)(2,1)S(1)} collective-permute-done((bf16[136,512]{1,0:T(8,128)(2,1)S(1)}, bf16[136,512]{1,0:T(8,128)(2,1)S(1)}, u32[]{:S(2)}, u32[]{:S(2)}) %collective-permute-start.5) | collective-permute-done | bytes 139296 | tf_op jit(solution)/shard_map/ppermute | solution.py:128
  17.1 0.2 collective-permute-done.6.refs_7_
  17.3 0.8 %shard_map.38 = (f32[1,128]{1,0:T(1,128)S(1)}, f32[1,128]{1,0:T(1,128)S(1)}, f32[1,128]{1,0:T(1,128)S(1)}) custom-call(bf16[64,64]{1,0:T(8,128)(2,1)S(1)} %get-tuple-element.12.table_ref, bf16[136,512]{1,0:T(8,128)(2,1)S(1)} %get-tuple-element.13.refs_0_.refs_8_, bf16[136,512]{1,0:T(8,128)(2,1)S(1)} %collective-permute-done.refs_1_, ...), custom_call_target="tpu_custom_call" | custom-call | flops 402653184 | bytes 1441792 | tf_op jit(solution)/shard_map/pallas_call | solution.py:103
  18.1 0.3 %collective-permute-start.10 = (f32[1,128]{1,0:T(1,128)S(1)}, f32[1,128]{1,0:T(1,128)S(1)}, u32[]{:S(2)}, u32[]{:S(2)}) collective-permute-start(f32[1,128]{1,0:T(1,128)S(1)} %get-tuple-element.18), channel_id=1, source_target_pairs={{24,0},{25,1},{26,2},{27,3},{28,4},{29,5},{30,6},{31,7},{16,8},{17... | collective-permute-start | bytes 1544 | tf_op jit(solution)/shard_map/ppermute | solution.py:128
  18.4 0.9 %collective-permute-start.9 = (f32[1,128]{1,0:T(1,128)S(1)}, f32[1,128]{1,0:T(1,128)S(1)}, u32[]{:S(2)}, u32[]{:S(2)}) collective-permute-start(f32[1,128]{1,0:T(1,128)S(1)} %get-tuple-element.17), channel_id=1, source_target_pairs={{8,0},{9,1},{10,2},{11,3},{12,4},{13,5},{14,6},{15,7},{0,8},{1,9},... | collective-permute-start | bytes 1544 | tf_op jit(solution)/shard_map/ppermute | solution.py:128
  19.3 2.6 %collective-permute-done.11.refs_8_ = bf16[136,512]{1,0:T(8,128)(2,1)S(1)} collective-permute-done((bf16[136,512]{1,0:T(8,128)(2,1)S(1)}, bf16[136,512]{1,0:T(8,128)(2,1)S(1)}, u32[]{:S(2)}, u32[]{:S(2)}) %collective-permute-start.11) | collective-permute-done | bytes 139296 | tf_op jit(solution)/shard_map/ppermute | solution.py:128
  21.9 0.5 %shard_map.39 = f32[1,128]{1,0:T(1,128)S(1)} custom-call(bf16[64,64]{1,0:T(8,128)(2,1)S(1)} %get-tuple-element.12.table_ref, bf16[136,512]{1,0:T(8,128)(2,1)S(1)} %get-tuple-element.13.refs_0_.refs_8_, bf16[136,512]{1,0:T(8,128)(2,1)S(1)} %collective-permute-done.refs_1_, bf16[136,512]{1,0:T(8,128)(2,1)S(1)} %collective-permute-done.1.refs_2_, ...), custom_call_target="tpu_custom_call" | custom-call | flops 134217728 | bytes 1179648 | tf_op jit(solution)/shard_map/pallas_call | solution.py:103
  22.4 0.7 %collective-permute-start.12 = (f32[1,128]{1,0:T(1,128)S(1)}, f32[1,128]{1,0:T(1,128)S(1)}, u32[]{:S(2)}, u32[]{:S(2)}) collective-permute-start(f32[1,128]{1,0:T(1,128)S(1)} %shard_map.39), channel_id=1, source_target_pairs={{16,0},{17,1},{18,2},{19,3},{20,4},{21,5},{22,6},{23,7},{24,8},{25... | collective-permute-start | bytes 1544 | tf_op jit(solution)/shard_map/ppermute | solution.py:128
  23.1 0.4 %collective-permute-done.10 = f32[1,128]{1,0:T(1,128)S(1)} collective-permute-done((f32[1,128]{1,0:T(1,128)S(1)}, f32[1,128]{1,0:T(1,128)S(1)}, u32[]{:S(2)}, u32[]{:S(2)}) %collective-permute-start.10) | collective-permute-done | bytes 544 | tf_op jit(solution)/shard_map/ppermute | solution.py:128
  23.5 0.0 collective-permute-done.9
  23.5 3.4 %collective-permute-done.12 = f32[1,128]{1,0:T(1,128)S(1)} collective-permute-done((f32[1,128]{1,0:T(1,128)S(1)}, f32[1,128]{1,0:T(1,128)S(1)}, u32[]{:S(2)}, u32[]{:S(2)}) %collective-permute-start.12) | collective-permute-done | bytes 544 | tf_op jit(solution)/shard_map/ppermute | solution.py:128
  26.9 0.5 %maximum_bitcast_fusion = f32[128]{0:T(128)} fusion(f32[1,128]{1,0:T(1,128)S(1)} %collective-permute-done.12, f32[1,128]{1,0:T(1,128)S(1)} %collective-permute-done.10, f32[1,128]{1,0:T(1,128)S(1)} %get-tuple-element.16, f32[1,128]{1,0:T(1,128)S(1)} %collective-permute-done.9), kind=kLoop, calls=%fused_computation | loop fusion | flops 384 | bytes 2560 | tf_op jit(solution)/shard_map/reshape | solution.py:173
Async XLA Ops:
  1.1 8.9 %collective-permute-start.7 = (bf16[136,512]{1,0:T(8,128)(2,1)S(1)}, bf16[136,512]{1,0:T(8,128)(2,1)S(1)}, u32[]{:S(2)}, u32[]{:S(2)}) collective-permute-start(bf16[136,512]{1,0:T(8,128)(2,1)S(1)} %get-tuple-element.13.refs_0_.refs_8_), channel_id=1, source_target_pairs={{24,0},{25,1},{26,2},{27,3},{28,4},{29,5},{30,6},{31,7},{16,8},{17... | collective-permute-start | bytes 417800 | tf_op jit(solution)/shard_map/ppermute | solution.py:128
  6.2 5.7 %collective-permute-start = (bf16[136,512]{1,0:T(8,128)(2,1)S(1)}, bf16[136,512]{1,0:T(8,128)(2,1)S(1)}, u32[]{:S(2)}, u32[]{:S(2)}) collective-permute-start(bf16[136,512]{1,0:T(8,128)(2,1)S(1)} %get-tuple-element.13.refs_0_.refs_8_), channel_id=1, source_target_pairs={{2,0},{3,1},{0,2},{1,3},{6,4},{7,5},{4,6},{5,7},{10,8},{11,9},{8,1... | collective-permute-start | bytes 417800 | tf_op jit(solution)/shard_map/ppermute | solution.py:128
  7.7 8.0 %collective-permute-start.1 = (bf16[136,512]{1,0:T(8,128)(2,1)S(1)}, bf16[136,512]{1,0:T(8,128)(2,1)S(1)}, u32[]{:S(2)}, u32[]{:S(2)}) collective-permute-start(bf16[136,512]{1,0:T(8,128)(2,1)S(1)} %get-tuple-element.13.refs_0_.refs_8_), channel_id=1, source_target_pairs={{4,0},{5,1},{6,2},{7,3},{0,4},{1,5},{2,6},{3,7},{12,8},{13,9},{14,... | collective-permute-start | bytes 417800 | tf_op jit(solution)/shard_map/ppermute | solution.py:128
  9.2 6.5 %collective-permute-start.2 = (bf16[136,512]{1,0:T(8,128)(2,1)S(1)}, bf16[136,512]{1,0:T(8,128)(2,1)S(1)}, u32[]{:S(2)}, u32[]{:S(2)}) collective-permute-start(bf16[136,512]{1,0:T(8,128)(2,1)S(1)} %get-tuple-element.13.refs_0_.refs_8_), channel_id=1, source_target_pairs={{6,0},{7,1},{4,2},{5,3},{2,4},{3,5},{0,6},{1,7},{14,8},{15,9},{12,... | collective-permute-start | bytes 417800 | tf_op jit(solution)/shard_map/ppermute | solution.py:128
  9.7 6.6 %collective-permute-start.8 = (bf16[136,512]{1,0:T(8,128)(2,1)S(1)}, bf16[136,512]{1,0:T(8,128)(2,1)S(1)}, u32[]{:S(2)}, u32[]{:S(2)}) collective-permute-start(bf16[136,512]{1,0:T(8,128)(2,1)S(1)} %get-tuple-element.13.refs_0_.refs_8_), channel_id=1, source_target_pairs={{8,0},{9,1},{10,2},{11,3},{12,4},{13,5},{14,6},{15,7},{0,8},{1,9},... | collective-permute-start | bytes 417800 | tf_op jit(solution)/shard_map/ppermute | solution.py:128
  10.0 6.3 %collective-permute-start.3 = (bf16[136,512]{1,0:T(8,128)(2,1)S(1)}, bf16[136,512]{1,0:T(8,128)(2,1)S(1)}, u32[]{:S(2)}, u32[]{:S(2)}) collective-permute-start(bf16[136,512]{1,0:T(8,128)(2,1)S(1)} %get-tuple-element.13.refs_0_.refs_8_), channel_id=1, source_target_pairs={{1,0},{0,1},{3,2},{2,3},{5,4},{4,5},{7,6},{6,7},{9,8},{8,9},{11,10... | collective-permute-start | bytes 417800 | tf_op jit(solution)/shard_map/ppermute | solution.py:128
  11.9 4.3 %collective-permute-start.4 = (bf16[136,512]{1,0:T(8,128)(2,1)S(1)}, bf16[136,512]{1,0:T(8,128)(2,1)S(1)}, u32[]{:S(2)}, u32[]{:S(2)}) collective-permute-start(bf16[136,512]{1,0:T(8,128)(2,1)S(1)} %collective-permute-done.refs_1_), channel_id=1, source_target_pairs={{1,0},{0,1},{3,2},{2,3},{5,4},{4,5},{7,6},{6,7},{9,8},{8,9},{11,10... | collective-permute-start | bytes 417800 | tf_op jit(solution)/shard_map/ppermute | solution.py:128
  15.8 1.4 %collective-permute-start.5 = (bf16[136,512]{1,0:T(8,128)(2,1)S(1)}, bf16[136,512]{1,0:T(8,128)(2,1)S(1)}, u32[]{:S(2)}, u32[]{:S(2)}) collective-permute-start(bf16[136,512]{1,0:T(8,128)(2,1)S(1)} %collective-permute-done.1.refs_2_), channel_id=1, source_target_pairs={{1,0},{0,1},{3,2},{2,3},{5,4},{4,5},{7,6},{6,7},{9,8},{8,9},{11,10... | collective-permute-start | bytes 417800 | tf_op jit(solution)/shard_map/ppermute | solution.py:128
  15.8 1.6 %collective-permute-start.6 = (bf16[136,512]{1,0:T(8,128)(2,1)S(1)}, bf16[136,512]{1,0:T(8,128)(2,1)S(1)}, u32[]{:S(2)}, u32[]{:S(2)}) collective-permute-start(bf16[136,512]{1,0:T(8,128)(2,1)S(1)} %collective-permute-done.2.refs_3_), channel_id=1, source_target_pairs={{1,0},{0,1},{3,2},{2,3},{5,4},{4,5},{7,6},{6,7},{9,8},{8,9},{11,10... | collective-permute-start | bytes 417800 | tf_op jit(solution)/shard_map/ppermute | solution.py:128
  16.3 5.6 %collective-permute-start.11 = (bf16[136,512]{1,0:T(8,128)(2,1)S(1)}, bf16[136,512]{1,0:T(8,128)(2,1)S(1)}, u32[]{:S(2)}, u32[]{:S(2)}) collective-permute-start(bf16[136,512]{1,0:T(8,128)(2,1)S(1)} %collective-permute-done.7.refs_10_), channel_id=1, source_target_pairs={{8,0},{9,1},{10,2},{11,3},{12,4},{13,5},{14,6},{15,7},{0,8},{1,9},... | collective-permute-start | bytes 417800 | tf_op jit(solution)/shard_map/ppermute | solution.py:128
  18.1 5.4 %collective-permute-start.10 = (f32[1,128]{1,0:T(1,128)S(1)}, f32[1,128]{1,0:T(1,128)S(1)}, u32[]{:S(2)}, u32[]{:S(2)}) collective-permute-start(f32[1,128]{1,0:T(1,128)S(1)} %get-tuple-element.18), channel_id=1, source_target_pairs={{24,0},{25,1},{26,2},{27,3},{28,4},{29,5},{30,6},{31,7},{16,8},{17... | collective-permute-start | bytes 1544 | tf_op jit(solution)/shard_map/ppermute | solution.py:128
  18.4 5.1 %collective-permute-start.9 = (f32[1,128]{1,0:T(1,128)S(1)}, f32[1,128]{1,0:T(1,128)S(1)}, u32[]{:S(2)}, u32[]{:S(2)}) collective-permute-start(f32[1,128]{1,0:T(1,128)S(1)} %get-tuple-element.17), channel_id=1, source_target_pairs={{8,0},{9,1},{10,2},{11,3},{12,4},{13,5},{14,6},{15,7},{0,8},{1,9},... | collective-permute-start | bytes 1544 | tf_op jit(solution)/shard_map/ppermute | solution.py:128
  22.4 4.5 %collective-permute-start.12 = (f32[1,128]{1,0:T(1,128)S(1)}, f32[1,128]{1,0:T(1,128)S(1)}, u32[]{:S(2)}, u32[]{:S(2)}) collective-permute-start(f32[1,128]{1,0:T(1,128)S(1)} %shard_map.39), channel_id=1, source_target_pairs={{16,0},{17,1},{18,2},{19,3},{20,4},{21,5},{22,6},{23,7},{24,8},{25... | collective-permute-start | bytes 1544 | tf_op jit(solution)/shard_map/ppermute | solution.py:128

commit v26 on v23

--- a/solution.py
+++ b/solution.py
@@ -8,6 +8,7 @@
 from jax.experimental.pallas import tpu as pltpu
 from jax.sharding import PartitionSpec as P
 
+LANES = 128
 AUX = 8
 DIGIT = 256
 
@@ -16,13 +17,15 @@
     rows, width = emb_ref.shape
     values = emb_ref[...].astype(jnp.float32)
     scale = lax.rsqrt(jnp.sum(values * values, axis=-1, keepdims=True) + 1e-06)
-    out_ref[:rows, :] = (values * scale).astype(jnp.bfloat16)
+    unit = (values * scale).astype(jnp.bfloat16)
+    for panel in range(width // LANES):
+        out_ref[panel * rows : (panel + 1) * rows, :] = unit[:, panel * LANES : (panel + 1) * LANES]
     ids = jnp.broadcast_to(id_ref[...], (AUX, rows))
     row = lax.broadcasted_iota(jnp.int32, (AUX, rows), 0)
     digits = jnp.where(row == 0, ids % DIGIT, ids // DIGIT)
-    if width > rows:
-        digits = jnp.concatenate([digits, jnp.zeros((AUX, width - rows), jnp.int32)], axis=1)
-    out_ref[rows:, :] = digits.astype(jnp.float32).astype(jnp.bfloat16)
+    if LANES > rows:
+        digits = jnp.concatenate([digits, jnp.zeros((AUX, LANES - rows), jnp.int32)], axis=1)
+    out_ref[width // LANES * rows :, :] = digits.astype(jnp.float32).astype(jnp.bfloat16)
     clusters = group_ref.shape[1]
     index = lax.broadcasted_iota(jnp.int32, (groups, clusters), 0)
     member = jnp.where(index == group_ref[...], 1.0, 0.0).astype(jnp.bfloat16)
@@ -34,10 +37,11 @@
 
 def pack(embeddings, cluster_id, cluster_group, groups):
     rows, width = embeddings.shape
+    assert rows <= LANES and width % LANES == 0
     clusters = cluster_group.shape[0]
     return pl.pallas_call(
         functools.partial(pack_kernel, groups),
-        out_shape=[pltpu.VMEM((rows + AUX, width), jnp.bfloat16), pltpu.VMEM((clusters, clusters), jnp.bfloat16)],
+        out_shape=[pltpu.VMEM((width // LANES * rows + AUX, LANES), jnp.bfloat16), pltpu.VMEM((clusters, clusters), jnp.bfloat16)],
     )(embeddings, cluster_id.reshape(1, rows), cluster_group.reshape(1, clusters))
 
 
@@ -47,16 +51,19 @@
     return jnp.where(index == number, 1.0, 0.0).astype(jnp.bfloat16)
 
 
-def best_kernel(n_keys, n_spans, own, ranks, table_ref, *refs):
+def best_kernel(rows, n_keys, n_spans, own, ranks, table_ref, *refs):
     n_queries = (len(refs) - n_keys) // 2
     keys, queries, outs = refs[:n_keys], refs[n_keys : n_keys + n_queries], refs[n_keys + n_queries :]
-    rows = keys[0].shape[0] - AUX
+    panels = (keys[0].shape[0] - AUX) // rows
     clusters = table_ref.shape[0]
     clu, grp = lax.axis_index("clu"), lax.axis_index("grp")
     ranks = [rank(clu, grp) for rank in ranks]
 
     def hot(block):
-        return one_hot(block[rows:, :rows].astype(jnp.float32), clusters)
+        return one_hot(block[panels * rows :, :rows].astype(jnp.float32), clusters)
+
+    def unit(block):
+        return jnp.concatenate([block[p * rows : (p + 1) * rows, :] for p in range(panels)], axis=1)
 
     mixed = [
         jnp.dot(table_ref[...], hot(query), preferred_element_type=jnp.float32).astype(jnp.bfloat16)
@@ -65,13 +72,13 @@
 
     def search(span, first):
         key_hot = jnp.concatenate([hot(keys[i]) for i in span], axis=1)
-        key_rows = jnp.concatenate([keys[i][:rows, :] for i in span], axis=0)
+        key_rows = jnp.concatenate([unit(keys[i]) for i in span], axis=0)
         for j in range(n_queries):
             weight = lax.dot_general(
                 key_hot, mixed[j], (((0,), (0,)), ((), ())), preferred_element_type=jnp.float32
             )
             sims = lax.dot_general(
-                key_rows, queries[j][:rows, :], (((1,), (1,)), ((), ())), preferred_element_type=jnp.float32
+                key_rows, unit(queries[j]), (((1,), (1,)), ((), ())), preferred_element_type=jnp.float32
             )
             score = jnp.where(weight > 0, weight * sims, -1.0)
             best = jnp.full((1, rows), -1.0, jnp.float32) if first else outs[j][...]
@@ -95,13 +102,13 @@
             search(range(t * width, (t + 1) * width), False)
 
 
-def best_of(keys, n_spans, queries, table, own):
-    rows, width = keys[0][0].shape[0] - AUX, keys[0][0].shape[1]
+def best_of(rows, keys, n_spans, queries, table, own):
+    width = (keys[0][0].shape[0] - AUX) // rows * LANES
     vmem = pl.BlockSpec(memory_space=pltpu.VMEM)
     ranks = [r for _, r in keys + queries]
     pairs = len(keys) * len(queries) * rows * rows
     return pl.pallas_call(
-        functools.partial(best_kernel, len(keys), n_spans, own, ranks),
+        functools.partial(best_kernel, rows, len(keys), n_spans, own, ranks),
         out_shape=[jax.ShapeDtypeStruct((1, rows), jnp.float32)] * len(queries),
         in_specs=[vmem] * (1 + len(keys) + len(queries)),
         out_specs=[vmem] * len(queries),
@@ -167,9 +174,9 @@
         visit_rank = [rank(z=s) for s in offsets]
         first = list(zip(first, visit_rank))
         last = list(zip(last, visit_rank[len(first) :]))
-        best = best_of(near + far, n_grp, near[:1] + first, table, True)
+        best = best_of(rows, near + far, n_grp, near[:1] + first, table, True)
         if last:
-            best = best + best_of(near + far, n_grp, last, table, False)
+            best = best + best_of(rows, near + far, n_grp, last, table, False)
         found = [best[0]] + [along(b, -s) for b, s in zip(best[1:], offsets)]
         return functools.reduce(jnp.maximum, found).reshape(rows)
 

time: 26.3 us -> 26 us (0.989)
  waiting for transfers between devices: 8.82 us -> 8.36 us
    ppermute x13, waiting for transfers between devices: 8.82 us -> 8.36 us  [permute(): return lax.ppermute(x, ('clu', 'grp'), pairs)]
where the time goes in v26:
time: 26 us; the launch traced here: 25.8 us
  starting transfers between devices  14.5 us (56%)
  waiting for transfers between devices  8.36 us (32%)
  Pallas kernels  2.37 us (9%)
  other arithmetic  0.52 us (2%)
    ppermute x13, starting transfers between devices, permute(): return lax.ppermute(x, ('clu', 'grp'), pairs)  14.5 us
    ppermute x13, waiting for transfers between devices, permute(): return lax.ppermute(x, ('clu', 'grp'), pairs)  8.36 us
    pallas_call x2, Pallas kernels, best_of(): pl.pallas_call(functools.partial(best_kernel, rows, len(keys), n_spans, o...  1.27 us
    pallas_call x1, Pallas kernels, pack(): pl.pallas_call(functools.partial(pack_kernel, groups), out_shape=[pltpu.V...  1.1 us
  transfers between devices with their start and end apart: 13, of which 7 were waited for; matrix products, arithmetic and copies ran while one was open for 0% of the time, Pallas kernels for 5%

profile of v26, /device:TPU:0, one launch (start us, length us, event | category | flops | bytes accessed | tf_op | source)
XLA Modules:
  0.0 25.8 jit_solution(13972989747593559390)
XLA Ops:
  0.0 1.1 %shard_map.37 = (bf16[520,128]{1,0:T(8,128)(2,1)S(1)}, bf16[64,64]{1,0:T(8,128)(2,1)S(1)}) custom-call(bf16[128,512]{1,0:T(8,128)(2,1)} %emb_ref.1, s32[1,128]{1,0:T(1,128)} %bitcast.4, s32[1,64]{1,0:T(1,128)} %bitcast.5), custom_call_target="tpu_custom_call" | custom-call | tf_op jit(solution)/shard_map/pallas_call | solution.py:42
  1.1 4.0 %collective-permute-start = (bf16[520,128]{1,0:T(8,128)(2,1)S(1)}, bf16[520,128]{1,0:T(8,128)(2,1)S(1)}, u32[]{:S(2)}, u32[]{:S(2)}) collective-permute-start(bf16[520,128]{1,0:T(8,128)(2,1)S(1)} %get-tuple-element.16.refs_0_.refs_8_), channel_id=1, source_target_pairs={{6,0},{7,1},{4,2},{5,3},{2,4},{3,5},{0,6},{1,7},{14,8},{15,9},{12,... | collective-permute-start | bytes 399368 | tf_op jit(solution)/shard_map/ppermute | solution.py:135
  5.1 0.5 %collective-permute-start.1 = (bf16[520,128]{1,0:T(8,128)(2,1)S(1)}, bf16[520,128]{1,0:T(8,128)(2,1)S(1)}, u32[]{:S(2)}, u32[]{:S(2)}) collective-permute-start(bf16[520,128]{1,0:T(8,128)(2,1)S(1)} %get-tuple-element.16.refs_0_.refs_8_), channel_id=1, source_target_pairs={{4,0},{5,1},{6,2},{7,3},{0,4},{1,5},{2,6},{3,7},{12,8},{13,9},{14,... | collective-permute-start | bytes 399368 | tf_op jit(solution)/shard_map/ppermute | solution.py:135
  5.6 0.1 collective-permute-start.2
  5.7 4.0 %collective-permute-start.7 = (bf16[520,128]{1,0:T(8,128)(2,1)S(1)}, bf16[520,128]{1,0:T(8,128)(2,1)S(1)}, u32[]{:S(2)}, u32[]{:S(2)}) collective-permute-start(bf16[520,128]{1,0:T(8,128)(2,1)S(1)} %get-tuple-element.16.refs_0_.refs_8_), channel_id=1, source_target_pairs={{24,0},{25,1},{26,2},{27,3},{28,4},{29,5},{30,6},{31,7},{16,8},{17... | collective-permute-start | bytes 399368 | tf_op jit(solution)/shard_map/ppermute | solution.py:135
  9.7 0.0 collective-permute-start.8
  9.7 0.0 collective-permute-done.refs_3_
  9.7 0.0 collective-permute-start.3
  9.7 1.7 %collective-permute-done.1.refs_2_ = bf16[520,128]{1,0:T(8,128)(2,1)S(1)} collective-permute-done((bf16[520,128]{1,0:T(8,128)(2,1)S(1)}, bf16[520,128]{1,0:T(8,128)(2,1)S(1)}, u32[]{:S(2)}, u32[]{:S(2)}) %collective-permute-start.1) | collective-permute-done | bytes 133152 | tf_op jit(solution)/shard_map/ppermute | solution.py:135
  11.5 0.2 collective-permute-done.2.refs_1_
  11.7 0.0 collective-permute-start.4
  11.7 0.5 %collective-permute-start.5 = (bf16[520,128]{1,0:T(8,128)(2,1)S(1)}, bf16[520,128]{1,0:T(8,128)(2,1)S(1)}, u32[]{:S(2)}, u32[]{:S(2)}) collective-permute-start(bf16[520,128]{1,0:T(8,128)(2,1)S(1)} %collective-permute-done.1.refs_2_), channel_id=1, source_target_pairs={{1,0},{0,1},{3,2},{2,3},{5,4},{4,5},{7,6},{6,7},{9,8},{8,9},{11,10... | collective-permute-start | bytes 399368 | tf_op jit(solution)/shard_map/ppermute | solution.py:135
  12.2 1.7 %collective-permute-done.7.refs_10_ = bf16[520,128]{1,0:T(8,128)(2,1)S(1)} collective-permute-done((bf16[520,128]{1,0:T(8,128)(2,1)S(1)}, bf16[520,128]{1,0:T(8,128)(2,1)S(1)}, u32[]{:S(2)}, u32[]{:S(2)}) %collective-permute-start.7) | collective-permute-done | bytes 133152 | tf_op jit(solution)/shard_map/ppermute | solution.py:135
  13.9 0.0 collective-permute-start.6
  13.9 1.4 %collective-permute-done.8.refs_9_ = bf16[520,128]{1,0:T(8,128)(2,1)S(1)} collective-permute-done((bf16[520,128]{1,0:T(8,128)(2,1)S(1)}, bf16[520,128]{1,0:T(8,128)(2,1)S(1)}, u32[]{:S(2)}, u32[]{:S(2)}) %collective-permute-start.8) | collective-permute-done | bytes 133152 | tf_op jit(solution)/shard_map/ppermute | solution.py:135
  15.4 1.6 %collective-permute-start.11 = (bf16[520,128]{1,0:T(8,128)(2,1)S(1)}, bf16[520,128]{1,0:T(8,128)(2,1)S(1)}, u32[]{:S(2)}, u32[]{:S(2)}) collective-permute-start(bf16[520,128]{1,0:T(8,128)(2,1)S(1)} %collective-permute-done.7.refs_10_), channel_id=1, source_target_pairs={{8,0},{9,1},{10,2},{11,3},{12,4},{13,5},{14,6},{15,7},{0,8},{1,9},... | collective-permute-start | bytes 399368 | tf_op jit(solution)/shard_map/ppermute | solution.py:135
  17.0 0.0 collective-permute-done.3.refs_4_
  17.0 0.0 collective-permute-done.4.refs_5_
  17.0 0.0 collective-permute-done.5.refs_6_
  17.0 0.0 collective-permute-done.6.refs_7_
  17.0 0.8 %shard_map.38 = (f32[1,128]{1,0:T(1,128)S(1)}, f32[1,128]{1,0:T(1,128)S(1)}, f32[1,128]{1,0:T(1,128)S(1)}) custom-call(bf16[64,64]{1,0:T(8,128)(2,1)S(1)} %get-tuple-element.15.table_ref, bf16[520,128]{1,0:T(8,128)(2,1)S(1)} %get-tuple-element.16.refs_0_.refs_8_, bf16[520,128]{1,0:T(8,128)(2,1)S(1)} %collective-permute-done.2.refs_1_, ...), custom_call_target="tpu_custom_call" | custom-call | flops 402653184 | bytes 1441792 | tf_op jit(solution)/shard_map/pallas_call | solution.py:110
  17.8 1.8 %collective-permute-start.10 = (f32[1,128]{1,0:T(1,128)S(1)}, f32[1,128]{1,0:T(1,128)S(1)}, u32[]{:S(2)}, u32[]{:S(2)}) collective-permute-start(f32[1,128]{1,0:T(1,128)S(1)} %get-tuple-element.24), channel_id=1, source_target_pairs={{24,0},{25,1},{26,2},{27,3},{28,4},{29,5},{30,6},{31,7},{16,8},{17... | collective-permute-start | bytes 1544 | tf_op jit(solution)/shard_map/ppermute | solution.py:135
  19.6 0.0 collective-permute-start.9
  19.6 0.7 %collective-permute-done.11.refs_8_ = bf16[520,128]{1,0:T(8,128)(2,1)S(1)} collective-permute-done((bf16[520,128]{1,0:T(8,128)(2,1)S(1)}, bf16[520,128]{1,0:T(8,128)(2,1)S(1)}, u32[]{:S(2)}, u32[]{:S(2)}) %collective-permute-start.11) | collective-permute-done | bytes 133152 | tf_op jit(solution)/shard_map/ppermute | solution.py:135
  20.4 0.5 %shard_map.39 = f32[1,128]{1,0:T(1,128)S(1)} custom-call(bf16[64,64]{1,0:T(8,128)(2,1)S(1)} %get-tuple-element.15.table_ref, bf16[520,128]{1,0:T(8,128)(2,1)S(1)} %get-tuple-element.16.refs_0_.refs_8_, bf16[520,128]{1,0:T(8,128)(2,1)S(1)} %collective-permute-done.2.refs_1_, bf16[520,128]{1,0:T(8,128)(2,1)S(1)} %collective-permute-done.1.refs_2_, ...), custom_call_target="tpu_custom_call" | custom-call | flops 134217728 | bytes 1179648 | tf_op jit(solution)/shard_map/pallas_call | solution.py:110
  20.8 2.0 %collective-permute-start.12 = (f32[1,128]{1,0:T(1,128)S(1)}, f32[1,128]{1,0:T(1,128)S(1)}, u32[]{:S(2)}, u32[]{:S(2)}) collective-permute-start(f32[1,128]{1,0:T(1,128)S(1)} %shard_map.39), channel_id=1, source_target_pairs={{16,0},{17,1},{18,2},{19,3},{20,4},{21,5},{22,6},{23,7},{24,8},{25... | collective-permute-start | bytes 1544 | tf_op jit(solution)/shard_map/ppermute | solution.py:135
  22.8 0.4 %collective-permute-done.10 = f32[1,128]{1,0:T(1,128)S(1)} collective-permute-done((f32[1,128]{1,0:T(1,128)S(1)}, f32[1,128]{1,0:T(1,128)S(1)}, u32[]{:S(2)}, u32[]{:S(2)}) %collective-permute-start.10) | collective-permute-done | bytes 544 | tf_op jit(solution)/shard_map/ppermute | solution.py:135
  23.3 0.0 collective-permute-done.9
  23.3 2.1 %collective-permute-done.12 = f32[1,128]{1,0:T(1,128)S(1)} collective-permute-done((f32[1,128]{1,0:T(1,128)S(1)}, f32[1,128]{1,0:T(1,128)S(1)}, u32[]{:S(2)}, u32[]{:S(2)}) %collective-permute-start.12) | collective-permute-done | bytes 544 | tf_op jit(solution)/shard_map/ppermute | solution.py:135
  25.3 0.5 %maximum_bitcast_fusion = f32[128]{0:T(128)} fusion(f32[1,128]{1,0:T(1,128)S(1)} %collective-permute-done.12, f32[1,128]{1,0:T(1,128)S(1)} %collective-permute-done.10, f32[1,128]{1,0:T(1,128)S(1)} %get-tuple-element.22, f32[1,128]{1,0:T(1,128)S(1)} %collective-permute-done.9), kind=kLoop, calls=%fused_computation | loop fusion | flops 384 | bytes 2560 | tf_op jit(solution)/shard_map/reshape | solution.py:181
Async XLA Ops:
  1.1 8.6 %collective-permute-start = (bf16[520,128]{1,0:T(8,128)(2,1)S(1)}, bf16[520,128]{1,0:T(8,128)(2,1)S(1)}, u32[]{:S(2)}, u32[]{:S(2)}) collective-permute-start(bf16[520,128]{1,0:T(8,128)(2,1)S(1)} %get-tuple-element.16.refs_0_.refs_8_), channel_id=1, source_target_pairs={{6,0},{7,1},{4,2},{5,3},{2,4},{3,5},{0,6},{1,7},{14,8},{15,9},{12,... | collective-permute-start | bytes 399368 | tf_op jit(solution)/shard_map/ppermute | solution.py:135
  5.1 6.4 %collective-permute-start.1 = (bf16[520,128]{1,0:T(8,128)(2,1)S(1)}, bf16[520,128]{1,0:T(8,128)(2,1)S(1)}, u32[]{:S(2)}, u32[]{:S(2)}) collective-permute-start(bf16[520,128]{1,0:T(8,128)(2,1)S(1)} %get-tuple-element.16.refs_0_.refs_8_), channel_id=1, source_target_pairs={{4,0},{5,1},{6,2},{7,3},{0,4},{1,5},{2,6},{3,7},{12,8},{13,9},{14,... | collective-permute-start | bytes 399368 | tf_op jit(solution)/shard_map/ppermute | solution.py:135
  5.6 6.1 %collective-permute-start.2 = (bf16[520,128]{1,0:T(8,128)(2,1)S(1)}, bf16[520,128]{1,0:T(8,128)(2,1)S(1)}, u32[]{:S(2)}, u32[]{:S(2)}) collective-permute-start(bf16[520,128]{1,0:T(8,128)(2,1)S(1)} %get-tuple-element.16.refs_0_.refs_8_), channel_id=1, source_target_pairs={{2,0},{3,1},{0,2},{1,3},{6,4},{7,5},{4,6},{5,7},{10,8},{11,9},{8,1... | collective-permute-start | bytes 399368 | tf_op jit(solution)/shard_map/ppermute | solution.py:135
  5.7 8.2 %collective-permute-start.7 = (bf16[520,128]{1,0:T(8,128)(2,1)S(1)}, bf16[520,128]{1,0:T(8,128)(2,1)S(1)}, u32[]{:S(2)}, u32[]{:S(2)}) collective-permute-start(bf16[520,128]{1,0:T(8,128)(2,1)S(1)} %get-tuple-element.16.refs_0_.refs_8_), channel_id=1, source_target_pairs={{24,0},{25,1},{26,2},{27,3},{28,4},{29,5},{30,6},{31,7},{16,8},{17... | collective-permute-start | bytes 399368 | tf_op jit(solution)/shard_map/ppermute | solution.py:135
  9.7 5.7 %collective-permute-start.8 = (bf16[520,128]{1,0:T(8,128)(2,1)S(1)}, bf16[520,128]{1,0:T(8,128)(2,1)S(1)}, u32[]{:S(2)}, u32[]{:S(2)}) collective-permute-start(bf16[520,128]{1,0:T(8,128)(2,1)S(1)} %get-tuple-element.16.refs_0_.refs_8_), channel_id=1, source_target_pairs={{8,0},{9,1},{10,2},{11,3},{12,4},{13,5},{14,6},{15,7},{0,8},{1,9},... | collective-permute-start | bytes 399368 | tf_op jit(solution)/shard_map/ppermute | solution.py:135
  9.7 7.3 %collective-permute-start.3 = (bf16[520,128]{1,0:T(8,128)(2,1)S(1)}, bf16[520,128]{1,0:T(8,128)(2,1)S(1)}, u32[]{:S(2)}, u32[]{:S(2)}) collective-permute-start(bf16[520,128]{1,0:T(8,128)(2,1)S(1)} %get-tuple-element.16.refs_0_.refs_8_), channel_id=1, source_target_pairs={{1,0},{0,1},{3,2},{2,3},{5,4},{4,5},{7,6},{6,7},{9,8},{8,9},{11,10... | collective-permute-start | bytes 399368 | tf_op jit(solution)/shard_map/ppermute | solution.py:135
  11.7 5.3 %collective-permute-start.4 = (bf16[520,128]{1,0:T(8,128)(2,1)S(1)}, bf16[520,128]{1,0:T(8,128)(2,1)S(1)}, u32[]{:S(2)}, u32[]{:S(2)}) collective-permute-start(bf16[520,128]{1,0:T(8,128)(2,1)S(1)} %collective-permute-done.2.refs_1_), channel_id=1, source_target_pairs={{1,0},{0,1},{3,2},{2,3},{5,4},{4,5},{7,6},{6,7},{9,8},{8,9},{11,10... | collective-permute-start | bytes 399368 | tf_op jit(solution)/shard_map/ppermute | solution.py:135
  11.7 5.3 %collective-permute-start.5 = (bf16[520,128]{1,0:T(8,128)(2,1)S(1)}, bf16[520,128]{1,0:T(8,128)(2,1)S(1)}, u32[]{:S(2)}, u32[]{:S(2)}) collective-permute-start(bf16[520,128]{1,0:T(8,128)(2,1)S(1)} %collective-permute-done.1.refs_2_), channel_id=1, source_target_pairs={{1,0},{0,1},{3,2},{2,3},{5,4},{4,5},{7,6},{6,7},{9,8},{8,9},{11,10... | collective-permute-start | bytes 399368 | tf_op jit(solution)/shard_map/ppermute | solution.py:135
  13.9 3.1 %collective-permute-start.6 = (bf16[520,128]{1,0:T(8,128)(2,1)S(1)}, bf16[520,128]{1,0:T(8,128)(2,1)S(1)}, u32[]{:S(2)}, u32[]{:S(2)}) collective-permute-start(bf16[520,128]{1,0:T(8,128)(2,1)S(1)} %collective-permute-done.refs_3_), channel_id=1, source_target_pairs={{1,0},{0,1},{3,2},{2,3},{5,4},{4,5},{7,6},{6,7},{9,8},{8,9},{11,10... | collective-permute-start | bytes 399368 | tf_op jit(solution)/shard_map/ppermute | solution.py:135
  15.4 5.0 %collective-permute-start.11 = (bf16[520,128]{1,0:T(8,128)(2,1)S(1)}, bf16[520,128]{1,0:T(8,128)(2,1)S(1)}, u32[]{:S(2)}, u32[]{:S(2)}) collective-permute-start(bf16[520,128]{1,0:T(8,128)(2,1)S(1)} %collective-permute-done.7.refs_10_), channel_id=1, source_target_pairs={{8,0},{9,1},{10,2},{11,3},{12,4},{13,5},{14,6},{15,7},{0,8},{1,9},... | collective-permute-start | bytes 399368 | tf_op jit(solution)/shard_map/ppermute | solution.py:135
  17.8 5.4 %collective-permute-start.10 = (f32[1,128]{1,0:T(1,128)S(1)}, f32[1,128]{1,0:T(1,128)S(1)}, u32[]{:S(2)}, u32[]{:S(2)}) collective-permute-start(f32[1,128]{1,0:T(1,128)S(1)} %get-tuple-element.24), channel_id=1, source_target_pairs={{24,0},{25,1},{26,2},{27,3},{28,4},{29,5},{30,6},{31,7},{16,8},{17... | collective-permute-start | bytes 1544 | tf_op jit(solution)/shard_map/ppermute | solution.py:135
  19.6 3.6 %collective-permute-start.9 = (f32[1,128]{1,0:T(1,128)S(1)}, f32[1,128]{1,0:T(1,128)S(1)}, u32[]{:S(2)}, u32[]{:S(2)}) collective-permute-start(f32[1,128]{1,0:T(1,128)S(1)} %get-tuple-element.23), channel_id=1, source_target_pairs={{8,0},{9,1},{10,2},{11,3},{12,4},{13,5},{14,6},{15,7},{0,8},{1,9},... | collective-permute-start | bytes 1544 | tf_op jit(solution)/shard_map/ppermute | solution.py:135
  20.8 4.5 %collective-permute-start.12 = (f32[1,128]{1,0:T(1,128)S(1)}, f32[1,128]{1,0:T(1,128)S(1)}, u32[]{:S(2)}, u32[]{:S(2)}) collective-permute-start(f32[1,128]{1,0:T(1,128)S(1)} %shard_map.39), channel_id=1, source_target_pairs={{16,0},{17,1},{18,2},{19,3},{20,4},{21,5},{22,6},{23,7},{24,8},{25... | collective-permute-start | bytes 1544 | tf_op jit(solution)/shard_map/ppermute | solution.py:135

commit v27 on v26

--- a/solution.py
+++ b/solution.py
@@ -155,6 +155,7 @@
         near = [permute(own, lambda z, a, g: (z, turned(a, s, wide), g)) for s in reversed(range(1, wide))]
         middle = along(own, length - 1) if half < length else None
         first = [along(own, s) for s in range(1, half)]
+        near[0], middle = lax.optimization_barrier((near[0], middle))
         near = lax.optimization_barrier(near)
         middle, first = lax.optimization_barrier((middle, first))
         near = near[::-1]

time: 26 us -> 26.3 us (1.012)
  no operation moved by 1% of the time
where the time goes in v27:
time: 26.3 us; the launch traced here: 26.1 us
  starting transfers between devices  14.6 us (56%)
  waiting for transfers between devices  8.58 us (33%)
  Pallas kernels  2.37 us (9%)
  other arithmetic  0.52 us (2%)
    ppermute x13, starting transfers between devices, permute(): return lax.ppermute(x, ('clu', 'grp'), pairs)  14.6 us
    ppermute x13, waiting for transfers between devices, permute(): return lax.ppermute(x, ('clu', 'grp'), pairs)  8.58 us
    pallas_call x2, Pallas kernels, best_of(): pl.pallas_call(functools.partial(best_kernel, rows, len(keys), n_spans, o...  1.27 us
    pallas_call x1, Pallas kernels, pack(): pl.pallas_call(functools.partial(pack_kernel, groups), out_shape=[pltpu.V...  1.1 us
  transfers between devices with their start and end apart: 13, of which 7 were waited for; matrix products, arithmetic and copies ran while one was open for 0% of the time, Pallas kernels for 5%

profile of v27, /device:TPU:0, one launch (start us, length us, event | category | flops | bytes accessed | tf_op | source)
XLA Modules:
  0.0 26.1 jit_solution(1243858971275090475)
XLA Ops:
  0.0 1.1 %shard_map.37 = (bf16[520,128]{1,0:T(8,128)(2,1)S(1)}, bf16[64,64]{1,0:T(8,128)(2,1)S(1)}) custom-call(bf16[128,512]{1,0:T(8,128)(2,1)} %emb_ref.1, s32[1,128]{1,0:T(1,128)} %bitcast.4, s32[1,64]{1,0:T(1,128)} %bitcast.5), custom_call_target="tpu_custom_call" | custom-call | tf_op jit(solution)/shard_map/pallas_call | solution.py:42
  1.1 4.0 %collective-permute-start = (bf16[520,128]{1,0:T(8,128)(2,1)S(1)}, bf16[520,128]{1,0:T(8,128)(2,1)S(1)}, u32[]{:S(2)}, u32[]{:S(2)}) collective-permute-start(bf16[520,128]{1,0:T(8,128)(2,1)S(1)} %get-tuple-element.18.refs_0_.refs_8_), channel_id=1, source_target_pairs={{6,0},{7,1},{4,2},{5,3},{2,4},{3,5},{0,6},{1,7},{14,8},{15,9},{12,... | collective-permute-start | bytes 399368 | tf_op jit(solution)/shard_map/ppermute | solution.py:135
  5.1 3.6 %collective-permute-start.1 = (bf16[520,128]{1,0:T(8,128)(2,1)S(1)}, bf16[520,128]{1,0:T(8,128)(2,1)S(1)}, u32[]{:S(2)}, u32[]{:S(2)}) collective-permute-start(bf16[520,128]{1,0:T(8,128)(2,1)S(1)} %get-tuple-element.18.refs_0_.refs_8_), channel_id=1, source_target_pairs={{24,0},{25,1},{26,2},{27,3},{28,4},{29,5},{30,6},{31,7},{16,8},{17... | collective-permute-start | bytes 399368 | tf_op jit(solution)/shard_map/ppermute | solution.py:135
  8.7 0.5 %collective-permute-start.2 = (bf16[520,128]{1,0:T(8,128)(2,1)S(1)}, bf16[520,128]{1,0:T(8,128)(2,1)S(1)}, u32[]{:S(2)}, u32[]{:S(2)}) collective-permute-start(bf16[520,128]{1,0:T(8,128)(2,1)S(1)} %get-tuple-element.18.refs_0_.refs_8_), channel_id=1, source_target_pairs={{4,0},{5,1},{6,2},{7,3},{0,4},{1,5},{2,6},{3,7},{12,8},{13,9},{14,... | collective-permute-start | bytes 399368 | tf_op jit(solution)/shard_map/ppermute | solution.py:135
  9.2 0.5 %collective-permute-start.3 = (bf16[520,128]{1,0:T(8,128)(2,1)S(1)}, bf16[520,128]{1,0:T(8,128)(2,1)S(1)}, u32[]{:S(2)}, u32[]{:S(2)}) collective-permute-start(bf16[520,128]{1,0:T(8,128)(2,1)S(1)} %get-tuple-element.18.refs_0_.refs_8_), channel_id=1, source_target_pairs={{2,0},{3,1},{0,2},{1,3},{6,4},{7,5},{4,6},{5,7},{10,8},{11,9},{8,1... | collective-permute-start | bytes 399368 | tf_op jit(solution)/shard_map/ppermute | solution.py:135
  9.7 0.0 collective-permute-start.8
  9.7 0.0 collective-permute-done.refs_3_
  9.7 0.0 collective-permute-start.4
  9.7 3.6 %collective-permute-done.1.refs_10_ = bf16[520,128]{1,0:T(8,128)(2,1)S(1)} collective-permute-done((bf16[520,128]{1,0:T(8,128)(2,1)S(1)}, bf16[520,128]{1,0:T(8,128)(2,1)S(1)}, u32[]{:S(2)}, u32[]{:S(2)}) %collective-permute-start.1) | collective-permute-done | bytes 133152 | tf_op jit(solution)/shard_map/ppermute | solution.py:135
  13.3 0.3 %collective-permute-done.2.refs_2_ = bf16[520,128]{1,0:T(8,128)(2,1)S(1)} collective-permute-done((bf16[520,128]{1,0:T(8,128)(2,1)S(1)}, bf16[520,128]{1,0:T(8,128)(2,1)S(1)}, u32[]{:S(2)}, u32[]{:S(2)}) %collective-permute-start.2) | collective-permute-done | bytes 133152 | tf_op jit(solution)/shard_map/ppermute | solution.py:135
  13.7 0.5 %collective-permute-done.3.refs_1_ = bf16[520,128]{1,0:T(8,128)(2,1)S(1)} collective-permute-done((bf16[520,128]{1,0:T(8,128)(2,1)S(1)}, bf16[520,128]{1,0:T(8,128)(2,1)S(1)}, u32[]{:S(2)}, u32[]{:S(2)}) %collective-permute-start.3) | collective-permute-done | bytes 133152 | tf_op jit(solution)/shard_map/ppermute | solution.py:135
  14.2 0.0 collective-permute-start.5
  14.2 0.5 %collective-permute-start.6 = (bf16[520,128]{1,0:T(8,128)(2,1)S(1)}, bf16[520,128]{1,0:T(8,128)(2,1)S(1)}, u32[]{:S(2)}, u32[]{:S(2)}) collective-permute-start(bf16[520,128]{1,0:T(8,128)(2,1)S(1)} %collective-permute-done.2.refs_2_), channel_id=1, source_target_pairs={{1,0},{0,1},{3,2},{2,3},{5,4},{4,5},{7,6},{6,7},{9,8},{8,9},{11,10... | collective-permute-start | bytes 399368 | tf_op jit(solution)/shard_map/ppermute | solution.py:135
  14.7 0.0 collective-permute-start.7
  14.7 0.3 %collective-permute-done.8.refs_9_ = bf16[520,128]{1,0:T(8,128)(2,1)S(1)} collective-permute-done((bf16[520,128]{1,0:T(8,128)(2,1)S(1)}, bf16[520,128]{1,0:T(8,128)(2,1)S(1)}, u32[]{:S(2)}, u32[]{:S(2)}) %collective-permute-start.8) | collective-permute-done | bytes 133152 | tf_op jit(solution)/shard_map/ppermute | solution.py:135
  15.0 1.5 %collective-permute-start.11 = (bf16[520,128]{1,0:T(8,128)(2,1)S(1)}, bf16[520,128]{1,0:T(8,128)(2,1)S(1)}, u32[]{:S(2)}, u32[]{:S(2)}) collective-permute-start(bf16[520,128]{1,0:T(8,128)(2,1)S(1)} %collective-permute-done.1.refs_10_), channel_id=1, source_target_pairs={{8,0},{9,1},{10,2},{11,3},{12,4},{13,5},{14,6},{15,7},{0,8},{1,9},... | collective-permute-start | bytes 399368 | tf_op jit(solution)/shard_map/ppermute | solution.py:135
  16.6 0.0 collective-permute-done.4.refs_4_
  16.6 0.0 collective-permute-done.5.refs_5_
  16.6 0.0 collective-permute-done.6.refs_6_
  16.6 0.0 collective-permute-done.7.refs_7_
  16.6 0.8 %shard_map.38 = (f32[1,128]{1,0:T(1,128)S(1)}, f32[1,128]{1,0:T(1,128)S(1)}, f32[1,128]{1,0:T(1,128)S(1)}) custom-call(bf16[64,64]{1,0:T(8,128)(2,1)S(1)} %get-tuple-element.17.table_ref, bf16[520,128]{1,0:T(8,128)(2,1)S(1)} %get-tuple-element.18.refs_0_.refs_8_, bf16[520,128]{1,0:T(8,128)(2,1)S(1)} %collective-permute-done.3.refs_1_, ...), custom_call_target="tpu_custom_call" | custom-call | flops 402653184 | bytes 1441792 | tf_op jit(solution)/shard_map/pallas_call | solution.py:110
  17.4 2.3 %collective-permute-start.10 = (f32[1,128]{1,0:T(1,128)S(1)}, f32[1,128]{1,0:T(1,128)S(1)}, u32[]{:S(2)}, u32[]{:S(2)}) collective-permute-start(f32[1,128]{1,0:T(1,128)S(1)} %get-tuple-element.28), channel_id=1, source_target_pairs={{24,0},{25,1},{26,2},{27,3},{28,4},{29,5},{30,6},{31,7},{16,8},{17... | collective-permute-start | bytes 1544 | tf_op jit(solution)/shard_map/ppermute | solution.py:135
  19.7 0.0 collective-permute-start.9
  19.7 0.9 %collective-permute-done.11.refs_8_ = bf16[520,128]{1,0:T(8,128)(2,1)S(1)} collective-permute-done((bf16[520,128]{1,0:T(8,128)(2,1)S(1)}, bf16[520,128]{1,0:T(8,128)(2,1)S(1)}, u32[]{:S(2)}, u32[]{:S(2)}) %collective-permute-start.11) | collective-permute-done | bytes 133152 | tf_op jit(solution)/shard_map/ppermute | solution.py:135
  20.6 0.5 %shard_map.39 = f32[1,128]{1,0:T(1,128)S(1)} custom-call(bf16[64,64]{1,0:T(8,128)(2,1)S(1)} %get-tuple-element.17.table_ref, bf16[520,128]{1,0:T(8,128)(2,1)S(1)} %get-tuple-element.18.refs_0_.refs_8_, bf16[520,128]{1,0:T(8,128)(2,1)S(1)} %collective-permute-done.3.refs_1_, bf16[520,128]{1,0:T(8,128)(2,1)S(1)} %collective-permute-done.2.refs_2_, ...), custom_call_target="tpu_custom_call" | custom-call | flops 134217728 | bytes 1179648 | tf_op jit(solution)/shard_map/pallas_call | solution.py:110
  21.1 1.7 %collective-permute-start.12 = (f32[1,128]{1,0:T(1,128)S(1)}, f32[1,128]{1,0:T(1,128)S(1)}, u32[]{:S(2)}, u32[]{:S(2)}) collective-permute-start(f32[1,128]{1,0:T(1,128)S(1)} %shard_map.39), channel_id=1, source_target_pairs={{16,0},{17,1},{18,2},{19,3},{20,4},{21,5},{22,6},{23,7},{24,8},{25... | collective-permute-start | bytes 1544 | tf_op jit(solution)/shard_map/ppermute | solution.py:135
  22.8 0.0 collective-permute-done.10
  22.8 0.4 %collective-permute-done.9 = f32[1,128]{1,0:T(1,128)S(1)} collective-permute-done((f32[1,128]{1,0:T(1,128)S(1)}, f32[1,128]{1,0:T(1,128)S(1)}, u32[]{:S(2)}, u32[]{:S(2)}) %collective-permute-start.9) | collective-permute-done | bytes 544 | tf_op jit(solution)/shard_map/ppermute | solution.py:135
  23.2 2.4 %collective-permute-done.12 = f32[1,128]{1,0:T(1,128)S(1)} collective-permute-done((f32[1,128]{1,0:T(1,128)S(1)}, f32[1,128]{1,0:T(1,128)S(1)}, u32[]{:S(2)}, u32[]{:S(2)}) %collective-permute-start.12) | collective-permute-done | bytes 544 | tf_op jit(solution)/shard_map/ppermute | solution.py:135
  25.6 0.5 %maximum_bitcast_fusion = f32[128]{0:T(128)} fusion(f32[1,128]{1,0:T(1,128)S(1)} %collective-permute-done.12, f32[1,128]{1,0:T(1,128)S(1)} %collective-permute-done.10, f32[1,128]{1,0:T(1,128)S(1)} %get-tuple-element.26, f32[1,128]{1,0:T(1,128)S(1)} %collective-permute-done.9), kind=kLoop, calls=%fused_computation | loop fusion | flops 384 | bytes 2560 | tf_op jit(solution)/shard_map/reshape | solution.py:182
Async XLA Ops:
  1.1 8.6 %collective-permute-start = (bf16[520,128]{1,0:T(8,128)(2,1)S(1)}, bf16[520,128]{1,0:T(8,128)(2,1)S(1)}, u32[]{:S(2)}, u32[]{:S(2)}) collective-permute-start(bf16[520,128]{1,0:T(8,128)(2,1)S(1)} %get-tuple-element.18.refs_0_.refs_8_), channel_id=1, source_target_pairs={{6,0},{7,1},{4,2},{5,3},{2,4},{3,5},{0,6},{1,7},{14,8},{15,9},{12,... | collective-permute-start | bytes 399368 | tf_op jit(solution)/shard_map/ppermute | solution.py:135
  5.1 8.3 %collective-permute-start.1 = (bf16[520,128]{1,0:T(8,128)(2,1)S(1)}, bf16[520,128]{1,0:T(8,128)(2,1)S(1)}, u32[]{:S(2)}, u32[]{:S(2)}) collective-permute-start(bf16[520,128]{1,0:T(8,128)(2,1)S(1)} %get-tuple-element.18.refs_0_.refs_8_), channel_id=1, source_target_pairs={{24,0},{25,1},{26,2},{27,3},{28,4},{29,5},{30,6},{31,7},{16,8},{17... | collective-permute-start | bytes 399368 | tf_op jit(solution)/shard_map/ppermute | solution.py:135
  8.7 5.0 %collective-permute-start.2 = (bf16[520,128]{1,0:T(8,128)(2,1)S(1)}, bf16[520,128]{1,0:T(8,128)(2,1)S(1)}, u32[]{:S(2)}, u32[]{:S(2)}) collective-permute-start(bf16[520,128]{1,0:T(8,128)(2,1)S(1)} %get-tuple-element.18.refs_0_.refs_8_), channel_id=1, source_target_pairs={{4,0},{5,1},{6,2},{7,3},{0,4},{1,5},{2,6},{3,7},{12,8},{13,9},{14,... | collective-permute-start | bytes 399368 | tf_op jit(solution)/shard_map/ppermute | solution.py:135
  9.2 5.0 %collective-permute-start.3 = (bf16[520,128]{1,0:T(8,128)(2,1)S(1)}, bf16[520,128]{1,0:T(8,128)(2,1)S(1)}, u32[]{:S(2)}, u32[]{:S(2)}) collective-permute-start(bf16[520,128]{1,0:T(8,128)(2,1)S(1)} %get-tuple-element.18.refs_0_.refs_8_), channel_id=1, source_target_pairs={{2,0},{3,1},{0,2},{1,3},{6,4},{7,5},{4,6},{5,7},{10,8},{11,9},{8,1... | collective-permute-start | bytes 399368 | tf_op jit(solution)/shard_map/ppermute | solution.py:135
  9.7 5.3 %collective-permute-start.8 = (bf16[520,128]{1,0:T(8,128)(2,1)S(1)}, bf16[520,128]{1,0:T(8,128)(2,1)S(1)}, u32[]{:S(2)}, u32[]{:S(2)}) collective-permute-start(bf16[520,128]{1,0:T(8,128)(2,1)S(1)} %get-tuple-element.18.refs_0_.refs_8_), channel_id=1, source_target_pairs={{8,0},{9,1},{10,2},{11,3},{12,4},{13,5},{14,6},{15,7},{0,8},{1,9},... | collective-permute-start | bytes 399368 | tf_op jit(solution)/shard_map/ppermute | solution.py:135
  9.7 6.9 %collective-permute-start.4 = (bf16[520,128]{1,0:T(8,128)(2,1)S(1)}, bf16[520,128]{1,0:T(8,128)(2,1)S(1)}, u32[]{:S(2)}, u32[]{:S(2)}) collective-permute-start(bf16[520,128]{1,0:T(8,128)(2,1)S(1)} %get-tuple-element.18.refs_0_.refs_8_), channel_id=1, source_target_pairs={{1,0},{0,1},{3,2},{2,3},{5,4},{4,5},{7,6},{6,7},{9,8},{8,9},{11,10... | collective-permute-start | bytes 399368 | tf_op jit(solution)/shard_map/ppermute | solution.py:135
  14.2 2.4 %collective-permute-start.5 = (bf16[520,128]{1,0:T(8,128)(2,1)S(1)}, bf16[520,128]{1,0:T(8,128)(2,1)S(1)}, u32[]{:S(2)}, u32[]{:S(2)}) collective-permute-start(bf16[520,128]{1,0:T(8,128)(2,1)S(1)} %collective-permute-done.3.refs_1_), channel_id=1, source_target_pairs={{1,0},{0,1},{3,2},{2,3},{5,4},{4,5},{7,6},{6,7},{9,8},{8,9},{11,10... | collective-permute-start | bytes 399368 | tf_op jit(solution)/shard_map/ppermute | solution.py:135
  14.2 2.4 %collective-permute-start.6 = (bf16[520,128]{1,0:T(8,128)(2,1)S(1)}, bf16[520,128]{1,0:T(8,128)(2,1)S(1)}, u32[]{:S(2)}, u32[]{:S(2)}) collective-permute-start(bf16[520,128]{1,0:T(8,128)(2,1)S(1)} %collective-permute-done.2.refs_2_), channel_id=1, source_target_pairs={{1,0},{0,1},{3,2},{2,3},{5,4},{4,5},{7,6},{6,7},{9,8},{8,9},{11,10... | collective-permute-start | bytes 399368 | tf_op jit(solution)/shard_map/ppermute | solution.py:135
  14.7 1.9 %collective-permute-start.7 = (bf16[520,128]{1,0:T(8,128)(2,1)S(1)}, bf16[520,128]{1,0:T(8,128)(2,1)S(1)}, u32[]{:S(2)}, u32[]{:S(2)}) collective-permute-start(bf16[520,128]{1,0:T(8,128)(2,1)S(1)} %collective-permute-done.refs_3_), channel_id=1, source_target_pairs={{1,0},{0,1},{3,2},{2,3},{5,4},{4,5},{7,6},{6,7},{9,8},{8,9},{11,10... | collective-permute-start | bytes 399368 | tf_op jit(solution)/shard_map/ppermute | solution.py:135
  15.0 5.6 %collective-permute-start.11 = (bf16[520,128]{1,0:T(8,128)(2,1)S(1)}, bf16[520,128]{1,0:T(8,128)(2,1)S(1)}, u32[]{:S(2)}, u32[]{:S(2)}) collective-permute-start(bf16[520,128]{1,0:T(8,128)(2,1)S(1)} %collective-permute-done.1.refs_10_), channel_id=1, source_target_pairs={{8,0},{9,1},{10,2},{11,3},{12,4},{13,5},{14,6},{15,7},{0,8},{1,9},... | collective-permute-start | bytes 399368 | tf_op jit(solution)/shard_map/ppermute | solution.py:135
  17.4 5.4 %collective-permute-start.10 = (f32[1,128]{1,0:T(1,128)S(1)}, f32[1,128]{1,0:T(1,128)S(1)}, u32[]{:S(2)}, u32[]{:S(2)}) collective-permute-start(f32[1,128]{1,0:T(1,128)S(1)} %get-tuple-element.28), channel_id=1, source_target_pairs={{24,0},{25,1},{26,2},{27,3},{28,4},{29,5},{30,6},{31,7},{16,8},{17... | collective-permute-start | bytes 1544 | tf_op jit(solution)/shard_map/ppermute | solution.py:135
  19.7 3.5 %collective-permute-start.9 = (f32[1,128]{1,0:T(1,128)S(1)}, f32[1,128]{1,0:T(1,128)S(1)}, u32[]{:S(2)}, u32[]{:S(2)}) collective-permute-start(f32[1,128]{1,0:T(1,128)S(1)} %get-tuple-element.27), channel_id=1, source_target_pairs={{8,0},{9,1},{10,2},{11,3},{12,4},{13,5},{14,6},{15,7},{0,8},{1,9},... | collective-permute-start | bytes 1544 | tf_op jit(solution)/shard_map/ppermute | solution.py:135
  21.1 4.5 %collective-permute-start.12 = (f32[1,128]{1,0:T(1,128)S(1)}, f32[1,128]{1,0:T(1,128)S(1)}, u32[]{:S(2)}, u32[]{:S(2)}) collective-permute-start(f32[1,128]{1,0:T(1,128)S(1)} %shard_map.39), channel_id=1, source_target_pairs={{16,0},{17,1},{18,2},{19,3},{20,4},{21,5},{22,6},{23,7},{24,8},{25... | collective-permute-start | bytes 1544 | tf_op jit(solution)/shard_map/ppermute | solution.py:135

commit v28 on v26

--- a/solution.py
+++ b/solution.py
@@ -165,10 +165,14 @@
             offsets += [length - 1] + [(length - 1) ^ s for s in range(1, half)]
         far, far_rank = [], []
         for t in range(1, n_grp):
+            swapped = []
             for s in range(wide):
                 block = near[s - 1] if s else own
-                far.append(permute(block, lambda z, a, g: (z, a, turned(g, t, n_grp))))
+                if s and s == wide - 1:
+                    swapped[0], block = lax.optimization_barrier((swapped[0], block))
+                swapped.append(permute(block, lambda z, a, g: (z, a, turned(g, t, n_grp))))
                 far_rank.append(rank(a=s, g=t))
+            far += swapped
         near = list(zip([own] + near, [rank(a=s) for s in range(wide)]))
         far = list(zip(far, far_rank))
         visit_rank = [rank(z=s) for s in offsets]

time: 26 us -> 28 us (1.077)
  starting transfers between devices: 14.5 us -> 15.7 us
  waiting for transfers between devices: 8.36 us -> 9.28 us
    ppermute x13, starting transfers between devices: 14.5 us -> 15.7 us  [permute(): return lax.ppermute(x, ('clu', 'grp'), pairs)]
    ppermute x13, waiting for transfers between devices: 8.36 us -> 9.28 us  [permute(): return lax.ppermute(x, ('clu', 'grp'), pairs)]
where the time goes in v28:
time: 28 us; the launch traced here: 27.9 us
  starting transfers between devices  15.7 us (56%)
  waiting for transfers between devices  9.28 us (33%)
  Pallas kernels  2.37 us (8%)
  other arithmetic  0.52 us (2%)
    ppermute x13, starting transfers between devices, permute(): return lax.ppermute(x, ('clu', 'grp'), pairs)  15.7 us
    ppermute x13, waiting for transfers between devices, permute(): return lax.ppermute(x, ('clu', 'grp'), pairs)  9.28 us
    pallas_call x2, Pallas kernels, best_of(): pl.pallas_call(functools.partial(best_kernel, rows, len(keys), n_spans, o...  1.27 us
    pallas_call x1, Pallas kernels, pack(): pl.pallas_call(functools.partial(pack_kernel, groups), out_shape=[pltpu.V...  1.1 us
  transfers between devices with their start and end apart: 13, of which 7 were waited for; matrix products, arithmetic and copies ran while one was open for 0% of the time, Pallas kernels for 5%

profile of v28, /device:TPU:0, one launch (start us, length us, event | category | flops | bytes accessed | tf_op | source)
XLA Modules:
  0.0 27.9 jit_solution(4835772167512050299)
XLA Ops:
  0.0 1.1 %shard_map.37 = (bf16[520,128]{1,0:T(8,128)(2,1)S(1)}, bf16[64,64]{1,0:T(8,128)(2,1)S(1)}) custom-call(bf16[128,512]{1,0:T(8,128)(2,1)} %emb_ref.1, s32[1,128]{1,0:T(1,128)} %bitcast.4, s32[1,64]{1,0:T(1,128)} %bitcast.5), custom_call_target="tpu_custom_call" | custom-call | tf_op jit(solution)/shard_map/pallas_call | solution.py:42
  1.1 4.0 %collective-permute-start = (bf16[520,128]{1,0:T(8,128)(2,1)S(1)}, bf16[520,128]{1,0:T(8,128)(2,1)S(1)}, u32[]{:S(2)}, u32[]{:S(2)}) collective-permute-start(bf16[520,128]{1,0:T(8,128)(2,1)S(1)} %get-tuple-element.18.refs_0_.refs_8_), channel_id=1, source_target_pairs={{6,0},{7,1},{4,2},{5,3},{2,4},{3,5},{0,6},{1,7},{14,8},{15,9},{12,... | collective-permute-start | bytes 399368 | tf_op jit(solution)/shard_map/ppermute | solution.py:135
  5.1 0.5 %collective-permute-start.1 = (bf16[520,128]{1,0:T(8,128)(2,1)S(1)}, bf16[520,128]{1,0:T(8,128)(2,1)S(1)}, u32[]{:S(2)}, u32[]{:S(2)}) collective-permute-start(bf16[520,128]{1,0:T(8,128)(2,1)S(1)} %get-tuple-element.18.refs_0_.refs_8_), channel_id=1, source_target_pairs={{4,0},{5,1},{6,2},{7,3},{0,4},{1,5},{2,6},{3,7},{12,8},{13,9},{14,... | collective-permute-start | bytes 399368 | tf_op jit(solution)/shard_map/ppermute | solution.py:135
  5.6 0.1 collective-permute-start.2
  5.7 0.0 collective-permute-start.3
  5.7 4.0 %collective-permute-start.7 = (bf16[520,128]{1,0:T(8,128)(2,1)S(1)}, bf16[520,128]{1,0:T(8,128)(2,1)S(1)}, u32[]{:S(2)}, u32[]{:S(2)}) collective-permute-start(bf16[520,128]{1,0:T(8,128)(2,1)S(1)} %get-tuple-element.18.refs_0_.refs_8_), channel_id=1, source_target_pairs={{24,0},{25,1},{26,2},{27,3},{28,4},{29,5},{30,6},{31,7},{16,8},{17... | collective-permute-start | bytes 399368 | tf_op jit(solution)/shard_map/ppermute | solution.py:135
  9.7 0.0 collective-permute-done.refs_3_
  9.7 1.0 %collective-permute-start.8 = (bf16[520,128]{1,0:T(8,128)(2,1)S(1)}, bf16[520,128]{1,0:T(8,128)(2,1)S(1)}, u32[]{:S(2)}, u32[]{:S(2)}) collective-permute-start(bf16[520,128]{1,0:T(8,128)(2,1)S(1)} %get-tuple-element.18.refs_0_.refs_8_), channel_id=1, source_target_pairs={{8,0},{9,1},{10,2},{11,3},{12,4},{13,5},{14,6},{15,7},{0,8},{1,9},... | collective-permute-start | bytes 399368 | tf_op jit(solution)/shard_map/ppermute | solution.py:135
  10.7 0.7 %collective-permute-done.1.refs_2_ = bf16[520,128]{1,0:T(8,128)(2,1)S(1)} collective-permute-done((bf16[520,128]{1,0:T(8,128)(2,1)S(1)}, bf16[520,128]{1,0:T(8,128)(2,1)S(1)}, u32[]{:S(2)}, u32[]{:S(2)}) %collective-permute-start.1) | collective-permute-done | bytes 133152 | tf_op jit(solution)/shard_map/ppermute | solution.py:135
  11.5 0.2 collective-permute-done.2.refs_1_
  11.7 0.0 collective-permute-done.3.refs_4_
  11.7 0.0 collective-permute-start.6
  11.7 0.5 %collective-permute-start.4 = (bf16[520,128]{1,0:T(8,128)(2,1)S(1)}, bf16[520,128]{1,0:T(8,128)(2,1)S(1)}, u32[]{:S(2)}, u32[]{:S(2)}) collective-permute-start(bf16[520,128]{1,0:T(8,128)(2,1)S(1)} %collective-permute-done.2.refs_1_), channel_id=1, source_target_pairs={{1,0},{0,1},{3,2},{2,3},{5,4},{4,5},{7,6},{6,7},{9,8},{8,9},{11,10... | collective-permute-start | bytes 399368 | tf_op jit(solution)/shard_map/ppermute | solution.py:135
  12.2 0.0 collective-permute-start.5
  12.2 1.9 %collective-permute-done.7.refs_10_ = bf16[520,128]{1,0:T(8,128)(2,1)S(1)} collective-permute-done((bf16[520,128]{1,0:T(8,128)(2,1)S(1)}, bf16[520,128]{1,0:T(8,128)(2,1)S(1)}, u32[]{:S(2)}, u32[]{:S(2)}) %collective-permute-start.7) | collective-permute-done | bytes 133152 | tf_op jit(solution)/shard_map/ppermute | solution.py:135
  14.2 2.7 %collective-permute-done.8.refs_9_ = bf16[520,128]{1,0:T(8,128)(2,1)S(1)} collective-permute-done((bf16[520,128]{1,0:T(8,128)(2,1)S(1)}, bf16[520,128]{1,0:T(8,128)(2,1)S(1)}, u32[]{:S(2)}, u32[]{:S(2)}) %collective-permute-start.8) | collective-permute-done | bytes 133152 | tf_op jit(solution)/shard_map/ppermute | solution.py:135
  16.9 1.7 %collective-permute-start.11 = (bf16[520,128]{1,0:T(8,128)(2,1)S(1)}, bf16[520,128]{1,0:T(8,128)(2,1)S(1)}, u32[]{:S(2)}, u32[]{:S(2)}) collective-permute-start(bf16[520,128]{1,0:T(8,128)(2,1)S(1)} %collective-permute-done.7.refs_10_), channel_id=1, source_target_pairs={{8,0},{9,1},{10,2},{11,3},{12,4},{13,5},{14,6},{15,7},{0,8},{1,9},... | collective-permute-start | bytes 399368 | tf_op jit(solution)/shard_map/ppermute | solution.py:135
  18.6 0.0 collective-permute-done.6.refs_7_
  18.6 0.0 collective-permute-done.4.refs_5_
  18.6 0.0 collective-permute-done.5.refs_6_
  18.6 0.8 %shard_map.38 = (f32[1,128]{1,0:T(1,128)S(1)}, f32[1,128]{1,0:T(1,128)S(1)}, f32[1,128]{1,0:T(1,128)S(1)}) custom-call(bf16[64,64]{1,0:T(8,128)(2,1)S(1)} %get-tuple-element.17.table_ref, bf16[520,128]{1,0:T(8,128)(2,1)S(1)} %get-tuple-element.18.refs_0_.refs_8_, bf16[520,128]{1,0:T(8,128)(2,1)S(1)} %collective-permute-done.2.refs_1_, ...), custom_call_target="tpu_custom_call" | custom-call | flops 402653184 | bytes 1441792 | tf_op jit(solution)/shard_map/pallas_call | solution.py:110
  19.4 1.2 %collective-permute-start.10 = (f32[1,128]{1,0:T(1,128)S(1)}, f32[1,128]{1,0:T(1,128)S(1)}, u32[]{:S(2)}, u32[]{:S(2)}) collective-permute-start(f32[1,128]{1,0:T(1,128)S(1)} %get-tuple-element.28), channel_id=1, source_target_pairs={{24,0},{25,1},{26,2},{27,3},{28,4},{29,5},{30,6},{31,7},{16,8},{17... | collective-permute-start | bytes 1544 | tf_op jit(solution)/shard_map/ppermute | solution.py:135
  20.6 1.1 %collective-permute-start.9 = (f32[1,128]{1,0:T(1,128)S(1)}, f32[1,128]{1,0:T(1,128)S(1)}, u32[]{:S(2)}, u32[]{:S(2)}) collective-permute-start(f32[1,128]{1,0:T(1,128)S(1)} %get-tuple-element.27), channel_id=1, source_target_pairs={{8,0},{9,1},{10,2},{11,3},{12,4},{13,5},{14,6},{15,7},{0,8},{1,9},... | collective-permute-start | bytes 1544 | tf_op jit(solution)/shard_map/ppermute | solution.py:135
  21.7 0.7 %collective-permute-done.11.refs_8_ = bf16[520,128]{1,0:T(8,128)(2,1)S(1)} collective-permute-done((bf16[520,128]{1,0:T(8,128)(2,1)S(1)}, bf16[520,128]{1,0:T(8,128)(2,1)S(1)}, u32[]{:S(2)}, u32[]{:S(2)}) %collective-permute-start.11) | collective-permute-done | bytes 133152 | tf_op jit(solution)/shard_map/ppermute | solution.py:135
  22.4 0.5 %shard_map.39 = f32[1,128]{1,0:T(1,128)S(1)} custom-call(bf16[64,64]{1,0:T(8,128)(2,1)S(1)} %get-tuple-element.17.table_ref, bf16[520,128]{1,0:T(8,128)(2,1)S(1)} %get-tuple-element.18.refs_0_.refs_8_, bf16[520,128]{1,0:T(8,128)(2,1)S(1)} %collective-permute-done.2.refs_1_, bf16[520,128]{1,0:T(8,128)(2,1)S(1)} %collective-permute-done.1.refs_2_, ...), custom_call_target="tpu_custom_call" | custom-call | flops 134217728 | bytes 1179648 | tf_op jit(solution)/shard_map/pallas_call | solution.py:110
  22.8 1.5 %collective-permute-start.12 = (f32[1,128]{1,0:T(1,128)S(1)}, f32[1,128]{1,0:T(1,128)S(1)}, u32[]{:S(2)}, u32[]{:S(2)}) collective-permute-start(f32[1,128]{1,0:T(1,128)S(1)} %shard_map.39), channel_id=1, source_target_pairs={{16,0},{17,1},{18,2},{19,3},{20,4},{21,5},{22,6},{23,7},{24,8},{25... | collective-permute-start | bytes 1544 | tf_op jit(solution)/shard_map/ppermute | solution.py:135
  24.4 0.4 %collective-permute-done.10 = f32[1,128]{1,0:T(1,128)S(1)} collective-permute-done((f32[1,128]{1,0:T(1,128)S(1)}, f32[1,128]{1,0:T(1,128)S(1)}, u32[]{:S(2)}, u32[]{:S(2)}) %collective-permute-start.10) | collective-permute-done | bytes 544 | tf_op jit(solution)/shard_map/ppermute | solution.py:135
  24.8 0.0 collective-permute-done.9
  24.8 2.5 %collective-permute-done.12 = f32[1,128]{1,0:T(1,128)S(1)} collective-permute-done((f32[1,128]{1,0:T(1,128)S(1)}, f32[1,128]{1,0:T(1,128)S(1)}, u32[]{:S(2)}, u32[]{:S(2)}) %collective-permute-start.12) | collective-permute-done | bytes 544 | tf_op jit(solution)/shard_map/ppermute | solution.py:135
  27.3 0.5 %maximum_bitcast_fusion = f32[128]{0:T(128)} fusion(f32[1,128]{1,0:T(1,128)S(1)} %collective-permute-done.12, f32[1,128]{1,0:T(1,128)S(1)} %collective-permute-done.10, f32[1,128]{1,0:T(1,128)S(1)} %get-tuple-element.26, f32[1,128]{1,0:T(1,128)S(1)} %collective-permute-done.9), kind=kLoop, calls=%fused_computation | loop fusion | flops 384 | bytes 2560 | tf_op jit(solution)/shard_map/reshape | solution.py:185
Async XLA Ops:
  1.1 8.6 %collective-permute-start = (bf16[520,128]{1,0:T(8,128)(2,1)S(1)}, bf16[520,128]{1,0:T(8,128)(2,1)S(1)}, u32[]{:S(2)}, u32[]{:S(2)}) collective-permute-start(bf16[520,128]{1,0:T(8,128)(2,1)S(1)} %get-tuple-element.18.refs_0_.refs_8_), channel_id=1, source_target_pairs={{6,0},{7,1},{4,2},{5,3},{2,4},{3,5},{0,6},{1,7},{14,8},{15,9},{12,... | collective-permute-start | bytes 399368 | tf_op jit(solution)/shard_map/ppermute | solution.py:135
  5.1 6.4 %collective-permute-start.1 = (bf16[520,128]{1,0:T(8,128)(2,1)S(1)}, bf16[520,128]{1,0:T(8,128)(2,1)S(1)}, u32[]{:S(2)}, u32[]{:S(2)}) collective-permute-start(bf16[520,128]{1,0:T(8,128)(2,1)S(1)} %get-tuple-element.18.refs_0_.refs_8_), channel_id=1, source_target_pairs={{4,0},{5,1},{6,2},{7,3},{0,4},{1,5},{2,6},{3,7},{12,8},{13,9},{14,... | collective-permute-start | bytes 399368 | tf_op jit(solution)/shard_map/ppermute | solution.py:135
  5.6 6.1 %collective-permute-start.2 = (bf16[520,128]{1,0:T(8,128)(2,1)S(1)}, bf16[520,128]{1,0:T(8,128)(2,1)S(1)}, u32[]{:S(2)}, u32[]{:S(2)}) collective-permute-start(bf16[520,128]{1,0:T(8,128)(2,1)S(1)} %get-tuple-element.18.refs_0_.refs_8_), channel_id=1, source_target_pairs={{2,0},{3,1},{0,2},{1,3},{6,4},{7,5},{4,6},{5,7},{10,8},{11,9},{8,1... | collective-permute-start | bytes 399368 | tf_op jit(solution)/shard_map/ppermute | solution.py:135
  5.7 6.0 %collective-permute-start.3 = (bf16[520,128]{1,0:T(8,128)(2,1)S(1)}, bf16[520,128]{1,0:T(8,128)(2,1)S(1)}, u32[]{:S(2)}, u32[]{:S(2)}) collective-permute-start(bf16[520,128]{1,0:T(8,128)(2,1)S(1)} %get-tuple-element.18.refs_0_.refs_8_), channel_id=1, source_target_pairs={{1,0},{0,1},{3,2},{2,3},{5,4},{4,5},{7,6},{6,7},{9,8},{8,9},{11,10... | collective-permute-start | bytes 399368 | tf_op jit(solution)/shard_map/ppermute | solution.py:135
  5.7 8.4 %collective-permute-start.7 = (bf16[520,128]{1,0:T(8,128)(2,1)S(1)}, bf16[520,128]{1,0:T(8,128)(2,1)S(1)}, u32[]{:S(2)}, u32[]{:S(2)}) collective-permute-start(bf16[520,128]{1,0:T(8,128)(2,1)S(1)} %get-tuple-element.18.refs_0_.refs_8_), channel_id=1, source_target_pairs={{24,0},{25,1},{26,2},{27,3},{28,4},{29,5},{30,6},{31,7},{16,8},{17... | collective-permute-start | bytes 399368 | tf_op jit(solution)/shard_map/ppermute | solution.py:135
  9.7 7.2 %collective-permute-start.8 = (bf16[520,128]{1,0:T(8,128)(2,1)S(1)}, bf16[520,128]{1,0:T(8,128)(2,1)S(1)}, u32[]{:S(2)}, u32[]{:S(2)}) collective-permute-start(bf16[520,128]{1,0:T(8,128)(2,1)S(1)} %get-tuple-element.18.refs_0_.refs_8_), channel_id=1, source_target_pairs={{8,0},{9,1},{10,2},{11,3},{12,4},{13,5},{14,6},{15,7},{0,8},{1,9},... | collective-permute-start | bytes 399368 | tf_op jit(solution)/shard_map/ppermute | solution.py:135
  11.7 6.9 %collective-permute-start.6 = (bf16[520,128]{1,0:T(8,128)(2,1)S(1)}, bf16[520,128]{1,0:T(8,128)(2,1)S(1)}, u32[]{:S(2)}, u32[]{:S(2)}) collective-permute-start(bf16[520,128]{1,0:T(8,128)(2,1)S(1)} %collective-permute-done.refs_3_), channel_id=1, source_target_pairs={{1,0},{0,1},{3,2},{2,3},{5,4},{4,5},{7,6},{6,7},{9,8},{8,9},{11,10... | collective-permute-start | bytes 399368 | tf_op jit(solution)/shard_map/ppermute | solution.py:135
  11.7 6.9 %collective-permute-start.4 = (bf16[520,128]{1,0:T(8,128)(2,1)S(1)}, bf16[520,128]{1,0:T(8,128)(2,1)S(1)}, u32[]{:S(2)}, u32[]{:S(2)}) collective-permute-start(bf16[520,128]{1,0:T(8,128)(2,1)S(1)} %collective-permute-done.2.refs_1_), channel_id=1, source_target_pairs={{1,0},{0,1},{3,2},{2,3},{5,4},{4,5},{7,6},{6,7},{9,8},{8,9},{11,10... | collective-permute-start | bytes 399368 | tf_op jit(solution)/shard_map/ppermute | solution.py:135
  12.2 6.4 %collective-permute-start.5 = (bf16[520,128]{1,0:T(8,128)(2,1)S(1)}, bf16[520,128]{1,0:T(8,128)(2,1)S(1)}, u32[]{:S(2)}, u32[]{:S(2)}) collective-permute-start(bf16[520,128]{1,0:T(8,128)(2,1)S(1)} %collective-permute-done.1.refs_2_), channel_id=1, source_target_pairs={{1,0},{0,1},{3,2},{2,3},{5,4},{4,5},{7,6},{6,7},{9,8},{8,9},{11,10... | collective-permute-start | bytes 399368 | tf_op jit(solution)/shard_map/ppermute | solution.py:135
  16.9 5.5 %collective-permute-start.11 = (bf16[520,128]{1,0:T(8,128)(2,1)S(1)}, bf16[520,128]{1,0:T(8,128)(2,1)S(1)}, u32[]{:S(2)}, u32[]{:S(2)}) collective-permute-start(bf16[520,128]{1,0:T(8,128)(2,1)S(1)} %collective-permute-done.7.refs_10_), channel_id=1, source_target_pairs={{8,0},{9,1},{10,2},{11,3},{12,4},{13,5},{14,6},{15,7},{0,8},{1,9},... | collective-permute-start | bytes 399368 | tf_op jit(solution)/shard_map/ppermute | solution.py:135
  19.4 5.4 %collective-permute-start.10 = (f32[1,128]{1,0:T(1,128)S(1)}, f32[1,128]{1,0:T(1,128)S(1)}, u32[]{:S(2)}, u32[]{:S(2)}) collective-permute-start(f32[1,128]{1,0:T(1,128)S(1)} %get-tuple-element.28), channel_id=1, source_target_pairs={{24,0},{25,1},{26,2},{27,3},{28,4},{29,5},{30,6},{31,7},{16,8},{17... | collective-permute-start | bytes 1544 | tf_op jit(solution)/shard_map/ppermute | solution.py:135
  20.6 4.2 %collective-permute-start.9 = (f32[1,128]{1,0:T(1,128)S(1)}, f32[1,128]{1,0:T(1,128)S(1)}, u32[]{:S(2)}, u32[]{:S(2)}) collective-permute-start(f32[1,128]{1,0:T(1,128)S(1)} %get-tuple-element.27), channel_id=1, source_target_pairs={{8,0},{9,1},{10,2},{11,3},{12,4},{13,5},{14,6},{15,7},{0,8},{1,9},... | collective-permute-start | bytes 1544 | tf_op jit(solution)/shard_map/ppermute | solution.py:135
  22.8 4.5 %collective-permute-start.12 = (f32[1,128]{1,0:T(1,128)S(1)}, f32[1,128]{1,0:T(1,128)S(1)}, u32[]{:S(2)}, u32[]{:S(2)}) collective-permute-start(f32[1,128]{1,0:T(1,128)S(1)} %shard_map.39), channel_id=1, source_target_pairs={{16,0},{17,1},{18,2},{19,3},{20,4},{21,5},{22,6},{23,7},{24,8},{25... | collective-permute-start | bytes 1544 | tf_op jit(solution)/shard_map/ppermute | solution.py:135

commit v29 on v26

--- a/solution.py
+++ b/solution.py
@@ -13,7 +13,7 @@
 DIGIT = 256
 
 
-def pack_kernel(groups, emb_ref, id_ref, group_ref, out_ref, table_ref):
+def pack_kernel(emb_ref, id_ref, out_ref):
     rows, width = emb_ref.shape
     values = emb_ref[...].astype(jnp.float32)
     scale = lax.rsqrt(jnp.sum(values * values, axis=-1, keepdims=True) + 1e-06)
@@ -26,23 +26,25 @@
     if LANES > rows:
         digits = jnp.concatenate([digits, jnp.zeros((AUX, LANES - rows), jnp.int32)], axis=1)
     out_ref[width // LANES * rows :, :] = digits.astype(jnp.float32).astype(jnp.bfloat16)
+
+
+def pack(embeddings, cluster_id):
+    rows, width = embeddings.shape
+    assert rows <= LANES and width % LANES == 0
+    return pl.pallas_call(
+        pack_kernel,
+        out_shape=pltpu.VMEM((width // LANES * rows + AUX, LANES), jnp.bfloat16),
+    )(embeddings, cluster_id.reshape(1, rows))
+
+
+def make_table(group_ref, groups):
     clusters = group_ref.shape[1]
     index = lax.broadcasted_iota(jnp.int32, (groups, clusters), 0)
     member = jnp.where(index == group_ref[...], 1.0, 0.0).astype(jnp.bfloat16)
     same = lax.dot_general(member, member, (((0,), (0,)), ((), ())), preferred_element_type=jnp.float32)
     one = lax.broadcasted_iota(jnp.int32, (clusters, clusters), 0)
     other = lax.broadcasted_iota(jnp.int32, (clusters, clusters), 1)
-    table_ref[...] = jnp.where(one == other, 1.0, 0.5 * same).astype(jnp.bfloat16)
-
-
-def pack(embeddings, cluster_id, cluster_group, groups):
-    rows, width = embeddings.shape
-    assert rows <= LANES and width % LANES == 0
-    clusters = cluster_group.shape[0]
-    return pl.pallas_call(
-        functools.partial(pack_kernel, groups),
-        out_shape=[pltpu.VMEM((width // LANES * rows + AUX, LANES), jnp.bfloat16), pltpu.VMEM((clusters, clusters), jnp.bfloat16)],
-    )(embeddings, cluster_id.reshape(1, rows), cluster_group.reshape(1, clusters))
+    return jnp.where(one == other, 1.0, 0.5 * same).astype(jnp.bfloat16)
 
 
 def one_hot(digits, clusters):
@@ -51,11 +53,16 @@
     return jnp.where(index == number, 1.0, 0.0).astype(jnp.bfloat16)
 
 
-def best_kernel(rows, n_keys, n_spans, own, ranks, table_ref, *refs):
+def best_kernel(rows, groups, n_keys, n_spans, own, ranks, first_ref, *refs):
     n_queries = (len(refs) - n_keys) // 2
     keys, queries, outs = refs[:n_keys], refs[n_keys : n_keys + n_queries], refs[n_keys + n_queries :]
     panels = (keys[0].shape[0] - AUX) // rows
-    clusters = table_ref.shape[0]
+    clusters = first_ref.shape[1]
+    if own:
+        table = make_table(first_ref, groups)
+        outs[n_queries][...] = table
+    else:
+        table = first_ref[...]
     clu, grp = lax.axis_index("clu"), lax.axis_index("grp")
     ranks = [rank(clu, grp) for rank in ranks]
 
@@ -66,7 +73,7 @@
         return jnp.concatenate([block[p * rows : (p + 1) * rows, :] for p in range(panels)], axis=1)
 
     mixed = [
-        jnp.dot(table_ref[...], hot(query), preferred_element_type=jnp.float32).astype(jnp.bfloat16)
+        jnp.dot(table, hot(query), preferred_element_type=jnp.float32).astype(jnp.bfloat16)
         for query in queries
     ]
 
@@ -102,21 +109,23 @@
             search(range(t * width, (t + 1) * width), False)
 
 
-def best_of(rows, keys, n_spans, queries, table, own):
+def best_of(rows, groups, keys, n_spans, queries, first, own):
     width = (keys[0][0].shape[0] - AUX) // rows * LANES
     vmem = pl.BlockSpec(memory_space=pltpu.VMEM)
     ranks = [r for _, r in keys + queries]
     pairs = len(keys) * len(queries) * rows * rows
+    clusters = first.shape[1]
+    made = [jax.ShapeDtypeStruct((clusters, clusters), jnp.bfloat16)] if own else []
     return pl.pallas_call(
-        functools.partial(best_kernel, rows, len(keys), n_spans, own, ranks),
-        out_shape=[jax.ShapeDtypeStruct((1, rows), jnp.float32)] * len(queries),
+        functools.partial(best_kernel, rows, groups, len(keys), n_spans, own, ranks),
+        out_shape=[jax.ShapeDtypeStruct((1, rows), jnp.float32)] * len(queries) + made,
         in_specs=[vmem] * (1 + len(keys) + len(queries)),
-        out_specs=[vmem] * len(queries),
+        out_specs=[vmem] * (len(queries) + len(made)),
         compiler_params=pltpu.CompilerParams(vmem_limit_bytes=40 * 2**20),
         cost_estimate=pl.CostEstimate(
             flops=2 * pairs * width, bytes_accessed=2 * (len(keys) + len(queries)) * rows * width, transcendentals=0
         ),
-    )(table, *[b for b, _ in keys + queries])
+    )(first, *[b for b, _ in keys + queries])
 
 
 def solution(mesh):
@@ -139,7 +148,7 @@
 
     def shards(embeddings, cluster_id, cluster_group):
         rows = embeddings.shape[0]
-        own, table = pack(embeddings, cluster_id, cluster_group, n_clu)
+        own = pack(embeddings, cluster_id)
 
         def rank(z=0, a=0, g=0):
             def of(clu, grp):
@@ -174,9 +183,9 @@
         visit_rank = [rank(z=s) for s in offsets]
         first = list(zip(first, visit_rank))
         last = list(zip(last, visit_rank[len(first) :]))
-        best = best_of(rows, near + far, n_grp, near[:1] + first, table, True)
+        *best, table = best_of(rows, n_clu, near + far, n_grp, near[:1] + first, cluster_group.reshape(1, -1), True)
         if last:
-            best = best + best_of(rows, near + far, n_grp, last, table, False)
+            best += best_of(rows, n_clu, near + far, n_grp, last, table, False)
         found = [best[0]] + [along(b, -s) for b, s in zip(best[1:], offsets)]
         return functools.reduce(jnp.maximum, found).reshape(rows)
 

time: 26 us -> 29 us (1.12)
  waiting for transfers between devices: 8.36 us -> 11 us
  starting transfers between devices: 14.5 us -> 14.8 us
    ppermute x13, waiting for transfers between devices: 8.36 us -> 11 us  [permute(): return lax.ppermute(x, ('clu', 'grp'), pairs)]
  transfers between devices with their start and end apart: 13 -> 13, of which waited for: 7 -> 8; matrix products, arithmetic and copies ran while one was open for 0% -> 0% of each run, Pallas kernels for 5% -> 3%
where the time goes in v29:
time: 29 us; the launch traced here: 28.9 us
  starting transfers between devices  14.8 us (51%)
  waiting for transfers between devices  11 us (38%)
  Pallas kernels  2.44 us (8%)
  other arithmetic  0.52 us (2%)
    ppermute x13, starting transfers between devices, permute(): return lax.ppermute(x, ('clu', 'grp'), pairs)  14.8 us
    ppermute x13, waiting for transfers between devices, permute(): return lax.ppermute(x, ('clu', 'grp'), pairs)  11 us
    pallas_call x2, Pallas kernels, best_of(): pl.pallas_call(functools.partial(best_kernel, rows, groups, len(keys), n_...  1.42 us
    pallas_call x1, Pallas kernels, pack(): pl.pallas_call(pack_kernel, out_shape=pltpu.VMEM((width // LANES * rows +...  1.02 us
  transfers between devices with their start and end apart: 13, of which 8 were waited for; matrix products, arithmetic and copies ran while one was open for 0% of the time, Pallas kernels for 3%

profile of v29, /device:TPU:0, one launch (start us, length us, event | category | flops | bytes accessed | tf_op | source)
XLA Modules:
  0.0 28.9 jit_solution(9254120145072859999)
XLA Ops:
  0.0 1.0 %shard_map.37.refs_0_.refs_8_ = bf16[520,128]{1,0:T(8,128)(2,1)S(1)} custom-call(bf16[128,512]{1,0:T(8,128)(2,1)} %emb_ref.1, s32[1,128]{1,0:T(1,128)} %bitcast.5), custom_call_target="tpu_custom_call" | custom-call | tf_op jit(solution)/shard_map/pallas_call | solution.py:34
  1.0 0.0 copy-start
  1.0 4.0 %collective-permute-start = (bf16[520,128]{1,0:T(8,128)(2,1)S(1)}, bf16[520,128]{1,0:T(8,128)(2,1)S(1)}, u32[]{:S(2)}, u32[]{:S(2)}) collective-permute-start(bf16[520,128]{1,0:T(8,128)(2,1)S(1)} %shard_map.37.refs_0_.refs_8_), channel_id=1, source_target_pairs={{6,0},{7,1},{4,2},{5,3},{2,4},{3,5},{0,6},{1,7},{14,8},{15,9},{12,... | collective-permute-start | bytes 399368 | tf_op jit(solution)/shard_map/ppermute | solution.py:144
  5.0 0.5 %collective-permute-start.1 = (bf16[520,128]{1,0:T(8,128)(2,1)S(1)}, bf16[520,128]{1,0:T(8,128)(2,1)S(1)}, u32[]{:S(2)}, u32[]{:S(2)}) collective-permute-start(bf16[520,128]{1,0:T(8,128)(2,1)S(1)} %shard_map.37.refs_0_.refs_8_), channel_id=1, source_target_pairs={{4,0},{5,1},{6,2},{7,3},{0,4},{1,5},{2,6},{3,7},{12,8},{13,9},{14,... | collective-permute-start | bytes 399368 | tf_op jit(solution)/shard_map/ppermute | solution.py:144
  5.5 0.1 collective-permute-start.2
  5.6 4.0 %collective-permute-start.7 = (bf16[520,128]{1,0:T(8,128)(2,1)S(1)}, bf16[520,128]{1,0:T(8,128)(2,1)S(1)}, u32[]{:S(2)}, u32[]{:S(2)}) collective-permute-start(bf16[520,128]{1,0:T(8,128)(2,1)S(1)} %shard_map.37.refs_0_.refs_8_), channel_id=1, source_target_pairs={{24,0},{25,1},{26,2},{27,3},{28,4},{29,5},{30,6},{31,7},{16,8},{17... | collective-permute-start | bytes 399368 | tf_op jit(solution)/shard_map/ppermute | solution.py:144
  9.6 0.0 collective-permute-start.8
  9.6 0.0 collective-permute-done.refs_3_
  9.6 0.0 collective-permute-start.3
  9.7 1.7 %collective-permute-done.1.refs_2_ = bf16[520,128]{1,0:T(8,128)(2,1)S(1)} collective-permute-done((bf16[520,128]{1,0:T(8,128)(2,1)S(1)}, bf16[520,128]{1,0:T(8,128)(2,1)S(1)}, u32[]{:S(2)}, u32[]{:S(2)}) %collective-permute-start.1) | collective-permute-done | bytes 133152 | tf_op jit(solution)/shard_map/ppermute | solution.py:144
  11.4 0.2 collective-permute-done.2.refs_1_
  11.6 0.0 collective-permute-start.4
  11.6 0.5 %collective-permute-start.5 = (bf16[520,128]{1,0:T(8,128)(2,1)S(1)}, bf16[520,128]{1,0:T(8,128)(2,1)S(1)}, u32[]{:S(2)}, u32[]{:S(2)}) collective-permute-start(bf16[520,128]{1,0:T(8,128)(2,1)S(1)} %collective-permute-done.1.refs_2_), channel_id=1, source_target_pairs={{1,0},{0,1},{3,2},{2,3},{5,4},{4,5},{7,6},{6,7},{9,8},{8,9},{11,10... | collective-permute-start | bytes 399368 | tf_op jit(solution)/shard_map/ppermute | solution.py:144
  12.2 1.7 %collective-permute-done.7.refs_10_ = bf16[520,128]{1,0:T(8,128)(2,1)S(1)} collective-permute-done((bf16[520,128]{1,0:T(8,128)(2,1)S(1)}, bf16[520,128]{1,0:T(8,128)(2,1)S(1)}, u32[]{:S(2)}, u32[]{:S(2)}) %collective-permute-start.7) | collective-permute-done | bytes 133152 | tf_op jit(solution)/shard_map/ppermute | solution.py:144
  13.8 0.0 collective-permute-start.6
  13.8 1.4 %collective-permute-done.8.refs_9_ = bf16[520,128]{1,0:T(8,128)(2,1)S(1)} collective-permute-done((bf16[520,128]{1,0:T(8,128)(2,1)S(1)}, bf16[520,128]{1,0:T(8,128)(2,1)S(1)}, u32[]{:S(2)}, u32[]{:S(2)}) %collective-permute-start.8) | collective-permute-done | bytes 133152 | tf_op jit(solution)/shard_map/ppermute | solution.py:144
  15.3 1.6 %collective-permute-start.11 = (bf16[520,128]{1,0:T(8,128)(2,1)S(1)}, bf16[520,128]{1,0:T(8,128)(2,1)S(1)}, u32[]{:S(2)}, u32[]{:S(2)}) collective-permute-start(bf16[520,128]{1,0:T(8,128)(2,1)S(1)} %collective-permute-done.7.refs_10_), channel_id=1, source_target_pairs={{8,0},{9,1},{10,2},{11,3},{12,4},{13,5},{14,6},{15,7},{0,8},{1,9},... | collective-permute-start | bytes 399368 | tf_op jit(solution)/shard_map/ppermute | solution.py:144
  16.9 0.0 collective-permute-done.3.refs_4_
  16.9 0.0 collective-permute-done.4.refs_5_
  16.9 0.0 collective-permute-done.5.refs_6_
  16.9 0.0 collective-permute-done.6.refs_7_
  17.0 0.0 copy-done
  17.0 1.0 %shard_map.38 = (f32[1,128]{1,0:T(1,128)S(1)}, f32[1,128]{1,0:T(1,128)S(1)}, f32[1,128]{1,0:T(1,128)S(1)}, bf16[64,64]{1,0:T(8,128)(2,1)S(1)}) custom-call(s32[1,64]{1,0:T(1,128)S(1)} %bitcast.4, bf16[520,128]{1,0:T(8,128)(2,1)S(1)} %shard_map.37.refs_0_.refs_8_, bf16[520,128]{1,0:T(8,128)(2,1)S(1)} %collective-permute-done.2.refs_1_, ...), custom_call_target="tpu_custom_call" | custom-call | flops 402653184 | bytes 1441792 | tf_op jit(solution)/shard_map/pallas_call | solution.py:119
  17.9 2.3 %collective-permute-done.11.refs_8_ = bf16[520,128]{1,0:T(8,128)(2,1)S(1)} collective-permute-done((bf16[520,128]{1,0:T(8,128)(2,1)S(1)}, bf16[520,128]{1,0:T(8,128)(2,1)S(1)}, u32[]{:S(2)}, u32[]{:S(2)}) %collective-permute-start.11) | collective-permute-done | bytes 133152 | tf_op jit(solution)/shard_map/ppermute | solution.py:144
  20.3 0.5 %shard_map.39 = f32[1,128]{1,0:T(1,128)S(1)} custom-call(bf16[64,64]{1,0:T(8,128)(2,1)S(1)} %get-tuple-element.22.first_ref, bf16[520,128]{1,0:T(8,128)(2,1)S(1)} %shard_map.37.refs_0_.refs_8_, bf16[520,128]{1,0:T(8,128)(2,1)S(1)} %collective-permute-done.2.refs_1_, bf16[520,128]{1,0:T(8,128)(2,1)S(1)} %collective-permute-done.1.refs_2_, ...), custom_call_target="tpu_custom_call" | custom-call | flops 134217728 | bytes 1179648 | tf_op jit(solution)/shard_map/pallas_call | solution.py:119
  20.7 1.9 %collective-permute-start.12 = (f32[1,128]{1,0:T(1,128)S(1)}, f32[1,128]{1,0:T(1,128)S(1)}, u32[]{:S(2)}, u32[]{:S(2)}) collective-permute-start(f32[1,128]{1,0:T(1,128)S(1)} %shard_map.39), channel_id=1, source_target_pairs={{16,0},{17,1},{18,2},{19,3},{20,4},{21,5},{22,6},{23,7},{24,8},{25... | collective-permute-start | bytes 1544 | tf_op jit(solution)/shard_map/ppermute | solution.py:144
  22.6 2.2 %collective-permute-start.10 = (f32[1,128]{1,0:T(1,128)S(1)}, f32[1,128]{1,0:T(1,128)S(1)}, u32[]{:S(2)}, u32[]{:S(2)}) collective-permute-start(f32[1,128]{1,0:T(1,128)S(1)} %get-tuple-element.21), channel_id=1, source_target_pairs={{24,0},{25,1},{26,2},{27,3},{28,4},{29,5},{30,6},{31,7},{16,8},{17... | collective-permute-start | bytes 1544 | tf_op jit(solution)/shard_map/ppermute | solution.py:144
  24.8 0.0 collective-permute-start.9
  24.8 0.4 %collective-permute-done.12 = f32[1,128]{1,0:T(1,128)S(1)} collective-permute-done((f32[1,128]{1,0:T(1,128)S(1)}, f32[1,128]{1,0:T(1,128)S(1)}, u32[]{:S(2)}, u32[]{:S(2)}) %collective-permute-start.12) | collective-permute-done | bytes 544 | tf_op jit(solution)/shard_map/ppermute | solution.py:144
  25.2 2.7 %collective-permute-done.10 = f32[1,128]{1,0:T(1,128)S(1)} collective-permute-done((f32[1,128]{1,0:T(1,128)S(1)}, f32[1,128]{1,0:T(1,128)S(1)}, u32[]{:S(2)}, u32[]{:S(2)}) %collective-permute-start.10) | collective-permute-done | bytes 544 | tf_op jit(solution)/shard_map/ppermute | solution.py:144
  28.0 0.4 %collective-permute-done.9 = f32[1,128]{1,0:T(1,128)S(1)} collective-permute-done((f32[1,128]{1,0:T(1,128)S(1)}, f32[1,128]{1,0:T(1,128)S(1)}, u32[]{:S(2)}, u32[]{:S(2)}) %collective-permute-start.9) | collective-permute-done | bytes 544 | tf_op jit(solution)/shard_map/ppermute | solution.py:144
  28.4 0.5 %maximum_bitcast_fusion = f32[128]{0:T(128)} fusion(f32[1,128]{1,0:T(1,128)S(1)} %collective-permute-done.12, f32[1,128]{1,0:T(1,128)S(1)} %collective-permute-done.10, f32[1,128]{1,0:T(1,128)S(1)} %get-tuple-element.19, f32[1,128]{1,0:T(1,128)S(1)} %collective-permute-done.9), kind=kLoop, calls=%fused_computation | loop fusion | flops 384 | bytes 2560 | tf_op jit(solution)/shard_map/reshape | solution.py:190
Async XLA Ops:
  1.0 15.9 %copy-start = (s32[64]{0:T(128)S(1)}, s32[64]{0:T(128)}, u32[]{:S(2)}) copy-start(s32[64]{0:T(128)} %param.5) | copy-start | bytes 772
  1.0 8.6 %collective-permute-start = (bf16[520,128]{1,0:T(8,128)(2,1)S(1)}, bf16[520,128]{1,0:T(8,128)(2,1)S(1)}, u32[]{:S(2)}, u32[]{:S(2)}) collective-permute-start(bf16[520,128]{1,0:T(8,128)(2,1)S(1)} %shard_map.37.refs_0_.refs_8_), channel_id=1, source_target_pairs={{6,0},{7,1},{4,2},{5,3},{2,4},{3,5},{0,6},{1,7},{14,8},{15,9},{12,... | collective-permute-start | bytes 399368 | tf_op jit(solution)/shard_map/ppermute | solution.py:144
  5.0 6.4 %collective-permute-start.1 = (bf16[520,128]{1,0:T(8,128)(2,1)S(1)}, bf16[520,128]{1,0:T(8,128)(2,1)S(1)}, u32[]{:S(2)}, u32[]{:S(2)}) collective-permute-start(bf16[520,128]{1,0:T(8,128)(2,1)S(1)} %shard_map.37.refs_0_.refs_8_), channel_id=1, source_target_pairs={{4,0},{5,1},{6,2},{7,3},{0,4},{1,5},{2,6},{3,7},{12,8},{13,9},{14,... | collective-permute-start | bytes 399368 | tf_op jit(solution)/shard_map/ppermute | solution.py:144
  5.5 6.1 %collective-permute-start.2 = (bf16[520,128]{1,0:T(8,128)(2,1)S(1)}, bf16[520,128]{1,0:T(8,128)(2,1)S(1)}, u32[]{:S(2)}, u32[]{:S(2)}) collective-permute-start(bf16[520,128]{1,0:T(8,128)(2,1)S(1)} %shard_map.37.refs_0_.refs_8_), channel_id=1, source_target_pairs={{2,0},{3,1},{0,2},{1,3},{6,4},{7,5},{4,6},{5,7},{10,8},{11,9},{8,1... | collective-permute-start | bytes 399368 | tf_op jit(solution)/shard_map/ppermute | solution.py:144
  5.6 8.2 %collective-permute-start.7 = (bf16[520,128]{1,0:T(8,128)(2,1)S(1)}, bf16[520,128]{1,0:T(8,128)(2,1)S(1)}, u32[]{:S(2)}, u32[]{:S(2)}) collective-permute-start(bf16[520,128]{1,0:T(8,128)(2,1)S(1)} %shard_map.37.refs_0_.refs_8_), channel_id=1, source_target_pairs={{24,0},{25,1},{26,2},{27,3},{28,4},{29,5},{30,6},{31,7},{16,8},{17... | collective-permute-start | bytes 399368 | tf_op jit(solution)/shard_map/ppermute | solution.py:144
  9.6 5.7 %collective-permute-start.8 = (bf16[520,128]{1,0:T(8,128)(2,1)S(1)}, bf16[520,128]{1,0:T(8,128)(2,1)S(1)}, u32[]{:S(2)}, u32[]{:S(2)}) collective-permute-start(bf16[520,128]{1,0:T(8,128)(2,1)S(1)} %shard_map.37.refs_0_.refs_8_), channel_id=1, source_target_pairs={{8,0},{9,1},{10,2},{11,3},{12,4},{13,5},{14,6},{15,7},{0,8},{1,9},... | collective-permute-start | bytes 399368 | tf_op jit(solution)/shard_map/ppermute | solution.py:144
  9.6 7.3 %collective-permute-start.3 = (bf16[520,128]{1,0:T(8,128)(2,1)S(1)}, bf16[520,128]{1,0:T(8,128)(2,1)S(1)}, u32[]{:S(2)}, u32[]{:S(2)}) collective-permute-start(bf16[520,128]{1,0:T(8,128)(2,1)S(1)} %shard_map.37.refs_0_.refs_8_), channel_id=1, source_target_pairs={{1,0},{0,1},{3,2},{2,3},{5,4},{4,5},{7,6},{6,7},{9,8},{8,9},{11,10... | collective-permute-start | bytes 399368 | tf_op jit(solution)/shard_map/ppermute | solution.py:144
  11.6 5.3 %collective-permute-start.4 = (bf16[520,128]{1,0:T(8,128)(2,1)S(1)}, bf16[520,128]{1,0:T(8,128)(2,1)S(1)}, u32[]{:S(2)}, u32[]{:S(2)}) collective-permute-start(bf16[520,128]{1,0:T(8,128)(2,1)S(1)} %collective-permute-done.2.refs_1_), channel_id=1, source_target_pairs={{1,0},{0,1},{3,2},{2,3},{5,4},{4,5},{7,6},{6,7},{9,8},{8,9},{11,10... | collective-permute-start | bytes 399368 | tf_op jit(solution)/shard_map/ppermute | solution.py:144
  11.6 5.3 %collective-permute-start.5 = (bf16[520,128]{1,0:T(8,128)(2,1)S(1)}, bf16[520,128]{1,0:T(8,128)(2,1)S(1)}, u32[]{:S(2)}, u32[]{:S(2)}) collective-permute-start(bf16[520,128]{1,0:T(8,128)(2,1)S(1)} %collective-permute-done.1.refs_2_), channel_id=1, source_target_pairs={{1,0},{0,1},{3,2},{2,3},{5,4},{4,5},{7,6},{6,7},{9,8},{8,9},{11,10... | collective-permute-start | bytes 399368 | tf_op jit(solution)/shard_map/ppermute | solution.py:144
  13.8 3.1 %collective-permute-start.6 = (bf16[520,128]{1,0:T(8,128)(2,1)S(1)}, bf16[520,128]{1,0:T(8,128)(2,1)S(1)}, u32[]{:S(2)}, u32[]{:S(2)}) collective-permute-start(bf16[520,128]{1,0:T(8,128)(2,1)S(1)} %collective-permute-done.refs_3_), channel_id=1, source_target_pairs={{1,0},{0,1},{3,2},{2,3},{5,4},{4,5},{7,6},{6,7},{9,8},{8,9},{11,10... | collective-permute-start | bytes 399368 | tf_op jit(solution)/shard_map/ppermute | solution.py:144
  15.3 5.0 %collective-permute-start.11 = (bf16[520,128]{1,0:T(8,128)(2,1)S(1)}, bf16[520,128]{1,0:T(8,128)(2,1)S(1)}, u32[]{:S(2)}, u32[]{:S(2)}) collective-permute-start(bf16[520,128]{1,0:T(8,128)(2,1)S(1)} %collective-permute-done.7.refs_10_), channel_id=1, source_target_pairs={{8,0},{9,1},{10,2},{11,3},{12,4},{13,5},{14,6},{15,7},{0,8},{1,9},... | collective-permute-start | bytes 399368 | tf_op jit(solution)/shard_map/ppermute | solution.py:144
  20.7 4.5 %collective-permute-start.12 = (f32[1,128]{1,0:T(1,128)S(1)}, f32[1,128]{1,0:T(1,128)S(1)}, u32[]{:S(2)}, u32[]{:S(2)}) collective-permute-start(f32[1,128]{1,0:T(1,128)S(1)} %shard_map.39), channel_id=1, source_target_pairs={{16,0},{17,1},{18,2},{19,3},{20,4},{21,5},{22,6},{23,7},{24,8},{25... | collective-permute-start | bytes 1544 | tf_op jit(solution)/shard_map/ppermute | solution.py:144
  22.6 5.3 %collective-permute-start.10 = (f32[1,128]{1,0:T(1,128)S(1)}, f32[1,128]{1,0:T(1,128)S(1)}, u32[]{:S(2)}, u32[]{:S(2)}) collective-permute-start(f32[1,128]{1,0:T(1,128)S(1)} %get-tuple-element.21), channel_id=1, source_target_pairs={{24,0},{25,1},{26,2},{27,3},{28,4},{29,5},{30,6},{31,7},{16,8},{17... | collective-permute-start | bytes 1544 | tf_op jit(solution)/shard_map/ppermute | solution.py:144
  24.8 3.5 %collective-permute-start.9 = (f32[1,128]{1,0:T(1,128)S(1)}, f32[1,128]{1,0:T(1,128)S(1)}, u32[]{:S(2)}, u32[]{:S(2)}) collective-permute-start(f32[1,128]{1,0:T(1,128)S(1)} %get-tuple-element.20), channel_id=1, source_target_pairs={{8,0},{9,1},{10,2},{11,3},{12,4},{13,5},{14,6},{15,7},{0,8},{1,9},... | collective-permute-start | bytes 1544 | tf_op jit(solution)/shard_map/ppermute | solution.py:144

commit v30 on v26

--- a/solution.py
+++ b/solution.py
@@ -152,12 +152,11 @@
             return permute(x, lambda z, a, g: (turned(z, s, length), a, g))
 
         half = length // 2 if length & (length - 1) == 0 else length
-        near = [permute(own, lambda z, a, g: (z, turned(a, s, wide), g)) for s in reversed(range(1, wide))]
+        near = [permute(own, lambda z, a, g: (z, turned(a, s, wide), g)) for s in range(1, wide)]
         middle = along(own, length - 1) if half < length else None
         first = [along(own, s) for s in range(1, half)]
         near = lax.optimization_barrier(near)
         middle, first = lax.optimization_barrier((middle, first))
-        near = near[::-1]
         last = [along(middle, s) for s in range(1, half)] if half < length else []
         offsets = list(range(1, half))
         if half < length:

time: 26 us -> 26 us (level)
  transfers between devices with their start and end apart: 13 -> 13, of which waited for: 7 -> 6; matrix products, arithmetic and copies ran while one was open for 0% -> 0% of each run, Pallas kernels for 5% -> 5%
where the time goes in v30:
time: 26 us; the launch traced here: 25.8 us
  starting transfers between devices  14.6 us (56%)
  waiting for transfers between devices  8.35 us (32%)
  Pallas kernels  2.38 us (9%)
  other arithmetic  0.52 us (2%)
    ppermute x13, starting transfers between devices, permute(): return lax.ppermute(x, ('clu', 'grp'), pairs)  14.6 us
    ppermute x13, waiting for transfers between devices, permute(): return lax.ppermute(x, ('clu', 'grp'), pairs)  8.35 us
    pallas_call x2, Pallas kernels, best_of(): pl.pallas_call(functools.partial(best_kernel, rows, len(keys), n_spans, o...  1.27 us
    pallas_call x1, Pallas kernels, pack(): pl.pallas_call(functools.partial(pack_kernel, groups), out_shape=[pltpu.V...  1.1 us
  transfers between devices with their start and end apart: 13, of which 6 were waited for; matrix products, arithmetic and copies ran while one was open for 0% of the time, Pallas kernels for 5%

profile of v30, /device:TPU:0, one launch (start us, length us, event | category | flops | bytes accessed | tf_op | source)
XLA Modules:
  0.0 25.8 jit_solution(4734322141719390648)
XLA Ops:
  0.0 1.1 %shard_map.37 = (bf16[520,128]{1,0:T(8,128)(2,1)S(1)}, bf16[64,64]{1,0:T(8,128)(2,1)S(1)}) custom-call(bf16[128,512]{1,0:T(8,128)(2,1)} %emb_ref.1, s32[1,128]{1,0:T(1,128)} %bitcast.4, s32[1,64]{1,0:T(1,128)} %bitcast.5), custom_call_target="tpu_custom_call" | custom-call | tf_op jit(solution)/shard_map/pallas_call | solution.py:42
  1.1 3.0 %collective-permute-start = (bf16[520,128]{1,0:T(8,128)(2,1)S(1)}, bf16[520,128]{1,0:T(8,128)(2,1)S(1)}, u32[]{:S(2)}, u32[]{:S(2)}) collective-permute-start(bf16[520,128]{1,0:T(8,128)(2,1)S(1)} %get-tuple-element.16.refs_0_.refs_8_), channel_id=1, source_target_pairs={{2,0},{3,1},{0,2},{1,3},{6,4},{7,5},{4,6},{5,7},{10,8},{11,9},{8,1... | collective-permute-start | bytes 399368 | tf_op jit(solution)/shard_map/ppermute | solution.py:135
  4.1 1.5 %collective-permute-start.1 = (bf16[520,128]{1,0:T(8,128)(2,1)S(1)}, bf16[520,128]{1,0:T(8,128)(2,1)S(1)}, u32[]{:S(2)}, u32[]{:S(2)}) collective-permute-start(bf16[520,128]{1,0:T(8,128)(2,1)S(1)} %get-tuple-element.16.refs_0_.refs_8_), channel_id=1, source_target_pairs={{4,0},{5,1},{6,2},{7,3},{0,4},{1,5},{2,6},{3,7},{12,8},{13,9},{14,... | collective-permute-start | bytes 399368 | tf_op jit(solution)/shard_map/ppermute | solution.py:135
  5.6 0.0 collective-permute-start.2
  5.7 4.1 %collective-permute-start.7 = (bf16[520,128]{1,0:T(8,128)(2,1)S(1)}, bf16[520,128]{1,0:T(8,128)(2,1)S(1)}, u32[]{:S(2)}, u32[]{:S(2)}) collective-permute-start(bf16[520,128]{1,0:T(8,128)(2,1)S(1)} %get-tuple-element.16.refs_0_.refs_8_), channel_id=1, source_target_pairs={{24,0},{25,1},{26,2},{27,3},{28,4},{29,5},{30,6},{31,7},{16,8},{17... | collective-permute-start | bytes 399368 | tf_op jit(solution)/shard_map/ppermute | solution.py:135
  9.7 0.0 collective-permute-start.8
  9.7 0.0 collective-permute-done.refs_1_
  9.7 0.0 collective-permute-start.3
  9.7 2.2 %collective-permute-done.1.refs_2_ = bf16[520,128]{1,0:T(8,128)(2,1)S(1)} collective-permute-done((bf16[520,128]{1,0:T(8,128)(2,1)S(1)}, bf16[520,128]{1,0:T(8,128)(2,1)S(1)}, u32[]{:S(2)}, u32[]{:S(2)}) %collective-permute-start.1) | collective-permute-done | bytes 133152 | tf_op jit(solution)/shard_map/ppermute | solution.py:135
  12.0 0.0 collective-permute-done.2.refs_3_
  12.0 0.0 collective-permute-start.4
  12.0 0.5 %collective-permute-start.5 = (bf16[520,128]{1,0:T(8,128)(2,1)S(1)}, bf16[520,128]{1,0:T(8,128)(2,1)S(1)}, u32[]{:S(2)}, u32[]{:S(2)}) collective-permute-start(bf16[520,128]{1,0:T(8,128)(2,1)S(1)} %collective-permute-done.1.refs_2_), channel_id=1, source_target_pairs={{1,0},{0,1},{3,2},{2,3},{5,4},{4,5},{7,6},{6,7},{9,8},{8,9},{11,10... | collective-permute-start | bytes 399368 | tf_op jit(solution)/shard_map/ppermute | solution.py:135
  12.5 1.4 %collective-permute-done.7.refs_10_ = bf16[520,128]{1,0:T(8,128)(2,1)S(1)} collective-permute-done((bf16[520,128]{1,0:T(8,128)(2,1)S(1)}, bf16[520,128]{1,0:T(8,128)(2,1)S(1)}, u32[]{:S(2)}, u32[]{:S(2)}) %collective-permute-start.7) | collective-permute-done | bytes 133152 | tf_op jit(solution)/shard_map/ppermute | solution.py:135
  13.9 0.0 collective-permute-start.6
  13.9 1.4 %collective-permute-done.8.refs_9_ = bf16[520,128]{1,0:T(8,128)(2,1)S(1)} collective-permute-done((bf16[520,128]{1,0:T(8,128)(2,1)S(1)}, bf16[520,128]{1,0:T(8,128)(2,1)S(1)}, u32[]{:S(2)}, u32[]{:S(2)}) %collective-permute-start.8) | collective-permute-done | bytes 133152 | tf_op jit(solution)/shard_map/ppermute | solution.py:135
  15.4 1.6 %collective-permute-start.11 = (bf16[520,128]{1,0:T(8,128)(2,1)S(1)}, bf16[520,128]{1,0:T(8,128)(2,1)S(1)}, u32[]{:S(2)}, u32[]{:S(2)}) collective-permute-start(bf16[520,128]{1,0:T(8,128)(2,1)S(1)} %collective-permute-done.7.refs_10_), channel_id=1, source_target_pairs={{8,0},{9,1},{10,2},{11,3},{12,4},{13,5},{14,6},{15,7},{0,8},{1,9},... | collective-permute-start | bytes 399368 | tf_op jit(solution)/shard_map/ppermute | solution.py:135
  17.0 0.0 collective-permute-done.3.refs_4_
  17.0 0.0 collective-permute-done.4.refs_5_
  17.0 0.0 collective-permute-done.5.refs_6_
  17.0 0.0 collective-permute-done.6.refs_7_
  17.0 0.8 %shard_map.38 = (f32[1,128]{1,0:T(1,128)S(1)}, f32[1,128]{1,0:T(1,128)S(1)}, f32[1,128]{1,0:T(1,128)S(1)}) custom-call(bf16[64,64]{1,0:T(8,128)(2,1)S(1)} %get-tuple-element.15.table_ref, bf16[520,128]{1,0:T(8,128)(2,1)S(1)} %get-tuple-element.16.refs_0_.refs_8_, bf16[520,128]{1,0:T(8,128)(2,1)S(1)} %collective-permute-done.refs_1_, ...), custom_call_target="tpu_custom_call" | custom-call | flops 402653184 | bytes 1441792 | tf_op jit(solution)/shard_map/pallas_call | solution.py:110
  17.8 1.8 %collective-permute-start.10 = (f32[1,128]{1,0:T(1,128)S(1)}, f32[1,128]{1,0:T(1,128)S(1)}, u32[]{:S(2)}, u32[]{:S(2)}) collective-permute-start(f32[1,128]{1,0:T(1,128)S(1)} %get-tuple-element.24), channel_id=1, source_target_pairs={{24,0},{25,1},{26,2},{27,3},{28,4},{29,5},{30,6},{31,7},{16,8},{17... | collective-permute-start | bytes 1544 | tf_op jit(solution)/shard_map/ppermute | solution.py:135
  19.6 0.0 collective-permute-start.9
  19.6 0.7 %collective-permute-done.11.refs_8_ = bf16[520,128]{1,0:T(8,128)(2,1)S(1)} collective-permute-done((bf16[520,128]{1,0:T(8,128)(2,1)S(1)}, bf16[520,128]{1,0:T(8,128)(2,1)S(1)}, u32[]{:S(2)}, u32[]{:S(2)}) %collective-permute-start.11) | collective-permute-done | bytes 133152 | tf_op jit(solution)/shard_map/ppermute | solution.py:135
  20.4 0.5 %shard_map.39 = f32[1,128]{1,0:T(1,128)S(1)} custom-call(bf16[64,64]{1,0:T(8,128)(2,1)S(1)} %get-tuple-element.15.table_ref, bf16[520,128]{1,0:T(8,128)(2,1)S(1)} %get-tuple-element.16.refs_0_.refs_8_, bf16[520,128]{1,0:T(8,128)(2,1)S(1)} %collective-permute-done.refs_1_, bf16[520,128]{1,0:T(8,128)(2,1)S(1)} %collective-permute-done.1.refs_2_, ...), custom_call_target="tpu_custom_call" | custom-call | flops 134217728 | bytes 1179648 | tf_op jit(solution)/shard_map/pallas_call | solution.py:110
  20.8 2.0 %collective-permute-start.12 = (f32[1,128]{1,0:T(1,128)S(1)}, f32[1,128]{1,0:T(1,128)S(1)}, u32[]{:S(2)}, u32[]{:S(2)}) collective-permute-start(f32[1,128]{1,0:T(1,128)S(1)} %shard_map.39), channel_id=1, source_target_pairs={{16,0},{17,1},{18,2},{19,3},{20,4},{21,5},{22,6},{23,7},{24,8},{25... | collective-permute-start | bytes 1544 | tf_op jit(solution)/shard_map/ppermute | solution.py:135
  22.8 0.4 %collective-permute-done.10 = f32[1,128]{1,0:T(1,128)S(1)} collective-permute-done((f32[1,128]{1,0:T(1,128)S(1)}, f32[1,128]{1,0:T(1,128)S(1)}, u32[]{:S(2)}, u32[]{:S(2)}) %collective-permute-start.10) | collective-permute-done | bytes 544 | tf_op jit(solution)/shard_map/ppermute | solution.py:135
  23.3 0.0 collective-permute-done.9
  23.3 2.1 %collective-permute-done.12 = f32[1,128]{1,0:T(1,128)S(1)} collective-permute-done((f32[1,128]{1,0:T(1,128)S(1)}, f32[1,128]{1,0:T(1,128)S(1)}, u32[]{:S(2)}, u32[]{:S(2)}) %collective-permute-start.12) | collective-permute-done | bytes 544 | tf_op jit(solution)/shard_map/ppermute | solution.py:135
  25.3 0.5 %maximum_bitcast_fusion = f32[128]{0:T(128)} fusion(f32[1,128]{1,0:T(1,128)S(1)} %collective-permute-done.12, f32[1,128]{1,0:T(1,128)S(1)} %collective-permute-done.10, f32[1,128]{1,0:T(1,128)S(1)} %get-tuple-element.22, f32[1,128]{1,0:T(1,128)S(1)} %collective-permute-done.9), kind=kLoop, calls=%fused_computation | loop fusion | flops 384 | bytes 2560 | tf_op jit(solution)/shard_map/reshape | solution.py:180
Async XLA Ops:
  1.1 8.6 %collective-permute-start = (bf16[520,128]{1,0:T(8,128)(2,1)S(1)}, bf16[520,128]{1,0:T(8,128)(2,1)S(1)}, u32[]{:S(2)}, u32[]{:S(2)}) collective-permute-start(bf16[520,128]{1,0:T(8,128)(2,1)S(1)} %get-tuple-element.16.refs_0_.refs_8_), channel_id=1, source_target_pairs={{2,0},{3,1},{0,2},{1,3},{6,4},{7,5},{4,6},{5,7},{10,8},{11,9},{8,1... | collective-permute-start | bytes 399368 | tf_op jit(solution)/shard_map/ppermute | solution.py:135
  4.1 7.9 %collective-permute-start.1 = (bf16[520,128]{1,0:T(8,128)(2,1)S(1)}, bf16[520,128]{1,0:T(8,128)(2,1)S(1)}, u32[]{:S(2)}, u32[]{:S(2)}) collective-permute-start(bf16[520,128]{1,0:T(8,128)(2,1)S(1)} %get-tuple-element.16.refs_0_.refs_8_), channel_id=1, source_target_pairs={{4,0},{5,1},{6,2},{7,3},{0,4},{1,5},{2,6},{3,7},{12,8},{13,9},{14,... | collective-permute-start | bytes 399368 | tf_op jit(solution)/shard_map/ppermute | solution.py:135
  5.6 6.3 %collective-permute-start.2 = (bf16[520,128]{1,0:T(8,128)(2,1)S(1)}, bf16[520,128]{1,0:T(8,128)(2,1)S(1)}, u32[]{:S(2)}, u32[]{:S(2)}) collective-permute-start(bf16[520,128]{1,0:T(8,128)(2,1)S(1)} %get-tuple-element.16.refs_0_.refs_8_), channel_id=1, source_target_pairs={{6,0},{7,1},{4,2},{5,3},{2,4},{3,5},{0,6},{1,7},{14,8},{15,9},{12,... | collective-permute-start | bytes 399368 | tf_op jit(solution)/shard_map/ppermute | solution.py:135
  5.7 8.3 %collective-permute-start.7 = (bf16[520,128]{1,0:T(8,128)(2,1)S(1)}, bf16[520,128]{1,0:T(8,128)(2,1)S(1)}, u32[]{:S(2)}, u32[]{:S(2)}) collective-permute-start(bf16[520,128]{1,0:T(8,128)(2,1)S(1)} %get-tuple-element.16.refs_0_.refs_8_), channel_id=1, source_target_pairs={{24,0},{25,1},{26,2},{27,3},{28,4},{29,5},{30,6},{31,7},{16,8},{17... | collective-permute-start | bytes 399368 | tf_op jit(solution)/shard_map/ppermute | solution.py:135
  9.7 5.7 %collective-permute-start.8 = (bf16[520,128]{1,0:T(8,128)(2,1)S(1)}, bf16[520,128]{1,0:T(8,128)(2,1)S(1)}, u32[]{:S(2)}, u32[]{:S(2)}) collective-permute-start(bf16[520,128]{1,0:T(8,128)(2,1)S(1)} %get-tuple-element.16.refs_0_.refs_8_), channel_id=1, source_target_pairs={{8,0},{9,1},{10,2},{11,3},{12,4},{13,5},{14,6},{15,7},{0,8},{1,9},... | collective-permute-start | bytes 399368 | tf_op jit(solution)/shard_map/ppermute | solution.py:135
  9.7 7.3 %collective-permute-start.3 = (bf16[520,128]{1,0:T(8,128)(2,1)S(1)}, bf16[520,128]{1,0:T(8,128)(2,1)S(1)}, u32[]{:S(2)}, u32[]{:S(2)}) collective-permute-start(bf16[520,128]{1,0:T(8,128)(2,1)S(1)} %get-tuple-element.16.refs_0_.refs_8_), channel_id=1, source_target_pairs={{1,0},{0,1},{3,2},{2,3},{5,4},{4,5},{7,6},{6,7},{9,8},{8,9},{11,10... | collective-permute-start | bytes 399368 | tf_op jit(solution)/shard_map/ppermute | solution.py:135
  12.0 5.0 %collective-permute-start.4 = (bf16[520,128]{1,0:T(8,128)(2,1)S(1)}, bf16[520,128]{1,0:T(8,128)(2,1)S(1)}, u32[]{:S(2)}, u32[]{:S(2)}) collective-permute-start(bf16[520,128]{1,0:T(8,128)(2,1)S(1)} %collective-permute-done.refs_1_), channel_id=1, source_target_pairs={{1,0},{0,1},{3,2},{2,3},{5,4},{4,5},{7,6},{6,7},{9,8},{8,9},{11,10... | collective-permute-start | bytes 399368 | tf_op jit(solution)/shard_map/ppermute | solution.py:135
  12.0 5.0 %collective-permute-start.5 = (bf16[520,128]{1,0:T(8,128)(2,1)S(1)}, bf16[520,128]{1,0:T(8,128)(2,1)S(1)}, u32[]{:S(2)}, u32[]{:S(2)}) collective-permute-start(bf16[520,128]{1,0:T(8,128)(2,1)S(1)} %collective-permute-done.1.refs_2_), channel_id=1, source_target_pairs={{1,0},{0,1},{3,2},{2,3},{5,4},{4,5},{7,6},{6,7},{9,8},{8,9},{11,10... | collective-permute-start | bytes 399368 | tf_op jit(solution)/shard_map/ppermute | solution.py:135
  13.9 3.1 %collective-permute-start.6 = (bf16[520,128]{1,0:T(8,128)(2,1)S(1)}, bf16[520,128]{1,0:T(8,128)(2,1)S(1)}, u32[]{:S(2)}, u32[]{:S(2)}) collective-permute-start(bf16[520,128]{1,0:T(8,128)(2,1)S(1)} %collective-permute-done.2.refs_3_), channel_id=1, source_target_pairs={{1,0},{0,1},{3,2},{2,3},{5,4},{4,5},{7,6},{6,7},{9,8},{8,9},{11,10... | collective-permute-start | bytes 399368 | tf_op jit(solution)/shard_map/ppermute | solution.py:135
  15.4 5.0 %collective-permute-start.11 = (bf16[520,128]{1,0:T(8,128)(2,1)S(1)}, bf16[520,128]{1,0:T(8,128)(2,1)S(1)}, u32[]{:S(2)}, u32[]{:S(2)}) collective-permute-start(bf16[520,128]{1,0:T(8,128)(2,1)S(1)} %collective-permute-done.7.refs_10_), channel_id=1, source_target_pairs={{8,0},{9,1},{10,2},{11,3},{12,4},{13,5},{14,6},{15,7},{0,8},{1,9},... | collective-permute-start | bytes 399368 | tf_op jit(solution)/shard_map/ppermute | solution.py:135
  17.8 5.4 %collective-permute-start.10 = (f32[1,128]{1,0:T(1,128)S(1)}, f32[1,128]{1,0:T(1,128)S(1)}, u32[]{:S(2)}, u32[]{:S(2)}) collective-permute-start(f32[1,128]{1,0:T(1,128)S(1)} %get-tuple-element.24), channel_id=1, source_target_pairs={{24,0},{25,1},{26,2},{27,3},{28,4},{29,5},{30,6},{31,7},{16,8},{17... | collective-permute-start | bytes 1544 | tf_op jit(solution)/shard_map/ppermute | solution.py:135
  19.6 3.6 %collective-permute-start.9 = (f32[1,128]{1,0:T(1,128)S(1)}, f32[1,128]{1,0:T(1,128)S(1)}, u32[]{:S(2)}, u32[]{:S(2)}) collective-permute-start(f32[1,128]{1,0:T(1,128)S(1)} %get-tuple-element.23), channel_id=1, source_target_pairs={{8,0},{9,1},{10,2},{11,3},{12,4},{13,5},{14,6},{15,7},{0,8},{1,9},... | collective-permute-start | bytes 1544 | tf_op jit(solution)/shard_map/ppermute | solution.py:135
  20.8 4.5 %collective-permute-start.12 = (f32[1,128]{1,0:T(1,128)S(1)}, f32[1,128]{1,0:T(1,128)S(1)}, u32[]{:S(2)}, u32[]{:S(2)}) collective-permute-start(f32[1,128]{1,0:T(1,128)S(1)} %shard_map.39), channel_id=1, source_target_pairs={{16,0},{17,1},{18,2},{19,3},{20,4},{21,5},{22,6},{23,7},{24,8},{25... | collective-permute-start | bytes 1544 | tf_op jit(solution)/shard_map/ppermute | solution.py:135

commit v31 on v30

--- a/solution.py
+++ b/solution.py
@@ -155,6 +155,7 @@
         near = [permute(own, lambda z, a, g: (z, turned(a, s, wide), g)) for s in range(1, wide)]
         middle = along(own, length - 1) if half < length else None
         first = [along(own, s) for s in range(1, half)]
+        near[0], middle = lax.optimization_barrier((near[0], middle))
         near = lax.optimization_barrier(near)
         middle, first = lax.optimization_barrier((middle, first))
         last = [along(middle, s) for s in range(1, half)] if half < length else []

time: 26 us -> 27.7 us (1.065)
  waiting for transfers between devices: 8.35 us -> 13.9 us
  starting transfers between devices: 14.6 us -> 10.7 us
    ppermute x13, waiting for transfers between devices: 8.35 us -> 13.9 us  [permute(): return lax.ppermute(x, ('clu', 'grp'), pairs)]
    ppermute x13, starting transfers between devices: 14.6 us -> 10.7 us  [permute(): return lax.ppermute(x, ('clu', 'grp'), pairs)]
  transfers between devices with their start and end apart: 13 -> 13, of which waited for: 6 -> 8; matrix products, arithmetic and copies ran while one was open for 0% -> 0% of each run, Pallas kernels for 5% -> 5%
where the time goes in v31:
time: 27.7 us; the launch traced here: 27.5 us
  waiting for transfers between devices  13.9 us (50%)
  starting transfers between devices  10.7 us (39%)
  Pallas kernels  2.37 us (9%)
  other arithmetic  0.52 us (2%)
    ppermute x13, waiting for transfers between devices, permute(): return lax.ppermute(x, ('clu', 'grp'), pairs)  13.9 us
    ppermute x13, starting transfers between devices, permute(): return lax.ppermute(x, ('clu', 'grp'), pairs)  10.7 us
    pallas_call x2, Pallas kernels, best_of(): pl.pallas_call(functools.partial(best_kernel, rows, len(keys), n_spans, o...  1.27 us
    pallas_call x1, Pallas kernels, pack(): pl.pallas_call(functools.partial(pack_kernel, groups), out_shape=[pltpu.V...  1.1 us
  transfers between devices with their start and end apart: 13, of which 8 were waited for; matrix products, arithmetic and copies ran while one was open for 0% of the time, Pallas kernels for 5%

profile of v31, /device:TPU:0, one launch (start us, length us, event | category | flops | bytes accessed | tf_op | source)
XLA Modules:
  0.0 27.5 jit_solution(11683966360547870087)
XLA Ops:
  0.0 1.1 %shard_map.37 = (bf16[520,128]{1,0:T(8,128)(2,1)S(1)}, bf16[64,64]{1,0:T(8,128)(2,1)S(1)}) custom-call(bf16[128,512]{1,0:T(8,128)(2,1)} %emb_ref.1, s32[1,128]{1,0:T(1,128)} %bitcast.4, s32[1,64]{1,0:T(1,128)} %bitcast.5), custom_call_target="tpu_custom_call" | custom-call | tf_op jit(solution)/shard_map/pallas_call | solution.py:42
  1.1 3.0 %collective-permute-start = (bf16[520,128]{1,0:T(8,128)(2,1)S(1)}, bf16[520,128]{1,0:T(8,128)(2,1)S(1)}, u32[]{:S(2)}, u32[]{:S(2)}) collective-permute-start(bf16[520,128]{1,0:T(8,128)(2,1)S(1)} %get-tuple-element.18.refs_0_.refs_8_), channel_id=1, source_target_pairs={{2,0},{3,1},{0,2},{1,3},{6,4},{7,5},{4,6},{5,7},{10,8},{11,9},{8,1... | collective-permute-start | bytes 399368 | tf_op jit(solution)/shard_map/ppermute | solution.py:135
  4.1 3.6 %collective-permute-start.1 = (bf16[520,128]{1,0:T(8,128)(2,1)S(1)}, bf16[520,128]{1,0:T(8,128)(2,1)S(1)}, u32[]{:S(2)}, u32[]{:S(2)}) collective-permute-start(bf16[520,128]{1,0:T(8,128)(2,1)S(1)} %get-tuple-element.18.refs_0_.refs_8_), channel_id=1, source_target_pairs={{24,0},{25,1},{26,2},{27,3},{28,4},{29,5},{30,6},{31,7},{16,8},{17... | collective-permute-start | bytes 399368 | tf_op jit(solution)/shard_map/ppermute | solution.py:135
  7.7 1.5 %collective-permute-start.2 = (bf16[520,128]{1,0:T(8,128)(2,1)S(1)}, bf16[520,128]{1,0:T(8,128)(2,1)S(1)}, u32[]{:S(2)}, u32[]{:S(2)}) collective-permute-start(bf16[520,128]{1,0:T(8,128)(2,1)S(1)} %get-tuple-element.18.refs_0_.refs_8_), channel_id=1, source_target_pairs={{4,0},{5,1},{6,2},{7,3},{0,4},{1,5},{2,6},{3,7},{12,8},{13,9},{14,... | collective-permute-start | bytes 399368 | tf_op jit(solution)/shard_map/ppermute | solution.py:135
  9.2 0.5 %collective-permute-start.3 = (bf16[520,128]{1,0:T(8,128)(2,1)S(1)}, bf16[520,128]{1,0:T(8,128)(2,1)S(1)}, u32[]{:S(2)}, u32[]{:S(2)}) collective-permute-start(bf16[520,128]{1,0:T(8,128)(2,1)S(1)} %get-tuple-element.18.refs_0_.refs_8_), channel_id=1, source_target_pairs={{6,0},{7,1},{4,2},{5,3},{2,4},{3,5},{0,6},{1,7},{14,8},{15,9},{12,... | collective-permute-start | bytes 399368 | tf_op jit(solution)/shard_map/ppermute | solution.py:135
  9.7 0.0 collective-permute-start.8
  9.7 0.0 collective-permute-done.refs_1_
  9.7 0.0 collective-permute-start.4
  9.7 2.4 %collective-permute-done.1.refs_10_ = bf16[520,128]{1,0:T(8,128)(2,1)S(1)} collective-permute-done((bf16[520,128]{1,0:T(8,128)(2,1)S(1)}, bf16[520,128]{1,0:T(8,128)(2,1)S(1)}, u32[]{:S(2)}, u32[]{:S(2)}) %collective-permute-start.1) | collective-permute-done | bytes 133152 | tf_op jit(solution)/shard_map/ppermute | solution.py:135
  12.1 3.4 %collective-permute-done.2.refs_2_ = bf16[520,128]{1,0:T(8,128)(2,1)S(1)} collective-permute-done((bf16[520,128]{1,0:T(8,128)(2,1)S(1)}, bf16[520,128]{1,0:T(8,128)(2,1)S(1)}, u32[]{:S(2)}, u32[]{:S(2)}) %collective-permute-start.2) | collective-permute-done | bytes 133152 | tf_op jit(solution)/shard_map/ppermute | solution.py:135
  15.6 0.0 collective-permute-done.3.refs_3_
  15.6 0.0 collective-permute-start.5
  15.6 0.5 %collective-permute-start.6 = (bf16[520,128]{1,0:T(8,128)(2,1)S(1)}, bf16[520,128]{1,0:T(8,128)(2,1)S(1)}, u32[]{:S(2)}, u32[]{:S(2)}) collective-permute-start(bf16[520,128]{1,0:T(8,128)(2,1)S(1)} %collective-permute-done.2.refs_2_), channel_id=1, source_target_pairs={{1,0},{0,1},{3,2},{2,3},{5,4},{4,5},{7,6},{6,7},{9,8},{8,9},{11,10... | collective-permute-start | bytes 399368 | tf_op jit(solution)/shard_map/ppermute | solution.py:135
  16.1 0.0 collective-permute-start.7
  16.1 0.0 collective-permute-done.8.refs_9_
  16.1 0.0 collective-permute-start.11
  16.1 0.0 collective-permute-done.4.refs_4_
  16.1 0.8 %collective-permute-done.5.refs_5_ = bf16[520,128]{1,0:T(8,128)(2,1)S(1)} collective-permute-done((bf16[520,128]{1,0:T(8,128)(2,1)S(1)}, bf16[520,128]{1,0:T(8,128)(2,1)S(1)}, u32[]{:S(2)}, u32[]{:S(2)}) %collective-permute-start.5) | collective-permute-done | bytes 133152 | tf_op jit(solution)/shard_map/ppermute | solution.py:135
  16.9 0.2 collective-permute-done.6.refs_6_
  17.1 0.3 %collective-permute-done.7.refs_7_ = bf16[520,128]{1,0:T(8,128)(2,1)S(1)} collective-permute-done((bf16[520,128]{1,0:T(8,128)(2,1)S(1)}, bf16[520,128]{1,0:T(8,128)(2,1)S(1)}, u32[]{:S(2)}, u32[]{:S(2)}) %collective-permute-start.7) | collective-permute-done | bytes 133152 | tf_op jit(solution)/shard_map/ppermute | solution.py:135
  17.4 0.8 %shard_map.38 = (f32[1,128]{1,0:T(1,128)S(1)}, f32[1,128]{1,0:T(1,128)S(1)}, f32[1,128]{1,0:T(1,128)S(1)}) custom-call(bf16[64,64]{1,0:T(8,128)(2,1)S(1)} %get-tuple-element.17.table_ref, bf16[520,128]{1,0:T(8,128)(2,1)S(1)} %get-tuple-element.18.refs_0_.refs_8_, bf16[520,128]{1,0:T(8,128)(2,1)S(1)} %collective-permute-done.refs_1_, ...), custom_call_target="tpu_custom_call" | custom-call | flops 402653184 | bytes 1441792 | tf_op jit(solution)/shard_map/pallas_call | solution.py:110
  18.2 0.5 %collective-permute-start.10 = (f32[1,128]{1,0:T(1,128)S(1)}, f32[1,128]{1,0:T(1,128)S(1)}, u32[]{:S(2)}, u32[]{:S(2)}) collective-permute-start(f32[1,128]{1,0:T(1,128)S(1)} %get-tuple-element.28), channel_id=1, source_target_pairs={{24,0},{25,1},{26,2},{27,3},{28,4},{29,5},{30,6},{31,7},{16,8},{17... | collective-permute-start | bytes 1544 | tf_op jit(solution)/shard_map/ppermute | solution.py:135
  18.7 0.4 %collective-permute-start.9 = (f32[1,128]{1,0:T(1,128)S(1)}, f32[1,128]{1,0:T(1,128)S(1)}, u32[]{:S(2)}, u32[]{:S(2)}) collective-permute-start(f32[1,128]{1,0:T(1,128)S(1)} %get-tuple-element.27), channel_id=1, source_target_pairs={{8,0},{9,1},{10,2},{11,3},{12,4},{13,5},{14,6},{15,7},{0,8},{1,9},... | collective-permute-start | bytes 1544 | tf_op jit(solution)/shard_map/ppermute | solution.py:135
  19.1 2.9 %collective-permute-done.11.refs_8_ = bf16[520,128]{1,0:T(8,128)(2,1)S(1)} collective-permute-done((bf16[520,128]{1,0:T(8,128)(2,1)S(1)}, bf16[520,128]{1,0:T(8,128)(2,1)S(1)}, u32[]{:S(2)}, u32[]{:S(2)}) %collective-permute-start.11) | collective-permute-done | bytes 133152 | tf_op jit(solution)/shard_map/ppermute | solution.py:135
  22.0 0.5 %shard_map.39 = f32[1,128]{1,0:T(1,128)S(1)} custom-call(bf16[64,64]{1,0:T(8,128)(2,1)S(1)} %get-tuple-element.17.table_ref, bf16[520,128]{1,0:T(8,128)(2,1)S(1)} %get-tuple-element.18.refs_0_.refs_8_, bf16[520,128]{1,0:T(8,128)(2,1)S(1)} %collective-permute-done.refs_1_, bf16[520,128]{1,0:T(8,128)(2,1)S(1)} %collective-permute-done.2.refs_2_, ...), custom_call_target="tpu_custom_call" | custom-call | flops 134217728 | bytes 1179648 | tf_op jit(solution)/shard_map/pallas_call | solution.py:110
  22.5 0.7 %collective-permute-start.12 = (f32[1,128]{1,0:T(1,128)S(1)}, f32[1,128]{1,0:T(1,128)S(1)}, u32[]{:S(2)}, u32[]{:S(2)}) collective-permute-start(f32[1,128]{1,0:T(1,128)S(1)} %shard_map.39), channel_id=1, source_target_pairs={{16,0},{17,1},{18,2},{19,3},{20,4},{21,5},{22,6},{23,7},{24,8},{25... | collective-permute-start | bytes 1544 | tf_op jit(solution)/shard_map/ppermute | solution.py:135
  23.2 0.4 %collective-permute-done.10 = f32[1,128]{1,0:T(1,128)S(1)} collective-permute-done((f32[1,128]{1,0:T(1,128)S(1)}, f32[1,128]{1,0:T(1,128)S(1)}, u32[]{:S(2)}, u32[]{:S(2)}) %collective-permute-start.10) | collective-permute-done | bytes 544 | tf_op jit(solution)/shard_map/ppermute | solution.py:135
  23.6 0.0 collective-permute-done.9
  23.6 3.4 %collective-permute-done.12 = f32[1,128]{1,0:T(1,128)S(1)} collective-permute-done((f32[1,128]{1,0:T(1,128)S(1)}, f32[1,128]{1,0:T(1,128)S(1)}, u32[]{:S(2)}, u32[]{:S(2)}) %collective-permute-start.12) | collective-permute-done | bytes 544 | tf_op jit(solution)/shard_map/ppermute | solution.py:135
  27.0 0.5 %maximum_bitcast_fusion = f32[128]{0:T(128)} fusion(f32[1,128]{1,0:T(1,128)S(1)} %collective-permute-done.12, f32[1,128]{1,0:T(1,128)S(1)} %collective-permute-done.10, f32[1,128]{1,0:T(1,128)S(1)} %get-tuple-element.26, f32[1,128]{1,0:T(1,128)S(1)} %collective-permute-done.9), kind=kLoop, calls=%fused_computation | loop fusion | flops 384 | bytes 2560 | tf_op jit(solution)/shard_map/reshape | solution.py:181
Async XLA Ops:
  1.1 8.6 %collective-permute-start = (bf16[520,128]{1,0:T(8,128)(2,1)S(1)}, bf16[520,128]{1,0:T(8,128)(2,1)S(1)}, u32[]{:S(2)}, u32[]{:S(2)}) collective-permute-start(bf16[520,128]{1,0:T(8,128)(2,1)S(1)} %get-tuple-element.18.refs_0_.refs_8_), channel_id=1, source_target_pairs={{2,0},{3,1},{0,2},{1,3},{6,4},{7,5},{4,6},{5,7},{10,8},{11,9},{8,1... | collective-permute-start | bytes 399368 | tf_op jit(solution)/shard_map/ppermute | solution.py:135
  4.1 8.0 %collective-permute-start.1 = (bf16[520,128]{1,0:T(8,128)(2,1)S(1)}, bf16[520,128]{1,0:T(8,128)(2,1)S(1)}, u32[]{:S(2)}, u32[]{:S(2)}) collective-permute-start(bf16[520,128]{1,0:T(8,128)(2,1)S(1)} %get-tuple-element.18.refs_0_.refs_8_), channel_id=1, source_target_pairs={{24,0},{25,1},{26,2},{27,3},{28,4},{29,5},{30,6},{31,7},{16,8},{17... | collective-permute-start | bytes 399368 | tf_op jit(solution)/shard_map/ppermute | solution.py:135
  7.7 7.8 %collective-permute-start.2 = (bf16[520,128]{1,0:T(8,128)(2,1)S(1)}, bf16[520,128]{1,0:T(8,128)(2,1)S(1)}, u32[]{:S(2)}, u32[]{:S(2)}) collective-permute-start(bf16[520,128]{1,0:T(8,128)(2,1)S(1)} %get-tuple-element.18.refs_0_.refs_8_), channel_id=1, source_target_pairs={{4,0},{5,1},{6,2},{7,3},{0,4},{1,5},{2,6},{3,7},{12,8},{13,9},{14,... | collective-permute-start | bytes 399368 | tf_op jit(solution)/shard_map/ppermute | solution.py:135
  9.2 6.3 %collective-permute-start.3 = (bf16[520,128]{1,0:T(8,128)(2,1)S(1)}, bf16[520,128]{1,0:T(8,128)(2,1)S(1)}, u32[]{:S(2)}, u32[]{:S(2)}) collective-permute-start(bf16[520,128]{1,0:T(8,128)(2,1)S(1)} %get-tuple-element.18.refs_0_.refs_8_), channel_id=1, source_target_pairs={{6,0},{7,1},{4,2},{5,3},{2,4},{3,5},{0,6},{1,7},{14,8},{15,9},{12,... | collective-permute-start | bytes 399368 | tf_op jit(solution)/shard_map/ppermute | solution.py:135
  9.7 6.4 %collective-permute-start.8 = (bf16[520,128]{1,0:T(8,128)(2,1)S(1)}, bf16[520,128]{1,0:T(8,128)(2,1)S(1)}, u32[]{:S(2)}, u32[]{:S(2)}) collective-permute-start(bf16[520,128]{1,0:T(8,128)(2,1)S(1)} %get-tuple-element.18.refs_0_.refs_8_), channel_id=1, source_target_pairs={{8,0},{9,1},{10,2},{11,3},{12,4},{13,5},{14,6},{15,7},{0,8},{1,9},... | collective-permute-start | bytes 399368 | tf_op jit(solution)/shard_map/ppermute | solution.py:135
  9.7 6.4 %collective-permute-start.4 = (bf16[520,128]{1,0:T(8,128)(2,1)S(1)}, bf16[520,128]{1,0:T(8,128)(2,1)S(1)}, u32[]{:S(2)}, u32[]{:S(2)}) collective-permute-start(bf16[520,128]{1,0:T(8,128)(2,1)S(1)} %get-tuple-element.18.refs_0_.refs_8_), channel_id=1, source_target_pairs={{1,0},{0,1},{3,2},{2,3},{5,4},{4,5},{7,6},{6,7},{9,8},{8,9},{11,10... | collective-permute-start | bytes 399368 | tf_op jit(solution)/shard_map/ppermute | solution.py:135
  15.6 1.4 %collective-permute-start.5 = (bf16[520,128]{1,0:T(8,128)(2,1)S(1)}, bf16[520,128]{1,0:T(8,128)(2,1)S(1)}, u32[]{:S(2)}, u32[]{:S(2)}) collective-permute-start(bf16[520,128]{1,0:T(8,128)(2,1)S(1)} %collective-permute-done.refs_1_), channel_id=1, source_target_pairs={{1,0},{0,1},{3,2},{2,3},{5,4},{4,5},{7,6},{6,7},{9,8},{8,9},{11,10... | collective-permute-start | bytes 399368 | tf_op jit(solution)/shard_map/ppermute | solution.py:135
  15.6 1.5 %collective-permute-start.6 = (bf16[520,128]{1,0:T(8,128)(2,1)S(1)}, bf16[520,128]{1,0:T(8,128)(2,1)S(1)}, u32[]{:S(2)}, u32[]{:S(2)}) collective-permute-start(bf16[520,128]{1,0:T(8,128)(2,1)S(1)} %collective-permute-done.2.refs_2_), channel_id=1, source_target_pairs={{1,0},{0,1},{3,2},{2,3},{5,4},{4,5},{7,6},{6,7},{9,8},{8,9},{11,10... | collective-permute-start | bytes 399368 | tf_op jit(solution)/shard_map/ppermute | solution.py:135
  16.1 1.4 %collective-permute-start.7 = (bf16[520,128]{1,0:T(8,128)(2,1)S(1)}, bf16[520,128]{1,0:T(8,128)(2,1)S(1)}, u32[]{:S(2)}, u32[]{:S(2)}) collective-permute-start(bf16[520,128]{1,0:T(8,128)(2,1)S(1)} %collective-permute-done.3.refs_3_), channel_id=1, source_target_pairs={{1,0},{0,1},{3,2},{2,3},{5,4},{4,5},{7,6},{6,7},{9,8},{8,9},{11,10... | collective-permute-start | bytes 399368 | tf_op jit(solution)/shard_map/ppermute | solution.py:135
  16.1 6.0 %collective-permute-start.11 = (bf16[520,128]{1,0:T(8,128)(2,1)S(1)}, bf16[520,128]{1,0:T(8,128)(2,1)S(1)}, u32[]{:S(2)}, u32[]{:S(2)}) collective-permute-start(bf16[520,128]{1,0:T(8,128)(2,1)S(1)} %collective-permute-done.1.refs_10_), channel_id=1, source_target_pairs={{8,0},{9,1},{10,2},{11,3},{12,4},{13,5},{14,6},{15,7},{0,8},{1,9},... | collective-permute-start | bytes 399368 | tf_op jit(solution)/shard_map/ppermute | solution.py:135
  18.2 5.4 %collective-permute-start.10 = (f32[1,128]{1,0:T(1,128)S(1)}, f32[1,128]{1,0:T(1,128)S(1)}, u32[]{:S(2)}, u32[]{:S(2)}) collective-permute-start(f32[1,128]{1,0:T(1,128)S(1)} %get-tuple-element.28), channel_id=1, source_target_pairs={{24,0},{25,1},{26,2},{27,3},{28,4},{29,5},{30,6},{31,7},{16,8},{17... | collective-permute-start | bytes 1544 | tf_op jit(solution)/shard_map/ppermute | solution.py:135
  18.7 4.9 %collective-permute-start.9 = (f32[1,128]{1,0:T(1,128)S(1)}, f32[1,128]{1,0:T(1,128)S(1)}, u32[]{:S(2)}, u32[]{:S(2)}) collective-permute-start(f32[1,128]{1,0:T(1,128)S(1)} %get-tuple-element.27), channel_id=1, source_target_pairs={{8,0},{9,1},{10,2},{11,3},{12,4},{13,5},{14,6},{15,7},{0,8},{1,9},... | collective-permute-start | bytes 1544 | tf_op jit(solution)/shard_map/ppermute | solution.py:135
  22.5 4.5 %collective-permute-start.12 = (f32[1,128]{1,0:T(1,128)S(1)}, f32[1,128]{1,0:T(1,128)S(1)}, u32[]{:S(2)}, u32[]{:S(2)}) collective-permute-start(f32[1,128]{1,0:T(1,128)S(1)} %shard_map.39), channel_id=1, source_target_pairs={{16,0},{17,1},{18,2},{19,3},{20,4},{21,5},{22,6},{23,7},{24,8},{25... | collective-permute-start | bytes 1544 | tf_op jit(solution)/shard_map/ppermute | solution.py:135

commit v32 on v30

--- a/solution.py
+++ b/solution.py
@@ -152,10 +152,13 @@
             return permute(x, lambda z, a, g: (turned(z, s, length), a, g))
 
         half = length // 2 if length & (length - 1) == 0 else length
-        near = [permute(own, lambda z, a, g: (z, turned(a, s, wide), g)) for s in range(1, wide)]
+        order = sorted(range(1, wide), key=lambda s: (s & (s - 1) != 0, -s))
+        sent = {s: permute(own, lambda z, a, g: (z, turned(a, s, wide), g)) for s in order}
+        near = [sent[s] for s in order]
         middle = along(own, length - 1) if half < length else None
         first = [along(own, s) for s in range(1, half)]
         near = lax.optimization_barrier(near)
+        near = [near[order.index(s)] for s in range(1, wide)]
         middle, first = lax.optimization_barrier((middle, first))
         last = [along(middle, s) for s in range(1, half)] if half < length else []
         offsets = list(range(1, half))

time: 26 us -> 26 us (level)
  transfers between devices with their start and end apart: 13 -> 13, of which waited for: 6 -> 7; matrix products, arithmetic and copies ran while one was open for 0% -> 0% of each run, Pallas kernels for 5% -> 5%
where the time goes in v32:
time: 26 us; the launch traced here: 25.8 us
  starting transfers between devices  14.5 us (56%)
  waiting for transfers between devices  8.36 us (32%)
  Pallas kernels  2.38 us (9%)
  other arithmetic  0.52 us (2%)
    ppermute x13, starting transfers between devices, permute(): return lax.ppermute(x, ('clu', 'grp'), pairs)  14.5 us
    ppermute x13, waiting for transfers between devices, permute(): return lax.ppermute(x, ('clu', 'grp'), pairs)  8.36 us
    pallas_call x2, Pallas kernels, best_of(): pl.pallas_call(functools.partial(best_kernel, rows, len(keys), n_spans, o...  1.27 us
    pallas_call x1, Pallas kernels, pack(): pl.pallas_call(functools.partial(pack_kernel, groups), out_shape=[pltpu.V...  1.1 us
  transfers between devices with their start and end apart: 13, of which 7 were waited for; matrix products, arithmetic and copies ran while one was open for 0% of the time, Pallas kernels for 5%

profile of v32, /device:TPU:0, one launch (start us, length us, event | category | flops | bytes accessed | tf_op | source)
XLA Modules:
  0.0 25.8 jit_solution(18394183771352072885)
XLA Ops:
  0.0 1.1 %shard_map.37 = (bf16[520,128]{1,0:T(8,128)(2,1)S(1)}, bf16[64,64]{1,0:T(8,128)(2,1)S(1)}) custom-call(bf16[128,512]{1,0:T(8,128)(2,1)} %emb_ref.1, s32[1,128]{1,0:T(1,128)} %bitcast.4, s32[1,64]{1,0:T(1,128)} %bitcast.5), custom_call_target="tpu_custom_call" | custom-call | tf_op jit(solution)/shard_map/pallas_call | solution.py:42
  1.1 3.0 %collective-permute-start = (bf16[520,128]{1,0:T(8,128)(2,1)S(1)}, bf16[520,128]{1,0:T(8,128)(2,1)S(1)}, u32[]{:S(2)}, u32[]{:S(2)}) collective-permute-start(bf16[520,128]{1,0:T(8,128)(2,1)S(1)} %get-tuple-element.16.refs_0_.refs_8_), channel_id=1, source_target_pairs={{4,0},{5,1},{6,2},{7,3},{0,4},{1,5},{2,6},{3,7},{12,8},{13,9},{14,... | collective-permute-start | bytes 399368 | tf_op jit(solution)/shard_map/ppermute | solution.py:135
  4.1 1.5 %collective-permute-start.1 = (bf16[520,128]{1,0:T(8,128)(2,1)S(1)}, bf16[520,128]{1,0:T(8,128)(2,1)S(1)}, u32[]{:S(2)}, u32[]{:S(2)}) collective-permute-start(bf16[520,128]{1,0:T(8,128)(2,1)S(1)} %get-tuple-element.16.refs_0_.refs_8_), channel_id=1, source_target_pairs={{2,0},{3,1},{0,2},{1,3},{6,4},{7,5},{4,6},{5,7},{10,8},{11,9},{8,1... | collective-permute-start | bytes 399368 | tf_op jit(solution)/shard_map/ppermute | solution.py:135
  5.6 0.0 collective-permute-start.2
  5.7 4.0 %collective-permute-start.7 = (bf16[520,128]{1,0:T(8,128)(2,1)S(1)}, bf16[520,128]{1,0:T(8,128)(2,1)S(1)}, u32[]{:S(2)}, u32[]{:S(2)}) collective-permute-start(bf16[520,128]{1,0:T(8,128)(2,1)S(1)} %get-tuple-element.16.refs_0_.refs_8_), channel_id=1, source_target_pairs={{24,0},{25,1},{26,2},{27,3},{28,4},{29,5},{30,6},{31,7},{16,8},{17... | collective-permute-start | bytes 399368 | tf_op jit(solution)/shard_map/ppermute | solution.py:135
  9.7 0.0 collective-permute-start.8
  9.7 0.0 collective-permute-done.refs_2_
  9.7 0.0 collective-permute-start.3
  9.7 0.8 %collective-permute-done.1.refs_1_ = bf16[520,128]{1,0:T(8,128)(2,1)S(1)} collective-permute-done((bf16[520,128]{1,0:T(8,128)(2,1)S(1)}, bf16[520,128]{1,0:T(8,128)(2,1)S(1)}, u32[]{:S(2)}, u32[]{:S(2)}) %collective-permute-start.1) | collective-permute-done | bytes 133152 | tf_op jit(solution)/shard_map/ppermute | solution.py:135
  10.6 1.2 %collective-permute-done.2.refs_3_ = bf16[520,128]{1,0:T(8,128)(2,1)S(1)} collective-permute-done((bf16[520,128]{1,0:T(8,128)(2,1)S(1)}, bf16[520,128]{1,0:T(8,128)(2,1)S(1)}, u32[]{:S(2)}, u32[]{:S(2)}) %collective-permute-start.2) | collective-permute-done | bytes 133152 | tf_op jit(solution)/shard_map/ppermute | solution.py:135
  11.8 0.0 collective-permute-start.4
  11.8 0.5 %collective-permute-start.5 = (bf16[520,128]{1,0:T(8,128)(2,1)S(1)}, bf16[520,128]{1,0:T(8,128)(2,1)S(1)}, u32[]{:S(2)}, u32[]{:S(2)}) collective-permute-start(bf16[520,128]{1,0:T(8,128)(2,1)S(1)} %collective-permute-done.refs_2_), channel_id=1, source_target_pairs={{1,0},{0,1},{3,2},{2,3},{5,4},{4,5},{7,6},{6,7},{9,8},{8,9},{11,10... | collective-permute-start | bytes 399368 | tf_op jit(solution)/shard_map/ppermute | solution.py:135
  12.3 1.6 %collective-permute-done.7.refs_10_ = bf16[520,128]{1,0:T(8,128)(2,1)S(1)} collective-permute-done((bf16[520,128]{1,0:T(8,128)(2,1)S(1)}, bf16[520,128]{1,0:T(8,128)(2,1)S(1)}, u32[]{:S(2)}, u32[]{:S(2)}) %collective-permute-start.7) | collective-permute-done | bytes 133152 | tf_op jit(solution)/shard_map/ppermute | solution.py:135
  13.9 0.0 collective-permute-start.6
  13.9 1.4 %collective-permute-done.8.refs_9_ = bf16[520,128]{1,0:T(8,128)(2,1)S(1)} collective-permute-done((bf16[520,128]{1,0:T(8,128)(2,1)S(1)}, bf16[520,128]{1,0:T(8,128)(2,1)S(1)}, u32[]{:S(2)}, u32[]{:S(2)}) %collective-permute-start.8) | collective-permute-done | bytes 133152 | tf_op jit(solution)/shard_map/ppermute | solution.py:135
  15.4 1.6 %collective-permute-start.11 = (bf16[520,128]{1,0:T(8,128)(2,1)S(1)}, bf16[520,128]{1,0:T(8,128)(2,1)S(1)}, u32[]{:S(2)}, u32[]{:S(2)}) collective-permute-start(bf16[520,128]{1,0:T(8,128)(2,1)S(1)} %collective-permute-done.7.refs_10_), channel_id=1, source_target_pairs={{8,0},{9,1},{10,2},{11,3},{12,4},{13,5},{14,6},{15,7},{0,8},{1,9},... | collective-permute-start | bytes 399368 | tf_op jit(solution)/shard_map/ppermute | solution.py:135
  17.0 0.0 collective-permute-done.3.refs_4_
  17.0 0.0 collective-permute-done.4.refs_5_
  17.0 0.0 collective-permute-done.5.refs_6_
  17.0 0.0 collective-permute-done.6.refs_7_
  17.0 0.8 %shard_map.38 = (f32[1,128]{1,0:T(1,128)S(1)}, f32[1,128]{1,0:T(1,128)S(1)}, f32[1,128]{1,0:T(1,128)S(1)}) custom-call(bf16[64,64]{1,0:T(8,128)(2,1)S(1)} %get-tuple-element.15.table_ref, bf16[520,128]{1,0:T(8,128)(2,1)S(1)} %get-tuple-element.16.refs_0_.refs_8_, bf16[520,128]{1,0:T(8,128)(2,1)S(1)} %collective-permute-done.1.refs_1_, ...), custom_call_target="tpu_custom_call" | custom-call | flops 402653184 | bytes 1441792 | tf_op jit(solution)/shard_map/pallas_call | solution.py:110
  17.8 1.8 %collective-permute-start.10 = (f32[1,128]{1,0:T(1,128)S(1)}, f32[1,128]{1,0:T(1,128)S(1)}, u32[]{:S(2)}, u32[]{:S(2)}) collective-permute-start(f32[1,128]{1,0:T(1,128)S(1)} %get-tuple-element.24), channel_id=1, source_target_pairs={{24,0},{25,1},{26,2},{27,3},{28,4},{29,5},{30,6},{31,7},{16,8},{17... | collective-permute-start | bytes 1544 | tf_op jit(solution)/shard_map/ppermute | solution.py:135
  19.6 0.0 collective-permute-start.9
  19.6 0.7 %collective-permute-done.11.refs_8_ = bf16[520,128]{1,0:T(8,128)(2,1)S(1)} collective-permute-done((bf16[520,128]{1,0:T(8,128)(2,1)S(1)}, bf16[520,128]{1,0:T(8,128)(2,1)S(1)}, u32[]{:S(2)}, u32[]{:S(2)}) %collective-permute-start.11) | collective-permute-done | bytes 133152 | tf_op jit(solution)/shard_map/ppermute | solution.py:135
  20.4 0.5 %shard_map.39 = f32[1,128]{1,0:T(1,128)S(1)} custom-call(bf16[64,64]{1,0:T(8,128)(2,1)S(1)} %get-tuple-element.15.table_ref, bf16[520,128]{1,0:T(8,128)(2,1)S(1)} %get-tuple-element.16.refs_0_.refs_8_, bf16[520,128]{1,0:T(8,128)(2,1)S(1)} %collective-permute-done.1.refs_1_, bf16[520,128]{1,0:T(8,128)(2,1)S(1)} %collective-permute-done.refs_2_, ...), custom_call_target="tpu_custom_call" | custom-call | flops 134217728 | bytes 1179648 | tf_op jit(solution)/shard_map/pallas_call | solution.py:110
  20.8 2.0 %collective-permute-start.12 = (f32[1,128]{1,0:T(1,128)S(1)}, f32[1,128]{1,0:T(1,128)S(1)}, u32[]{:S(2)}, u32[]{:S(2)}) collective-permute-start(f32[1,128]{1,0:T(1,128)S(1)} %shard_map.39), channel_id=1, source_target_pairs={{16,0},{17,1},{18,2},{19,3},{20,4},{21,5},{22,6},{23,7},{24,8},{25... | collective-permute-start | bytes 1544 | tf_op jit(solution)/shard_map/ppermute | solution.py:135
  22.8 0.4 %collective-permute-done.10 = f32[1,128]{1,0:T(1,128)S(1)} collective-permute-done((f32[1,128]{1,0:T(1,128)S(1)}, f32[1,128]{1,0:T(1,128)S(1)}, u32[]{:S(2)}, u32[]{:S(2)}) %collective-permute-start.10) | collective-permute-done | bytes 544 | tf_op jit(solution)/shard_map/ppermute | solution.py:135
  23.3 0.0 collective-permute-done.9
  23.3 2.1 %collective-permute-done.12 = f32[1,128]{1,0:T(1,128)S(1)} collective-permute-done((f32[1,128]{1,0:T(1,128)S(1)}, f32[1,128]{1,0:T(1,128)S(1)}, u32[]{:S(2)}, u32[]{:S(2)}) %collective-permute-start.12) | collective-permute-done | bytes 544 | tf_op jit(solution)/shard_map/ppermute | solution.py:135
  25.3 0.5 %maximum_bitcast_fusion = f32[128]{0:T(128)} fusion(f32[1,128]{1,0:T(1,128)S(1)} %collective-permute-done.12, f32[1,128]{1,0:T(1,128)S(1)} %collective-permute-done.10, f32[1,128]{1,0:T(1,128)S(1)} %get-tuple-element.22, f32[1,128]{1,0:T(1,128)S(1)} %collective-permute-done.9), kind=kLoop, calls=%fused_computation | loop fusion | flops 384 | bytes 2560 | tf_op jit(solution)/shard_map/reshape | solution.py:183
Async XLA Ops:
  1.1 8.6 %collective-permute-start = (bf16[520,128]{1,0:T(8,128)(2,1)S(1)}, bf16[520,128]{1,0:T(8,128)(2,1)S(1)}, u32[]{:S(2)}, u32[]{:S(2)}) collective-permute-start(bf16[520,128]{1,0:T(8,128)(2,1)S(1)} %get-tuple-element.16.refs_0_.refs_8_), channel_id=1, source_target_pairs={{4,0},{5,1},{6,2},{7,3},{0,4},{1,5},{2,6},{3,7},{12,8},{13,9},{14,... | collective-permute-start | bytes 399368 | tf_op jit(solution)/shard_map/ppermute | solution.py:135
  4.1 6.4 %collective-permute-start.1 = (bf16[520,128]{1,0:T(8,128)(2,1)S(1)}, bf16[520,128]{1,0:T(8,128)(2,1)S(1)}, u32[]{:S(2)}, u32[]{:S(2)}) collective-permute-start(bf16[520,128]{1,0:T(8,128)(2,1)S(1)} %get-tuple-element.16.refs_0_.refs_8_), channel_id=1, source_target_pairs={{2,0},{3,1},{0,2},{1,3},{6,4},{7,5},{4,6},{5,7},{10,8},{11,9},{8,1... | collective-permute-start | bytes 399368 | tf_op jit(solution)/shard_map/ppermute | solution.py:135
  5.6 6.2 %collective-permute-start.2 = (bf16[520,128]{1,0:T(8,128)(2,1)S(1)}, bf16[520,128]{1,0:T(8,128)(2,1)S(1)}, u32[]{:S(2)}, u32[]{:S(2)}) collective-permute-start(bf16[520,128]{1,0:T(8,128)(2,1)S(1)} %get-tuple-element.16.refs_0_.refs_8_), channel_id=1, source_target_pairs={{6,0},{7,1},{4,2},{5,3},{2,4},{3,5},{0,6},{1,7},{14,8},{15,9},{12,... | collective-permute-start | bytes 399368 | tf_op jit(solution)/shard_map/ppermute | solution.py:135
  5.7 8.2 %collective-permute-start.7 = (bf16[520,128]{1,0:T(8,128)(2,1)S(1)}, bf16[520,128]{1,0:T(8,128)(2,1)S(1)}, u32[]{:S(2)}, u32[]{:S(2)}) collective-permute-start(bf16[520,128]{1,0:T(8,128)(2,1)S(1)} %get-tuple-element.16.refs_0_.refs_8_), channel_id=1, source_target_pairs={{24,0},{25,1},{26,2},{27,3},{28,4},{29,5},{30,6},{31,7},{16,8},{17... | collective-permute-start | bytes 399368 | tf_op jit(solution)/shard_map/ppermute | solution.py:135
  9.7 5.7 %collective-permute-start.8 = (bf16[520,128]{1,0:T(8,128)(2,1)S(1)}, bf16[520,128]{1,0:T(8,128)(2,1)S(1)}, u32[]{:S(2)}, u32[]{:S(2)}) collective-permute-start(bf16[520,128]{1,0:T(8,128)(2,1)S(1)} %get-tuple-element.16.refs_0_.refs_8_), channel_id=1, source_target_pairs={{8,0},{9,1},{10,2},{11,3},{12,4},{13,5},{14,6},{15,7},{0,8},{1,9},... | collective-permute-start | bytes 399368 | tf_op jit(solution)/shard_map/ppermute | solution.py:135
  9.7 7.3 %collective-permute-start.3 = (bf16[520,128]{1,0:T(8,128)(2,1)S(1)}, bf16[520,128]{1,0:T(8,128)(2,1)S(1)}, u32[]{:S(2)}, u32[]{:S(2)}) collective-permute-start(bf16[520,128]{1,0:T(8,128)(2,1)S(1)} %get-tuple-element.16.refs_0_.refs_8_), channel_id=1, source_target_pairs={{1,0},{0,1},{3,2},{2,3},{5,4},{4,5},{7,6},{6,7},{9,8},{8,9},{11,10... | collective-permute-start | bytes 399368 | tf_op jit(solution)/shard_map/ppermute | solution.py:135
  11.8 5.2 %collective-permute-start.4 = (bf16[520,128]{1,0:T(8,128)(2,1)S(1)}, bf16[520,128]{1,0:T(8,128)(2,1)S(1)}, u32[]{:S(2)}, u32[]{:S(2)}) collective-permute-start(bf16[520,128]{1,0:T(8,128)(2,1)S(1)} %collective-permute-done.1.refs_1_), channel_id=1, source_target_pairs={{1,0},{0,1},{3,2},{2,3},{5,4},{4,5},{7,6},{6,7},{9,8},{8,9},{11,10... | collective-permute-start | bytes 399368 | tf_op jit(solution)/shard_map/ppermute | solution.py:135
  11.8 5.2 %collective-permute-start.5 = (bf16[520,128]{1,0:T(8,128)(2,1)S(1)}, bf16[520,128]{1,0:T(8,128)(2,1)S(1)}, u32[]{:S(2)}, u32[]{:S(2)}) collective-permute-start(bf16[520,128]{1,0:T(8,128)(2,1)S(1)} %collective-permute-done.refs_2_), channel_id=1, source_target_pairs={{1,0},{0,1},{3,2},{2,3},{5,4},{4,5},{7,6},{6,7},{9,8},{8,9},{11,10... | collective-permute-start | bytes 399368 | tf_op jit(solution)/shard_map/ppermute | solution.py:135
  13.9 3.1 %collective-permute-start.6 = (bf16[520,128]{1,0:T(8,128)(2,1)S(1)}, bf16[520,128]{1,0:T(8,128)(2,1)S(1)}, u32[]{:S(2)}, u32[]{:S(2)}) collective-permute-start(bf16[520,128]{1,0:T(8,128)(2,1)S(1)} %collective-permute-done.2.refs_3_), channel_id=1, source_target_pairs={{1,0},{0,1},{3,2},{2,3},{5,4},{4,5},{7,6},{6,7},{9,8},{8,9},{11,10... | collective-permute-start | bytes 399368 | tf_op jit(solution)/shard_map/ppermute | solution.py:135
  15.4 5.0 %collective-permute-start.11 = (bf16[520,128]{1,0:T(8,128)(2,1)S(1)}, bf16[520,128]{1,0:T(8,128)(2,1)S(1)}, u32[]{:S(2)}, u32[]{:S(2)}) collective-permute-start(bf16[520,128]{1,0:T(8,128)(2,1)S(1)} %collective-permute-done.7.refs_10_), channel_id=1, source_target_pairs={{8,0},{9,1},{10,2},{11,3},{12,4},{13,5},{14,6},{15,7},{0,8},{1,9},... | collective-permute-start | bytes 399368 | tf_op jit(solution)/shard_map/ppermute | solution.py:135
  17.8 5.4 %collective-permute-start.10 = (f32[1,128]{1,0:T(1,128)S(1)}, f32[1,128]{1,0:T(1,128)S(1)}, u32[]{:S(2)}, u32[]{:S(2)}) collective-permute-start(f32[1,128]{1,0:T(1,128)S(1)} %get-tuple-element.24), channel_id=1, source_target_pairs={{24,0},{25,1},{26,2},{27,3},{28,4},{29,5},{30,6},{31,7},{16,8},{17... | collective-permute-start | bytes 1544 | tf_op jit(solution)/shard_map/ppermute | solution.py:135
  19.6 3.6 %collective-permute-start.9 = (f32[1,128]{1,0:T(1,128)S(1)}, f32[1,128]{1,0:T(1,128)S(1)}, u32[]{:S(2)}, u32[]{:S(2)}) collective-permute-start(f32[1,128]{1,0:T(1,128)S(1)} %get-tuple-element.23), channel_id=1, source_target_pairs={{8,0},{9,1},{10,2},{11,3},{12,4},{13,5},{14,6},{15,7},{0,8},{1,9},... | collective-permute-start | bytes 1544 | tf_op jit(solution)/shard_map/ppermute | solution.py:135
  20.8 4.5 %collective-permute-start.12 = (f32[1,128]{1,0:T(1,128)S(1)}, f32[1,128]{1,0:T(1,128)S(1)}, u32[]{:S(2)}, u32[]{:S(2)}) collective-permute-start(f32[1,128]{1,0:T(1,128)S(1)} %shard_map.39), channel_id=1, source_target_pairs={{16,0},{17,1},{18,2},{19,3},{20,4},{21,5},{22,6},{23,7},{24,8},{25... | collective-permute-start | bytes 1544 | tf_op jit(solution)/shard_map/ppermute | solution.py:135

commit v33 on v30

--- a/solution.py
+++ b/solution.py
@@ -95,7 +95,16 @@
             outs[j][...] = best
 
     width = n_keys // n_spans
-    search(range(width), True)
+    if own:
+        search(range(width), True)
+    else:
+        for out in outs:
+            out[...] = jnp.full((1, rows), -1.0, jnp.float32)
+
+        @pl.when(functools.reduce(jnp.maximum, ranks[n_keys:]) > ranks[0])
+        def _():
+            search(range(width), False)
+
     for t in range(1, n_spans):
         @pl.when(ranks[t * width] < ranks[0])
         def _():

time: 26 us -> 26 us (level)
  starting transfers between devices: 14.6 us -> 14.1 us
  waiting for transfers between devices: 8.35 us -> 8.8 us
    ppermute x13, waiting for transfers between devices: 8.35 us -> 8.8 us  [permute(): return lax.ppermute(x, ('clu', 'grp'), pairs)]
    ppermute x13, starting transfers between devices: 14.6 us -> 14.1 us  [permute(): return lax.ppermute(x, ('clu', 'grp'), pairs)]
where the time goes in v33:
time: 26 us; the launch traced here: 25.9 us
  starting transfers between devices  14.1 us (54%)
  waiting for transfers between devices  8.8 us (34%)
  Pallas kernels  2.44 us (9%)
  other arithmetic  0.52 us (2%)
    ppermute x13, starting transfers between devices, permute(): return lax.ppermute(x, ('clu', 'grp'), pairs)  14.1 us
    ppermute x13, waiting for transfers between devices, permute(): return lax.ppermute(x, ('clu', 'grp'), pairs)  8.8 us
    pallas_call x2, Pallas kernels, best_of(): pl.pallas_call(functools.partial(best_kernel, rows, len(keys), n_spans, o...  1.33 us
    pallas_call x1, Pallas kernels, pack(): pl.pallas_call(functools.partial(pack_kernel, groups), out_shape=[pltpu.V...  1.1 us
  transfers between devices with their start and end apart: 13, of which 6 were waited for; matrix products, arithmetic and copies ran while one was open for 0% of the time, Pallas kernels for 5%

profile of v33, /device:TPU:0, one launch (start us, length us, event | category | flops | bytes accessed | tf_op | source)
XLA Modules:
  0.0 25.9 jit_solution(9245846989360238581)
XLA Ops:
  0.0 1.1 %shard_map.37 = (bf16[520,128]{1,0:T(8,128)(2,1)S(1)}, bf16[64,64]{1,0:T(8,128)(2,1)S(1)}) custom-call(bf16[128,512]{1,0:T(8,128)(2,1)} %emb_ref.1, s32[1,128]{1,0:T(1,128)} %bitcast.4, s32[1,64]{1,0:T(1,128)} %bitcast.5), custom_call_target="tpu_custom_call" | custom-call | tf_op jit(solution)/shard_map/pallas_call | solution.py:42
  1.1 3.0 %collective-permute-start = (bf16[520,128]{1,0:T(8,128)(2,1)S(1)}, bf16[520,128]{1,0:T(8,128)(2,1)S(1)}, u32[]{:S(2)}, u32[]{:S(2)}) collective-permute-start(bf16[520,128]{1,0:T(8,128)(2,1)S(1)} %get-tuple-element.16.refs_0_.refs_8_), channel_id=1, source_target_pairs={{2,0},{3,1},{0,2},{1,3},{6,4},{7,5},{4,6},{5,7},{10,8},{11,9},{8,1... | collective-permute-start | bytes 399368 | tf_op jit(solution)/shard_map/ppermute | solution.py:144
  4.1 1.5 %collective-permute-start.1 = (bf16[520,128]{1,0:T(8,128)(2,1)S(1)}, bf16[520,128]{1,0:T(8,128)(2,1)S(1)}, u32[]{:S(2)}, u32[]{:S(2)}) collective-permute-start(bf16[520,128]{1,0:T(8,128)(2,1)S(1)} %get-tuple-element.16.refs_0_.refs_8_), channel_id=1, source_target_pairs={{4,0},{5,1},{6,2},{7,3},{0,4},{1,5},{2,6},{3,7},{12,8},{13,9},{14,... | collective-permute-start | bytes 399368 | tf_op jit(solution)/shard_map/ppermute | solution.py:144
  5.6 0.0 collective-permute-start.2
  5.7 4.1 %collective-permute-start.7 = (bf16[520,128]{1,0:T(8,128)(2,1)S(1)}, bf16[520,128]{1,0:T(8,128)(2,1)S(1)}, u32[]{:S(2)}, u32[]{:S(2)}) collective-permute-start(bf16[520,128]{1,0:T(8,128)(2,1)S(1)} %get-tuple-element.16.refs_0_.refs_8_), channel_id=1, source_target_pairs={{24,0},{25,1},{26,2},{27,3},{28,4},{29,5},{30,6},{31,7},{16,8},{17... | collective-permute-start | bytes 399368 | tf_op jit(solution)/shard_map/ppermute | solution.py:144
  9.7 0.0 collective-permute-start.8
  9.7 0.0 collective-permute-done.refs_1_
  9.7 0.0 collective-permute-start.3
  9.7 2.2 %collective-permute-done.1.refs_2_ = bf16[520,128]{1,0:T(8,128)(2,1)S(1)} collective-permute-done((bf16[520,128]{1,0:T(8,128)(2,1)S(1)}, bf16[520,128]{1,0:T(8,128)(2,1)S(1)}, u32[]{:S(2)}, u32[]{:S(2)}) %collective-permute-start.1) | collective-permute-done | bytes 133152 | tf_op jit(solution)/shard_map/ppermute | solution.py:144
  12.0 0.0 collective-permute-done.2.refs_3_
  12.0 0.0 collective-permute-start.4
  12.0 0.5 %collective-permute-start.5 = (bf16[520,128]{1,0:T(8,128)(2,1)S(1)}, bf16[520,128]{1,0:T(8,128)(2,1)S(1)}, u32[]{:S(2)}, u32[]{:S(2)}) collective-permute-start(bf16[520,128]{1,0:T(8,128)(2,1)S(1)} %collective-permute-done.1.refs_2_), channel_id=1, source_target_pairs={{1,0},{0,1},{3,2},{2,3},{5,4},{4,5},{7,6},{6,7},{9,8},{8,9},{11,10... | collective-permute-start | bytes 399368 | tf_op jit(solution)/shard_map/ppermute | solution.py:144
  12.5 1.4 %collective-permute-done.7.refs_10_ = bf16[520,128]{1,0:T(8,128)(2,1)S(1)} collective-permute-done((bf16[520,128]{1,0:T(8,128)(2,1)S(1)}, bf16[520,128]{1,0:T(8,128)(2,1)S(1)}, u32[]{:S(2)}, u32[]{:S(2)}) %collective-permute-start.7) | collective-permute-done | bytes 133152 | tf_op jit(solution)/shard_map/ppermute | solution.py:144
  13.9 0.0 collective-permute-start.6
  13.9 1.4 %collective-permute-done.8.refs_9_ = bf16[520,128]{1,0:T(8,128)(2,1)S(1)} collective-permute-done((bf16[520,128]{1,0:T(8,128)(2,1)S(1)}, bf16[520,128]{1,0:T(8,128)(2,1)S(1)}, u32[]{:S(2)}, u32[]{:S(2)}) %collective-permute-start.8) | collective-permute-done | bytes 133152 | tf_op jit(solution)/shard_map/ppermute | solution.py:144
  15.4 1.6 %collective-permute-start.11 = (bf16[520,128]{1,0:T(8,128)(2,1)S(1)}, bf16[520,128]{1,0:T(8,128)(2,1)S(1)}, u32[]{:S(2)}, u32[]{:S(2)}) collective-permute-start(bf16[520,128]{1,0:T(8,128)(2,1)S(1)} %collective-permute-done.7.refs_10_), channel_id=1, source_target_pairs={{8,0},{9,1},{10,2},{11,3},{12,4},{13,5},{14,6},{15,7},{0,8},{1,9},... | collective-permute-start | bytes 399368 | tf_op jit(solution)/shard_map/ppermute | solution.py:144
  17.0 0.0 collective-permute-done.3.refs_4_
  17.0 0.0 collective-permute-done.4.refs_5_
  17.0 0.0 collective-permute-done.5.refs_6_
  17.0 0.0 collective-permute-done.6.refs_7_
  17.0 0.8 %shard_map.38 = (f32[1,128]{1,0:T(1,128)S(1)}, f32[1,128]{1,0:T(1,128)S(1)}, f32[1,128]{1,0:T(1,128)S(1)}) custom-call(bf16[64,64]{1,0:T(8,128)(2,1)S(1)} %get-tuple-element.15.table_ref, bf16[520,128]{1,0:T(8,128)(2,1)S(1)} %get-tuple-element.16.refs_0_.refs_8_, bf16[520,128]{1,0:T(8,128)(2,1)S(1)} %collective-permute-done.refs_1_, ...), custom_call_target="tpu_custom_call" | custom-call | flops 402653184 | bytes 1441792 | tf_op jit(solution)/shard_map/pallas_call | solution.py:119
  17.8 1.8 %collective-permute-start.10 = (f32[1,128]{1,0:T(1,128)S(1)}, f32[1,128]{1,0:T(1,128)S(1)}, u32[]{:S(2)}, u32[]{:S(2)}) collective-permute-start(f32[1,128]{1,0:T(1,128)S(1)} %get-tuple-element.24), channel_id=1, source_target_pairs={{24,0},{25,1},{26,2},{27,3},{28,4},{29,5},{30,6},{31,7},{16,8},{17... | collective-permute-start | bytes 1544 | tf_op jit(solution)/shard_map/ppermute | solution.py:144
  19.6 0.0 collective-permute-start.9
  19.6 0.7 %collective-permute-done.11.refs_8_ = bf16[520,128]{1,0:T(8,128)(2,1)S(1)} collective-permute-done((bf16[520,128]{1,0:T(8,128)(2,1)S(1)}, bf16[520,128]{1,0:T(8,128)(2,1)S(1)}, u32[]{:S(2)}, u32[]{:S(2)}) %collective-permute-start.11) | collective-permute-done | bytes 133152 | tf_op jit(solution)/shard_map/ppermute | solution.py:144
  20.4 0.5 %shard_map.39 = f32[1,128]{1,0:T(1,128)S(1)} custom-call(bf16[64,64]{1,0:T(8,128)(2,1)S(1)} %get-tuple-element.15.table_ref, bf16[520,128]{1,0:T(8,128)(2,1)S(1)} %get-tuple-element.16.refs_0_.refs_8_, bf16[520,128]{1,0:T(8,128)(2,1)S(1)} %collective-permute-done.refs_1_, bf16[520,128]{1,0:T(8,128)(2,1)S(1)} %collective-permute-done.1.refs_2_, ...), custom_call_target="tpu_custom_call" | custom-call | flops 134217728 | bytes 1179648 | tf_op jit(solution)/shard_map/pallas_call | solution.py:119
  20.9 1.6 %collective-permute-start.12 = (f32[1,128]{1,0:T(1,128)S(1)}, f32[1,128]{1,0:T(1,128)S(1)}, u32[]{:S(2)}, u32[]{:S(2)}) collective-permute-start(f32[1,128]{1,0:T(1,128)S(1)} %shard_map.39), channel_id=1, source_target_pairs={{16,0},{17,1},{18,2},{19,3},{20,4},{21,5},{22,6},{23,7},{24,8},{25... | collective-permute-start | bytes 1544 | tf_op jit(solution)/shard_map/ppermute | solution.py:144
  22.4 0.8 %collective-permute-done.10 = f32[1,128]{1,0:T(1,128)S(1)} collective-permute-done((f32[1,128]{1,0:T(1,128)S(1)}, f32[1,128]{1,0:T(1,128)S(1)}, u32[]{:S(2)}, u32[]{:S(2)}) %collective-permute-start.10) | collective-permute-done | bytes 544 | tf_op jit(solution)/shard_map/ppermute | solution.py:144
  23.3 0.0 collective-permute-done.9
  23.3 2.1 %collective-permute-done.12 = f32[1,128]{1,0:T(1,128)S(1)} collective-permute-done((f32[1,128]{1,0:T(1,128)S(1)}, f32[1,128]{1,0:T(1,128)S(1)}, u32[]{:S(2)}, u32[]{:S(2)}) %collective-permute-start.12) | collective-permute-done | bytes 544 | tf_op jit(solution)/shard_map/ppermute | solution.py:144
  25.4 0.5 %maximum_bitcast_fusion = f32[128]{0:T(128)} fusion(f32[1,128]{1,0:T(1,128)S(1)} %collective-permute-done.12, f32[1,128]{1,0:T(1,128)S(1)} %collective-permute-done.10, f32[1,128]{1,0:T(1,128)S(1)} %get-tuple-element.22, f32[1,128]{1,0:T(1,128)S(1)} %collective-permute-done.9), kind=kLoop, calls=%fused_computation | loop fusion | flops 384 | bytes 2560 | tf_op jit(solution)/shard_map/reshape | solution.py:189
Async XLA Ops:
  1.1 8.6 %collective-permute-start = (bf16[520,128]{1,0:T(8,128)(2,1)S(1)}, bf16[520,128]{1,0:T(8,128)(2,1)S(1)}, u32[]{:S(2)}, u32[]{:S(2)}) collective-permute-start(bf16[520,128]{1,0:T(8,128)(2,1)S(1)} %get-tuple-element.16.refs_0_.refs_8_), channel_id=1, source_target_pairs={{2,0},{3,1},{0,2},{1,3},{6,4},{7,5},{4,6},{5,7},{10,8},{11,9},{8,1... | collective-permute-start | bytes 399368 | tf_op jit(solution)/shard_map/ppermute | solution.py:144
  4.1 7.9 %collective-permute-start.1 = (bf16[520,128]{1,0:T(8,128)(2,1)S(1)}, bf16[520,128]{1,0:T(8,128)(2,1)S(1)}, u32[]{:S(2)}, u32[]{:S(2)}) collective-permute-start(bf16[520,128]{1,0:T(8,128)(2,1)S(1)} %get-tuple-element.16.refs_0_.refs_8_), channel_id=1, source_target_pairs={{4,0},{5,1},{6,2},{7,3},{0,4},{1,5},{2,6},{3,7},{12,8},{13,9},{14,... | collective-permute-start | bytes 399368 | tf_op jit(solution)/shard_map/ppermute | solution.py:144
  5.6 6.3 %collective-permute-start.2 = (bf16[520,128]{1,0:T(8,128)(2,1)S(1)}, bf16[520,128]{1,0:T(8,128)(2,1)S(1)}, u32[]{:S(2)}, u32[]{:S(2)}) collective-permute-start(bf16[520,128]{1,0:T(8,128)(2,1)S(1)} %get-tuple-element.16.refs_0_.refs_8_), channel_id=1, source_target_pairs={{6,0},{7,1},{4,2},{5,3},{2,4},{3,5},{0,6},{1,7},{14,8},{15,9},{12,... | collective-permute-start | bytes 399368 | tf_op jit(solution)/shard_map/ppermute | solution.py:144
  5.7 8.3 %collective-permute-start.7 = (bf16[520,128]{1,0:T(8,128)(2,1)S(1)}, bf16[520,128]{1,0:T(8,128)(2,1)S(1)}, u32[]{:S(2)}, u32[]{:S(2)}) collective-permute-start(bf16[520,128]{1,0:T(8,128)(2,1)S(1)} %get-tuple-element.16.refs_0_.refs_8_), channel_id=1, source_target_pairs={{24,0},{25,1},{26,2},{27,3},{28,4},{29,5},{30,6},{31,7},{16,8},{17... | collective-permute-start | bytes 399368 | tf_op jit(solution)/shard_map/ppermute | solution.py:144
  9.7 5.7 %collective-permute-start.8 = (bf16[520,128]{1,0:T(8,128)(2,1)S(1)}, bf16[520,128]{1,0:T(8,128)(2,1)S(1)}, u32[]{:S(2)}, u32[]{:S(2)}) collective-permute-start(bf16[520,128]{1,0:T(8,128)(2,1)S(1)} %get-tuple-element.16.refs_0_.refs_8_), channel_id=1, source_target_pairs={{8,0},{9,1},{10,2},{11,3},{12,4},{13,5},{14,6},{15,7},{0,8},{1,9},... | collective-permute-start | bytes 399368 | tf_op jit(solution)/shard_map/ppermute | solution.py:144
  9.7 7.3 %collective-permute-start.3 = (bf16[520,128]{1,0:T(8,128)(2,1)S(1)}, bf16[520,128]{1,0:T(8,128)(2,1)S(1)}, u32[]{:S(2)}, u32[]{:S(2)}) collective-permute-start(bf16[520,128]{1,0:T(8,128)(2,1)S(1)} %get-tuple-element.16.refs_0_.refs_8_), channel_id=1, source_target_pairs={{1,0},{0,1},{3,2},{2,3},{5,4},{4,5},{7,6},{6,7},{9,8},{8,9},{11,10... | collective-permute-start | bytes 399368 | tf_op jit(solution)/shard_map/ppermute | solution.py:144
  12.0 5.0 %collective-permute-start.4 = (bf16[520,128]{1,0:T(8,128)(2,1)S(1)}, bf16[520,128]{1,0:T(8,128)(2,1)S(1)}, u32[]{:S(2)}, u32[]{:S(2)}) collective-permute-start(bf16[520,128]{1,0:T(8,128)(2,1)S(1)} %collective-permute-done.refs_1_), channel_id=1, source_target_pairs={{1,0},{0,1},{3,2},{2,3},{5,4},{4,5},{7,6},{6,7},{9,8},{8,9},{11,10... | collective-permute-start | bytes 399368 | tf_op jit(solution)/shard_map/ppermute | solution.py:144
  12.0 5.0 %collective-permute-start.5 = (bf16[520,128]{1,0:T(8,128)(2,1)S(1)}, bf16[520,128]{1,0:T(8,128)(2,1)S(1)}, u32[]{:S(2)}, u32[]{:S(2)}) collective-permute-start(bf16[520,128]{1,0:T(8,128)(2,1)S(1)} %collective-permute-done.1.refs_2_), channel_id=1, source_target_pairs={{1,0},{0,1},{3,2},{2,3},{5,4},{4,5},{7,6},{6,7},{9,8},{8,9},{11,10... | collective-permute-start | bytes 399368 | tf_op jit(solution)/shard_map/ppermute | solution.py:144
  13.9 3.1 %collective-permute-start.6 = (bf16[520,128]{1,0:T(8,128)(2,1)S(1)}, bf16[520,128]{1,0:T(8,128)(2,1)S(1)}, u32[]{:S(2)}, u32[]{:S(2)}) collective-permute-start(bf16[520,128]{1,0:T(8,128)(2,1)S(1)} %collective-permute-done.2.refs_3_), channel_id=1, source_target_pairs={{1,0},{0,1},{3,2},{2,3},{5,4},{4,5},{7,6},{6,7},{9,8},{8,9},{11,10... | collective-permute-start | bytes 399368 | tf_op jit(solution)/shard_map/ppermute | solution.py:144
  15.4 5.0 %collective-permute-start.11 = (bf16[520,128]{1,0:T(8,128)(2,1)S(1)}, bf16[520,128]{1,0:T(8,128)(2,1)S(1)}, u32[]{:S(2)}, u32[]{:S(2)}) collective-permute-start(bf16[520,128]{1,0:T(8,128)(2,1)S(1)} %collective-permute-done.7.refs_10_), channel_id=1, source_target_pairs={{8,0},{9,1},{10,2},{11,3},{12,4},{13,5},{14,6},{15,7},{0,8},{1,9},... | collective-permute-start | bytes 399368 | tf_op jit(solution)/shard_map/ppermute | solution.py:144
  17.8 5.4 %collective-permute-start.10 = (f32[1,128]{1,0:T(1,128)S(1)}, f32[1,128]{1,0:T(1,128)S(1)}, u32[]{:S(2)}, u32[]{:S(2)}) collective-permute-start(f32[1,128]{1,0:T(1,128)S(1)} %get-tuple-element.24), channel_id=1, source_target_pairs={{24,0},{25,1},{26,2},{27,3},{28,4},{29,5},{30,6},{31,7},{16,8},{17... | collective-permute-start | bytes 1544 | tf_op jit(solution)/shard_map/ppermute | solution.py:144
  19.6 3.6 %collective-permute-start.9 = (f32[1,128]{1,0:T(1,128)S(1)}, f32[1,128]{1,0:T(1,128)S(1)}, u32[]{:S(2)}, u32[]{:S(2)}) collective-permute-start(f32[1,128]{1,0:T(1,128)S(1)} %get-tuple-element.23), channel_id=1, source_target_pairs={{8,0},{9,1},{10,2},{11,3},{12,4},{13,5},{14,6},{15,7},{0,8},{1,9},... | collective-permute-start | bytes 1544 | tf_op jit(solution)/shard_map/ppermute | solution.py:144
  20.9 4.5 %collective-permute-start.12 = (f32[1,128]{1,0:T(1,128)S(1)}, f32[1,128]{1,0:T(1,128)S(1)}, u32[]{:S(2)}, u32[]{:S(2)}) collective-permute-start(f32[1,128]{1,0:T(1,128)S(1)} %shard_map.39), channel_id=1, source_target_pairs={{16,0},{17,1},{18,2},{19,3},{20,4},{21,5},{22,6},{23,7},{24,8},{25... | collective-permute-start | bytes 1544 | tf_op jit(solution)/shard_map/ppermute | solution.py:144
